TPU v7x, 256 devices: a whole 4x4x8 slice. The times are simulated.
256 devices in a mesh: grp: 16 (over y_hi, z), tp: 16 (over y_lo, x, core).
Axes of the slice: x: 4, y: 4 (y_hi: 2, y_lo: 2; y = y_hi * 2 + y_lo), z: 8, core: 2. Of those that a mesh axis runs over, the one named last changes fastest.
Arguments:
- attention_output: bfloat16 [8192, 8192], P('grp', 'tp'), parts along dimension 0, may hold values from -6 to 6
- output_projection_weight: bfloat16 [8192, 8192], P('tp'), may hold values from -0.0625 to 0.0625
- residual: bfloat16 [512, 131072], P('tp', 'grp'), parts along dimension 1, may hold values from -6 to 6
- resident_down_maps: bfloat16 [8192, 16384], P('tp', 'grp'), parts along dimension 1, may hold values from -0.0625 to 0.0625
- resident_up_maps: bfloat16 [16384, 8192], P('grp', 'tp'), parts along dimension 0, may hold values from -0.75 to 0.75
- fresh_adapter_bundle: bfloat16 [256, 4096, 128], P(('grp', 'tp')), parts along dimension 0, as said below
- fresh_slot_targets: int32 [256], P('grp'), parts along dimension 0, may hold values from 0 to 15, each once
- request_adapter_slot: int32 [8192], P('grp'), parts along dimension 0, may hold values from 0 to 15
Outputs:
- hidden: bfloat16 [512, 131072], P('tp', 'grp'), parts along dimension 1
There are 16 independent parts, one for each index of `grp`. A program takes and returns all parts, laid end to end along the dimension named above; an argument that names none is the same for every part. Nothing has to cross between parts.
Inputs may be any that keep to these rules, and one draw needn't show every extreme that they name: `fresh_adapter_bundle`: entries 2k hold down maps of deviation about 8192 ** -0.5, entries 2k + 1 up maps of deviation about 64 ** -0.5.
All inputs are finite; a program needn't handle non-finite values.
Results may differ from a plain program's by a relative error of at most 0.0055.
Values may be sent and summed in bfloat16 or wider, within the bound.
No kernel may reach another device: no remote copies, remote signals or barrier semaphores. Data moves between devices by JAX's collectives and lax.ppermute only.
A program may use at most 128 MiB of HBM per device.

v0:
```python
import jax
import jax.numpy as jnp
from jax import lax
from jax.experimental import pallas as pl
from jax.experimental.pallas import tpu as pltpu
from jax.sharding import PartitionSpec as P

RANK = 64
SLOTS = 16
CHIPS = 8
SCALE = 0.5
F32 = jnp.float32
BF16 = jnp.bfloat16
WIDE = 4608
VMEM_LIMIT = 40 * 1024 * 1024
PRODUCT_LIMIT = 56 * 1024 * 1024


def place(y, x, core):
    return ((y % 2) * 4 + x % 4) * 2 + core % 2


def route(yy, xx, cc):
    return [
        (place(y, x, c), place(y + yy, x + xx, c + cc))
        for y in range(2)
        for x in range(4)
        for c in range(2)
    ]


def send(array, yy, xx, cc):
    return lax.ppermute(array, "tp", route(yy, xx, cc))


def spot():
    t = lax.axis_index("tp")
    return t // 8, lax.rem(t // 2, 4), lax.rem(t, 2)


def partner(yy, xx, cc):
    y, x, c = spot()
    return (lax.rem(y + yy, 2) * 4 + lax.rem(x + xx, 4)) * 2 + lax.rem(c + cc, 2)


def rows_at(index, size):
    return pl.ds(pl.multiple_of(index * size, size), size)


def whole(shape, dtype):
    return jax.ShapeDtypeStruct(shape, dtype)


def plus(a, *others):
    total = a.astype(F32)
    for other in others:
        total = total + other.astype(F32)
    return total


VM = pl.BlockSpec(memory_space=pltpu.VMEM)
SM = pl.BlockSpec(memory_space=pltpu.SMEM)
LATER = pl.BlockSpec(memory_space=pl.ANY)


def call(kernel, name, out_shape, args, specs=None, after=(), limit=VMEM_LIMIT, **options):
    count = len(args)

    def body(*refs):
        kernel(*refs[:count], *refs[count + len(after) :])

    return pl.pallas_call(
        body,
        in_specs=list(specs or [VM] * count) + [LATER] * len(after),
        out_shape=out_shape,
        compiler_params=pltpu.CompilerParams(vmem_limit_bytes=limit),
        name=name,
        **options,
    )(*args, *after)


X_MAJOR = [(yy, xx) for xx in range(4) for yy in range(2)]
Y_MAJOR = [(yy, xx) for yy in range(2) for xx in range(4)]


def product(x, w, order, cc, first, width, tile, after=()):
    def kernel(x_ref, w_ref, out_ref, rows_ref):
        @pl.when(pl.program_id(0) == 0)
        def _():
            for i, (yy, xx) in enumerate(order):
                rows_ref[i * 32 : (i + 1) * 32, :] = x_ref[rows_at(partner(yy, xx, cc), 32), :]

        out_ref[...] = jnp.dot(
            rows_ref[...], w_ref[...], preferred_element_type=F32
        ).astype(BF16)

    return call(
        kernel,
        "product",
        whole((256, width), BF16),
        (x, w),
        [
            pl.BlockSpec((512, 512), lambda j: (0, 0)),
            pl.BlockSpec(
                (pl.Element(512), pl.Element(tile)),
                lambda j: (0, (first // 128 + j * (tile // 128)) * 128),
            ),
        ],
        after,
        limit=PRODUCT_LIMIT,
        grid=(width // tile,),
        out_specs=pl.BlockSpec((256, tile), lambda j: (0, j)),
        scratch_shapes=[pltpu.VMEM((256, 512), BF16)],
    )


def chip_narrow(own, away, after=()):
    width = own.shape[1]
    tile = width // 4

    def kernel(own_ref, away_ref, keep_ref, send_ref):
        total = plus(own_ref[...], away_ref[...]).astype(BF16)
        keep_ref[...] = total[:128]
        send_ref[...] = total[128:]

    piece = pl.BlockSpec((256, tile), lambda j: (0, j))
    half = pl.BlockSpec((128, tile), lambda j: (0, j))
    return call(
        kernel,
        "chip_narrow",
        [whole((128, width), BF16)] * 2,
        (own, away),
        [piece, piece],
        after,
        grid=(4,),
        out_specs=[half, half],
    )


def chip_wide(own, away, after=()):
    width = own.shape[1]
    tile = width // 4

    def kernel(own_ref, away_ref, here_ref, right_ref, left_ref, far_right_ref, far_left_ref):
        j = pl.program_id(0)
        total = plus(own_ref[...], away_ref[...]).astype(BF16)
        here_ref[...] = total[:64]
        right_ref[...] = total[64:128]
        left_ref[...] = total[192:]

        @pl.when(j < 2)
        def _():
            far_right_ref[...] = total[128:192]

        @pl.when(j >= 2)
        def _():
            far_left_ref[...] = total[128:192]

    piece = pl.BlockSpec((256, tile), lambda j: (0, j))
    block = pl.BlockSpec((64, tile), lambda j: (0, j))
    return call(
        kernel,
        "chip_wide",
        [whole((64, width), BF16)] * 3 + [whole((64, width // 2), BF16)] * 2,
        (own, away),
        [piece, piece],
        after,
        grid=(4,),
        out_specs=[block] * 3
        + [
            pl.BlockSpec((64, tile), lambda j: (0, jnp.minimum(j, 1))),
            pl.BlockSpec((64, tile), lambda j: (0, jnp.maximum(j - 2, 0))),
        ],
    )


def turn_narrow(keep, landed, after=()):
    width = keep.shape[1]
    half = width // 2

    def kernel(keep_ref, landed_ref, here_ref, right_ref, left_ref, far_right_ref, far_left_ref):
        total = plus(keep_ref[...], landed_ref[...]).astype(BF16)
        here_ref[...] = total[:32]
        right_ref[...] = total[32:64]
        left_ref[...] = total[96:]
        far_right_ref[...] = total[64:96, :half]
        far_left_ref[...] = total[64:96, half:]

    return call(
        kernel,
        "turn_narrow",
        [whole((32, width), BF16)] * 3 + [whole((32, half), BF16)] * 2,
        (keep, landed),
        after=after,
    )


def near(right, left, far_right, far_left, after=()):
    half = right.shape[1] // 2

    def kernel(right_ref, left_ref, far_right_ref, far_left_ref, to_right_ref, to_left_ref):
        to_right_ref[:, :half] = plus(right_ref[:, :half], far_right_ref[...]).astype(BF16)
        to_right_ref[:, half:] = right_ref[:, half:]
        to_left_ref[:, :half] = left_ref[:, :half]
        to_left_ref[:, half:] = plus(left_ref[:, half:], far_left_ref[...]).astype(BF16)

    return call(
        kernel, "near", [whole(right.shape, BF16)] * 2, (right, left, far_right, far_left), after=after
    )


def turn_wide(here, from_left, from_right, after=()):
    width = here.shape[1]

    def kernel(here_ref, from_left_ref, from_right_ref, keep_ref, send_ref):
        total = plus(here_ref[...], from_left_ref[...], from_right_ref[...])
        keep_ref[...] = total[:32]
        send_ref[...] = total[32:].astype(BF16)

    return call(
        kernel,
        "turn_wide",
        [whole((32, width), F32), whole((32, width), BF16)],
        (here, from_left, from_right),
        after=after,
    )


def add_parts(parts, after=()):
    def kernel(*refs):
        refs[-1][...] = plus(*[ref[...] for ref in refs[:-1]]).astype(BF16)

    return call(kernel, "add_parts", whole(parts[0].shape, BF16), parts, after=after)


def lanes(rows):
    return lax.broadcasted_iota(jnp.int32, (rows, 128), 1)


def resident_slot(slot, target_ref):
    for k in range(CHIPS):
        slot = jnp.where(slot == target_ref[k], -1, slot)
    return slot


def shrink_resident_kernel(x_ref, down_ref, slot_ref, target_ref, acc_ref, split_ref):
    x = x_ref[...]
    row = lax.broadcasted_iota(jnp.int32, (512, 512), 0)
    col = lax.broadcasted_iota(jnp.int32, (512, 512), 1)
    source = jnp.where(col < 256, 2 * col, 2 * (col - 256) + 1)
    chooser = jnp.where(row == source, 1.0, 0.0).astype(BF16)
    split_ref[...] = jnp.dot(x, chooser, preferred_element_type=F32).astype(BF16)
    slot = jnp.broadcast_to(resident_slot(slot_ref[...], target_ref), (512, 128))
    high = (lanes(512) >= RANK).astype(jnp.int32)
    acc = jnp.zeros((512, 128), F32)
    for j in range(CHIPS):
        part = jnp.dot(x, down_ref[:, j * 128 : (j + 1) * 128], preferred_element_type=F32)
        acc += jnp.where(slot == 2 * j + high, part, 0.0)
    acc_ref[...] = acc


def shrink_resident(x, down, slot, target, after=()):
    return call(
        shrink_resident_kernel,
        "shrink_resident",
        [whole((512, 128), F32), whole((512, 512), BF16)],
        (x, down, slot, target),
        [VM, VM, VM, SM],
        after,
    )


def shrink_fresh_kernel(split_ref, acc_ref, slot_ref, target_ref, maps_ref, out_ref):
    even, odd = split_ref[:, :256], split_ref[:, 256:]
    slot = jnp.broadcast_to(slot_ref[...], (512, 128))
    low = lanes(512) < RANK
    acc = acc_ref[...]
    for k in range(CHIPS):
        maps = maps_ref[2 * k]
        part = jnp.where(
            low,
            jnp.dot(even, maps, preferred_element_type=F32),
            jnp.dot(odd, maps, preferred_element_type=F32),
        )
        acc += jnp.where(slot == target_ref[k], part, 0.0)
    acc = acc + pltpu.roll(acc, RANK, 1)
    out_ref[...] = jnp.where(lanes(256) < RANK, acc[:256], acc[256:]).astype(BF16)


def shrink_fresh(split, acc, slot, target, maps, after=()):
    return call(
        shrink_fresh_kernel,
        "shrink_fresh",
        whole((256, 128), BF16),
        (split, acc, slot, target, maps),
        [VM, VM, VM, SM, VM],
        after,
    )


def raise_kernel(mine_ref, other_ref, up_ref, slot_ref, target_ref, maps_ref, out_ref):
    packed = (mine_ref[...].astype(F32) + other_ref[...].astype(F32)).astype(BF16).astype(F32)
    turned = pltpu.roll(packed, RANK, 1)
    left = lanes(256) < RANK
    both = jnp.concatenate(
        [jnp.where(left, packed, turned), jnp.where(left, turned, packed)], axis=0
    )
    slot = jnp.broadcast_to(slot_ref[...], (512, 128))
    kept = resident_slot(slot, target_ref)
    high = (lanes(512) >= RANK).astype(jnp.int32)
    total = jnp.zeros((512, 512), F32)
    for j in range(CHIPS):
        raised = jnp.where(kept == 2 * j + high, both, 0.0).astype(BF16)
        total += jnp.dot(raised, up_ref[j * 128 : (j + 1) * 128, :], preferred_element_type=F32)
    even = jnp.zeros((512, 256), F32)
    odd = jnp.zeros((512, 256), F32)
    turn = (((1,), (1,)), ((), ()))
    for k in range(CHIPS):
        maps = maps_ref[2 * k + 1]
        fresh = jnp.where(slot == target_ref[k], both, 0.0)
        even += lax.dot_general(
            jnp.where(high == 0, fresh, 0.0).astype(BF16), maps, turn, preferred_element_type=F32
        )
        odd += lax.dot_general(
            jnp.where(high == 1, fresh, 0.0).astype(BF16), maps, turn, preferred_element_type=F32
        )
    row = lax.broadcasted_iota(jnp.int32, (256, 512), 0)
    col = lax.broadcasted_iota(jnp.int32, (256, 512), 1)
    to_even = jnp.where(col == 2 * row, 1.0, 0.0).astype(BF16)
    to_odd = jnp.where(col == 2 * row + 1, 1.0, 0.0).astype(BF16)
    total += jnp.dot(even.astype(BF16), to_even, preferred_element_type=F32)
    total += jnp.dot(odd.astype(BF16), to_odd, preferred_element_type=F32)
    out_ref[...] = (SCALE * total).astype(BF16).reshape(16, 32, 512)


def raise_features(mine, other, up, slot, target, maps, after=()):
    return call(
        raise_kernel,
        "raise_features",
        whole((16, 32, 512), BF16),
        (mine, other, up, slot, target, maps),
        [VM, VM, VM, VM, SM, VM],
        after,
    )


def finish_kernel(
    residual_ref, wide_ref, wide_y_ref, narrow_ref, narrow_left_ref, narrow_right_ref, delta_ref, out_ref
):
    for t in range(16):
        cols = slice(t * 512, (t + 1) * 512)
        if (t + 1) * 512 <= WIDE:
            base = wide_ref[:, cols] + wide_y_ref[:, cols].astype(F32)
        else:
            part = slice(t * 512 - WIDE, (t + 1) * 512 - WIDE)
            base = plus(narrow_ref[:, part], narrow_left_ref[:, part], narrow_right_ref[:, part])
        out_ref[:, cols] = (
            residual_ref[:, cols].astype(F32) + base + delta_ref[t].astype(F32)
        ).astype(BF16)


def local(
    attention_output,
    output_projection_weight,
    residual,
    resident_down_maps,
    resident_up_maps,
    fresh_adapter_bundle,
    fresh_slot_targets,
    request_adapter_slot,
):
    x, w = attention_output, output_projection_weight
    slot = request_adapter_slot.reshape(512, 1)
    target = fresh_slot_targets

    maps = lax.all_to_all(
        fresh_adapter_bundle.reshape(16, 256, 128), "tp", split_axis=0, concat_axis=0, tiled=True
    )
    narrow = x.shape[0] * 16 - WIDE
    narrow_away = product(x, w, Y_MAJOR, 1, WIDE, narrow, 1792)
    narrow_in = send(narrow_away, 0, 0, 1)
    wide_away = product(x, w, X_MAJOR, 1, 0, WIDE, 1536, [narrow_away])
    wide_in = send(wide_away, 0, 0, 1)
    narrow_own = product(x, w, Y_MAJOR, 0, WIDE, narrow, 1792, [wide_away])
    wide_own = product(x, w, X_MAJOR, 0, 0, WIDE, 1536, [narrow_own])

    keep, away = chip_narrow(narrow_own, narrow_in, [wide_own])
    narrow_y = send(away, 1, 0, 0)
    here, right, left, far_right, far_left = chip_wide(wide_own, wide_in, [away])
    far_right, far_left = send(far_right, 0, 1, 0), send(far_left, 0, 3, 0)
    acc, split = shrink_resident(x, resident_down_maps, slot, target, [here])

    right, left = near(right, left, far_right, far_left, [acc])
    from_left, from_right = send(right, 0, 1, 0), send(left, 0, 3, 0)

    part = shrink_fresh(split, acc, slot, target, maps, [right])
    part = add_parts([part, send(part, 0, 0, 1)])
    rest = [send(part, 0, 1, 0), send(part, 0, 2, 0), send(part, 0, 3, 0)]

    low_here, low_right, low_left, low_far_right, low_far_left = turn_narrow(keep, narrow_y, [part])
    low_far_right, low_far_left = send(low_far_right, 0, 1, 0), send(low_far_left, 0, 3, 0)

    part = add_parts([part, *rest], [low_here])
    other = send(part, 1, 0, 0)

    low_right, low_left = near(low_right, low_left, low_far_right, low_far_left, [part])
    low_from_left, low_from_right = send(low_right, 0, 1, 0), send(low_left, 0, 3, 0)

    raised = raise_features(part, other, resident_up_maps, slot, target, maps, [low_right])
    delta = lax.all_to_all(raised, "tp", split_axis=0, concat_axis=0, tiled=True)

    wide_keep, wide_send = turn_wide(here, from_left, from_right, [raised])
    wide_y = send(wide_send, 1, 0, 0)
    return call(
        finish_kernel,
        "finish",
        whole((32, 8192), BF16),
        (residual, wide_keep, wide_y, low_here, low_from_left, low_from_right, delta),
    )


def solution(mesh):
    return jax.shard_map(
        local,
        mesh=mesh,
        in_specs=(
            P("grp", "tp"),
            P("tp", None),
            P("tp", "grp"),
            P("tp", "grp"),
            P("grp", "tp"),
            P(("grp", "tp"), None, None),
            P("grp"),
            P("grp"),
        ),
        out_specs=P("tp", "grp"),
        check_vma=False,
    )
```

profile of v0, /device:TPU:1, one launch (start us, length us, event | category | flops | bytes accessed | tf_op | source)
XLA Modules:
  0.0 100.6 jit_solution(8878172768258045655)
XLA Ops:
  0.0 4.0 %product.4.refs_2_ = bf16[256,3584]{1,0:T(8,128)(2,1)} custom-call(bf16[512,512]{1,0:T(8,128)(2,1)} %refs_0_.10, bf16[512,8192]{1,0:T(8,128)(2,1)} %refs_1_.8), custom_call_target="tpu_custom_call" | custom-call | tf_op jit(solution)/shard_map/product/pallas_call | solution.py:72
  4.0 5.6 %product.5.refs_2_ = bf16[256,4608]{1,0:T(8,128)(2,1)} custom-call(bf16[512,512]{1,0:T(8,128)(2,1)} %refs_0_.10, bf16[512,8192]{1,0:T(8,128)(2,1)} %refs_1_.8, bf16[256,3584]{1,0:T(8,128)(2,1)} %product.4.refs_2_), custom_call_target="tpu_custom_call" | custom-call | tf_op jit(solution)/shard_map/product/pallas_call | solution.py:72
  9.6 3.2 %collective-permute-start = (bf16[256,4608]{1,0:T(8,128)(2,1)}, bf16[256,4608]{1,0:T(8,128)(2,1)}, u32[]{:S(2)}, u32[]{:S(2)}) collective-permute-start(bf16[256,4608]{1,0:T(8,128)(2,1)} %product.5.refs_2_), channel_id=1, source_target_pairs={{0,1},{1,0},{2,3},{3,2},{4,5},{5,4},{6,7},{7,6},{8,9},{9,8},{10,11... | collective-permute-start | bytes 7077896 | tf_op jit(solution)/shard_map/ppermute | solution.py:33
  12.9 0.0 collective-permute-start.1
  12.9 4.1 %all-to-all-start = ((bf16[16,256,128]{2,1,0:T(8,128)(2,1)}), bf16[16,256,128]{2,1,0:T(8,128)(2,1)S(1)}, u32[]{:S(2)}, u32[]{:S(2)}) async-start(bf16[16,256,128]{2,1,0:T(8,128)(2,1)} %bitcast.2), calls=%async_computation | async-start | bytes 2097152 | tf_op jit(solution)/shard_map/all_to_all | solution.py:376
  16.9 3.9 %product.6.refs_2_.refs_0_ = bf16[256,3584]{1,0:T(8,128)(2,1)} custom-call(bf16[512,512]{1,0:T(8,128)(2,1)} %refs_0_.10, bf16[512,8192]{1,0:T(8,128)(2,1)} %refs_1_.8, bf16[256,4608]{1,0:T(8,128)(2,1)} %product.5.refs_2_), custom_call_target="tpu_custom_call" | custom-call | tf_op jit(solution)/shard_map/product/pallas_call | solution.py:72
  20.9 5.8 %product.7.refs_2_.refs_0_ = bf16[256,4608]{1,0:T(8,128)(2,1)} custom-call(bf16[512,512]{1,0:T(8,128)(2,1)} %refs_0_.10, bf16[512,8192]{1,0:T(8,128)(2,1)} %refs_1_.8, bf16[256,3584]{1,0:T(8,128)(2,1)} %product.6.refs_2_.refs_0_), custom_call_target="tpu_custom_call" | custom-call | tf_op jit(solution)/shard_map/product/pallas_call | solution.py:72
  26.6 0.0 collective-permute-done.1.refs_1_
  26.6 1.7 %copy-done = bf16[256,4608]{1,0:T(8,128)(2,1)S(1)} copy-done((bf16[256,4608]{1,0:T(8,128)(2,1)S(1)}, bf16[256,4608]{1,0:T(8,128)(2,1)}, u32[]{:S(2)}) %copy-start) | copy-done | bytes 2359320
  28.3 2.1 %chip_narrow.1 = (bf16[128,3584]{1,0:T(8,128)(2,1)S(1)}, bf16[128,3584]{1,0:T(8,128)(2,1)}) custom-call(bf16[256,3584]{1,0:T(8,128)(2,1)S(1)} %copy-done.2, bf16[256,3584]{1,0:T(8,128)(2,1)S(1)} %collective-permute-done.1.refs_1_, bf16[256,4608]{1,0:T(8,128)(2,1)S(1)} %copy-done), custom_call_target="tpu_custom_call" | custom-call | tf_op jit(solution)/shard_map/chip_narrow/pallas_call | solution.py:72
  30.4 0.0 copy-start.17
  30.4 1.5 %collective-permute-start.10 = (bf16[128,3584]{1,0:T(8,128)(2,1)}, bf16[128,3584]{1,0:T(8,128)(2,1)}, u32[]{:S(2)}, u32[]{:S(2)}) collective-permute-start(bf16[128,3584]{1,0:T(8,128)(2,1)} %get-tuple-element.25.refs_2_), channel_id=1, source_target_pairs={{0,8},{1,9},{2,10},{3,11},{4,12},{5,13},{6,14},{7,15},{8,0},{9,1},... | collective-permute-start | bytes 2752520 | tf_op jit(solution)/shard_map/ppermute | solution.py:33
  31.9 0.0 collective-permute-done.refs_1_
  31.9 4.1 %chip_wide.1 = (bf16[64,4608]{1,0:T(8,128)(2,1)S(1)}, bf16[64,4608]{1,0:T(8,128)(2,1)S(1)}, bf16[64,4608]{1,0:T(8,128)(2,1)S(1)}, bf16[64,2304]{1,0:T(8,128)(2,1)}, bf16[64,2304]{1,0:T(8,128)(2,1)}) custom-call(bf16[256,4608]{1,0:T(8,128)(2,1)S(1)} %copy-done.1, bf16[256,4608]{1,0:T(8,128)(2,1)} %collective-permute-done.refs_1_, ...), custom_call_target="tpu_custom_call" | custom-call | tf_op jit(solution)/shard_map/chip_wide/pallas_call | solution.py:72
  36.0 0.8 copy-done.10
  36.8 0.8 copy-done.12
  37.6 1.2 %collective-permute-start.2 = (bf16[64,2304]{1,0:T(8,128)(2,1)}, bf16[64,2304]{1,0:T(8,128)(2,1)}, u32[]{:S(2)}, u32[]{:S(2)}) collective-permute-start(bf16[64,2304]{1,0:T(8,128)(2,1)} %get-tuple-element.29), channel_id=1, source_target_pairs={{0,2},{1,3},{2,4},{3,5},{4,6},{5,7},{6,0},{7,1},{8,10},{9,11},{10,... | collective-permute-start | bytes 884744 | tf_op jit(solution)/shard_map/ppermute | solution.py:33
  38.8 1.5 %collective-permute-start.3 = (bf16[64,2304]{1,0:T(8,128)(2,1)}, bf16[64,2304]{1,0:T(8,128)(2,1)}, u32[]{:S(2)}, u32[]{:S(2)}) collective-permute-start(bf16[64,2304]{1,0:T(8,128)(2,1)} %get-tuple-element.30), channel_id=1, source_target_pairs={{0,6},{1,7},{2,0},{3,1},{4,2},{5,3},{6,4},{7,5},{8,14},{9,15},{10,... | collective-permute-start | bytes 884744 | tf_op jit(solution)/shard_map/ppermute | solution.py:33
  40.3 0.1 copy.9.refs_2_.refs_3_
  40.5 2.1 %shrink_resident.1 = (f32[512,128]{1,0:T(8,128)S(1)}, bf16[512,512]{1,0:T(8,128)(2,1)S(1)}) custom-call(bf16[512,512]{1,0:T(8,128)(2,1)S(1)} %copy-done.3, bf16[512,1024]{1,0:T(8,128)(2,1)S(1)} %copy-done.5, s32[512,1]{1,0:T(8,128)S(1)} %copy.9.refs_2_.refs_3_, s32[16]{0:T(128)S(1)} %copy-done.17, bf16[64,4608]{1,0:T(8,128)(2,1)S(1)} %get-tuple-element.26.refs_4_.refs_0_), custom_call_target="tpu_custom_call" | custom-call | tf_op jit(solution)/shard_map/shrink_resident/pallas_call | solution.py:72
  42.6 0.0 copy-start.15
  42.6 0.8 copy-done.15
  43.4 3.7 %collective-permute-done.2.refs_2_ = bf16[64,2304]{1,0:T(8,128)(2,1)} collective-permute-done((bf16[64,2304]{1,0:T(8,128)(2,1)}, bf16[64,2304]{1,0:T(8,128)(2,1)}, u32[]{:S(2)}, u32[]{:S(2)}) %collective-permute-start.2) | collective-permute-done | bytes 294944 | tf_op jit(solution)/shard_map/ppermute | solution.py:33
  47.1 0.0 collective-permute-done.3.refs_3_
  47.1 2.2 %near.2 = (bf16[64,4608]{1,0:T(8,128)(2,1)}, bf16[64,4608]{1,0:T(8,128)(2,1)}) custom-call(bf16[64,4608]{1,0:T(8,128)(2,1)S(1)} %copy-done.11, bf16[64,4608]{1,0:T(8,128)(2,1)S(1)} %copy-done.13, bf16[64,2304]{1,0:T(8,128)(2,1)} %collective-permute-done.2.refs_2_, bf16[64,2304]{1,0:T(8,128)(2,1)} %collective-permute-done.3.refs_3_, ...), custom_call_target="tpu_custom_call" | custom-call | tf_op jit(solution)/shard_map/near/pallas_call | solution.py:72
  49.3 0.8 collective-permute-start.4
  50.1 0.0 copy-done.6
  50.1 1.9 %collective-permute-start.5 = (bf16[64,4608]{1,0:T(8,128)(2,1)}, bf16[64,4608]{1,0:T(8,128)(2,1)}, u32[]{:S(2)}, u32[]{:S(2)}) collective-permute-start(bf16[64,4608]{1,0:T(8,128)(2,1)} %get-tuple-element.33), channel_id=1, source_target_pairs={{0,6},{1,7},{2,0},{3,1},{4,2},{5,3},{6,4},{7,5},{8,14},{9,15},{10,... | collective-permute-start | bytes 1769480 | tf_op jit(solution)/shard_map/ppermute | solution.py:33
  52.0 0.0 all-to-all-done.refs_4_.refs_5_
  52.0 0.9 copy-done.7
  53.0 1.9 %shrink_fresh.1.refs_0_ = bf16[256,128]{1,0:T(8,128)(2,1)S(1)} custom-call(bf16[512,512]{1,0:T(8,128)(2,1)S(1)} %copy-done.16, f32[512,128]{1,0:T(8,128)S(1)} %copy-done.7, s32[512,1]{1,0:T(8,128)S(1)} %copy.9.refs_2_.refs_3_, s32[16]{0:T(128)S(1)} %copy-done.17, bf16[16,256,128]{2,1,0:T(8,128)(2,1)S(1)} %all-to-all-done.refs_4_.refs_5_, ...), custom_call_target="tpu_custom_call" | custom-call | tf_op jit(solution)/shard_map/shrink_fresh/pallas_call | solution.py:72
  54.9 0.0 copy-start.4
  54.9 2.2 %collective-permute-start.6 = (bf16[256,128]{1,0:T(8,128)(2,1)S(1)}, bf16[256,128]{1,0:T(8,128)(2,1)S(1)}, u32[]{:S(2)}, u32[]{:S(2)}) collective-permute-start(bf16[256,128]{1,0:T(8,128)(2,1)S(1)} %shrink_fresh.1.refs_0_), channel_id=1, source_target_pairs={{0,1},{1,0},{2,3},{3,2},{4,5},{5,4},{6,7},{7,6},{8,9},{9,8},{10,11... | collective-permute-start | bytes 196616 | tf_op jit(solution)/shard_map/ppermute | solution.py:33
  57.1 0.9 collective-permute-done.6.refs_1_
  58.0 0.1 collective-permute-start.7
  58.1 2.6 %collective-permute-start.8 = (bf16[256,128]{1,0:T(8,128)(2,1)S(1)}, bf16[256,128]{1,0:T(8,128)(2,1)S(1)}, u32[]{:S(2)}, u32[]{:S(2)}) collective-permute-start(bf16[256,128]{1,0:T(8,128)(2,1)S(1)} %add_parts.2.refs_2_.refs_0_), channel_id=1, source_target_pairs={{0,4},{1,5},{2,6},{3,7},{4,0},{5,1},{6,2},{7,3},{8,12},{9,13},{10,... | collective-permute-start | bytes 196616 | tf_op jit(solution)/shard_map/ppermute | solution.py:33
  60.7 0.0 collective-permute-done.10.refs_1_
  60.7 0.6 collective-permute-start.9
  61.3 1.2 %copy-done.9 = bf16[128,3584]{1,0:T(8,128)(2,1)S(1)} copy-done((bf16[128,3584]{1,0:T(8,128)(2,1)S(1)}, bf16[128,3584]{1,0:T(8,128)(2,1)}, u32[]{:S(2)}) %copy-start.9) | copy-done | bytes 917528
  62.4 1.5 %turn_narrow.1 = (bf16[32,3584]{1,0:T(8,128)(2,1)S(1)}, bf16[32,3584]{1,0:T(8,128)(2,1)S(1)}, bf16[32,3584]{1,0:T(8,128)(2,1)S(1)}, bf16[32,1792]{1,0:T(8,128)(2,1)S(1)}, bf16[32,1792]{1,0:T(8,128)(2,1)S(1)}) custom-call(bf16[128,3584]{1,0:T(8,128)(2,1)S(1)} %copy-done.9, bf16[128,3584]{1,0:T(8,128)(2,1)} %collective-permute-done.10.refs_1_, ...), custom_call_target="tpu_custom_call" | custom-call | tf_op jit(solution)/shard_map/turn_narrow/pallas_call | solution.py:72
  63.9 1.6 %collective-permute-done.7.refs_1_ = bf16[256,128]{1,0:T(8,128)(2,1)S(1)} collective-permute-done((bf16[256,128]{1,0:T(8,128)(2,1)S(1)}, bf16[256,128]{1,0:T(8,128)(2,1)S(1)}, u32[]{:S(2)}, u32[]{:S(2)}) %collective-permute-start.7) | collective-permute-done | bytes 65568 | tf_op jit(solution)/shard_map/ppermute | solution.py:33
  65.5 0.0 collective-permute-start.12
  65.5 1.6 %collective-permute-done.8.refs_2_ = bf16[256,128]{1,0:T(8,128)(2,1)S(1)} collective-permute-done((bf16[256,128]{1,0:T(8,128)(2,1)S(1)}, bf16[256,128]{1,0:T(8,128)(2,1)S(1)}, u32[]{:S(2)}, u32[]{:S(2)}) %collective-permute-start.8) | collective-permute-done | bytes 65568 | tf_op jit(solution)/shard_map/ppermute | solution.py:33
  67.1 1.1 %collective-permute-start.13 = (bf16[32,1792]{1,0:T(8,128)(2,1)S(1)}, bf16[32,1792]{1,0:T(8,128)(2,1)S(1)}, u32[]{:S(2)}, u32[]{:S(2)}) collective-permute-start(bf16[32,1792]{1,0:T(8,128)(2,1)S(1)} %get-tuple-element.40), channel_id=1, source_target_pairs={{0,6},{1,7},{2,0},{3,1},{4,2},{5,3},{6,4},{7,5},{8,14},{9,15},{10,... | collective-permute-start | bytes 344072 | tf_op jit(solution)/shard_map/ppermute | solution.py:33
  68.2 0.0 collective-permute-done.9.refs_3_
  68.2 1.3 %collective-permute-start.11 = (bf16[256,128]{1,0:T(8,128)(2,1)S(1)}, bf16[256,128]{1,0:T(8,128)(2,1)S(1)}, u32[]{:S(2)}, u32[]{:S(2)}) collective-permute-start(bf16[256,128]{1,0:T(8,128)(2,1)S(1)} %add_parts.3.refs_4_.refs_0_), channel_id=1, source_target_pairs={{0,8},{1,9},{2,10},{3,11},{4,12},{5,13},{6,14},{7,15},{8,0},{9,1},... | collective-permute-start | bytes 196616 | tf_op jit(solution)/shard_map/ppermute | solution.py:33
  69.5 1.4 %collective-permute-done.12.refs_2_ = bf16[32,1792]{1,0:T(8,128)(2,1)S(1)} collective-permute-done((bf16[32,1792]{1,0:T(8,128)(2,1)S(1)}, bf16[32,1792]{1,0:T(8,128)(2,1)S(1)}, u32[]{:S(2)}, u32[]{:S(2)}) %collective-permute-start.12) | collective-permute-done | bytes 114720 | tf_op jit(solution)/shard_map/ppermute | solution.py:33
  70.9 0.0 collective-permute-done.13.refs_3_
  70.9 0.1 near.3
  71.0 0.7 copy-done.18
  71.7 0.0 collective-permute-done.11.refs_1_
  71.7 4.0 %raise_features.1.refs_3_ = bf16[16,32,512]{2,1,0:T(8,128)(2,1)} custom-call(bf16[256,128]{1,0:T(8,128)(2,1)S(1)} %add_parts.3.refs_4_.refs_0_, bf16[256,128]{1,0:T(8,128)(2,1)S(1)} %collective-permute-done.11.refs_1_, bf16[1024,512]{1,0:T(8,128)(2,1)S(1)} %copy-done.4, s32[512,1]{1,0:T(8,128)S(1)} %copy.9.refs_2_.refs_3_, s32[16]{0:T(128)S(1)} %copy-done.17, ...), custom_call_target="tpu_custom_call" | custom-call | tf_op jit(solution)/shard_map/raise_features/pallas_call | solution.py:72
  75.7 9.0 %all-to-all-start.1 = ((bf16[16,32,512]{2,1,0:T(8,128)(2,1)}), bf16[16,32,512]{2,1,0:T(8,128)(2,1)S(1)}, u32[]{:S(2)}, u32[]{:S(2)}) async-start(bf16[16,32,512]{2,1,0:T(8,128)(2,1)} %raise_features.1.refs_3_), calls=%async_computation.1 | async-start | bytes 1048576 | tf_op jit(solution)/shard_map/all_to_all | solution.py:410
  84.7 0.0 collective-permute-done.4.refs_1_
  84.7 0.0 collective-permute-done.5.refs_2_
  84.7 1.9 %turn_wide.1 = (f32[32,4608]{1,0:T(8,128)S(1)}, bf16[32,4608]{1,0:T(8,128)(2,1)}) custom-call(bf16[64,4608]{1,0:T(8,128)(2,1)S(1)} %get-tuple-element.26.refs_4_.refs_0_, bf16[64,4608]{1,0:T(8,128)(2,1)S(1)} %collective-permute-done.4.refs_1_, bf16[64,4608]{1,0:T(8,128)(2,1)} %collective-permute-done.5.refs_2_, bf16[16,32,512]{2,1,0:T(8,128)(2,1)} %raise_features.1.refs_3_), custom_call_target="tpu_custom_call" | custom-call | tf_op jit(solution)/shard_map/turn_wide/pallas_call | solution.py:72
  86.6 1.4 %collective-permute-start.14 = (bf16[32,4608]{1,0:T(8,128)(2,1)}, bf16[32,4608]{1,0:T(8,128)(2,1)S(1)}, u32[]{:S(2)}, u32[]{:S(2)}) collective-permute-start(bf16[32,4608]{1,0:T(8,128)(2,1)} %get-tuple-element.43), channel_id=1, source_target_pairs={{0,8},{1,9},{2,10},{3,11},{4,12},{5,13},{6,14},{7,15},{8,0},{9,1},... | collective-permute-start | bytes 884744 | tf_op jit(solution)/shard_map/ppermute | solution.py:33
  88.0 1.2 %collective-permute-start.15 = (bf16[32,3584]{1,0:T(8,128)(2,1)S(1)}, bf16[32,3584]{1,0:T(8,128)(2,1)S(1)}, u32[]{:S(2)}, u32[]{:S(2)}) collective-permute-start(bf16[32,3584]{1,0:T(8,128)(2,1)S(1)} %get-tuple-element.41.refs_6_), channel_id=1, source_target_pairs={{0,2},{1,3},{2,4},{3,5},{4,6},{5,7},{6,0},{7,1},{8,10},{9,11},{10,... | collective-permute-start | bytes 688136 | tf_op jit(solution)/shard_map/ppermute | solution.py:33
  89.2 1.5 %collective-permute-start.16 = (bf16[32,3584]{1,0:T(8,128)(2,1)}, bf16[32,3584]{1,0:T(8,128)(2,1)S(1)}, u32[]{:S(2)}, u32[]{:S(2)}) collective-permute-start(bf16[32,3584]{1,0:T(8,128)(2,1)} %copy-done.18), channel_id=1, source_target_pairs={{0,6},{1,7},{2,0},{3,1},{4,2},{5,3},{6,4},{7,5},{8,14},{9,15},{10,... | collective-permute-start | bytes 688136 | tf_op jit(solution)/shard_map/ppermute | solution.py:33
  90.7 8.2 %collective-permute-done.15.refs_4_ = bf16[32,3584]{1,0:T(8,128)(2,1)S(1)} collective-permute-done((bf16[32,3584]{1,0:T(8,128)(2,1)S(1)}, bf16[32,3584]{1,0:T(8,128)(2,1)S(1)}, u32[]{:S(2)}, u32[]{:S(2)}) %collective-permute-start.15) | collective-permute-done | bytes 229408 | tf_op jit(solution)/shard_map/ppermute | solution.py:33
  98.9 0.0 collective-permute-done.16.refs_5_
  98.9 0.0 all-to-all-done.1.refs_6_
  98.9 0.6 collective-permute-done.14.refs_2_
  99.5 1.1 %finish.1 = bf16[32,8192]{1,0:T(8,128)(2,1)} custom-call(bf16[32,8192]{1,0:T(8,128)(2,1)S(1)} %copy-done.14, f32[32,4608]{1,0:T(8,128)S(1)} %get-tuple-element.42.refs_1_, bf16[32,4608]{1,0:T(8,128)(2,1)S(1)} %collective-permute-done.14.refs_2_, bf16[32,3584]{1,0:T(8,128)(2,1)S(1)} %get-tuple-element.36.refs_4_.refs_3_, ...), custom_call_target="tpu_custom_call" | custom-call | tf_op jit(solution)/shard_map/finish/pallas_call | solution.py:72
  (31 shorter events, 0.1 us)
Async XLA Ops:
  9.6 22.3 %collective-permute-start = (bf16[256,4608]{1,0:T(8,128)(2,1)}, bf16[256,4608]{1,0:T(8,128)(2,1)}, u32[]{:S(2)}, u32[]{:S(2)}) collective-permute-start(bf16[256,4608]{1,0:T(8,128)(2,1)} %product.5.refs_2_), channel_id=1, source_target_pairs={{0,1},{1,0},{2,3},{3,2},{4,5},{5,4},{6,7},{7,6},{8,9},{9,8},{10,11... | collective-permute-start | bytes 7077896 | tf_op jit(solution)/shard_map/ppermute | solution.py:33
  12.9 13.8 %collective-permute-start.1 = (bf16[256,3584]{1,0:T(8,128)(2,1)}, bf16[256,3584]{1,0:T(8,128)(2,1)S(1)}, u32[]{:S(2)}, u32[]{:S(2)}) collective-permute-start(bf16[256,3584]{1,0:T(8,128)(2,1)} %product.4.refs_2_), channel_id=1, source_target_pairs={{0,1},{1,0},{2,3},{3,2},{4,5},{5,4},{6,7},{7,6},{8,9},{9,8},{10,11... | collective-permute-start | bytes 5505032 | tf_op jit(solution)/shard_map/ppermute | solution.py:33
  12.9 39.2 %all-to-all-start = ((bf16[16,256,128]{2,1,0:T(8,128)(2,1)}), bf16[16,256,128]{2,1,0:T(8,128)(2,1)S(1)}, u32[]{:S(2)}, u32[]{:S(2)}) async-start(bf16[16,256,128]{2,1,0:T(8,128)(2,1)} %bitcast.2), calls=%async_computation | async-start | bytes 2097152 | tf_op jit(solution)/shard_map/all_to_all | solution.py:376
  20.9 5.8 %copy-start.2 = (bf16[256,3584]{1,0:T(8,128)(2,1)S(1)}, bf16[256,3584]{1,0:T(8,128)(2,1)}, u32[]{:S(2)}) copy-start(bf16[256,3584]{1,0:T(8,128)(2,1)} %product.6.refs_2_.refs_0_) | copy-start | bytes 5505028
  26.6 1.7 %copy-start = (bf16[256,4608]{1,0:T(8,128)(2,1)S(1)}, bf16[256,4608]{1,0:T(8,128)(2,1)}, u32[]{:S(2)}) copy-start(bf16[256,4608]{1,0:T(8,128)(2,1)} %product.7.refs_2_.refs_0_) | copy-start | bytes 7077892
  28.3 3.6 %copy-start.1 = (bf16[256,4608]{1,0:T(8,128)(2,1)S(1)}, bf16[256,4608]{1,0:T(8,128)(2,1)}, u32[]{:S(2)}) copy-start(bf16[256,4608]{1,0:T(8,128)(2,1)} %product.7.refs_2_.refs_0_) | copy-start | bytes 7077892
  30.4 5.6 %copy-start.8 = (bf16[128,3584]{1,0:T(8,128)(2,1)}, bf16[128,3584]{1,0:T(8,128)(2,1)S(1)}, u32[]{:S(2)}) copy-start(bf16[128,3584]{1,0:T(8,128)(2,1)S(1)} %get-tuple-element.35.refs_0_) | copy-start | bytes 2752516
  30.4 9.9 %copy-start.19 = (s32[512]{0:T(512)S(1)}, s32[512]{0:T(512)}, u32[]{:S(2)}) copy-start(s32[512]{0:T(512)} %param.15) | copy-start | bytes 6148
  30.4 10.1 %copy-start.3 = (bf16[512,512]{1,0:T(8,128)(2,1)S(1)}, bf16[512,512]{1,0:T(8,128)(2,1)}, u32[]{:S(2)}) copy-start(bf16[512,512]{1,0:T(8,128)(2,1)} %refs_0_.10) | copy-start | bytes 1572868
  30.4 10.1 %copy-start.5 = (bf16[512,1024]{1,0:T(8,128)(2,1)S(1)}, bf16[512,1024]{1,0:T(8,128)(2,1)}, u32[]{:S(2)}) copy-start(bf16[512,1024]{1,0:T(8,128)(2,1)} %refs_1_.9) | copy-start | bytes 3145732
  30.4 10.1 %copy-start.17 = (s32[16]{0:T(128)S(1)}, s32[16]{0:T(128)}, u32[]{:S(2)}) copy-start(s32[16]{0:T(128)} %refs_4_.1) | copy-start | bytes 196
  30.4 30.3 %collective-permute-start.10 = (bf16[128,3584]{1,0:T(8,128)(2,1)}, bf16[128,3584]{1,0:T(8,128)(2,1)}, u32[]{:S(2)}, u32[]{:S(2)}) collective-permute-start(bf16[128,3584]{1,0:T(8,128)(2,1)} %get-tuple-element.25.refs_2_), channel_id=1, source_target_pairs={{0,8},{1,9},{2,10},{3,11},{4,12},{5,13},{6,14},{7,15},{8,0},{9,1},... | collective-permute-start | bytes 2752520 | tf_op jit(solution)/shard_map/ppermute | solution.py:33
  36.0 0.8 copy-start.10
  36.8 0.8 copy-start.12
  37.6 9.4 %collective-permute-start.2 = (bf16[64,2304]{1,0:T(8,128)(2,1)}, bf16[64,2304]{1,0:T(8,128)(2,1)}, u32[]{:S(2)}, u32[]{:S(2)}) collective-permute-start(bf16[64,2304]{1,0:T(8,128)(2,1)} %get-tuple-element.29), channel_id=1, source_target_pairs={{0,2},{1,3},{2,4},{3,5},{4,6},{5,7},{6,0},{7,1},{8,10},{9,11},{10,... | collective-permute-start | bytes 884744 | tf_op jit(solution)/shard_map/ppermute | solution.py:33
  38.8 8.3 %collective-permute-start.3 = (bf16[64,2304]{1,0:T(8,128)(2,1)}, bf16[64,2304]{1,0:T(8,128)(2,1)}, u32[]{:S(2)}, u32[]{:S(2)}) collective-permute-start(bf16[64,2304]{1,0:T(8,128)(2,1)} %get-tuple-element.30), channel_id=1, source_target_pairs={{0,6},{1,7},{2,0},{3,1},{4,2},{5,3},{6,4},{7,5},{8,14},{9,15},{10,... | collective-permute-start | bytes 884744 | tf_op jit(solution)/shard_map/ppermute | solution.py:33
  40.5 6.6 %copy-start.11 = (bf16[64,4608]{1,0:T(8,128)(2,1)S(1)}, bf16[64,4608]{1,0:T(8,128)(2,1)}, u32[]{:S(2)}) copy-start(bf16[64,4608]{1,0:T(8,128)(2,1)} %copy-done.10) | copy-start | bytes 1769476
  40.5 6.6 %copy-start.13 = (bf16[64,4608]{1,0:T(8,128)(2,1)S(1)}, bf16[64,4608]{1,0:T(8,128)(2,1)}, u32[]{:S(2)}) copy-start(bf16[64,4608]{1,0:T(8,128)(2,1)} %copy-done.12) | copy-start | bytes 1769476
  42.6 0.8 copy-start.15
  43.4 6.7 %copy-start.6 = (f32[512,128]{1,0:T(8,128)}, f32[512,128]{1,0:T(8,128)S(1)}, u32[]{:S(2)}) copy-start(f32[512,128]{1,0:T(8,128)S(1)} %get-tuple-element.31.refs_4_.refs_1_) | copy-start | bytes 786436
  47.1 5.0 %copy-start.16 = (bf16[512,512]{1,0:T(8,128)(2,1)S(1)}, bf16[512,512]{1,0:T(8,128)(2,1)}, u32[]{:S(2)}) copy-start(bf16[512,512]{1,0:T(8,128)(2,1)} %copy-done.15) | copy-start | bytes 1572868
  49.3 35.3 %collective-permute-start.4 = (bf16[64,4608]{1,0:T(8,128)(2,1)}, bf16[64,4608]{1,0:T(8,128)(2,1)S(1)}, u32[]{:S(2)}, u32[]{:S(2)}) collective-permute-start(bf16[64,4608]{1,0:T(8,128)(2,1)} %get-tuple-element.32.refs_5_), channel_id=1, source_target_pairs={{0,2},{1,3},{2,4},{3,5},{4,6},{5,7},{6,0},{7,1},{8,10},{9,11},{10,... | collective-permute-start | bytes 1769480 | tf_op jit(solution)/shard_map/ppermute | solution.py:33
  50.1 34.6 %collective-permute-start.5 = (bf16[64,4608]{1,0:T(8,128)(2,1)}, bf16[64,4608]{1,0:T(8,128)(2,1)}, u32[]{:S(2)}, u32[]{:S(2)}) collective-permute-start(bf16[64,4608]{1,0:T(8,128)(2,1)} %get-tuple-element.33), channel_id=1, source_target_pairs={{0,6},{1,7},{2,0},{3,1},{4,2},{5,3},{6,4},{7,5},{8,14},{9,15},{10,... | collective-permute-start | bytes 1769480 | tf_op jit(solution)/shard_map/ppermute | solution.py:33
  52.0 1.0 copy-start.7
  54.9 16.8 %copy-start.4 = (bf16[1024,512]{1,0:T(8,128)(2,1)S(1)}, bf16[1024,512]{1,0:T(8,128)(2,1)}, u32[]{:S(2)}) copy-start(bf16[1024,512]{1,0:T(8,128)(2,1)} %refs_2_.1) | copy-start | bytes 3145732
  54.9 3.1 %collective-permute-start.6 = (bf16[256,128]{1,0:T(8,128)(2,1)S(1)}, bf16[256,128]{1,0:T(8,128)(2,1)S(1)}, u32[]{:S(2)}, u32[]{:S(2)}) collective-permute-start(bf16[256,128]{1,0:T(8,128)(2,1)S(1)} %shrink_fresh.1.refs_0_), channel_id=1, source_target_pairs={{0,1},{1,0},{2,3},{3,2},{4,5},{5,4},{6,7},{7,6},{8,9},{9,8},{10,11... | collective-permute-start | bytes 196616 | tf_op jit(solution)/shard_map/ppermute | solution.py:33
  58.0 7.5 %collective-permute-start.7 = (bf16[256,128]{1,0:T(8,128)(2,1)S(1)}, bf16[256,128]{1,0:T(8,128)(2,1)S(1)}, u32[]{:S(2)}, u32[]{:S(2)}) collective-permute-start(bf16[256,128]{1,0:T(8,128)(2,1)S(1)} %add_parts.2.refs_2_.refs_0_), channel_id=1, source_target_pairs={{0,2},{1,3},{2,4},{3,5},{4,6},{5,7},{6,0},{7,1},{8,10},{9,11},{10,... | collective-permute-start | bytes 196616 | tf_op jit(solution)/shard_map/ppermute | solution.py:33
  58.1 9.0 %collective-permute-start.8 = (bf16[256,128]{1,0:T(8,128)(2,1)S(1)}, bf16[256,128]{1,0:T(8,128)(2,1)S(1)}, u32[]{:S(2)}, u32[]{:S(2)}) collective-permute-start(bf16[256,128]{1,0:T(8,128)(2,1)S(1)} %add_parts.2.refs_2_.refs_0_), channel_id=1, source_target_pairs={{0,4},{1,5},{2,6},{3,7},{4,0},{5,1},{6,2},{7,3},{8,12},{9,13},{10,... | collective-permute-start | bytes 196616 | tf_op jit(solution)/shard_map/ppermute | solution.py:33
  60.7 7.5 %collective-permute-start.9 = (bf16[256,128]{1,0:T(8,128)(2,1)S(1)}, bf16[256,128]{1,0:T(8,128)(2,1)S(1)}, u32[]{:S(2)}, u32[]{:S(2)}) collective-permute-start(bf16[256,128]{1,0:T(8,128)(2,1)S(1)} %add_parts.2.refs_2_.refs_0_), channel_id=1, source_target_pairs={{0,6},{1,7},{2,0},{3,1},{4,2},{5,3},{6,4},{7,5},{8,14},{9,15},{10,... | collective-permute-start | bytes 196616 | tf_op jit(solution)/shard_map/ppermute | solution.py:33
  61.2 1.2 %copy-start.9 = (bf16[128,3584]{1,0:T(8,128)(2,1)S(1)}, bf16[128,3584]{1,0:T(8,128)(2,1)}, u32[]{:S(2)}) copy-start(bf16[128,3584]{1,0:T(8,128)(2,1)} %copy-done.8) | copy-start | bytes 2752516
  65.5 5.4 %collective-permute-start.12 = (bf16[32,1792]{1,0:T(8,128)(2,1)S(1)}, bf16[32,1792]{1,0:T(8,128)(2,1)S(1)}, u32[]{:S(2)}, u32[]{:S(2)}) collective-permute-start(bf16[32,1792]{1,0:T(8,128)(2,1)S(1)} %get-tuple-element.39), channel_id=1, source_target_pairs={{0,2},{1,3},{2,4},{3,5},{4,6},{5,7},{6,0},{7,1},{8,10},{9,11},{10,... | collective-permute-start | bytes 344072 | tf_op jit(solution)/shard_map/ppermute | solution.py:33
  67.1 3.9 %collective-permute-start.13 = (bf16[32,1792]{1,0:T(8,128)(2,1)S(1)}, bf16[32,1792]{1,0:T(8,128)(2,1)S(1)}, u32[]{:S(2)}, u32[]{:S(2)}) collective-permute-start(bf16[32,1792]{1,0:T(8,128)(2,1)S(1)} %get-tuple-element.40), channel_id=1, source_target_pairs={{0,6},{1,7},{2,0},{3,1},{4,2},{5,3},{6,4},{7,5},{8,14},{9,15},{10,... | collective-permute-start | bytes 344072 | tf_op jit(solution)/shard_map/ppermute | solution.py:33
  68.2 3.5 %collective-permute-start.11 = (bf16[256,128]{1,0:T(8,128)(2,1)S(1)}, bf16[256,128]{1,0:T(8,128)(2,1)S(1)}, u32[]{:S(2)}, u32[]{:S(2)}) collective-permute-start(bf16[256,128]{1,0:T(8,128)(2,1)S(1)} %add_parts.3.refs_4_.refs_0_), channel_id=1, source_target_pairs={{0,8},{1,9},{2,10},{3,11},{4,12},{5,13},{6,14},{7,15},{8,0},{9,1},... | collective-permute-start | bytes 196616 | tf_op jit(solution)/shard_map/ppermute | solution.py:33
  71.0 0.7 copy-start.18
  75.7 23.8 %copy-start.14 = (bf16[32,8192]{1,0:T(8,128)(2,1)S(1)}, bf16[32,8192]{1,0:T(8,128)(2,1)}, u32[]{:S(2)}) copy-start(bf16[32,8192]{1,0:T(8,128)(2,1)} %refs_0_.11) | copy-start | bytes 1572868
  75.7 23.2 %all-to-all-start.1 = ((bf16[16,32,512]{2,1,0:T(8,128)(2,1)}), bf16[16,32,512]{2,1,0:T(8,128)(2,1)S(1)}, u32[]{:S(2)}, u32[]{:S(2)}) async-start(bf16[16,32,512]{2,1,0:T(8,128)(2,1)} %raise_features.1.refs_3_), calls=%async_computation.1 | async-start | bytes 1048576 | tf_op jit(solution)/shard_map/all_to_all | solution.py:410
  86.6 12.9 %collective-permute-start.14 = (bf16[32,4608]{1,0:T(8,128)(2,1)}, bf16[32,4608]{1,0:T(8,128)(2,1)S(1)}, u32[]{:S(2)}, u32[]{:S(2)}) collective-permute-start(bf16[32,4608]{1,0:T(8,128)(2,1)} %get-tuple-element.43), channel_id=1, source_target_pairs={{0,8},{1,9},{2,10},{3,11},{4,12},{5,13},{6,14},{7,15},{8,0},{9,1},... | collective-permute-start | bytes 884744 | tf_op jit(solution)/shard_map/ppermute | solution.py:33
  88.0 10.9 %collective-permute-start.15 = (bf16[32,3584]{1,0:T(8,128)(2,1)S(1)}, bf16[32,3584]{1,0:T(8,128)(2,1)S(1)}, u32[]{:S(2)}, u32[]{:S(2)}) collective-permute-start(bf16[32,3584]{1,0:T(8,128)(2,1)S(1)} %get-tuple-element.41.refs_6_), channel_id=1, source_target_pairs={{0,2},{1,3},{2,4},{3,5},{4,6},{5,7},{6,0},{7,1},{8,10},{9,11},{10,... | collective-permute-start | bytes 688136 | tf_op jit(solution)/shard_map/ppermute | solution.py:33
  89.2 9.7 %collective-permute-start.16 = (bf16[32,3584]{1,0:T(8,128)(2,1)}, bf16[32,3584]{1,0:T(8,128)(2,1)S(1)}, u32[]{:S(2)}, u32[]{:S(2)}) collective-permute-start(bf16[32,3584]{1,0:T(8,128)(2,1)} %copy-done.18), channel_id=1, source_target_pairs={{0,6},{1,7},{2,0},{3,1},{4,2},{5,3},{6,4},{7,5},{8,14},{9,15},{10,... | collective-permute-start | bytes 688136 | tf_op jit(solution)/shard_map/ppermute | solution.py:33
where the time goes:
time: 101 us
  Pallas kernels  40.3 us (40%)
  starting transfers between devices  35 us (35%)
  waiting for transfers between devices  18 us (18%)
  local copies, waits for them, and re-layouts  7.1 us (7%)
    pallas_call x16, Pallas kernels, call(): pl.pallas_call(body, in_specs=list(specs or [VM] * count) + [LATER] * len...  40.3 us
    ppermute x17, starting transfers between devices, send(): return lax.ppermute(array, 'tp', route(yy, xx, cc))  21.9 us
    ppermute x17, waiting for transfers between devices, send(): return lax.ppermute(array, 'tp', route(yy, xx, cc))  18 us
    all_to_all x1, starting transfers between devices, local(): lax.all_to_all(raised, 'tp', split_axis=0, concat_axis=0, tiled=True)  8.97 us
    unnamed x40, local copies, waits for them, and re-layouts  6.96 us
    all_to_all x1, starting transfers between devices, local(): lax.all_to_all(fresh_adapter_bundle.reshape(16, 256, 128), 'tp', split_ax...  4.09 us
  transfers between devices with their start and end apart: 19, of which 7 were waited for; matrix products, arithmetic and copies ran while one was open for 0% of the time, Pallas kernels for 29%

commit v1 on v0

--- a/solution.py
+++ b/solution.py
@@ -12,8 +12,9 @@
 F32 = jnp.float32
 BF16 = jnp.bfloat16
 WIDE = 4608
-VMEM_LIMIT = 40 * 1024 * 1024
+VMEM_LIMIT = 16 * 1024 * 1024
 PRODUCT_LIMIT = 56 * 1024 * 1024
+CHUNK = 512
 
 
 def place(y, x, core):
@@ -74,6 +75,7 @@
         in_specs=list(specs or [VM] * count) + [LATER] * len(after),
         out_shape=out_shape,
         compiler_params=pltpu.CompilerParams(vmem_limit_bytes=limit),
+        cost_estimate=pl.CostEstimate(flops=1024, bytes_accessed=1024, transcendentals=0),
         name=name,
         **options,
     )(*args, *after)
@@ -83,94 +85,87 @@
 Y_MAJOR = [(yy, xx) for yy in range(2) for xx in range(4)]
 
 
-def product(x, w, order, cc, first, width, tile, after=()):
-    def kernel(x_ref, w_ref, out_ref, rows_ref):
-        @pl.when(pl.program_id(0) == 0)
-        def _():
-            for i, (yy, xx) in enumerate(order):
-                rows_ref[i * 32 : (i + 1) * 32, :] = x_ref[rows_at(partner(yy, xx, cc), 32), :]
-
-        out_ref[...] = jnp.dot(
-            rows_ref[...], w_ref[...], preferred_element_type=F32
-        ).astype(BF16)
+def product(x, w, order, first, width, after=()):
+    chunks = width // CHUNK
+
+    def kernel(x_ref, w_ref, away_ref, own_ref, rows_ref, held_ref, sems):
+        def copy(i):
+            cols = pl.ds(pl.multiple_of(first + i * CHUNK, CHUNK), CHUNK)
+            return pltpu.make_async_copy(w_ref.at[:, cols], held_ref.at[i], sems.at[i])
+
+        @pl.loop(0, chunks)
+        def _(i):
+            copy(i).start()
+
+        for i, (yy, xx) in enumerate(order):
+            for cc, top in ((1, 0), (0, 256)):
+                rows_ref[top + i * 32 : top + (i + 1) * 32, :] = x_ref[
+                    rows_at(partner(yy, xx, cc), 32), :
+                ]
+
+        @pl.loop(0, chunks)
+        def _(i):
+            copy(i).wait()
+            part = jnp.dot(rows_ref[...], held_ref[i], preferred_element_type=F32).astype(BF16)
+            cols = pl.ds(pl.multiple_of(i * CHUNK, CHUNK), CHUNK)
+            away_ref[:, cols] = part[:256]
+            own_ref[:, cols] = part[256:]
 
     return call(
         kernel,
         "product",
-        whole((256, width), BF16),
+        [whole((256, width), BF16)] * 2,
         (x, w),
-        [
-            pl.BlockSpec((512, 512), lambda j: (0, 0)),
-            pl.BlockSpec(
-                (pl.Element(512), pl.Element(tile)),
-                lambda j: (0, (first // 128 + j * (tile // 128)) * 128),
-            ),
-        ],
+        [VM, pl.BlockSpec(memory_space=pltpu.HBM)],
         after,
         limit=PRODUCT_LIMIT,
-        grid=(width // tile,),
-        out_specs=pl.BlockSpec((256, tile), lambda j: (0, j)),
-        scratch_shapes=[pltpu.VMEM((256, 512), BF16)],
+        scratch_shapes=[
+            pltpu.VMEM((512, 512), BF16),
+            pltpu.VMEM((chunks, 512, CHUNK), BF16),
+            pltpu.SemaphoreType.DMA((chunks,)),
+        ],
     )
 
 
 def chip_narrow(own, away, after=()):
     width = own.shape[1]
-    tile = width // 4
 
     def kernel(own_ref, away_ref, keep_ref, send_ref):
-        total = plus(own_ref[...], away_ref[...]).astype(BF16)
-        keep_ref[...] = total[:128]
-        send_ref[...] = total[128:]
-
-    piece = pl.BlockSpec((256, tile), lambda j: (0, j))
-    half = pl.BlockSpec((128, tile), lambda j: (0, j))
-    return call(
-        kernel,
-        "chip_narrow",
-        [whole((128, width), BF16)] * 2,
-        (own, away),
-        [piece, piece],
-        after,
-        grid=(4,),
-        out_specs=[half, half],
+        @pl.loop(0, width // CHUNK)
+        def _(j):
+            cols = pl.ds(pl.multiple_of(j * CHUNK, CHUNK), CHUNK)
+            total = plus(own_ref[:, cols], away_ref[:, cols]).astype(BF16)
+            keep_ref[:, cols] = total[:128]
+            send_ref[:, cols] = total[128:]
+
+    return call(
+        kernel, "chip_narrow", [whole((128, width), BF16)] * 2, (own, away), after=after
     )
 
 
 def chip_wide(own, away, after=()):
     width = own.shape[1]
-    tile = width // 4
+    half = width // 2
+    step = 256
 
     def kernel(own_ref, away_ref, here_ref, right_ref, left_ref, far_right_ref, far_left_ref):
-        j = pl.program_id(0)
-        total = plus(own_ref[...], away_ref[...]).astype(BF16)
-        here_ref[...] = total[:64]
-        right_ref[...] = total[64:128]
-        left_ref[...] = total[192:]
-
-        @pl.when(j < 2)
-        def _():
-            far_right_ref[...] = total[128:192]
-
-        @pl.when(j >= 2)
-        def _():
-            far_left_ref[...] = total[128:192]
-
-    piece = pl.BlockSpec((256, tile), lambda j: (0, j))
-    block = pl.BlockSpec((64, tile), lambda j: (0, j))
+        for side, far_ref in enumerate((far_right_ref, far_left_ref)):
+
+            @pl.loop(0, half // step)
+            def _(j):
+                cols = pl.ds(pl.multiple_of(side * half + j * step, step), step)
+                total = plus(own_ref[:, cols], away_ref[:, cols]).astype(BF16)
+                here_ref[:, cols] = total[:64]
+                right_ref[:, cols] = total[64:128]
+                far_ref[:, pl.ds(pl.multiple_of(j * step, step), step)] = total[128:192]
+                left_ref[:, cols] = total[192:]
+
     return call(
         kernel,
         "chip_wide",
-        [whole((64, width), BF16)] * 3 + [whole((64, width // 2), BF16)] * 2,
+        [whole((64, width), BF16)] * 3 + [whole((64, half), BF16)] * 2,
         (own, away),
-        [piece, piece],
-        after,
-        grid=(4,),
-        out_specs=[block] * 3
-        + [
-            pl.BlockSpec((64, tile), lambda j: (0, jnp.minimum(j, 1))),
-            pl.BlockSpec((64, tile), lambda j: (0, jnp.maximum(j - 2, 0))),
-        ],
+        after=after,
     )
 
 
@@ -298,7 +293,27 @@
     )
 
 
-def raise_kernel(mine_ref, other_ref, up_ref, slot_ref, target_ref, maps_ref, out_ref):
+def up_table_kernel(up_ref, target_ref, maps_ref, table_ref):
+    table_ref[...] = up_ref[...]
+    row = lax.broadcasted_iota(jnp.int32, (256, 512), 0)
+    col = lax.broadcasted_iota(jnp.int32, (256, 512), 1)
+    to_even = jnp.where(col == 2 * row, 1.0, 0.0).astype(BF16)
+    to_odd = jnp.where(col == 2 * row + 1, 1.0, 0.0).astype(BF16)
+    turn = (((0,), (0,)), ((), ()))
+    for k in range(CHIPS):
+        maps = maps_ref[2 * k + 1]
+        even = lax.dot_general(maps, to_even, turn, preferred_element_type=F32)
+        odd = lax.dot_general(maps, to_odd, turn, preferred_element_type=F32)
+        table_ref[rows_at(target_ref[k], RANK), :] = (even[:RANK] + odd[RANK:]).astype(BF16)
+
+
+def up_table(up, target, maps, after=()):
+    return call(
+        up_table_kernel, "up_table", whole((1024, 512), BF16), (up, target, maps), [VM, SM, VM], after
+    )
+
+
+def raise_kernel(mine_ref, other_ref, table_ref, slot_ref, out_ref):
     packed = (mine_ref[...].astype(F32) + other_ref[...].astype(F32)).astype(BF16).astype(F32)
     turned = pltpu.roll(packed, RANK, 1)
     left = lanes(256) < RANK
@@ -306,41 +321,21 @@
         [jnp.where(left, packed, turned), jnp.where(left, turned, packed)], axis=0
     )
     slot = jnp.broadcast_to(slot_ref[...], (512, 128))
-    kept = resident_slot(slot, target_ref)
     high = (lanes(512) >= RANK).astype(jnp.int32)
-    total = jnp.zeros((512, 512), F32)
-    for j in range(CHIPS):
-        raised = jnp.where(kept == 2 * j + high, both, 0.0).astype(BF16)
-        total += jnp.dot(raised, up_ref[j * 128 : (j + 1) * 128, :], preferred_element_type=F32)
-    even = jnp.zeros((512, 256), F32)
-    odd = jnp.zeros((512, 256), F32)
-    turn = (((1,), (1,)), ((), ()))
-    for k in range(CHIPS):
-        maps = maps_ref[2 * k + 1]
-        fresh = jnp.where(slot == target_ref[k], both, 0.0)
-        even += lax.dot_general(
-            jnp.where(high == 0, fresh, 0.0).astype(BF16), maps, turn, preferred_element_type=F32
-        )
-        odd += lax.dot_general(
-            jnp.where(high == 1, fresh, 0.0).astype(BF16), maps, turn, preferred_element_type=F32
-        )
-    row = lax.broadcasted_iota(jnp.int32, (256, 512), 0)
-    col = lax.broadcasted_iota(jnp.int32, (256, 512), 1)
-    to_even = jnp.where(col == 2 * row, 1.0, 0.0).astype(BF16)
-    to_odd = jnp.where(col == 2 * row + 1, 1.0, 0.0).astype(BF16)
-    total += jnp.dot(even.astype(BF16), to_even, preferred_element_type=F32)
-    total += jnp.dot(odd.astype(BF16), to_odd, preferred_element_type=F32)
+    raised = jnp.concatenate(
+        [jnp.where(slot == 2 * j + high, both, 0.0).astype(BF16) for j in range(CHIPS)], axis=1
+    )
+    total = jnp.dot(raised, table_ref[...], preferred_element_type=F32)
     out_ref[...] = (SCALE * total).astype(BF16).reshape(16, 32, 512)
 
 
-def raise_features(mine, other, up, slot, target, maps, after=()):
+def raise_features(mine, other, table, slot, after=()):
     return call(
         raise_kernel,
         "raise_features",
         whole((16, 32, 512), BF16),
-        (mine, other, up, slot, target, maps),
-        [VM, VM, VM, VM, SM, VM],
-        after,
+        (mine, other, table, slot),
+        after=after,
     )
 
 
@@ -377,12 +372,10 @@
         fresh_adapter_bundle.reshape(16, 256, 128), "tp", split_axis=0, concat_axis=0, tiled=True
     )
     narrow = x.shape[0] * 16 - WIDE
-    narrow_away = product(x, w, Y_MAJOR, 1, WIDE, narrow, 1792)
+    narrow_away, narrow_own = product(x, w, Y_MAJOR, WIDE, narrow)
     narrow_in = send(narrow_away, 0, 0, 1)
-    wide_away = product(x, w, X_MAJOR, 1, 0, WIDE, 1536, [narrow_away])
+    wide_away, wide_own = product(x, w, X_MAJOR, 0, WIDE, [narrow_away])
     wide_in = send(wide_away, 0, 0, 1)
-    narrow_own = product(x, w, Y_MAJOR, 0, WIDE, narrow, 1792, [wide_away])
-    wide_own = product(x, w, X_MAJOR, 0, 0, WIDE, 1536, [narrow_own])
 
     keep, away = chip_narrow(narrow_own, narrow_in, [wide_own])
     narrow_y = send(away, 1, 0, 0)
@@ -395,9 +388,10 @@
 
     part = shrink_fresh(split, acc, slot, target, maps, [right])
     part = add_parts([part, send(part, 0, 0, 1)])
+    table = up_table(resident_up_maps, target, maps, [part])
     rest = [send(part, 0, 1, 0), send(part, 0, 2, 0), send(part, 0, 3, 0)]
 
-    low_here, low_right, low_left, low_far_right, low_far_left = turn_narrow(keep, narrow_y, [part])
+    low_here, low_right, low_left, low_far_right, low_far_left = turn_narrow(keep, narrow_y, [table])
     low_far_right, low_far_left = send(low_far_right, 0, 1, 0), send(low_far_left, 0, 3, 0)
 
     part = add_parts([part, *rest], [low_here])
@@ -406,7 +400,7 @@
     low_right, low_left = near(low_right, low_left, low_far_right, low_far_left, [part])
     low_from_left, low_from_right = send(low_right, 0, 1, 0), send(low_left, 0, 3, 0)
 
-    raised = raise_features(part, other, resident_up_maps, slot, target, maps, [low_right])
+    raised = raise_features(part, other, table, slot, [low_right])
     delta = lax.all_to_all(raised, "tp", split_axis=0, concat_axis=0, tiled=True)
 
     wide_keep, wide_send = turn_wide(here, from_left, from_right, [raised])

time: 101 us -> 97.6 us (0.966)
  Pallas kernels: 40.3 us -> 34.8 us
  waiting for transfers between devices: 18 us -> 23.2 us
  starting transfers between devices: 35 us -> 32.7 us
    pallas_call x16 -> x15, Pallas kernels: 40.3 us -> 34.8 us  [call(): pl.pallas_call(body, in_specs=list(specs or [VM] * count) + [LATER] * len...]
    ppermute x17, waiting for transfers between devices: 18 us -> 23.2 us  [send(): return lax.ppermute(array, 'tp', route(yy, xx, cc))]
    ppermute x17, starting transfers between devices: 21.9 us -> 19.8 us  [send(): return lax.ppermute(array, 'tp', route(yy, xx, cc))]
  transfers between devices with their start and end apart: 19 -> 19, of which waited for: 7 -> 9; matrix products, arithmetic and copies ran while one was open for 0% -> 0% of each run, Pallas kernels for 29% -> 19%
where the time goes in v1:
time: 97.6 us; the launch traced here: 97.1 us
  Pallas kernels  34.8 us (36%)
  starting transfers between devices  32.7 us (34%)
  waiting for transfers between devices  23.2 us (24%)
  local copies, waits for them, and re-layouts  6.26 us (6%)
    pallas_call x15, Pallas kernels, call(): pl.pallas_call(body, in_specs=list(specs or [VM] * count) + [LATER] * len...  34.8 us
    ppermute x17, waiting for transfers between devices, send(): return lax.ppermute(array, 'tp', route(yy, xx, cc))  23.2 us
    ppermute x17, starting transfers between devices, send(): return lax.ppermute(array, 'tp', route(yy, xx, cc))  19.8 us
    all_to_all x1, starting transfers between devices, local(): lax.all_to_all(raised, 'tp', split_axis=0, concat_axis=0, tiled=True)  8.81 us
    unnamed x40, local copies, waits for them, and re-layouts  6.11 us
    all_to_all x1, starting transfers between devices, local(): lax.all_to_all(fresh_adapter_bundle.reshape(16, 256, 128), 'tp', split_ax...  4 us
  transfers between devices with their start and end apart: 19, of which 9 were waited for; matrix products, arithmetic and copies ran while one was open for 0% of the time, Pallas kernels for 19%

profile of v1, /device:TPU:1, one launch (start us, length us, event | category | flops | bytes accessed | tf_op | source)
XLA Modules:
  0.0 97.1 jit_solution(13004372121792387206)
XLA Ops:
  0.0 7.1 %product.2 = (bf16[256,3584]{1,0:T(8,128)(2,1)}, bf16[256,3584]{1,0:T(8,128)(2,1)}) custom-call(bf16[512,512]{1,0:T(8,128)(2,1)} %refs_0_.7, bf16[512,8192]{1,0:T(8,128)(2,1)} %refs_1_.5), custom_call_target="tpu_custom_call" | custom-call | flops 1024 | bytes 1024 | tf_op jit(solution)/shard_map/product/pallas_call | solution.py:73
  7.1 8.2 %product.3 = (bf16[256,4608]{1,0:T(8,128)(2,1)}, bf16[256,4608]{1,0:T(8,128)(2,1)}) custom-call(bf16[512,512]{1,0:T(8,128)(2,1)} %refs_0_.7, bf16[512,8192]{1,0:T(8,128)(2,1)} %refs_1_.5, bf16[256,3584]{1,0:T(8,128)(2,1)} %get-tuple-element.29.refs_2_), custom_call_target="tpu_custom_call" | custom-call | flops 1024 | bytes 1024 | tf_op jit(solution)/shard_map/product/pallas_call | solution.py:73
  15.3 3.3 %collective-permute-start = (bf16[256,4608]{1,0:T(8,128)(2,1)}, bf16[256,4608]{1,0:T(8,128)(2,1)}, u32[]{:S(2)}, u32[]{:S(2)}) collective-permute-start(bf16[256,4608]{1,0:T(8,128)(2,1)} %get-tuple-element.31), channel_id=1, source_target_pairs={{0,1},{1,0},{2,3},{3,2},{4,5},{5,4},{6,7},{7,6},{8,9},{9,8},{10,11... | collective-permute-start | bytes 7077896 | tf_op jit(solution)/shard_map/ppermute | solution.py:34
  18.6 0.1 collective-permute-start.1
  18.7 4.0 %all-to-all-start = ((bf16[16,256,128]{2,1,0:T(8,128)(2,1)}), bf16[16,256,128]{2,1,0:T(8,128)(2,1)S(1)}, u32[]{:S(2)}, u32[]{:S(2)}) async-start(bf16[16,256,128]{2,1,0:T(8,128)(2,1)} %bitcast.2), calls=%async_computation | async-start | bytes 2097152 | tf_op jit(solution)/shard_map/all_to_all | solution.py:371
  22.7 3.0 %collective-permute-done.1.refs_1_ = bf16[256,3584]{1,0:T(8,128)(2,1)} collective-permute-done((bf16[256,3584]{1,0:T(8,128)(2,1)}, bf16[256,3584]{1,0:T(8,128)(2,1)}, u32[]{:S(2)}, u32[]{:S(2)}) %collective-permute-start.1) | collective-permute-done | bytes 1835040 | tf_op jit(solution)/shard_map/ppermute | solution.py:34
  25.8 0.0 copy-done.3
  25.8 1.7 %copy-done = bf16[256,4608]{1,0:T(8,128)(2,1)S(1)} copy-done((bf16[256,4608]{1,0:T(8,128)(2,1)S(1)}, bf16[256,4608]{1,0:T(8,128)(2,1)}, u32[]{:S(2)}) %copy-start) | copy-done | bytes 2359320
  27.4 3.1 %chip_narrow.1 = (bf16[128,3584]{1,0:T(8,128)(2,1)S(1)}, bf16[128,3584]{1,0:T(8,128)(2,1)}) custom-call(bf16[256,3584]{1,0:T(8,128)(2,1)S(1)} %copy-done.3, bf16[256,3584]{1,0:T(8,128)(2,1)} %collective-permute-done.1.refs_1_, bf16[256,4608]{1,0:T(8,128)(2,1)S(1)} %copy-done), custom_call_target="tpu_custom_call" | custom-call | flops 1024 | bytes 1024 | tf_op jit(solution)/shard_map/chip_narrow/pallas_call | solution.py:73
  30.6 1.0 %copy-done.8 = bf16[128,3584]{1,0:T(8,128)(2,1)} copy-done((bf16[128,3584]{1,0:T(8,128)(2,1)}, bf16[128,3584]{1,0:T(8,128)(2,1)S(1)}, u32[]{:S(2)}) %copy-start.8) | copy-done | bytes 917528
  31.6 0.1 collective-permute-start.10
  31.7 0.0 collective-permute-done.refs_1_
  31.7 3.2 %chip_wide.1 = (bf16[64,4608]{1,0:T(8,128)(2,1)S(1)}, bf16[64,4608]{1,0:T(8,128)(2,1)S(1)}, bf16[64,4608]{1,0:T(8,128)(2,1)S(1)}, bf16[64,2304]{1,0:T(8,128)(2,1)}, bf16[64,2304]{1,0:T(8,128)(2,1)}) custom-call(bf16[256,4608]{1,0:T(8,128)(2,1)S(1)} %copy-done.1, bf16[256,4608]{1,0:T(8,128)(2,1)} %collective-permute-done.refs_1_, ...), custom_call_target="tpu_custom_call" | custom-call | flops 1024 | bytes 1024 | tf_op jit(solution)/shard_map/chip_wide/pallas_call | solution.py:73
  34.9 0.8 copy-done.10
  35.7 0.8 copy-done.12
  36.6 0.6 collective-permute-start.2
  37.2 2.0 %collective-permute-start.3 = (bf16[64,2304]{1,0:T(8,128)(2,1)}, bf16[64,2304]{1,0:T(8,128)(2,1)}, u32[]{:S(2)}, u32[]{:S(2)}) collective-permute-start(bf16[64,2304]{1,0:T(8,128)(2,1)} %get-tuple-element.38), channel_id=1, source_target_pairs={{0,6},{1,7},{2,0},{3,1},{4,2},{5,3},{6,4},{7,5},{8,14},{9,15},{10,... | collective-permute-start | bytes 884744 | tf_op jit(solution)/shard_map/ppermute | solution.py:34
  39.2 0.1 copy.9.refs_2_.refs_3_
  39.4 2.1 %shrink_resident.1 = (f32[512,128]{1,0:T(8,128)S(1)}, bf16[512,512]{1,0:T(8,128)(2,1)S(1)}) custom-call(bf16[512,512]{1,0:T(8,128)(2,1)S(1)} %copy-done.2, bf16[512,1024]{1,0:T(8,128)(2,1)S(1)} %copy-done.5, s32[512,1]{1,0:T(8,128)S(1)} %copy.9.refs_2_.refs_3_, s32[16]{0:T(128)S(1)} %copy-done.17, bf16[64,4608]{1,0:T(8,128)(2,1)S(1)} %get-tuple-element.34.refs_4_.refs_0_), custom_call_target="tpu_custom_call" | custom-call | flops 1024 | bytes 1024 | tf_op jit(solution)/shard_map/shrink_resident/pallas_call | solution.py:73
  41.5 0.0 copy-start.15
  41.5 0.8 copy-done.15
  42.3 4.0 %collective-permute-done.2.refs_2_ = bf16[64,2304]{1,0:T(8,128)(2,1)} collective-permute-done((bf16[64,2304]{1,0:T(8,128)(2,1)}, bf16[64,2304]{1,0:T(8,128)(2,1)}, u32[]{:S(2)}, u32[]{:S(2)}) %collective-permute-start.2) | collective-permute-done | bytes 294944 | tf_op jit(solution)/shard_map/ppermute | solution.py:34
  46.3 0.0 collective-permute-done.3.refs_3_
  46.3 0.0 copy-done.11
  46.3 0.0 copy-done.13
  46.3 0.0 copy-start.4
  46.3 2.3 %near.2 = (bf16[64,4608]{1,0:T(8,128)(2,1)}, bf16[64,4608]{1,0:T(8,128)(2,1)}) custom-call(bf16[64,4608]{1,0:T(8,128)(2,1)S(1)} %copy-done.11, bf16[64,4608]{1,0:T(8,128)(2,1)S(1)} %copy-done.13, bf16[64,2304]{1,0:T(8,128)(2,1)} %collective-permute-done.2.refs_2_, bf16[64,2304]{1,0:T(8,128)(2,1)} %collective-permute-done.3.refs_3_, ...), custom_call_target="tpu_custom_call" | custom-call | flops 1024 | bytes 1024 | tf_op jit(solution)/shard_map/near/pallas_call | solution.py:73
  48.6 0.0 collective-permute-start.4
  48.6 0.0 copy-done.6
  48.6 2.7 %collective-permute-start.5 = (bf16[64,4608]{1,0:T(8,128)(2,1)}, bf16[64,4608]{1,0:T(8,128)(2,1)}, u32[]{:S(2)}, u32[]{:S(2)}) collective-permute-start(bf16[64,4608]{1,0:T(8,128)(2,1)} %get-tuple-element.41), channel_id=1, source_target_pairs={{0,6},{1,7},{2,0},{3,1},{4,2},{5,3},{6,4},{7,5},{8,14},{9,15},{10,... | collective-permute-start | bytes 1769480 | tf_op jit(solution)/shard_map/ppermute | solution.py:34
  51.3 0.0 all-to-all-done.refs_4_.refs_2_
  51.3 0.9 copy-done.7
  52.3 1.9 %shrink_fresh.1.refs_0_ = bf16[256,128]{1,0:T(8,128)(2,1)S(1)} custom-call(bf16[512,512]{1,0:T(8,128)(2,1)S(1)} %copy-done.16, f32[512,128]{1,0:T(8,128)S(1)} %copy-done.7, s32[512,1]{1,0:T(8,128)S(1)} %copy.9.refs_2_.refs_3_, s32[16]{0:T(128)S(1)} %copy-done.17, bf16[16,256,128]{2,1,0:T(8,128)(2,1)S(1)} %all-to-all-done.refs_4_.refs_2_, ...), custom_call_target="tpu_custom_call" | custom-call | flops 1024 | bytes 1024 | tf_op jit(solution)/shard_map/shrink_fresh/pallas_call | solution.py:73
  54.2 1.8 %collective-permute-start.6 = (bf16[256,128]{1,0:T(8,128)(2,1)S(1)}, bf16[256,128]{1,0:T(8,128)(2,1)S(1)}, u32[]{:S(2)}, u32[]{:S(2)}) collective-permute-start(bf16[256,128]{1,0:T(8,128)(2,1)S(1)} %shrink_fresh.1.refs_0_), channel_id=1, source_target_pairs={{0,1},{1,0},{2,3},{3,2},{4,5},{5,4},{6,7},{7,6},{8,9},{9,8},{10,11... | collective-permute-start | bytes 196616 | tf_op jit(solution)/shard_map/ppermute | solution.py:34
  56.0 0.9 collective-permute-done.6.refs_1_
  56.9 0.1 collective-permute-start.7
  57.0 2.6 %collective-permute-start.8 = (bf16[256,128]{1,0:T(8,128)(2,1)S(1)}, bf16[256,128]{1,0:T(8,128)(2,1)S(1)}, u32[]{:S(2)}, u32[]{:S(2)}) collective-permute-start(bf16[256,128]{1,0:T(8,128)(2,1)S(1)} %add_parts.2.refs_3_.refs_0_), channel_id=1, source_target_pairs={{0,4},{1,5},{2,6},{3,7},{4,0},{5,1},{6,2},{7,3},{8,12},{9,13},{10,... | collective-permute-start | bytes 196616 | tf_op jit(solution)/shard_map/ppermute | solution.py:34
  59.6 0.0 collective-permute-done.10.refs_1_
  59.6 0.3 collective-permute-start.9
  60.0 1.3 %up_table.1.refs_2_ = bf16[1024,512]{1,0:T(8,128)(2,1)S(1)} custom-call(bf16[1024,512]{1,0:T(8,128)(2,1)S(1)} %copy-done.4, s32[16]{0:T(128)S(1)} %copy-done.17, bf16[16,256,128]{2,1,0:T(8,128)(2,1)S(1)} %all-to-all-done.refs_4_.refs_2_, bf16[256,128]{1,0:T(8,128)(2,1)S(1)} %add_parts.2.refs_3_.refs_0_), custom_call_target="tpu_custom_call" | custom-call | flops 1024 | bytes 1024 | tf_op jit(solution)/shard_map/up_table/pallas_call | solution.py:73
  61.3 1.4 %turn_narrow.1 = (bf16[32,3584]{1,0:T(8,128)(2,1)S(1)}, bf16[32,3584]{1,0:T(8,128)(2,1)S(1)}, bf16[32,3584]{1,0:T(8,128)(2,1)S(1)}, bf16[32,1792]{1,0:T(8,128)(2,1)S(1)}, bf16[32,1792]{1,0:T(8,128)(2,1)S(1)}) custom-call(bf16[128,3584]{1,0:T(8,128)(2,1)S(1)} %copy-done.9, bf16[128,3584]{1,0:T(8,128)(2,1)} %collective-permute-done.10.refs_1_, ...), custom_call_target="tpu_custom_call" | custom-call | flops 1024 | bytes 1024 | tf_op jit(solution)/shard_map/turn_narrow/pallas_call | solution.py:73
  62.7 2.5 %collective-permute-done.7.refs_1_ = bf16[256,128]{1,0:T(8,128)(2,1)S(1)} collective-permute-done((bf16[256,128]{1,0:T(8,128)(2,1)S(1)}, bf16[256,128]{1,0:T(8,128)(2,1)S(1)}, u32[]{:S(2)}, u32[]{:S(2)}) %collective-permute-start.7) | collective-permute-done | bytes 65568 | tf_op jit(solution)/shard_map/ppermute | solution.py:34
  65.2 0.0 collective-permute-start.12
  65.2 1.5 %collective-permute-done.8.refs_2_ = bf16[256,128]{1,0:T(8,128)(2,1)S(1)} collective-permute-done((bf16[256,128]{1,0:T(8,128)(2,1)S(1)}, bf16[256,128]{1,0:T(8,128)(2,1)S(1)}, u32[]{:S(2)}, u32[]{:S(2)}) %collective-permute-start.8) | collective-permute-done | bytes 65568 | tf_op jit(solution)/shard_map/ppermute | solution.py:34
  66.7 1.2 %collective-permute-start.13 = (bf16[32,1792]{1,0:T(8,128)(2,1)S(1)}, bf16[32,1792]{1,0:T(8,128)(2,1)S(1)}, u32[]{:S(2)}, u32[]{:S(2)}) collective-permute-start(bf16[32,1792]{1,0:T(8,128)(2,1)S(1)} %get-tuple-element.48), channel_id=1, source_target_pairs={{0,6},{1,7},{2,0},{3,1},{4,2},{5,3},{6,4},{7,5},{8,14},{9,15},{10,... | collective-permute-start | bytes 344072 | tf_op jit(solution)/shard_map/ppermute | solution.py:34
  67.9 0.0 collective-permute-done.9.refs_3_
  67.9 0.8 collective-permute-start.11
  68.7 1.6 %collective-permute-done.12.refs_2_ = bf16[32,1792]{1,0:T(8,128)(2,1)S(1)} collective-permute-done((bf16[32,1792]{1,0:T(8,128)(2,1)S(1)}, bf16[32,1792]{1,0:T(8,128)(2,1)S(1)}, u32[]{:S(2)}, u32[]{:S(2)}) %collective-permute-start.12) | collective-permute-done | bytes 114720 | tf_op jit(solution)/shard_map/ppermute | solution.py:34
  70.3 0.0 collective-permute-done.13.refs_3_
  70.3 0.1 near.3
  70.4 0.7 collective-permute-done.11.refs_1_
  71.1 1.6 %raise_features.1.refs_3_ = bf16[16,32,512]{2,1,0:T(8,128)(2,1)} custom-call(bf16[256,128]{1,0:T(8,128)(2,1)S(1)} %add_parts.3.refs_4_.refs_0_, bf16[256,128]{1,0:T(8,128)(2,1)S(1)} %collective-permute-done.11.refs_1_, bf16[1024,512]{1,0:T(8,128)(2,1)S(1)} %up_table.1.refs_2_, s32[512,1]{1,0:T(8,128)S(1)} %copy.9.refs_2_.refs_3_, ...), custom_call_target="tpu_custom_call" | custom-call | flops 1024 | bytes 1024 | tf_op jit(solution)/shard_map/raise_features/pallas_call | solution.py:73
  72.7 8.8 %all-to-all-start.1 = ((bf16[16,32,512]{2,1,0:T(8,128)(2,1)}), bf16[16,32,512]{2,1,0:T(8,128)(2,1)S(1)}, u32[]{:S(2)}, u32[]{:S(2)}) async-start(bf16[16,32,512]{2,1,0:T(8,128)(2,1)} %raise_features.1.refs_3_), calls=%async_computation.1 | async-start | bytes 1048576 | tf_op jit(solution)/shard_map/all_to_all | solution.py:404
  81.5 0.0 collective-permute-done.4.refs_1_
  81.5 0.0 collective-permute-done.5.refs_2_
  81.5 1.4 %turn_wide.1 = (f32[32,4608]{1,0:T(8,128)S(1)}, bf16[32,4608]{1,0:T(8,128)(2,1)S(1)}) custom-call(bf16[64,4608]{1,0:T(8,128)(2,1)S(1)} %get-tuple-element.34.refs_4_.refs_0_, bf16[64,4608]{1,0:T(8,128)(2,1)} %collective-permute-done.4.refs_1_, bf16[64,4608]{1,0:T(8,128)(2,1)} %collective-permute-done.5.refs_2_, bf16[16,32,512]{2,1,0:T(8,128)(2,1)} %raise_features.1.refs_3_), custom_call_target="tpu_custom_call" | custom-call | flops 1024 | bytes 1024 | tf_op jit(solution)/shard_map/turn_wide/pallas_call | solution.py:73
  83.0 1.5 %collective-permute-start.14 = (bf16[32,4608]{1,0:T(8,128)(2,1)S(1)}, bf16[32,4608]{1,0:T(8,128)(2,1)S(1)}, u32[]{:S(2)}, u32[]{:S(2)}) collective-permute-start(bf16[32,4608]{1,0:T(8,128)(2,1)S(1)} %get-tuple-element.51), channel_id=1, source_target_pairs={{0,8},{1,9},{2,10},{3,11},{4,12},{5,13},{6,14},{7,15},{8,0},{9,1},... | collective-permute-start | bytes 884744 | tf_op jit(solution)/shard_map/ppermute | solution.py:34
  84.4 1.2 %collective-permute-start.15 = (bf16[32,3584]{1,0:T(8,128)(2,1)S(1)}, bf16[32,3584]{1,0:T(8,128)(2,1)S(1)}, u32[]{:S(2)}, u32[]{:S(2)}) collective-permute-start(bf16[32,3584]{1,0:T(8,128)(2,1)S(1)} %get-tuple-element.49.refs_4_), channel_id=1, source_target_pairs={{0,2},{1,3},{2,4},{3,5},{4,6},{5,7},{6,0},{7,1},{8,10},{9,11},{10,... | collective-permute-start | bytes 688136 | tf_op jit(solution)/shard_map/ppermute | solution.py:34
  85.6 1.5 %collective-permute-start.16 = (bf16[32,3584]{1,0:T(8,128)(2,1)}, bf16[32,3584]{1,0:T(8,128)(2,1)S(1)}, u32[]{:S(2)}, u32[]{:S(2)}) collective-permute-start(bf16[32,3584]{1,0:T(8,128)(2,1)} %copy-done.18), channel_id=1, source_target_pairs={{0,6},{1,7},{2,0},{3,1},{4,2},{5,3},{6,4},{7,5},{8,14},{9,15},{10,... | collective-permute-start | bytes 688136 | tf_op jit(solution)/shard_map/ppermute | solution.py:34
  87.1 8.6 %collective-permute-done.15.refs_4_ = bf16[32,3584]{1,0:T(8,128)(2,1)S(1)} collective-permute-done((bf16[32,3584]{1,0:T(8,128)(2,1)S(1)}, bf16[32,3584]{1,0:T(8,128)(2,1)S(1)}, u32[]{:S(2)}, u32[]{:S(2)}) %collective-permute-start.15) | collective-permute-done | bytes 229408 | tf_op jit(solution)/shard_map/ppermute | solution.py:34
  95.7 0.0 collective-permute-done.16.refs_5_
  95.7 0.0 all-to-all-done.1.refs_6_
  95.7 0.3 collective-permute-done.14.refs_2_
  96.0 1.1 %finish.1 = bf16[32,8192]{1,0:T(8,128)(2,1)} custom-call(bf16[32,8192]{1,0:T(8,128)(2,1)S(1)} %copy-done.14, f32[32,4608]{1,0:T(8,128)S(1)} %get-tuple-element.50.refs_1_, bf16[32,4608]{1,0:T(8,128)(2,1)S(1)} %collective-permute-done.14.refs_2_, bf16[32,3584]{1,0:T(8,128)(2,1)S(1)} %get-tuple-element.44.refs_4_.refs_3_, ...), custom_call_target="tpu_custom_call" | custom-call | flops 1024 | bytes 1024 | tf_op jit(solution)/shard_map/finish/pallas_call | solution.py:73
  (30 shorter events, 0.1 us)
Async XLA Ops:
  15.3 10.5 %copy-start.3 = (bf16[256,3584]{1,0:T(8,128)(2,1)S(1)}, bf16[256,3584]{1,0:T(8,128)(2,1)}, u32[]{:S(2)}) copy-start(bf16[256,3584]{1,0:T(8,128)(2,1)} %get-tuple-element.32.refs_0_) | copy-start | bytes 5505028
  15.3 16.4 %collective-permute-start = (bf16[256,4608]{1,0:T(8,128)(2,1)}, bf16[256,4608]{1,0:T(8,128)(2,1)}, u32[]{:S(2)}, u32[]{:S(2)}) collective-permute-start(bf16[256,4608]{1,0:T(8,128)(2,1)} %get-tuple-element.31), channel_id=1, source_target_pairs={{0,1},{1,0},{2,3},{3,2},{4,5},{5,4},{6,7},{7,6},{8,9},{9,8},{10,11... | collective-permute-start | bytes 7077896 | tf_op jit(solution)/shard_map/ppermute | solution.py:34
  18.6 7.1 %collective-permute-start.1 = (bf16[256,3584]{1,0:T(8,128)(2,1)}, bf16[256,3584]{1,0:T(8,128)(2,1)}, u32[]{:S(2)}, u32[]{:S(2)}) collective-permute-start(bf16[256,3584]{1,0:T(8,128)(2,1)} %get-tuple-element.29.refs_2_), channel_id=1, source_target_pairs={{0,1},{1,0},{2,3},{3,2},{4,5},{5,4},{6,7},{7,6},{8,9},{9,8},{10,11... | collective-permute-start | bytes 5505032 | tf_op jit(solution)/shard_map/ppermute | solution.py:34
  18.7 32.6 %all-to-all-start = ((bf16[16,256,128]{2,1,0:T(8,128)(2,1)}), bf16[16,256,128]{2,1,0:T(8,128)(2,1)S(1)}, u32[]{:S(2)}, u32[]{:S(2)}) async-start(bf16[16,256,128]{2,1,0:T(8,128)(2,1)} %bitcast.2), calls=%async_computation | async-start | bytes 2097152 | tf_op jit(solution)/shard_map/all_to_all | solution.py:371
  25.8 1.7 %copy-start = (bf16[256,4608]{1,0:T(8,128)(2,1)S(1)}, bf16[256,4608]{1,0:T(8,128)(2,1)}, u32[]{:S(2)}) copy-start(bf16[256,4608]{1,0:T(8,128)(2,1)} %get-tuple-element.30.refs_2_.refs_0_) | copy-start | bytes 7077892
  27.4 4.3 %copy-start.1 = (bf16[256,4608]{1,0:T(8,128)(2,1)S(1)}, bf16[256,4608]{1,0:T(8,128)(2,1)}, u32[]{:S(2)}) copy-start(bf16[256,4608]{1,0:T(8,128)(2,1)} %get-tuple-element.30.refs_2_.refs_0_) | copy-start | bytes 7077892
  30.6 1.0 %copy-start.8 = (bf16[128,3584]{1,0:T(8,128)(2,1)}, bf16[128,3584]{1,0:T(8,128)(2,1)S(1)}, u32[]{:S(2)}) copy-start(bf16[128,3584]{1,0:T(8,128)(2,1)S(1)} %get-tuple-element.43.refs_0_) | copy-start | bytes 2752516
  31.6 7.7 %copy-start.19 = (s32[512]{0:T(512)S(1)}, s32[512]{0:T(512)}, u32[]{:S(2)}) copy-start(s32[512]{0:T(512)} %param.15) | copy-start | bytes 6148
  31.6 7.8 %copy-start.2 = (bf16[512,512]{1,0:T(8,128)(2,1)S(1)}, bf16[512,512]{1,0:T(8,128)(2,1)}, u32[]{:S(2)}) copy-start(bf16[512,512]{1,0:T(8,128)(2,1)} %refs_0_.7) | copy-start | bytes 1572868
  31.6 7.8 %copy-start.5 = (bf16[512,1024]{1,0:T(8,128)(2,1)S(1)}, bf16[512,1024]{1,0:T(8,128)(2,1)}, u32[]{:S(2)}) copy-start(bf16[512,1024]{1,0:T(8,128)(2,1)} %refs_1_.6) | copy-start | bytes 3145732
  31.6 7.9 %copy-start.17 = (s32[16]{0:T(128)S(1)}, s32[16]{0:T(128)}, u32[]{:S(2)}) copy-start(s32[16]{0:T(128)} %refs_1_.7) | copy-start | bytes 196
  31.6 28.0 %collective-permute-start.10 = (bf16[128,3584]{1,0:T(8,128)(2,1)}, bf16[128,3584]{1,0:T(8,128)(2,1)}, u32[]{:S(2)}, u32[]{:S(2)}) collective-permute-start(bf16[128,3584]{1,0:T(8,128)(2,1)} %get-tuple-element.33.refs_2_), channel_id=1, source_target_pairs={{0,8},{1,9},{2,10},{3,11},{4,12},{5,13},{6,14},{7,15},{8,0},{9,1},... | collective-permute-start | bytes 2752520 | tf_op jit(solution)/shard_map/ppermute | solution.py:34
  34.9 0.8 copy-start.10
  35.7 0.8 copy-start.12
  36.6 9.7 %collective-permute-start.2 = (bf16[64,2304]{1,0:T(8,128)(2,1)}, bf16[64,2304]{1,0:T(8,128)(2,1)}, u32[]{:S(2)}, u32[]{:S(2)}) collective-permute-start(bf16[64,2304]{1,0:T(8,128)(2,1)} %get-tuple-element.37), channel_id=1, source_target_pairs={{0,2},{1,3},{2,4},{3,5},{4,6},{5,7},{6,0},{7,1},{8,10},{9,11},{10,... | collective-permute-start | bytes 884744 | tf_op jit(solution)/shard_map/ppermute | solution.py:34
  37.2 9.1 %collective-permute-start.3 = (bf16[64,2304]{1,0:T(8,128)(2,1)}, bf16[64,2304]{1,0:T(8,128)(2,1)}, u32[]{:S(2)}, u32[]{:S(2)}) collective-permute-start(bf16[64,2304]{1,0:T(8,128)(2,1)} %get-tuple-element.38), channel_id=1, source_target_pairs={{0,6},{1,7},{2,0},{3,1},{4,2},{5,3},{6,4},{7,5},{8,14},{9,15},{10,... | collective-permute-start | bytes 884744 | tf_op jit(solution)/shard_map/ppermute | solution.py:34
  39.4 6.9 %copy-start.11 = (bf16[64,4608]{1,0:T(8,128)(2,1)S(1)}, bf16[64,4608]{1,0:T(8,128)(2,1)}, u32[]{:S(2)}) copy-start(bf16[64,4608]{1,0:T(8,128)(2,1)} %copy-done.10) | copy-start | bytes 1769476
  39.4 6.9 %copy-start.13 = (bf16[64,4608]{1,0:T(8,128)(2,1)S(1)}, bf16[64,4608]{1,0:T(8,128)(2,1)}, u32[]{:S(2)}) copy-start(bf16[64,4608]{1,0:T(8,128)(2,1)} %copy-done.12) | copy-start | bytes 1769476
  41.5 0.8 copy-start.15
  42.3 6.3 %copy-start.6 = (f32[512,128]{1,0:T(8,128)}, f32[512,128]{1,0:T(8,128)S(1)}, u32[]{:S(2)}) copy-start(f32[512,128]{1,0:T(8,128)S(1)} %get-tuple-element.39.refs_4_.refs_1_) | copy-start | bytes 786436
  46.3 5.0 %copy-start.16 = (bf16[512,512]{1,0:T(8,128)(2,1)S(1)}, bf16[512,512]{1,0:T(8,128)(2,1)}, u32[]{:S(2)}) copy-start(bf16[512,512]{1,0:T(8,128)(2,1)} %copy-done.15) | copy-start | bytes 1572868
  46.3 13.6 %copy-start.4 = (bf16[1024,512]{1,0:T(8,128)(2,1)S(1)}, bf16[1024,512]{1,0:T(8,128)(2,1)}, u32[]{:S(2)}) copy-start(bf16[1024,512]{1,0:T(8,128)(2,1)} %refs_0_.8) | copy-start | bytes 3145732
  48.6 32.9 %collective-permute-start.4 = (bf16[64,4608]{1,0:T(8,128)(2,1)}, bf16[64,4608]{1,0:T(8,128)(2,1)}, u32[]{:S(2)}, u32[]{:S(2)}) collective-permute-start(bf16[64,4608]{1,0:T(8,128)(2,1)} %get-tuple-element.40.refs_5_), channel_id=1, source_target_pairs={{0,2},{1,3},{2,4},{3,5},{4,6},{5,7},{6,0},{7,1},{8,10},{9,11},{10,... | collective-permute-start | bytes 1769480 | tf_op jit(solution)/shard_map/ppermute | solution.py:34
  48.6 32.9 %collective-permute-start.5 = (bf16[64,4608]{1,0:T(8,128)(2,1)}, bf16[64,4608]{1,0:T(8,128)(2,1)}, u32[]{:S(2)}, u32[]{:S(2)}) collective-permute-start(bf16[64,4608]{1,0:T(8,128)(2,1)} %get-tuple-element.41), channel_id=1, source_target_pairs={{0,6},{1,7},{2,0},{3,1},{4,2},{5,3},{6,4},{7,5},{8,14},{9,15},{10,... | collective-permute-start | bytes 1769480 | tf_op jit(solution)/shard_map/ppermute | solution.py:34
  51.3 1.0 copy-start.7
  54.1 7.2 %copy-start.9 = (bf16[128,3584]{1,0:T(8,128)(2,1)S(1)}, bf16[128,3584]{1,0:T(8,128)(2,1)}, u32[]{:S(2)}) copy-start(bf16[128,3584]{1,0:T(8,128)(2,1)} %copy-done.8) | copy-start | bytes 2752516
  54.2 2.8 %collective-permute-start.6 = (bf16[256,128]{1,0:T(8,128)(2,1)S(1)}, bf16[256,128]{1,0:T(8,128)(2,1)S(1)}, u32[]{:S(2)}, u32[]{:S(2)}) collective-permute-start(bf16[256,128]{1,0:T(8,128)(2,1)S(1)} %shrink_fresh.1.refs_0_), channel_id=1, source_target_pairs={{0,1},{1,0},{2,3},{3,2},{4,5},{5,4},{6,7},{7,6},{8,9},{9,8},{10,11... | collective-permute-start | bytes 196616 | tf_op jit(solution)/shard_map/ppermute | solution.py:34
  56.9 8.3 %collective-permute-start.7 = (bf16[256,128]{1,0:T(8,128)(2,1)S(1)}, bf16[256,128]{1,0:T(8,128)(2,1)S(1)}, u32[]{:S(2)}, u32[]{:S(2)}) collective-permute-start(bf16[256,128]{1,0:T(8,128)(2,1)S(1)} %add_parts.2.refs_3_.refs_0_), channel_id=1, source_target_pairs={{0,2},{1,3},{2,4},{3,5},{4,6},{5,7},{6,0},{7,1},{8,10},{9,11},{10,... | collective-permute-start | bytes 196616 | tf_op jit(solution)/shard_map/ppermute | solution.py:34
  57.0 9.7 %collective-permute-start.8 = (bf16[256,128]{1,0:T(8,128)(2,1)S(1)}, bf16[256,128]{1,0:T(8,128)(2,1)S(1)}, u32[]{:S(2)}, u32[]{:S(2)}) collective-permute-start(bf16[256,128]{1,0:T(8,128)(2,1)S(1)} %add_parts.2.refs_3_.refs_0_), channel_id=1, source_target_pairs={{0,4},{1,5},{2,6},{3,7},{4,0},{5,1},{6,2},{7,3},{8,12},{9,13},{10,... | collective-permute-start | bytes 196616 | tf_op jit(solution)/shard_map/ppermute | solution.py:34
  59.6 8.3 %collective-permute-start.9 = (bf16[256,128]{1,0:T(8,128)(2,1)S(1)}, bf16[256,128]{1,0:T(8,128)(2,1)S(1)}, u32[]{:S(2)}, u32[]{:S(2)}) collective-permute-start(bf16[256,128]{1,0:T(8,128)(2,1)S(1)} %add_parts.2.refs_3_.refs_0_), channel_id=1, source_target_pairs={{0,6},{1,7},{2,0},{3,1},{4,2},{5,3},{6,4},{7,5},{8,14},{9,15},{10,... | collective-permute-start | bytes 196616 | tf_op jit(solution)/shard_map/ppermute | solution.py:34
  65.2 5.1 %collective-permute-start.12 = (bf16[32,1792]{1,0:T(8,128)(2,1)S(1)}, bf16[32,1792]{1,0:T(8,128)(2,1)S(1)}, u32[]{:S(2)}, u32[]{:S(2)}) collective-permute-start(bf16[32,1792]{1,0:T(8,128)(2,1)S(1)} %get-tuple-element.47), channel_id=1, source_target_pairs={{0,2},{1,3},{2,4},{3,5},{4,6},{5,7},{6,0},{7,1},{8,10},{9,11},{10,... | collective-permute-start | bytes 344072 | tf_op jit(solution)/shard_map/ppermute | solution.py:34
  66.7 3.6 %collective-permute-start.13 = (bf16[32,1792]{1,0:T(8,128)(2,1)S(1)}, bf16[32,1792]{1,0:T(8,128)(2,1)S(1)}, u32[]{:S(2)}, u32[]{:S(2)}) collective-permute-start(bf16[32,1792]{1,0:T(8,128)(2,1)S(1)} %get-tuple-element.48), channel_id=1, source_target_pairs={{0,6},{1,7},{2,0},{3,1},{4,2},{5,3},{6,4},{7,5},{8,14},{9,15},{10,... | collective-permute-start | bytes 344072 | tf_op jit(solution)/shard_map/ppermute | solution.py:34
  67.9 3.2 %collective-permute-start.11 = (bf16[256,128]{1,0:T(8,128)(2,1)S(1)}, bf16[256,128]{1,0:T(8,128)(2,1)S(1)}, u32[]{:S(2)}, u32[]{:S(2)}) collective-permute-start(bf16[256,128]{1,0:T(8,128)(2,1)S(1)} %add_parts.3.refs_4_.refs_0_), channel_id=1, source_target_pairs={{0,8},{1,9},{2,10},{3,11},{4,12},{5,13},{6,14},{7,15},{8,0},{9,1},... | collective-permute-start | bytes 196616 | tf_op jit(solution)/shard_map/ppermute | solution.py:34
  70.4 0.7 copy-start.18
  71.1 24.9 %copy-start.14 = (bf16[32,8192]{1,0:T(8,128)(2,1)S(1)}, bf16[32,8192]{1,0:T(8,128)(2,1)}, u32[]{:S(2)}) copy-start(bf16[32,8192]{1,0:T(8,128)(2,1)} %refs_0_.9) | copy-start | bytes 1572868
  72.7 23.1 %all-to-all-start.1 = ((bf16[16,32,512]{2,1,0:T(8,128)(2,1)}), bf16[16,32,512]{2,1,0:T(8,128)(2,1)S(1)}, u32[]{:S(2)}, u32[]{:S(2)}) async-start(bf16[16,32,512]{2,1,0:T(8,128)(2,1)} %raise_features.1.refs_3_), calls=%async_computation.1 | async-start | bytes 1048576 | tf_op jit(solution)/shard_map/all_to_all | solution.py:404
  83.0 13.1 %collective-permute-start.14 = (bf16[32,4608]{1,0:T(8,128)(2,1)S(1)}, bf16[32,4608]{1,0:T(8,128)(2,1)S(1)}, u32[]{:S(2)}, u32[]{:S(2)}) collective-permute-start(bf16[32,4608]{1,0:T(8,128)(2,1)S(1)} %get-tuple-element.51), channel_id=1, source_target_pairs={{0,8},{1,9},{2,10},{3,11},{4,12},{5,13},{6,14},{7,15},{8,0},{9,1},... | collective-permute-start | bytes 884744 | tf_op jit(solution)/shard_map/ppermute | solution.py:34
  84.4 11.3 %collective-permute-start.15 = (bf16[32,3584]{1,0:T(8,128)(2,1)S(1)}, bf16[32,3584]{1,0:T(8,128)(2,1)S(1)}, u32[]{:S(2)}, u32[]{:S(2)}) collective-permute-start(bf16[32,3584]{1,0:T(8,128)(2,1)S(1)} %get-tuple-element.49.refs_4_), channel_id=1, source_target_pairs={{0,2},{1,3},{2,4},{3,5},{4,6},{5,7},{6,0},{7,1},{8,10},{9,11},{10,... | collective-permute-start | bytes 688136 | tf_op jit(solution)/shard_map/ppermute | solution.py:34
  85.6 10.1 %collective-permute-start.16 = (bf16[32,3584]{1,0:T(8,128)(2,1)}, bf16[32,3584]{1,0:T(8,128)(2,1)S(1)}, u32[]{:S(2)}, u32[]{:S(2)}) collective-permute-start(bf16[32,3584]{1,0:T(8,128)(2,1)} %copy-done.18), channel_id=1, source_target_pairs={{0,6},{1,7},{2,0},{3,1},{4,2},{5,3},{6,4},{7,5},{8,14},{9,15},{10,... | collective-permute-start | bytes 688136 | tf_op jit(solution)/shard_map/ppermute | solution.py:34

commit v2 on v1

--- a/solution.py
+++ b/solution.py
@@ -14,7 +14,8 @@
 WIDE = 4608
 VMEM_LIMIT = 16 * 1024 * 1024
 PRODUCT_LIMIT = 56 * 1024 * 1024
-CHUNK = 512
+NARROW_CHUNK = 1792
+WIDE_CHUNK = 1536
 
 
 def place(y, x, core):
@@ -85,43 +86,50 @@
 Y_MAJOR = [(yy, xx) for yy in range(2) for xx in range(4)]
 
 
-def product(x, w, order, first, width, after=()):
-    chunks = width // CHUNK
-
-    def kernel(x_ref, w_ref, away_ref, own_ref, rows_ref, held_ref, sems):
+def product(x, w, order, first, width, chunk, after=()):
+    chunks = width // chunk
+
+    def kernel(x_ref, w_ref, *refs):
+        away_refs = refs[:chunks]
+        own_ref, rows_ref, held_ref, done_ref, sems, away_sems = refs[chunks:]
+
         def copy(i):
-            cols = pl.ds(pl.multiple_of(first + i * CHUNK, CHUNK), CHUNK)
+            cols = pl.ds(pl.multiple_of(first + i * chunk, 128), chunk)
             return pltpu.make_async_copy(w_ref.at[:, cols], held_ref.at[i], sems.at[i])
 
-        @pl.loop(0, chunks)
-        def _(i):
+        def leave(i):
+            return pltpu.make_async_copy(done_ref.at[i], away_refs[i], away_sems.at[i])
+
+        for i in range(chunks):
             copy(i).start()
-
         for i, (yy, xx) in enumerate(order):
             for cc, top in ((1, 0), (0, 256)):
                 rows_ref[top + i * 32 : top + (i + 1) * 32, :] = x_ref[
                     rows_at(partner(yy, xx, cc), 32), :
                 ]
-
-        @pl.loop(0, chunks)
-        def _(i):
+        for i in range(chunks):
             copy(i).wait()
             part = jnp.dot(rows_ref[...], held_ref[i], preferred_element_type=F32).astype(BF16)
-            cols = pl.ds(pl.multiple_of(i * CHUNK, CHUNK), CHUNK)
-            away_ref[:, cols] = part[:256]
-            own_ref[:, cols] = part[256:]
+            done_ref[i] = part[:256]
+            leave(i).start()
+            own_ref[:, i * chunk : (i + 1) * chunk] = part[256:]
+        for i in range(chunks):
+            leave(i).wait()
 
     return call(
         kernel,
         "product",
-        [whole((256, width), BF16)] * 2,
+        [whole((256, chunk), BF16)] * chunks + [whole((256, width), BF16)],
         (x, w),
         [VM, pl.BlockSpec(memory_space=pltpu.HBM)],
         after,
         limit=PRODUCT_LIMIT,
+        out_specs=[pl.BlockSpec(memory_space=pltpu.HBM)] * chunks + [VM],
         scratch_shapes=[
             pltpu.VMEM((512, 512), BF16),
-            pltpu.VMEM((chunks, 512, CHUNK), BF16),
+            pltpu.VMEM((chunks, 512, chunk), BF16),
+            pltpu.VMEM((chunks, 256, chunk), BF16),
+            pltpu.SemaphoreType.DMA((chunks,)),
             pltpu.SemaphoreType.DMA((chunks,)),
         ],
     )
@@ -129,42 +137,52 @@
 
 def chip_narrow(own, away, after=()):
     width = own.shape[1]
-
-    def kernel(own_ref, away_ref, keep_ref, send_ref):
-        @pl.loop(0, width // CHUNK)
-        def _(j):
-            cols = pl.ds(pl.multiple_of(j * CHUNK, CHUNK), CHUNK)
-            total = plus(own_ref[:, cols], away_ref[:, cols]).astype(BF16)
-            keep_ref[:, cols] = total[:128]
-            send_ref[:, cols] = total[128:]
-
-    return call(
-        kernel, "chip_narrow", [whole((128, width), BF16)] * 2, (own, away), after=after
+    step = 256
+
+    def kernel(own_ref, *refs):
+        keep_ref, send_ref = refs[len(away) :]
+        for i, away_ref in enumerate(refs[: len(away)]):
+
+            @pl.loop(0, away_ref.shape[1] // step)
+            def _(j):
+                cols = pl.ds(pl.multiple_of(i * away_ref.shape[1] + j * step, step), step)
+                part = pl.ds(pl.multiple_of(j * step, step), step)
+                total = plus(own_ref[:, cols], away_ref[:, part]).astype(BF16)
+                keep_ref[:, cols] = total[:128]
+                send_ref[:, cols] = total[128:]
+
+    return call(
+        kernel, "chip_narrow", [whole((128, width), BF16)] * 2, (own, *away), after=after
     )
 
 
 def chip_wide(own, away, after=()):
     width = own.shape[1]
     half = width // 2
+    chunk = away[0].shape[1]
     step = 256
 
-    def kernel(own_ref, away_ref, here_ref, right_ref, left_ref, far_right_ref, far_left_ref):
-        for side, far_ref in enumerate((far_right_ref, far_left_ref)):
-
-            @pl.loop(0, half // step)
-            def _(j):
-                cols = pl.ds(pl.multiple_of(side * half + j * step, step), step)
-                total = plus(own_ref[:, cols], away_ref[:, cols]).astype(BF16)
-                here_ref[:, cols] = total[:64]
-                right_ref[:, cols] = total[64:128]
-                far_ref[:, pl.ds(pl.multiple_of(j * step, step), step)] = total[128:192]
-                left_ref[:, cols] = total[192:]
+    def kernel(own_ref, *refs):
+        here_ref, right_ref, left_ref, far_right_ref, far_left_ref = refs[len(away) :]
+        for first in range(0, width, step):
+            cols = slice(first, first + step)
+            part = first % chunk
+            total = plus(
+                own_ref[:, cols], refs[first // chunk][:, part : part + step]
+            ).astype(BF16)
+            here_ref[:, cols] = total[:64]
+            right_ref[:, cols] = total[64:128]
+            if first < half:
+                far_right_ref[:, cols] = total[128:192]
+            else:
+                far_left_ref[:, first - half : first - half + step] = total[128:192]
+            left_ref[:, cols] = total[192:]
 
     return call(
         kernel,
         "chip_wide",
         [whole((64, width), BF16)] * 3 + [whole((64, half), BF16)] * 2,
-        (own, away),
+        (own, *away),
         after=after,
     )
 
@@ -372,38 +390,36 @@
         fresh_adapter_bundle.reshape(16, 256, 128), "tp", split_axis=0, concat_axis=0, tiled=True
     )
     narrow = x.shape[0] * 16 - WIDE
-    narrow_away, narrow_own = product(x, w, Y_MAJOR, WIDE, narrow)
-    narrow_in = send(narrow_away, 0, 0, 1)
-    wide_away, wide_own = product(x, w, X_MAJOR, 0, WIDE, [narrow_away])
-    wide_in = send(wide_away, 0, 0, 1)
-
-    keep, away = chip_narrow(narrow_own, narrow_in, [wide_own])
+    *narrow_away, narrow_own = product(x, w, Y_MAJOR, WIDE, narrow, NARROW_CHUNK)
+    narrow_in = [send(away, 0, 0, 1) for away in narrow_away]
+    *wide_away, wide_own = product(x, w, X_MAJOR, 0, WIDE, WIDE_CHUNK, narrow_away[:1])
+    wide_in = [send(away, 0, 0, 1) for away in wide_away]
+
+    acc, split = shrink_resident(x, resident_down_maps, slot, target, [wide_own])
+    part = shrink_fresh(split, acc, slot, target, maps)
+    part_in = send(part, 0, 0, 1)
+
+    keep, away = chip_narrow(narrow_own, narrow_in, [part])
     narrow_y = send(away, 1, 0, 0)
-    here, right, left, far_right, far_left = chip_wide(wide_own, wide_in, [away])
+    part = add_parts([part, part_in], [away])
+    rest = [send(part, 0, 1, 0), send(part, 0, 2, 0), send(part, 0, 3, 0)]
+    here, right, left, far_right, far_left = chip_wide(wide_own, wide_in, [part])
     far_right, far_left = send(far_right, 0, 1, 0), send(far_left, 0, 3, 0)
-    acc, split = shrink_resident(x, resident_down_maps, slot, target, [here])
-
-    right, left = near(right, left, far_right, far_left, [acc])
+    part = add_parts([part, *rest], [here])
+    other = send(part, 1, 0, 0)
+    table = up_table(resident_up_maps, target, maps, [part])
+
+    right, left = near(right, left, far_right, far_left, [table])
     from_left, from_right = send(right, 0, 1, 0), send(left, 0, 3, 0)
-
-    part = shrink_fresh(split, acc, slot, target, maps, [right])
-    part = add_parts([part, send(part, 0, 0, 1)])
-    table = up_table(resident_up_maps, target, maps, [part])
-    rest = [send(part, 0, 1, 0), send(part, 0, 2, 0), send(part, 0, 3, 0)]
-
-    low_here, low_right, low_left, low_far_right, low_far_left = turn_narrow(keep, narrow_y, [table])
+    raised = raise_features(part, other, table, slot, [right])
+    delta = lax.all_to_all(raised, "tp", split_axis=0, concat_axis=0, tiled=True)
+
+    low_here, low_right, low_left, low_far_right, low_far_left = turn_narrow(keep, narrow_y, [raised])
     low_far_right, low_far_left = send(low_far_right, 0, 1, 0), send(low_far_left, 0, 3, 0)
-
-    part = add_parts([part, *rest], [low_here])
-    other = send(part, 1, 0, 0)
-
-    low_right, low_left = near(low_right, low_left, low_far_right, low_far_left, [part])
+    low_right, low_left = near(low_right, low_left, low_far_right, low_far_left, [low_here])
     low_from_left, low_from_right = send(low_right, 0, 1, 0), send(low_left, 0, 3, 0)
 
-    raised = raise_features(part, other, table, slot, [low_right])
-    delta = lax.all_to_all(raised, "tp", split_axis=0, concat_axis=0, tiled=True)
-
-    wide_keep, wide_send = turn_wide(here, from_left, from_right, [raised])
+    wide_keep, wide_send = turn_wide(here, from_left, from_right, [low_right])
     wide_y = send(wide_send, 1, 0, 0)
     return call(
         finish_kernel,

time: 97.6 us -> 99.5 us (1.019)
  waiting for transfers between devices: 23.2 us -> 26.8 us
  Pallas kernels: 34.8 us -> 32.9 us
  local copies, waits for them, and re-layouts: 6.26 us -> 4.97 us
    ppermute x17 -> x20, waiting for transfers between devices: 23.2 us -> 26.8 us  [send(): return lax.ppermute(array, 'tp', route(yy, xx, cc))]
    all_to_all x1, starting transfers between devices: 4 us -> 6.83 us  [local(): lax.all_to_all(fresh_adapter_bundle.reshape(16, 256, 128), 'tp', split_ax...]
    ppermute x17 -> x20, starting transfers between devices: 19.8 us -> 17.1 us  [send(): return lax.ppermute(array, 'tp', route(yy, xx, cc))]
    pallas_call x15, Pallas kernels: 34.8 us -> 32.9 us  [call(): pl.pallas_call(body, in_specs=list(specs or [VM] * count) + [LATER] * len...]
    unnamed x40 -> x22, local copies, waits for them, and re-layouts: 6.11 us -> 4.83 us
  transfers between devices with their start and end apart: 19 -> 22, of which waited for: 9 -> 7; matrix products, arithmetic and copies ran while one was open for 0% -> 0% of each run, Pallas kernels for 19% -> 32%
where the time goes in v2:
time: 99.5 us; the launch traced here: 98.1 us
  starting transfers between devices  33.2 us (33%)
  Pallas kernels  32.9 us (33%)
  waiting for transfers between devices  26.8 us (27%)
  local copies, waits for them, and re-layouts  4.97 us (5%)
    pallas_call x15, Pallas kernels, call(): pl.pallas_call(body, in_specs=list(specs or [VM] * count) + [LATER] * len...  32.9 us
    ppermute x20, waiting for transfers between devices, send(): return lax.ppermute(array, 'tp', route(yy, xx, cc))  26.8 us
    ppermute x20, starting transfers between devices, send(): return lax.ppermute(array, 'tp', route(yy, xx, cc))  17.1 us
    all_to_all x1, starting transfers between devices, local(): lax.all_to_all(raised, 'tp', split_axis=0, concat_axis=0, tiled=True)  9.32 us
    all_to_all x1, starting transfers between devices, local(): lax.all_to_all(fresh_adapter_bundle.reshape(16, 256, 128), 'tp', split_ax...  6.83 us
    unnamed x22, local copies, waits for them, and re-layouts  4.83 us
  transfers between devices with their start and end apart: 22, of which 7 were waited for; matrix products, arithmetic and copies ran while one was open for 0% of the time, Pallas kernels for 32%

profile of v2, /device:TPU:1, one launch (start us, length us, event | category | flops | bytes accessed | tf_op | source)
XLA Modules:
  0.0 98.1 jit_solution(683149007169576171)
XLA Ops:
  0.0 6.8 %all-to-all-start = ((bf16[16,256,128]{2,1,0:T(8,128)(2,1)}), bf16[16,256,128]{2,1,0:T(8,128)(2,1)S(1)}, u32[]{:S(2)}, u32[]{:S(2)}) async-start(bf16[16,256,128]{2,1,0:T(8,128)(2,1)} %bitcast.2), calls=%async_computation | async-start | bytes 2097152 | tf_op jit(solution)/shard_map/all_to_all | solution.py:389
  6.8 7.2 %product.2 = (bf16[256,1792]{1,0:T(8,128)(2,1)}, bf16[256,1792]{1,0:T(8,128)(2,1)}, bf16[256,3584]{1,0:T(8,128)(2,1)}) custom-call(bf16[512,512]{1,0:T(8,128)(2,1)} %refs_0_.7, bf16[512,8192]{1,0:T(8,128)(2,1)} %refs_1_.5), custom_call_target="tpu_custom_call" | custom-call | flops 1024 | bytes 1024 | tf_op jit(solution)/shard_map/product/pallas_call | solution.py:74
  14.1 0.2 collective-permute-start.5
  14.3 0.5 collective-permute-start.4
  14.7 7.7 %product.3 = (bf16[256,1536]{1,0:T(8,128)(2,1)}, bf16[256,1536]{1,0:T(8,128)(2,1)}, bf16[256,1536]{1,0:T(8,128)(2,1)}, bf16[256,4608]{1,0:T(8,128)(2,1)}) custom-call(bf16[512,512]{1,0:T(8,128)(2,1)} %refs_0_.7, bf16[512,8192]{1,0:T(8,128)(2,1)} %refs_1_.5, bf16[256,1792]{1,0:T(8,128)(2,1)} %get-tuple-element.32.refs_2_), custom_call_target="tpu_custom_call" | custom-call | flops 1024 | bytes 1024 | tf_op jit(solution)/shard_map/product/pallas_call | solution.py:74
  22.5 0.3 collective-permute-start
  22.8 0.3 collective-permute-start.1
  23.1 0.2 collective-permute-start.2
  23.3 0.1 copy.9.refs_2_.refs_3_
  23.5 1.7 %copy-done = bf16[256,4608]{1,0:T(8,128)(2,1)S(1)} copy-done((bf16[256,4608]{1,0:T(8,128)(2,1)S(1)}, bf16[256,4608]{1,0:T(8,128)(2,1)}, u32[]{:S(2)}) %copy-start) | copy-done | bytes 2359320
  25.1 2.1 %shrink_resident.1 = (f32[512,128]{1,0:T(8,128)S(1)}, bf16[512,512]{1,0:T(8,128)(2,1)S(1)}) custom-call(bf16[512,512]{1,0:T(8,128)(2,1)S(1)} %copy-done.2, bf16[512,1024]{1,0:T(8,128)(2,1)S(1)} %copy-done.4, s32[512,1]{1,0:T(8,128)S(1)} %copy.9.refs_2_.refs_3_, s32[16]{0:T(128)S(1)} %copy-done.9, bf16[256,4608]{1,0:T(8,128)(2,1)S(1)} %copy-done), custom_call_target="tpu_custom_call" | custom-call | flops 1024 | bytes 1024 | tf_op jit(solution)/shard_map/shrink_resident/pallas_call | solution.py:74
  27.2 0.0 copy-start.7
  27.2 0.7 copy-done.7
  27.9 0.0 all-to-all-done.refs_4_.refs_2_
  27.9 0.9 copy-done.8
  28.9 1.9 %shrink_fresh.1.refs_3_.refs_0_ = bf16[256,128]{1,0:T(8,128)(2,1)S(1)} custom-call(bf16[512,512]{1,0:T(8,128)(2,1)S(1)} %get-tuple-element.37.refs_0_, f32[512,128]{1,0:T(8,128)S(1)} %copy-done.8, s32[512,1]{1,0:T(8,128)S(1)} %copy.9.refs_2_.refs_3_, s32[16]{0:T(128)S(1)} %copy-done.9, bf16[16,256,128]{2,1,0:T(8,128)(2,1)S(1)} %all-to-all-done.refs_4_.refs_2_), custom_call_target="tpu_custom_call" | custom-call | flops 1024 | bytes 1024 | tf_op jit(solution)/shard_map/shrink_fresh/pallas_call | solution.py:74
  30.8 0.0 collective-permute-done.5.refs_2_
  30.8 0.0 collective-permute-done.4.refs_1_
  30.9 1.5 %copy-done.3 = bf16[256,3584]{1,0:T(8,128)(2,1)S(1)} copy-done((bf16[256,3584]{1,0:T(8,128)(2,1)S(1)}, bf16[256,3584]{1,0:T(8,128)(2,1)}, u32[]{:S(2)}) %copy-start.3) | copy-done | bytes 1835032
  32.3 3.0 %chip_narrow.1 = (bf16[128,3584]{1,0:T(8,128)(2,1)S(1)}, bf16[128,3584]{1,0:T(8,128)(2,1)}) custom-call(bf16[256,3584]{1,0:T(8,128)(2,1)S(1)} %copy-done.3, bf16[256,1792]{1,0:T(8,128)(2,1)} %collective-permute-done.4.refs_1_, bf16[256,1792]{1,0:T(8,128)(2,1)} %collective-permute-done.5.refs_2_, bf16[256,128]{1,0:T(8,128)(2,1)S(1)} %shrink_fresh.1.refs_3_.refs_0_), custom_call_target="tpu_custom_call" | custom-call | flops 1024 | bytes 1024 | tf_op jit(solution)/shard_map/chip_narrow/pallas_call | solution.py:74
  35.4 1.6 %collective-permute-start.13 = (bf16[128,3584]{1,0:T(8,128)(2,1)}, bf16[128,3584]{1,0:T(8,128)(2,1)}, u32[]{:S(2)}, u32[]{:S(2)}) collective-permute-start(bf16[128,3584]{1,0:T(8,128)(2,1)} %get-tuple-element.41.refs_2_), channel_id=1, source_target_pairs={{0,8},{1,9},{2,10},{3,11},{4,12},{5,13},{6,14},{7,15},{8,0},{9,1},... | collective-permute-start | bytes 2752520 | tf_op jit(solution)/shard_map/ppermute | solution.py:35
  37.0 0.5 collective-permute-start.3
  37.5 0.9 collective-permute-done.3.refs_1_
  38.4 0.0 copy-start.5
  38.4 0.0 collective-permute-done.refs_1_
  38.4 0.0 collective-permute-done.1.refs_2_
  38.4 0.0 collective-permute-done.2.refs_3_
  38.4 2.2 %chip_wide.1 = (bf16[64,4608]{1,0:T(8,128)(2,1)S(1)}, bf16[64,4608]{1,0:T(8,128)(2,1)S(1)}, bf16[64,4608]{1,0:T(8,128)(2,1)S(1)}, bf16[64,2304]{1,0:T(8,128)(2,1)S(1)}, bf16[64,2304]{1,0:T(8,128)(2,1)S(1)}) custom-call(bf16[256,4608]{1,0:T(8,128)(2,1)S(1)} %copy-done.1, bf16[256,1536]{1,0:T(8,128)(2,1)} %collective-permute-done.refs_1_, ...), custom_call_target="tpu_custom_call" | custom-call | flops 1024 | bytes 1024 | tf_op jit(solution)/shard_map/chip_wide/pallas_call | solution.py:74
  40.7 1.4 %collective-permute-start.6 = (bf16[64,2304]{1,0:T(8,128)(2,1)S(1)}, bf16[64,2304]{1,0:T(8,128)(2,1)S(1)}, u32[]{:S(2)}, u32[]{:S(2)}) collective-permute-start(bf16[64,2304]{1,0:T(8,128)(2,1)S(1)} %get-tuple-element.45), channel_id=1, source_target_pairs={{0,2},{1,3},{2,4},{3,5},{4,6},{5,7},{6,0},{7,1},{8,10},{9,11},{10,... | collective-permute-start | bytes 884744 | tf_op jit(solution)/shard_map/ppermute | solution.py:35
  42.1 1.5 %collective-permute-start.7 = (bf16[64,2304]{1,0:T(8,128)(2,1)S(1)}, bf16[64,2304]{1,0:T(8,128)(2,1)S(1)}, u32[]{:S(2)}, u32[]{:S(2)}) collective-permute-start(bf16[64,2304]{1,0:T(8,128)(2,1)S(1)} %get-tuple-element.46), channel_id=1, source_target_pairs={{0,6},{1,7},{2,0},{3,1},{4,2},{5,3},{6,4},{7,5},{8,14},{9,15},{10,... | collective-permute-start | bytes 884744 | tf_op jit(solution)/shard_map/ppermute | solution.py:35
  43.6 1.2 %collective-permute-start.10 = (bf16[256,128]{1,0:T(8,128)(2,1)S(1)}, bf16[256,128]{1,0:T(8,128)(2,1)S(1)}, u32[]{:S(2)}, u32[]{:S(2)}) collective-permute-start(bf16[256,128]{1,0:T(8,128)(2,1)S(1)} %add_parts.2.refs_4_.refs_0_), channel_id=1, source_target_pairs={{0,6},{1,7},{2,0},{3,1},{4,2},{5,3},{6,4},{7,5},{8,14},{9,15},{10,... | collective-permute-start | bytes 196616 | tf_op jit(solution)/shard_map/ppermute | solution.py:35
  44.8 0.6 collective-permute-start.9
  45.4 6.2 %collective-permute-done.10.refs_3_ = bf16[256,128]{1,0:T(8,128)(2,1)S(1)} collective-permute-done((bf16[256,128]{1,0:T(8,128)(2,1)S(1)}, bf16[256,128]{1,0:T(8,128)(2,1)S(1)}, u32[]{:S(2)}, u32[]{:S(2)}) %collective-permute-start.10) | collective-permute-done | bytes 65568 | tf_op jit(solution)/shard_map/ppermute | solution.py:35
  51.5 1.2 %collective-permute-start.8 = (bf16[256,128]{1,0:T(8,128)(2,1)S(1)}, bf16[256,128]{1,0:T(8,128)(2,1)S(1)}, u32[]{:S(2)}, u32[]{:S(2)}) collective-permute-start(bf16[256,128]{1,0:T(8,128)(2,1)S(1)} %add_parts.2.refs_4_.refs_0_), channel_id=1, source_target_pairs={{0,2},{1,3},{2,4},{3,5},{4,6},{5,7},{6,0},{7,1},{8,10},{9,11},{10,... | collective-permute-start | bytes 196616 | tf_op jit(solution)/shard_map/ppermute | solution.py:35
  52.7 0.0 collective-permute-done.9.refs_2_
  52.7 3.4 %collective-permute-done.8.refs_1_ = bf16[256,128]{1,0:T(8,128)(2,1)S(1)} collective-permute-done((bf16[256,128]{1,0:T(8,128)(2,1)S(1)}, bf16[256,128]{1,0:T(8,128)(2,1)S(1)}, u32[]{:S(2)}, u32[]{:S(2)}) %collective-permute-start.8) | collective-permute-done | bytes 65568 | tf_op jit(solution)/shard_map/ppermute | solution.py:35
  56.1 1.3 %up_table.1.refs_4_.refs_2_ = bf16[1024,512]{1,0:T(8,128)(2,1)S(1)} custom-call(bf16[1024,512]{1,0:T(8,128)(2,1)S(1)} %copy-done.5, s32[16]{0:T(128)S(1)} %copy-done.9, bf16[16,256,128]{2,1,0:T(8,128)(2,1)S(1)} %all-to-all-done.refs_4_.refs_2_, bf16[256,128]{1,0:T(8,128)(2,1)S(1)} %add_parts.3.refs_3_.refs_0_), custom_call_target="tpu_custom_call" | custom-call | flops 1024 | bytes 1024 | tf_op jit(solution)/shard_map/up_table/pallas_call | solution.py:74
  57.5 0.0 collective-permute-done.6.refs_2_
  57.5 0.0 collective-permute-done.7.refs_3_
  57.5 1.1 %near.2 = (bf16[64,4608]{1,0:T(8,128)(2,1)}, bf16[64,4608]{1,0:T(8,128)(2,1)}) custom-call(bf16[64,4608]{1,0:T(8,128)(2,1)S(1)} %get-tuple-element.43.refs_0_, bf16[64,4608]{1,0:T(8,128)(2,1)S(1)} %get-tuple-element.44.refs_1_, bf16[64,2304]{1,0:T(8,128)(2,1)S(1)} %collective-permute-done.6.refs_2_, bf16[64,2304]{1,0:T(8,128)(2,1)S(1)} %collective-permute-done.7.refs_3_, ...), custom_call_target="tpu_custom_call" | custom-call | flops 1024 | bytes 1024 | tf_op jit(solution)/shard_map/near/pallas_call | solution.py:74
  58.6 1.9 %collective-permute-start.12 = (bf16[64,4608]{1,0:T(8,128)(2,1)}, bf16[64,4608]{1,0:T(8,128)(2,1)}, u32[]{:S(2)}, u32[]{:S(2)}) collective-permute-start(bf16[64,4608]{1,0:T(8,128)(2,1)} %get-tuple-element.48), channel_id=1, source_target_pairs={{0,6},{1,7},{2,0},{3,1},{4,2},{5,3},{6,4},{7,5},{8,14},{9,15},{10,... | collective-permute-start | bytes 1769480 | tf_op jit(solution)/shard_map/ppermute | solution.py:35
  60.5 0.0 collective-permute-start.11
  60.5 0.3 collective-permute-start.14
  60.8 2.9 %collective-permute-done.14.refs_1_ = bf16[256,128]{1,0:T(8,128)(2,1)S(1)} collective-permute-done((bf16[256,128]{1,0:T(8,128)(2,1)S(1)}, bf16[256,128]{1,0:T(8,128)(2,1)S(1)}, u32[]{:S(2)}, u32[]{:S(2)}) %collective-permute-start.14) | collective-permute-done | bytes 65568 | tf_op jit(solution)/shard_map/ppermute | solution.py:35
  63.6 1.6 %raise_features.1.refs_2_ = bf16[16,32,512]{2,1,0:T(8,128)(2,1)} custom-call(bf16[256,128]{1,0:T(8,128)(2,1)S(1)} %add_parts.3.refs_3_.refs_0_, bf16[256,128]{1,0:T(8,128)(2,1)S(1)} %collective-permute-done.14.refs_1_, bf16[1024,512]{1,0:T(8,128)(2,1)S(1)} %up_table.1.refs_4_.refs_2_, s32[512,1]{1,0:T(8,128)S(1)} %copy.9.refs_2_.refs_3_, ...), custom_call_target="tpu_custom_call" | custom-call | flops 1024 | bytes 1024 | tf_op jit(solution)/shard_map/raise_features/pallas_call | solution.py:74
  65.2 9.3 %all-to-all-start.1 = ((bf16[16,32,512]{2,1,0:T(8,128)(2,1)}), bf16[16,32,512]{2,1,0:T(8,128)(2,1)S(1)}, u32[]{:S(2)}, u32[]{:S(2)}) async-start(bf16[16,32,512]{2,1,0:T(8,128)(2,1)} %raise_features.1.refs_2_), calls=%async_computation.1 | async-start | bytes 1048576 | tf_op jit(solution)/shard_map/all_to_all | solution.py:415
  74.5 0.0 collective-permute-done.13.refs_1_
  74.5 1.4 %turn_narrow.1 = (bf16[32,3584]{1,0:T(8,128)(2,1)S(1)}, bf16[32,3584]{1,0:T(8,128)(2,1)S(1)}, bf16[32,3584]{1,0:T(8,128)(2,1)S(1)}, bf16[32,1792]{1,0:T(8,128)(2,1)S(1)}, bf16[32,1792]{1,0:T(8,128)(2,1)S(1)}) custom-call(bf16[128,3584]{1,0:T(8,128)(2,1)S(1)} %get-tuple-element.49.refs_0_, bf16[128,3584]{1,0:T(8,128)(2,1)} %collective-permute-done.13.refs_1_, ...), custom_call_target="tpu_custom_call" | custom-call | flops 1024 | bytes 1024 | tf_op jit(solution)/shard_map/turn_narrow/pallas_call | solution.py:74
  75.9 0.0 copy-start.6
  75.9 1.5 %collective-permute-start.15 = (bf16[32,1792]{1,0:T(8,128)(2,1)S(1)}, bf16[32,1792]{1,0:T(8,128)(2,1)S(1)}, u32[]{:S(2)}, u32[]{:S(2)}) collective-permute-start(bf16[32,1792]{1,0:T(8,128)(2,1)S(1)} %get-tuple-element.52), channel_id=1, source_target_pairs={{0,2},{1,3},{2,4},{3,5},{4,6},{5,7},{6,0},{7,1},{8,10},{9,11},{10,... | collective-permute-start | bytes 344072 | tf_op jit(solution)/shard_map/ppermute | solution.py:35
  77.4 1.3 %collective-permute-start.16 = (bf16[32,1792]{1,0:T(8,128)(2,1)S(1)}, bf16[32,1792]{1,0:T(8,128)(2,1)S(1)}, u32[]{:S(2)}, u32[]{:S(2)}) collective-permute-start(bf16[32,1792]{1,0:T(8,128)(2,1)S(1)} %get-tuple-element.53), channel_id=1, source_target_pairs={{0,6},{1,7},{2,0},{3,1},{4,2},{5,3},{6,4},{7,5},{8,14},{9,15},{10,... | collective-permute-start | bytes 344072 | tf_op jit(solution)/shard_map/ppermute | solution.py:35
  78.7 7.6 %collective-permute-done.15.refs_2_ = bf16[32,1792]{1,0:T(8,128)(2,1)S(1)} collective-permute-done((bf16[32,1792]{1,0:T(8,128)(2,1)S(1)}, bf16[32,1792]{1,0:T(8,128)(2,1)S(1)}, u32[]{:S(2)}, u32[]{:S(2)}) %collective-permute-start.15) | collective-permute-done | bytes 114720 | tf_op jit(solution)/shard_map/ppermute | solution.py:35
  86.3 0.0 collective-permute-done.16.refs_3_
  86.3 0.7 near.3
  87.0 0.0 collective-permute-done.12.refs_2_
  87.0 0.0 collective-permute-done.11.refs_1_
  87.0 1.4 %turn_wide.1 = (f32[32,4608]{1,0:T(8,128)S(1)}, bf16[32,4608]{1,0:T(8,128)(2,1)S(1)}) custom-call(bf16[64,4608]{1,0:T(8,128)(2,1)S(1)} %get-tuple-element.42.refs_4_.refs_0_, bf16[64,4608]{1,0:T(8,128)(2,1)} %collective-permute-done.11.refs_1_, bf16[64,4608]{1,0:T(8,128)(2,1)} %collective-permute-done.12.refs_2_, bf16[32,3584]{1,0:T(8,128)(2,1)S(1)} %get-tuple-element.55.refs_3_), custom_call_target="tpu_custom_call" | custom-call | flops 1024 | bytes 1024 | tf_op jit(solution)/shard_map/turn_wide/pallas_call | solution.py:74
  88.5 1.3 %collective-permute-start.17 = (bf16[32,4608]{1,0:T(8,128)(2,1)S(1)}, bf16[32,4608]{1,0:T(8,128)(2,1)S(1)}, u32[]{:S(2)}, u32[]{:S(2)}) collective-permute-start(bf16[32,4608]{1,0:T(8,128)(2,1)S(1)} %get-tuple-element.57), channel_id=1, source_target_pairs={{0,8},{1,9},{2,10},{3,11},{4,12},{5,13},{6,14},{7,15},{8,0},{9,1},... | collective-permute-start | bytes 884744 | tf_op jit(solution)/shard_map/ppermute | solution.py:35
  89.8 0.4 collective-permute-start.19
  90.2 1.0 %collective-permute-start.18 = (bf16[32,3584]{1,0:T(8,128)(2,1)S(1)}, bf16[32,3584]{1,0:T(8,128)(2,1)S(1)}, u32[]{:S(2)}, u32[]{:S(2)}) collective-permute-start(bf16[32,3584]{1,0:T(8,128)(2,1)S(1)} %get-tuple-element.55.refs_3_), channel_id=1, source_target_pairs={{0,2},{1,3},{2,4},{3,5},{4,6},{5,7},{6,0},{7,1},{8,10},{9,11},{10,... | collective-permute-start | bytes 688136 | tf_op jit(solution)/shard_map/ppermute | solution.py:35
  91.2 4.8 %collective-permute-done.19.refs_5_ = bf16[32,3584]{1,0:T(8,128)(2,1)S(1)} collective-permute-done((bf16[32,3584]{1,0:T(8,128)(2,1)}, bf16[32,3584]{1,0:T(8,128)(2,1)S(1)}, u32[]{:S(2)}, u32[]{:S(2)}) %collective-permute-start.19) | collective-permute-done | bytes 229408 | tf_op jit(solution)/shard_map/ppermute | solution.py:35
  96.1 1.0 %collective-permute-done.18.refs_4_ = bf16[32,3584]{1,0:T(8,128)(2,1)S(1)} collective-permute-done((bf16[32,3584]{1,0:T(8,128)(2,1)S(1)}, bf16[32,3584]{1,0:T(8,128)(2,1)S(1)}, u32[]{:S(2)}, u32[]{:S(2)}) %collective-permute-start.18) | collective-permute-done | bytes 229408 | tf_op jit(solution)/shard_map/ppermute | solution.py:35
  97.1 0.0 collective-permute-done.17.refs_2_
  97.1 1.1 %finish.1 = bf16[32,8192]{1,0:T(8,128)(2,1)} custom-call(bf16[32,8192]{1,0:T(8,128)(2,1)S(1)} %copy-done.6, f32[32,4608]{1,0:T(8,128)S(1)} %get-tuple-element.56.refs_1_, bf16[32,4608]{1,0:T(8,128)(2,1)S(1)} %collective-permute-done.17.refs_2_, bf16[32,3584]{1,0:T(8,128)(2,1)S(1)} %get-tuple-element.54.refs_4_.refs_3_, ...), custom_call_target="tpu_custom_call" | custom-call | flops 1024 | bytes 1024 | tf_op jit(solution)/shard_map/finish/pallas_call | solution.py:74
  (18 shorter events, 0.1 us)
Async XLA Ops:
  0.0 27.9 %all-to-all-start = ((bf16[16,256,128]{2,1,0:T(8,128)(2,1)}), bf16[16,256,128]{2,1,0:T(8,128)(2,1)S(1)}, u32[]{:S(2)}, u32[]{:S(2)}) async-start(bf16[16,256,128]{2,1,0:T(8,128)(2,1)} %bitcast.2), calls=%async_computation | async-start | bytes 2097152 | tf_op jit(solution)/shard_map/all_to_all | solution.py:389
  14.1 16.8 %collective-permute-start.5 = (bf16[256,1792]{1,0:T(8,128)(2,1)}, bf16[256,1792]{1,0:T(8,128)(2,1)}, u32[]{:S(2)}, u32[]{:S(2)}) collective-permute-start(bf16[256,1792]{1,0:T(8,128)(2,1)} %get-tuple-element.40), channel_id=1, source_target_pairs={{0,1},{1,0},{2,3},{3,2},{4,5},{5,4},{6,7},{7,6},{8,9},{9,8},{10,11... | collective-permute-start | bytes 2752520 | tf_op jit(solution)/shard_map/ppermute | solution.py:35
  14.2 9.0 %copy-start.10 = (s32[512]{0:T(512)S(1)}, s32[512]{0:T(512)}, u32[]{:S(2)}) copy-start(s32[512]{0:T(512)} %param.15) | copy-start | bytes 6148
  14.2 9.2 %copy-start.2 = (bf16[512,512]{1,0:T(8,128)(2,1)S(1)}, bf16[512,512]{1,0:T(8,128)(2,1)}, u32[]{:S(2)}) copy-start(bf16[512,512]{1,0:T(8,128)(2,1)} %refs_0_.7) | copy-start | bytes 1572868
  14.2 9.2 %copy-start.4 = (bf16[512,1024]{1,0:T(8,128)(2,1)S(1)}, bf16[512,1024]{1,0:T(8,128)(2,1)}, u32[]{:S(2)}) copy-start(bf16[512,1024]{1,0:T(8,128)(2,1)} %refs_1_.6) | copy-start | bytes 3145732
  14.2 9.2 %copy-start.9 = (s32[16]{0:T(128)S(1)}, s32[16]{0:T(128)}, u32[]{:S(2)}) copy-start(s32[16]{0:T(128)} %refs_1_.7) | copy-start | bytes 196
  14.3 16.6 %collective-permute-start.4 = (bf16[256,1792]{1,0:T(8,128)(2,1)}, bf16[256,1792]{1,0:T(8,128)(2,1)}, u32[]{:S(2)}, u32[]{:S(2)}) collective-permute-start(bf16[256,1792]{1,0:T(8,128)(2,1)} %get-tuple-element.32.refs_2_), channel_id=1, source_target_pairs={{0,1},{1,0},{2,3},{3,2},{4,5},{5,4},{6,7},{7,6},{8,9},{9,8},{10,11... | collective-permute-start | bytes 2752520 | tf_op jit(solution)/shard_map/ppermute | solution.py:35
  22.5 15.9 %collective-permute-start = (bf16[256,1536]{1,0:T(8,128)(2,1)}, bf16[256,1536]{1,0:T(8,128)(2,1)}, u32[]{:S(2)}, u32[]{:S(2)}) collective-permute-start(bf16[256,1536]{1,0:T(8,128)(2,1)} %get-tuple-element.34), channel_id=1, source_target_pairs={{0,1},{1,0},{2,3},{3,2},{4,5},{5,4},{6,7},{7,6},{8,9},{9,8},{10,11... | collective-permute-start | bytes 2359304 | tf_op jit(solution)/shard_map/ppermute | solution.py:35
  22.8 15.6 %collective-permute-start.1 = (bf16[256,1536]{1,0:T(8,128)(2,1)}, bf16[256,1536]{1,0:T(8,128)(2,1)}, u32[]{:S(2)}, u32[]{:S(2)}) collective-permute-start(bf16[256,1536]{1,0:T(8,128)(2,1)} %get-tuple-element.35), channel_id=1, source_target_pairs={{0,1},{1,0},{2,3},{3,2},{4,5},{5,4},{6,7},{7,6},{8,9},{9,8},{10,11... | collective-permute-start | bytes 2359304 | tf_op jit(solution)/shard_map/ppermute | solution.py:35
  23.1 15.4 %collective-permute-start.2 = (bf16[256,1536]{1,0:T(8,128)(2,1)}, bf16[256,1536]{1,0:T(8,128)(2,1)}, u32[]{:S(2)}, u32[]{:S(2)}) collective-permute-start(bf16[256,1536]{1,0:T(8,128)(2,1)} %get-tuple-element.36), channel_id=1, source_target_pairs={{0,1},{1,0},{2,3},{3,2},{4,5},{5,4},{6,7},{7,6},{8,9},{9,8},{10,11... | collective-permute-start | bytes 2359304 | tf_op jit(solution)/shard_map/ppermute | solution.py:35
  23.5 1.7 %copy-start = (bf16[256,4608]{1,0:T(8,128)(2,1)S(1)}, bf16[256,4608]{1,0:T(8,128)(2,1)}, u32[]{:S(2)}) copy-start(bf16[256,4608]{1,0:T(8,128)(2,1)} %get-tuple-element.33.refs_4_.refs_0_) | copy-start | bytes 7077892
  27.2 0.7 copy-start.7
  27.9 1.0 copy-start.8
  30.8 1.5 %copy-start.3 = (bf16[256,3584]{1,0:T(8,128)(2,1)S(1)}, bf16[256,3584]{1,0:T(8,128)(2,1)}, u32[]{:S(2)}) copy-start(bf16[256,3584]{1,0:T(8,128)(2,1)} %get-tuple-element.39.refs_0_) | copy-start | bytes 5505028
  32.3 6.1 %copy-start.1 = (bf16[256,4608]{1,0:T(8,128)(2,1)S(1)}, bf16[256,4608]{1,0:T(8,128)(2,1)}, u32[]{:S(2)}) copy-start(bf16[256,4608]{1,0:T(8,128)(2,1)} %get-tuple-element.33.refs_4_.refs_0_) | copy-start | bytes 7077892
  35.4 39.1 %collective-permute-start.13 = (bf16[128,3584]{1,0:T(8,128)(2,1)}, bf16[128,3584]{1,0:T(8,128)(2,1)}, u32[]{:S(2)}, u32[]{:S(2)}) collective-permute-start(bf16[128,3584]{1,0:T(8,128)(2,1)} %get-tuple-element.41.refs_2_), channel_id=1, source_target_pairs={{0,8},{1,9},{2,10},{3,11},{4,12},{5,13},{6,14},{7,15},{8,0},{9,1},... | collective-permute-start | bytes 2752520 | tf_op jit(solution)/shard_map/ppermute | solution.py:35
  37.0 1.4 %collective-permute-start.3 = (bf16[256,128]{1,0:T(8,128)(2,1)S(1)}, bf16[256,128]{1,0:T(8,128)(2,1)S(1)}, u32[]{:S(2)}, u32[]{:S(2)}) collective-permute-start(bf16[256,128]{1,0:T(8,128)(2,1)S(1)} %shrink_fresh.1.refs_3_.refs_0_), channel_id=1, source_target_pairs={{0,1},{1,0},{2,3},{3,2},{4,5},{5,4},{6,7},{7,6},{8,9},{9,8},{10,11... | collective-permute-start | bytes 196616 | tf_op jit(solution)/shard_map/ppermute | solution.py:35
  38.4 17.7 %copy-start.5 = (bf16[1024,512]{1,0:T(8,128)(2,1)S(1)}, bf16[1024,512]{1,0:T(8,128)(2,1)}, u32[]{:S(2)}) copy-start(bf16[1024,512]{1,0:T(8,128)(2,1)} %refs_0_.8) | copy-start | bytes 3145732
  40.7 16.8 %collective-permute-start.6 = (bf16[64,2304]{1,0:T(8,128)(2,1)S(1)}, bf16[64,2304]{1,0:T(8,128)(2,1)S(1)}, u32[]{:S(2)}, u32[]{:S(2)}) collective-permute-start(bf16[64,2304]{1,0:T(8,128)(2,1)S(1)} %get-tuple-element.45), channel_id=1, source_target_pairs={{0,2},{1,3},{2,4},{3,5},{4,6},{5,7},{6,0},{7,1},{8,10},{9,11},{10,... | collective-permute-start | bytes 884744 | tf_op jit(solution)/shard_map/ppermute | solution.py:35
  42.1 15.4 %collective-permute-start.7 = (bf16[64,2304]{1,0:T(8,128)(2,1)S(1)}, bf16[64,2304]{1,0:T(8,128)(2,1)S(1)}, u32[]{:S(2)}, u32[]{:S(2)}) collective-permute-start(bf16[64,2304]{1,0:T(8,128)(2,1)S(1)} %get-tuple-element.46), channel_id=1, source_target_pairs={{0,6},{1,7},{2,0},{3,1},{4,2},{5,3},{6,4},{7,5},{8,14},{9,15},{10,... | collective-permute-start | bytes 884744 | tf_op jit(solution)/shard_map/ppermute | solution.py:35
  43.6 7.9 %collective-permute-start.10 = (bf16[256,128]{1,0:T(8,128)(2,1)S(1)}, bf16[256,128]{1,0:T(8,128)(2,1)S(1)}, u32[]{:S(2)}, u32[]{:S(2)}) collective-permute-start(bf16[256,128]{1,0:T(8,128)(2,1)S(1)} %add_parts.2.refs_4_.refs_0_), channel_id=1, source_target_pairs={{0,6},{1,7},{2,0},{3,1},{4,2},{5,3},{6,4},{7,5},{8,14},{9,15},{10,... | collective-permute-start | bytes 196616 | tf_op jit(solution)/shard_map/ppermute | solution.py:35
  44.8 7.9 %collective-permute-start.9 = (bf16[256,128]{1,0:T(8,128)(2,1)S(1)}, bf16[256,128]{1,0:T(8,128)(2,1)S(1)}, u32[]{:S(2)}, u32[]{:S(2)}) collective-permute-start(bf16[256,128]{1,0:T(8,128)(2,1)S(1)} %add_parts.2.refs_4_.refs_0_), channel_id=1, source_target_pairs={{0,4},{1,5},{2,6},{3,7},{4,0},{5,1},{6,2},{7,3},{8,12},{9,13},{10,... | collective-permute-start | bytes 196616 | tf_op jit(solution)/shard_map/ppermute | solution.py:35
  51.5 4.6 %collective-permute-start.8 = (bf16[256,128]{1,0:T(8,128)(2,1)S(1)}, bf16[256,128]{1,0:T(8,128)(2,1)S(1)}, u32[]{:S(2)}, u32[]{:S(2)}) collective-permute-start(bf16[256,128]{1,0:T(8,128)(2,1)S(1)} %add_parts.2.refs_4_.refs_0_), channel_id=1, source_target_pairs={{0,2},{1,3},{2,4},{3,5},{4,6},{5,7},{6,0},{7,1},{8,10},{9,11},{10,... | collective-permute-start | bytes 196616 | tf_op jit(solution)/shard_map/ppermute | solution.py:35
  58.6 28.4 %collective-permute-start.12 = (bf16[64,4608]{1,0:T(8,128)(2,1)}, bf16[64,4608]{1,0:T(8,128)(2,1)}, u32[]{:S(2)}, u32[]{:S(2)}) collective-permute-start(bf16[64,4608]{1,0:T(8,128)(2,1)} %get-tuple-element.48), channel_id=1, source_target_pairs={{0,6},{1,7},{2,0},{3,1},{4,2},{5,3},{6,4},{7,5},{8,14},{9,15},{10,... | collective-permute-start | bytes 1769480 | tf_op jit(solution)/shard_map/ppermute | solution.py:35
  60.5 26.5 %collective-permute-start.11 = (bf16[64,4608]{1,0:T(8,128)(2,1)}, bf16[64,4608]{1,0:T(8,128)(2,1)}, u32[]{:S(2)}, u32[]{:S(2)}) collective-permute-start(bf16[64,4608]{1,0:T(8,128)(2,1)} %get-tuple-element.47.refs_4_), channel_id=1, source_target_pairs={{0,2},{1,3},{2,4},{3,5},{4,6},{5,7},{6,0},{7,1},{8,10},{9,11},{10,... | collective-permute-start | bytes 1769480 | tf_op jit(solution)/shard_map/ppermute | solution.py:35
  60.5 3.1 %collective-permute-start.14 = (bf16[256,128]{1,0:T(8,128)(2,1)S(1)}, bf16[256,128]{1,0:T(8,128)(2,1)S(1)}, u32[]{:S(2)}, u32[]{:S(2)}) collective-permute-start(bf16[256,128]{1,0:T(8,128)(2,1)S(1)} %add_parts.3.refs_3_.refs_0_), channel_id=1, source_target_pairs={{0,8},{1,9},{2,10},{3,11},{4,12},{5,13},{6,14},{7,15},{8,0},{9,1},... | collective-permute-start | bytes 196616 | tf_op jit(solution)/shard_map/ppermute | solution.py:35
  65.2 26.0 %all-to-all-start.1 = ((bf16[16,32,512]{2,1,0:T(8,128)(2,1)}), bf16[16,32,512]{2,1,0:T(8,128)(2,1)S(1)}, u32[]{:S(2)}, u32[]{:S(2)}) async-start(bf16[16,32,512]{2,1,0:T(8,128)(2,1)} %raise_features.1.refs_2_), calls=%async_computation.1 | async-start | bytes 1048576 | tf_op jit(solution)/shard_map/all_to_all | solution.py:415
  75.9 21.2 %copy-start.6 = (bf16[32,8192]{1,0:T(8,128)(2,1)S(1)}, bf16[32,8192]{1,0:T(8,128)(2,1)}, u32[]{:S(2)}) copy-start(bf16[32,8192]{1,0:T(8,128)(2,1)} %refs_0_.9) | copy-start | bytes 1572868
  75.9 10.4 %collective-permute-start.15 = (bf16[32,1792]{1,0:T(8,128)(2,1)S(1)}, bf16[32,1792]{1,0:T(8,128)(2,1)S(1)}, u32[]{:S(2)}, u32[]{:S(2)}) collective-permute-start(bf16[32,1792]{1,0:T(8,128)(2,1)S(1)} %get-tuple-element.52), channel_id=1, source_target_pairs={{0,2},{1,3},{2,4},{3,5},{4,6},{5,7},{6,0},{7,1},{8,10},{9,11},{10,... | collective-permute-start | bytes 344072 | tf_op jit(solution)/shard_map/ppermute | solution.py:35
  77.4 8.9 %collective-permute-start.16 = (bf16[32,1792]{1,0:T(8,128)(2,1)S(1)}, bf16[32,1792]{1,0:T(8,128)(2,1)S(1)}, u32[]{:S(2)}, u32[]{:S(2)}) collective-permute-start(bf16[32,1792]{1,0:T(8,128)(2,1)S(1)} %get-tuple-element.53), channel_id=1, source_target_pairs={{0,6},{1,7},{2,0},{3,1},{4,2},{5,3},{6,4},{7,5},{8,14},{9,15},{10,... | collective-permute-start | bytes 344072 | tf_op jit(solution)/shard_map/ppermute | solution.py:35
  88.5 8.6 %collective-permute-start.17 = (bf16[32,4608]{1,0:T(8,128)(2,1)S(1)}, bf16[32,4608]{1,0:T(8,128)(2,1)S(1)}, u32[]{:S(2)}, u32[]{:S(2)}) collective-permute-start(bf16[32,4608]{1,0:T(8,128)(2,1)S(1)} %get-tuple-element.57), channel_id=1, source_target_pairs={{0,8},{1,9},{2,10},{3,11},{4,12},{5,13},{6,14},{7,15},{8,0},{9,1},... | collective-permute-start | bytes 884744 | tf_op jit(solution)/shard_map/ppermute | solution.py:35
  89.8 6.3 %collective-permute-start.19 = (bf16[32,3584]{1,0:T(8,128)(2,1)}, bf16[32,3584]{1,0:T(8,128)(2,1)S(1)}, u32[]{:S(2)}, u32[]{:S(2)}) collective-permute-start(bf16[32,3584]{1,0:T(8,128)(2,1)} %get-tuple-element.58), channel_id=1, source_target_pairs={{0,6},{1,7},{2,0},{3,1},{4,2},{5,3},{6,4},{7,5},{8,14},{9,15},{10,... | collective-permute-start | bytes 688136 | tf_op jit(solution)/shard_map/ppermute | solution.py:35
  90.2 6.9 %collective-permute-start.18 = (bf16[32,3584]{1,0:T(8,128)(2,1)S(1)}, bf16[32,3584]{1,0:T(8,128)(2,1)S(1)}, u32[]{:S(2)}, u32[]{:S(2)}) collective-permute-start(bf16[32,3584]{1,0:T(8,128)(2,1)S(1)} %get-tuple-element.55.refs_3_), channel_id=1, source_target_pairs={{0,2},{1,3},{2,4},{3,5},{4,6},{5,7},{6,0},{7,1},{8,10},{9,11},{10,... | collective-permute-start | bytes 688136 | tf_op jit(solution)/shard_map/ppermute | solution.py:35

commit v3 on v2

v3 whole, which is shorter than its diff:
```python
import jax
import jax.numpy as jnp
from jax import lax
from jax.experimental import pallas as pl
from jax.experimental.pallas import tpu as pltpu
from jax.sharding import PartitionSpec as P

RANK = 64
SLOTS = 16
CHIPS = 8
SCALE = 0.5
F32 = jnp.float32
BF16 = jnp.bfloat16
WIDE = 4608
VMEM_LIMIT = 16 * 1024 * 1024
PRODUCT_LIMIT = 56 * 1024 * 1024
CHIP_LIMIT = 56 * 1024 * 1024
NARROW_CHUNK = 1792
WIDE_CHUNK = 1536


def place(y, x, core):
    return ((y % 2) * 4 + x % 4) * 2 + core % 2


def route(yy, xx, cc):
    return [
        (place(y, x, c), place(y + yy, x + xx, c + cc))
        for y in range(2)
        for x in range(4)
        for c in range(2)
    ]


def send(array, yy, xx, cc):
    return lax.ppermute(array, "tp", route(yy, xx, cc))


def trade(array, partner_of):
    pairs = [
        (place(y, x, c), place(y, partner_of(x), c))
        for y in range(2)
        for x in range(4)
        for c in range(2)
    ]
    return lax.ppermute(array, "tp", pairs)


def spot():
    t = lax.axis_index("tp")
    return t // 8, lax.rem(t // 2, 4), lax.rem(t, 2)


def partner(yy, xx, cc):
    y, x, c = spot()
    return (lax.rem(y + yy, 2) * 4 + lax.rem(x + xx, 4)) * 2 + lax.rem(c + cc, 2)


def rows_at(index, size):
    return pl.ds(pl.multiple_of(index * size, size), size)


def whole(shape, dtype):
    return jax.ShapeDtypeStruct(shape, dtype)


def plus(a, *others):
    total = a.astype(F32)
    for other in others:
        total = total + other.astype(F32)
    return total


VM = pl.BlockSpec(memory_space=pltpu.VMEM)
SM = pl.BlockSpec(memory_space=pltpu.SMEM)
LATER = pl.BlockSpec(memory_space=pl.ANY)


def call(kernel, name, out_shape, args, specs=None, after=(), limit=VMEM_LIMIT, out_specs=None, scratch_shapes=()):
    count, outs = len(args), len(out_shape)

    def body(*refs):
        results = refs[count + len(after) :]
        results[outs][...] = jnp.zeros((8, 128), F32)
        kernel(*refs[:count], *results[:outs], *results[outs + 1 :])

    return pl.pallas_call(
        body,
        in_specs=list(specs or [VM] * count) + [LATER] * len(after),
        out_specs=list(out_specs or [VM] * outs) + [VM],
        out_shape=list(out_shape) + [whole((8, 128), F32)],
        scratch_shapes=list(scratch_shapes),
        compiler_params=pltpu.CompilerParams(vmem_limit_bytes=limit),
        cost_estimate=pl.CostEstimate(flops=1024, bytes_accessed=1024, transcendentals=0),
        name=name,
    )(*args, *after)


X_MAJOR = [(yy, xx) for xx in range(4) for yy in range(2)]
Y_MAJOR = [(yy, xx) for yy in range(2) for xx in range(4)]


HBM = pl.BlockSpec(memory_space=pltpu.HBM)


def product(x, w, order, first, width, chunk, after=()):
    chunks = width // chunk

    def kernel(x_ref, w_ref, *refs):
        away_refs = refs[:chunks]
        own_ref, rows_ref, held_ref, done_ref, sems, away_sems, own_sems = refs[chunks:]

        def copy(i):
            cols = pl.ds(pl.multiple_of(first + i * chunk, 128), chunk)
            return pltpu.make_async_copy(w_ref.at[:, cols], held_ref.at[i], sems.at[i])

        def leave(i):
            return pltpu.make_async_copy(done_ref.at[i, :256], away_refs[i], away_sems.at[i])

        def stay(i):
            cols = pl.ds(i * chunk, chunk)
            return pltpu.make_async_copy(
                done_ref.at[i, 256:], own_ref.at[:, cols], own_sems.at[i]
            )

        for i in range(chunks):
            copy(i).start()
        for i, (yy, xx) in enumerate(order):
            for cc, top in ((1, 0), (0, 256)):
                rows_ref[top + i * 32 : top + (i + 1) * 32, :] = x_ref[
                    rows_at(partner(yy, xx, cc), 32), :
                ]
        for i in range(chunks):
            copy(i).wait()
            done_ref[i] = jnp.dot(
                rows_ref[...], held_ref[i], preferred_element_type=F32
            ).astype(BF16)
            leave(i).start()
            stay(i).start()
        for i in range(chunks):
            leave(i).wait()
            stay(i).wait()

    return call(
        kernel,
        "product",
        [whole((256, chunk), BF16)] * chunks + [whole((256, width), BF16)],
        (x, w),
        [VM, HBM],
        after,
        limit=PRODUCT_LIMIT,
        out_specs=[HBM] * (chunks + 1),
        scratch_shapes=[
            pltpu.VMEM((512, 512), BF16),
            pltpu.VMEM((chunks, 512, chunk), BF16),
            pltpu.VMEM((chunks, 512, chunk), BF16),
            pltpu.SemaphoreType.DMA((chunks,)),
            pltpu.SemaphoreType.DMA((chunks,)),
            pltpu.SemaphoreType.DMA((chunks,)),
        ],
    )


def chip_sum(name, own, away, blocks, split, after=()):
    chunk = away[0].shape[1]
    chunks = len(away)
    width = own.shape[1]
    half = width // 2
    step = 256
    rows = [own.shape[0] // blocks] * blocks
    size = rows[0]
    shapes = []
    for d in range(blocks):
        shapes += [(size, half)] * 2 if d == split else [(size, width)]

    def kernel(own_ref, *refs):
        away_refs, outs = refs[:chunks], refs[chunks : chunks + len(shapes)]
        held_ref, came_ref, own_sems, away_sems = refs[chunks + len(shapes) :]

        def load_own(i):
            return pltpu.make_async_copy(
                own_ref.at[:, pl.ds(i * chunk, chunk)], held_ref.at[i], own_sems.at[i]
            )

        def load_away(i):
            return pltpu.make_async_copy(away_refs[i], came_ref.at[i], away_sems.at[i])

        for i in range(chunks):
            load_own(i).start()
            load_away(i).start()
        for i in range(chunks):
            load_own(i).wait()
            load_away(i).wait()
            for part in range(0, chunk, step):
                first = i * chunk + part
                total = plus(
                    held_ref[i, :, part : part + step], came_ref[i, :, part : part + step]
                ).astype(BF16)
                place_at = 0
                for d in range(blocks):
                    piece = total[d * size : (d + 1) * size]
                    if d == split:
                        side, at = divmod(first, half)
                        outs[place_at + side][:, at : at + step] = piece
                        place_at += 2
                    else:
                        outs[place_at][:, first : first + step] = piece
                        place_at += 1

    return call(
        kernel,
        name,
        [whole(shape, BF16) for shape in shapes],
        (own, *away),
        [HBM] * (1 + chunks),
        after,
        limit=CHIP_LIMIT,
        scratch_shapes=[
            pltpu.VMEM((chunks, own.shape[0], chunk), BF16),
            pltpu.VMEM((chunks, own.shape[0], chunk), BF16),
            pltpu.SemaphoreType.DMA((chunks,)),
            pltpu.SemaphoreType.DMA((chunks,)),
        ],
    )


def turn_narrow(keep, landed, after=()):
    width = keep.shape[1]

    def kernel(keep_ref, landed_ref, *refs):
        total = plus(keep_ref[...], landed_ref[...]).astype(BF16)
        for d, ref in enumerate(refs):
            ref[...] = total[d * 32 : (d + 1) * 32]

    return call(
        kernel, "turn_narrow", [whole((32, width), BF16)] * 4, (keep, landed), after=after
    )


def near(right, left, far_right, far_left, after=()):
    half = right.shape[1] // 2

    def kernel(right_ref, left_ref, far_right_ref, far_left_ref, to_right_ref, to_left_ref):
        to_right_ref[:, :half] = plus(right_ref[:, :half], far_right_ref[...]).astype(BF16)
        to_right_ref[:, half:] = right_ref[:, half:]
        to_left_ref[:, :half] = left_ref[:, :half]
        to_left_ref[:, half:] = plus(left_ref[:, half:], far_left_ref[...]).astype(BF16)

    return call(
        kernel, "near", [whole(right.shape, BF16)] * 2, (right, left, far_right, far_left), after=after
    )


def turn_wide(here, from_left, from_right, after=()):
    width = here.shape[1]

    def kernel(here_ref, from_left_ref, from_right_ref, keep_ref, send_ref):
        total = plus(here_ref[...], from_left_ref[...], from_right_ref[...])
        keep_ref[...] = total[:32]
        send_ref[...] = total[32:].astype(BF16)

    return call(
        kernel,
        "turn_wide",
        [whole((32, width), F32), whole((32, width), BF16)],
        (here, from_left, from_right),
        after=after,
    )


def add_parts(parts, after=(), dtype=BF16):
    def kernel(*refs):
        refs[-1][...] = plus(*[ref[...] for ref in refs[:-1]]).astype(dtype)

    return call(kernel, "add_parts", [whole(parts[0].shape, dtype)], parts, after=after)


def lanes(rows):
    return lax.broadcasted_iota(jnp.int32, (rows, 128), 1)


def resident_slot(slot, target_ref):
    for k in range(CHIPS):
        slot = jnp.where(slot == target_ref[k], -1, slot)
    return slot


def shrink_kernel(x_ref, down_ref, slot_ref, target_ref, maps_ref, out_ref):
    x = x_ref[...]
    row = lax.broadcasted_iota(jnp.int32, (512, 512), 0)
    col = lax.broadcasted_iota(jnp.int32, (512, 512), 1)
    source = jnp.where(col < 256, 2 * col, 2 * (col - 256) + 1)
    chooser = jnp.where(row == source, 1.0, 0.0).astype(BF16)
    split = jnp.dot(x, chooser, preferred_element_type=F32).astype(BF16)
    even, odd = split[:, :256], split[:, 256:]
    slot = jnp.broadcast_to(slot_ref[...], (512, 128))
    kept = resident_slot(slot, target_ref)
    high = (lanes(512) >= RANK).astype(jnp.int32)
    acc = jnp.zeros((512, 128), F32)
    for k in range(CHIPS):
        part = jnp.dot(x, down_ref[:, k * 128 : (k + 1) * 128], preferred_element_type=F32)
        acc += jnp.where(kept == 2 * k + high, part, 0.0)
        maps = maps_ref[2 * k]
        part = jnp.where(
            high == 0,
            jnp.dot(even, maps, preferred_element_type=F32),
            jnp.dot(odd, maps, preferred_element_type=F32),
        )
        acc += jnp.where(slot == target_ref[k], part, 0.0)
    acc = acc + pltpu.roll(acc, RANK, 1)
    out_ref[...] = jnp.where(lanes(256) < RANK, acc[:256], acc[256:]).astype(BF16)


def shrink_part(x, down, slot, target, maps, after=()):
    return call(
        shrink_kernel,
        "shrink_part",
        [whole((256, 128), BF16)],
        (x, down, slot, target, maps),
        [VM, VM, VM, SM, VM],
        after,
    )


def up_table_kernel(up_ref, target_ref, maps_ref, table_ref):
    table_ref[...] = up_ref[...]
    row = lax.broadcasted_iota(jnp.int32, (256, 512), 0)
    col = lax.broadcasted_iota(jnp.int32, (256, 512), 1)
    to_even = jnp.where(col == 2 * row, 1.0, 0.0).astype(BF16)
    to_odd = jnp.where(col == 2 * row + 1, 1.0, 0.0).astype(BF16)
    turn = (((0,), (0,)), ((), ()))
    for k in range(CHIPS):
        maps = maps_ref[2 * k + 1]
        even = lax.dot_general(maps, to_even, turn, preferred_element_type=F32)
        odd = lax.dot_general(maps, to_odd, turn, preferred_element_type=F32)
        table_ref[rows_at(target_ref[k], RANK), :] = (even[:RANK] + odd[RANK:]).astype(BF16)


def up_table(up, target, maps, after=()):
    return call(
        up_table_kernel, "up_table", [whole((1024, 512), BF16)], (up, target, maps), [VM, SM, VM], after
    )


def raise_kernel(mine_ref, other_ref, table_ref, slot_ref, out_ref):
    packed = (mine_ref[...].astype(F32) + other_ref[...].astype(F32)).astype(BF16).astype(F32)
    turned = pltpu.roll(packed, RANK, 1)
    left = lanes(256) < RANK
    both = jnp.concatenate(
        [jnp.where(left, packed, turned), jnp.where(left, turned, packed)], axis=0
    )
    slot = jnp.broadcast_to(slot_ref[...], (512, 128))
    high = (lanes(512) >= RANK).astype(jnp.int32)
    raised = jnp.concatenate(
        [jnp.where(slot == 2 * j + high, both, 0.0).astype(BF16) for j in range(CHIPS)], axis=1
    )
    total = jnp.dot(raised, table_ref[...], preferred_element_type=F32)
    out_ref[...] = (SCALE * total).astype(BF16).reshape(16, 32, 512)


def raise_features(mine, other, table, slot, after=()):
    return call(
        raise_kernel,
        "raise_features",
        [whole((16, 32, 512), BF16)],
        (mine, other, table, slot),
        after=after,
    )


def finish_kernel(
    residual_ref, wide_ref, wide_y_ref, narrow_ref, delta_ref, out_ref
):
    for t in range(16):
        cols = slice(t * 512, (t + 1) * 512)
        if (t + 1) * 512 <= WIDE:
            base = wide_ref[:, cols] + wide_y_ref[:, cols].astype(F32)
        else:
            part = slice(t * 512 - WIDE, (t + 1) * 512 - WIDE)
            base = narrow_ref[:, part]
        out_ref[:, cols] = (
            residual_ref[:, cols].astype(F32) + base + delta_ref[t].astype(F32)
        ).astype(BF16)


def local(
    attention_output,
    output_projection_weight,
    residual,
    resident_down_maps,
    resident_up_maps,
    fresh_adapter_bundle,
    fresh_slot_targets,
    request_adapter_slot,
):
    x, w = attention_output, output_projection_weight
    slot = request_adapter_slot.reshape(512, 1)
    target = fresh_slot_targets

    maps = lax.all_to_all(
        fresh_adapter_bundle.reshape(16, 256, 128), "tp", split_axis=0, concat_axis=0, tiled=True
    )
    narrow = x.shape[0] * 16 - WIDE
    *narrow_away, narrow_own, mark = product(x, w, Y_MAJOR, WIDE, narrow, NARROW_CHUNK)
    narrow_in = [send(away, 0, 0, 1) for away in narrow_away]
    *wide_away, wide_own, mark = product(x, w, X_MAJOR, 0, WIDE, WIDE_CHUNK, [mark])
    wide_in = [send(away, 0, 0, 1) for away in wide_away]

    part, mark = shrink_part(x, resident_down_maps, slot, target, maps, [mark])
    part_in = send(part, 0, 0, 1)

    keep, away, mark = chip_sum("chip_narrow", narrow_own, narrow_in, 2, None, [mark])
    narrow_y = send(away, 1, 0, 0)
    here, right, far_right, far_left, left, mark = chip_sum(
        "chip_wide", wide_own, wide_in, 4, 2, [mark]
    )
    far_right, far_left = send(far_right, 0, 1, 0), send(far_left, 0, 3, 0)
    part, mark = add_parts([part, part_in], [mark])
    part_in = trade(part, lambda x: x ^ 1)
    part, mark = add_parts([part, part_in], [mark])
    part_in = trade(part, lambda x: 3 - x)
    part, mark = add_parts([part, part_in], [mark])
    other = send(part, 1, 0, 0)

    right, left, mark = near(right, left, far_right, far_left, [mark])
    from_left, from_right = send(right, 0, 1, 0), send(left, 0, 3, 0)
    table, mark = up_table(resident_up_maps, target, maps, [mark])
    *low, mark = turn_narrow(keep, narrow_y, [mark])
    low_in = [send(low[d], 0, d, 0) for d in (1, 2, 3)]
    raised, mark = raise_features(part, other, table, slot, [mark])
    delta = lax.all_to_all(raised, "tp", split_axis=0, concat_axis=0, tiled=True)

    narrow_sum, mark = add_parts([low[0], *low_in], [mark], F32)
    wide_keep, wide_send, mark = turn_wide(here, from_left, from_right, [mark])
    wide_y = send(wide_send, 1, 0, 0)
    hidden, _ = call(
        finish_kernel,
        "finish",
        [whole((32, 8192), BF16)],
        (residual, wide_keep, wide_y, narrow_sum, delta),
    )
    return hidden


def solution(mesh):
    return jax.shard_map(
        local,
        mesh=mesh,
        in_specs=(
            P("grp", "tp"),
            P("tp", None),
            P("tp", "grp"),
            P("tp", "grp"),
            P("grp", "tp"),
            P(("grp", "tp"), None, None),
            P("grp"),
            P("grp"),
        ),
        out_specs=P("tp", "grp"),
        check_vma=False,
    )
```

time: 99.5 us -> 96.7 us (0.972)
  the two profiles are of different devices: /device:TPU:1 before, /device:TPU:230 now
where the time goes in v3:
time: 96.7 us; the launch traced here: 96.2 us
  Pallas kernels  33.2 us (34%)
  waiting for transfers between devices  29.3 us (30%)
  starting transfers between devices  28.2 us (29%)
  local copies, waits for them, and re-layouts  5.26 us (5%)
    pallas_call x15, Pallas kernels, call(): pl.pallas_call(body, in_specs=list(specs or [VM] * count) + [LATER] * len...  33.2 us
    ppermute x16, waiting for transfers between devices, send(): return lax.ppermute(array, 'tp', route(yy, xx, cc))  19.9 us
    ppermute x16, starting transfers between devices, send(): return lax.ppermute(array, 'tp', route(yy, xx, cc))  12.1 us
    ppermute x2, waiting for transfers between devices, trade(): return lax.ppermute(array, 'tp', pairs)  9.4 us
    all_to_all x1, starting transfers between devices, local(): lax.all_to_all(raised, 'tp', split_axis=0, concat_axis=0, tiled=True)  7.5 us
    all_to_all x1, starting transfers between devices, local(): lax.all_to_all(fresh_adapter_bundle.reshape(16, 256, 128), 'tp', split_ax...  5.8 us
    unnamed x30, local copies, waits for them, and re-layouts  5.11 us
    ppermute x2, starting transfers between devices, trade(): return lax.ppermute(array, 'tp', pairs)  2.78 us
  transfers between devices with their start and end apart: 20, of which 7 were waited for; matrix products, arithmetic and copies ran while one was open for 0% of the time, Pallas kernels for 33%

profile of v3, /device:TPU:230, one launch (start us, length us, event | category | flops | bytes accessed | tf_op | source)
XLA Modules:
  0.0 96.2 jit_solution(12019716691184866842)
XLA Ops:
  0.0 5.8 %all-to-all-start = ((bf16[16,256,128]{2,1,0:T(8,128)(2,1)}), bf16[16,256,128]{2,1,0:T(8,128)(2,1)S(1)}, u32[]{:S(2)}, u32[]{:S(2)}) async-start(bf16[16,256,128]{2,1,0:T(8,128)(2,1)} %bitcast.2), calls=%async_computation | async-start | bytes 2097152 | tf_op jit(solution)/shard_map/all_to_all | solution.py:400
  5.8 6.9 %product.2 = (bf16[256,1792]{1,0:T(8,128)(2,1)}, bf16[256,1792]{1,0:T(8,128)(2,1)}, bf16[256,3584]{1,0:T(8,128)(2,1)}, f32[8,128]{1,0:T(8,128)}) custom-call(bf16[512,512]{1,0:T(8,128)(2,1)} %refs_0_.7, bf16[512,8192]{1,0:T(8,128)(2,1)} %refs_1_.5), custom_call_target="tpu_custom_call" | custom-call | flops 1024 | bytes 1024 | tf_op jit(solution)/shard_map/product/pallas_call | solution.py:87
  12.7 0.2 collective-permute-start.3
  13.0 0.4 collective-permute-start.4
  13.3 7.4 %product.3 = (bf16[256,1536]{1,0:T(8,128)(2,1)}, bf16[256,1536]{1,0:T(8,128)(2,1)}, bf16[256,1536]{1,0:T(8,128)(2,1)}, bf16[256,4608]{1,0:T(8,128)(2,1)}, f32[8,128]{1,0:T(8,128)}) custom-call(bf16[512,512]{1,0:T(8,128)(2,1)} %refs_0_.7, bf16[512,8192]{1,0:T(8,128)(2,1)} %refs_1_.5, f32[8,128]{1,0:T(8,128)} %get-tuple-element.48.refs_2_), custom_call_target="tpu_custom_call" | custom-call | flops 1024 | bytes 1024 | tf_op jit(solution)/shard_map/product/pallas_call | solution.py:87
  20.7 0.2 collective-permute-start
  21.0 0.4 collective-permute-start.1
  21.3 0.1 collective-permute-start.2
  21.5 0.1 copy.9.refs_2_.refs_3_
  21.6 0.0 all-to-all-done.refs_4_.refs_2_
  21.6 0.0 copy-done
  21.7 0.0 copy-done.2
  21.7 0.0 copy-done.13
  21.7 0.7 copy-done.10
  22.4 3.4 %shrink_part.1 = (bf16[256,128]{1,0:T(8,128)(2,1)S(1)}, f32[8,128]{1,0:T(8,128)S(1)}) custom-call(bf16[512,512]{1,0:T(8,128)(2,1)S(1)} %copy-done, bf16[512,1024]{1,0:T(8,128)(2,1)S(1)} %copy-done.2, s32[512,1]{1,0:T(8,128)S(1)} %copy.9.refs_2_.refs_3_, s32[16]{0:T(128)S(1)} %copy-done.13, bf16[16,256,128]{2,1,0:T(8,128)(2,1)S(1)} %all-to-all-done.refs_4_.refs_2_, ...), custom_call_target="tpu_custom_call" | custom-call | flops 1024 | bytes 1024 | tf_op jit(solution)/shard_map/shrink_part/pallas_call | solution.py:87
  25.8 0.0 copy-start.12
  25.8 0.6 copy-done.12
  26.4 0.0 collective-permute-done.3.refs_1_
  26.4 0.0 collective-permute-done.4.refs_2_
  26.4 3.4 %chip_narrow.1 = (bf16[128,3584]{1,0:T(8,128)(2,1)}, bf16[128,3584]{1,0:T(8,128)(2,1)}, f32[8,128]{1,0:T(8,128)}) custom-call(bf16[256,3584]{1,0:T(8,128)(2,1)} %get-tuple-element.53.refs_0_, bf16[256,1792]{1,0:T(8,128)(2,1)} %collective-permute-done.3.refs_1_, bf16[256,1792]{1,0:T(8,128)(2,1)} %collective-permute-done.4.refs_2_, f32[8,128]{1,0:T(8,128)} %copy-done.12), custom_call_target="tpu_custom_call" | custom-call | flops 1024 | bytes 1024 | tf_op jit(solution)/shard_map/chip_narrow/pallas_call | solution.py:87
  29.8 1.6 %collective-permute-start.12 = (bf16[128,3584]{1,0:T(8,128)(2,1)}, bf16[128,3584]{1,0:T(8,128)(2,1)S(1)}, u32[]{:S(2)}, u32[]{:S(2)}) collective-permute-start(bf16[128,3584]{1,0:T(8,128)(2,1)} %get-tuple-element.74), channel_id=1, source_target_pairs={{0,8},{1,9},{2,10},{3,11},{4,12},{5,13},{6,14},{7,15},{8,0},{9,1},... | collective-permute-start | bytes 2752520 | tf_op jit(solution)/shard_map/ppermute | solution.py:36
  31.4 0.0 collective-permute-done.refs_1_
  31.4 0.0 collective-permute-done.1.refs_2_
  31.4 0.0 collective-permute-done.2.refs_3_
  31.4 0.0 copy-start.1
  31.4 4.0 %chip_wide.1 = (bf16[64,4608]{1,0:T(8,128)(2,1)}, bf16[64,4608]{1,0:T(8,128)(2,1)}, bf16[64,2304]{1,0:T(8,128)(2,1)}, bf16[64,2304]{1,0:T(8,128)(2,1)}, bf16[64,4608]{1,0:T(8,128)(2,1)}, /*index=5*/f32[8,128]{1,0:T(8,128)}) custom-call(bf16[256,4608]{1,0:T(8,128)(2,1)} %get-tuple-element.49.refs_0_, bf16[256,1536]{1,0:T(8,128)(2,1)} %collective-permute-done.refs_1_, ...), custom_call_target="tpu_custom_call" | custom-call | flops 1024 | bytes 1024 | tf_op jit(solution)/shard_map/chip_wide/pallas_call | solution.py:87
  35.4 0.8 collective-permute-start.5
  36.2 1.5 %collective-permute-start.6 = (bf16[64,2304]{1,0:T(8,128)(2,1)}, bf16[64,2304]{1,0:T(8,128)(2,1)S(1)}, u32[]{:S(2)}, u32[]{:S(2)}) collective-permute-start(bf16[64,2304]{1,0:T(8,128)(2,1)} %get-tuple-element.63), channel_id=1, source_target_pairs={{0,6},{1,7},{2,0},{3,1},{4,2},{5,3},{6,4},{7,5},{8,14},{9,15},{10,... | collective-permute-start | bytes 884744 | tf_op jit(solution)/shard_map/ppermute | solution.py:36
  37.6 0.0 collective-permute-start.7
  37.6 1.3 %collective-permute-done.7.refs_1_ = bf16[256,128]{1,0:T(8,128)(2,1)S(1)} collective-permute-done((bf16[256,128]{1,0:T(8,128)(2,1)S(1)}, bf16[256,128]{1,0:T(8,128)(2,1)S(1)}, u32[]{:S(2)}, u32[]{:S(2)}) %collective-permute-start.7) | collective-permute-done | bytes 65568 | tf_op jit(solution)/shard_map/ppermute | solution.py:36
  38.9 0.7 copy-done.11
  39.6 0.9 collective-permute-start.8
  40.5 5.7 %collective-permute-done.8.refs_1_ = bf16[256,128]{1,0:T(8,128)(2,1)S(1)} collective-permute-done((bf16[256,128]{1,0:T(8,128)(2,1)S(1)}, bf16[256,128]{1,0:T(8,128)(2,1)S(1)}, u32[]{:S(2)}, u32[]{:S(2)}) %collective-permute-start.8) | collective-permute-done | bytes 65568 | tf_op jit(solution)/shard_map/ppermute | solution.py:46
  46.2 1.8 %collective-permute-start.9 = (bf16[256,128]{1,0:T(8,128)(2,1)S(1)}, bf16[256,128]{1,0:T(8,128)(2,1)S(1)}, u32[]{:S(2)}, u32[]{:S(2)}) collective-permute-start(bf16[256,128]{1,0:T(8,128)(2,1)S(1)} %get-tuple-element.68.refs_0_), channel_id=1, source_target_pairs={{0,6},{1,7},{2,4},{3,5},{4,2},{5,3},{6,0},{7,1},{8,14},{9,15},{10,... | collective-permute-start | bytes 196616 | tf_op jit(solution)/shard_map/ppermute | solution.py:46
  48.1 3.7 %collective-permute-done.9.refs_1_ = bf16[256,128]{1,0:T(8,128)(2,1)S(1)} collective-permute-done((bf16[256,128]{1,0:T(8,128)(2,1)S(1)}, bf16[256,128]{1,0:T(8,128)(2,1)S(1)}, u32[]{:S(2)}, u32[]{:S(2)}) %collective-permute-start.9) | collective-permute-done | bytes 65568 | tf_op jit(solution)/shard_map/ppermute | solution.py:46
  51.8 0.0 collective-permute-done.5.refs_2_
  51.8 0.0 collective-permute-done.6.refs_3_
  51.9 1.1 %copy-done.5 = bf16[64,4608]{1,0:T(8,128)(2,1)S(1)} copy-done((bf16[64,4608]{1,0:T(8,128)(2,1)S(1)}, bf16[64,4608]{1,0:T(8,128)(2,1)}, u32[]{:S(2)}) %copy-start.5) | copy-done | bytes 589848
  52.9 1.1 %copy-done.6 = bf16[64,4608]{1,0:T(8,128)(2,1)S(1)} copy-done((bf16[64,4608]{1,0:T(8,128)(2,1)S(1)}, bf16[64,4608]{1,0:T(8,128)(2,1)}, u32[]{:S(2)}) %copy-start.6) | copy-done | bytes 589848
  54.0 1.1 %near.1 = (bf16[64,4608]{1,0:T(8,128)(2,1)}, bf16[64,4608]{1,0:T(8,128)(2,1)}, f32[8,128]{1,0:T(8,128)S(1)}) custom-call(bf16[64,4608]{1,0:T(8,128)(2,1)S(1)} %copy-done.5, bf16[64,4608]{1,0:T(8,128)(2,1)S(1)} %copy-done.6, bf16[64,2304]{1,0:T(8,128)(2,1)S(1)} %collective-permute-done.5.refs_2_, bf16[64,2304]{1,0:T(8,128)(2,1)S(1)} %collective-permute-done.6.refs_3_, ...), custom_call_target="tpu_custom_call" | custom-call | flops 1024 | bytes 1024 | tf_op jit(solution)/shard_map/near/pallas_call | solution.py:87
  55.1 1.7 %collective-permute-start.10 = (bf16[64,4608]{1,0:T(8,128)(2,1)}, bf16[64,4608]{1,0:T(8,128)(2,1)S(1)}, u32[]{:S(2)}, u32[]{:S(2)}) collective-permute-start(bf16[64,4608]{1,0:T(8,128)(2,1)} %get-tuple-element.71), channel_id=1, source_target_pairs={{0,2},{1,3},{2,4},{3,5},{4,6},{5,7},{6,0},{7,1},{8,10},{9,11},{10,... | collective-permute-start | bytes 1769480 | tf_op jit(solution)/shard_map/ppermute | solution.py:36
  56.8 0.3 collective-permute-start.11
  57.1 0.6 collective-permute-start.16
  57.7 1.3 %up_table.1 = (bf16[1024,512]{1,0:T(8,128)(2,1)S(1)}, f32[8,128]{1,0:T(8,128)S(1)}) custom-call(bf16[1024,512]{1,0:T(8,128)(2,1)S(1)} %copy-done.1, s32[16]{0:T(128)S(1)} %copy-done.13, bf16[16,256,128]{2,1,0:T(8,128)(2,1)S(1)} %all-to-all-done.refs_4_.refs_2_, f32[8,128]{1,0:T(8,128)S(1)} %get-tuple-element.75.refs_3_), custom_call_target="tpu_custom_call" | custom-call | flops 1024 | bytes 1024 | tf_op jit(solution)/shard_map/up_table/pallas_call | solution.py:87
  59.0 0.0 collective-permute-done.12.refs_1_
  59.1 1.0 turn_narrow.1
  60.0 3.0 %collective-permute-start.13 = (bf16[32,3584]{1,0:T(8,128)(2,1)}, bf16[32,3584]{1,0:T(8,128)(2,1)S(1)}, u32[]{:S(2)}, u32[]{:S(2)}) collective-permute-start(bf16[32,3584]{1,0:T(8,128)(2,1)} %get-tuple-element.78), channel_id=1, source_target_pairs={{0,2},{1,3},{2,4},{3,5},{4,6},{5,7},{6,0},{7,1},{8,10},{9,11},{10,... | collective-permute-start | bytes 688136 | tf_op jit(solution)/shard_map/ppermute | solution.py:36
  63.0 0.0 collective-permute-start.14
  63.0 0.0 collective-permute-done.16.refs_1_
  63.0 0.9 collective-permute-start.15
  63.8 1.6 %raise_features.1 = (bf16[16,32,512]{2,1,0:T(8,128)(2,1)}, f32[8,128]{1,0:T(8,128)S(1)}) custom-call(bf16[256,128]{1,0:T(8,128)(2,1)S(1)} %get-tuple-element.81.refs_0_, bf16[256,128]{1,0:T(8,128)(2,1)S(1)} %collective-permute-done.16.refs_1_, bf16[1024,512]{1,0:T(8,128)(2,1)S(1)} %get-tuple-element.82.refs_2_, s32[512,1]{1,0:T(8,128)S(1)} %copy.9.refs_2_.refs_3_, ...), custom_call_target="tpu_custom_call" | custom-call | flops 1024 | bytes 1024 | tf_op jit(solution)/shard_map/raise_features/pallas_call | solution.py:87
  65.4 7.5 %all-to-all-start.1 = ((bf16[16,32,512]{2,1,0:T(8,128)(2,1)}), bf16[16,32,512]{2,1,0:T(8,128)(2,1)S(1)}, u32[]{:S(2)}, u32[]{:S(2)}) async-start(bf16[16,32,512]{2,1,0:T(8,128)(2,1)} %get-tuple-element.89), calls=%async_computation.1 | async-start | bytes 1048576 | tf_op jit(solution)/shard_map/all_to_all | solution.py:431
  72.9 3.6 %collective-permute-done.13.refs_1_ = bf16[32,3584]{1,0:T(8,128)(2,1)S(1)} collective-permute-done((bf16[32,3584]{1,0:T(8,128)(2,1)}, bf16[32,3584]{1,0:T(8,128)(2,1)S(1)}, u32[]{:S(2)}, u32[]{:S(2)}) %collective-permute-start.13) | collective-permute-done | bytes 229408 | tf_op jit(solution)/shard_map/ppermute | solution.py:36
  76.5 1.3 %collective-permute-done.14.refs_2_ = bf16[32,3584]{1,0:T(8,128)(2,1)} collective-permute-done((bf16[32,3584]{1,0:T(8,128)(2,1)}, bf16[32,3584]{1,0:T(8,128)(2,1)}, u32[]{:S(2)}, u32[]{:S(2)}) %collective-permute-start.14) | collective-permute-done | bytes 229408 | tf_op jit(solution)/shard_map/ppermute | solution.py:36
  77.8 7.3 %collective-permute-done.15.refs_3_ = bf16[32,3584]{1,0:T(8,128)(2,1)} collective-permute-done((bf16[32,3584]{1,0:T(8,128)(2,1)}, bf16[32,3584]{1,0:T(8,128)(2,1)}, u32[]{:S(2)}, u32[]{:S(2)}) %collective-permute-start.15) | collective-permute-done | bytes 229408 | tf_op jit(solution)/shard_map/ppermute | solution.py:36
  85.1 1.2 %add_parts.7 = (f32[32,3584]{1,0:T(8,128)S(1)}, f32[8,128]{1,0:T(8,128)S(1)}) custom-call(bf16[32,3584]{1,0:T(8,128)(2,1)S(1)} %get-tuple-element.77.refs_0_, bf16[32,3584]{1,0:T(8,128)(2,1)S(1)} %collective-permute-done.13.refs_1_, bf16[32,3584]{1,0:T(8,128)(2,1)} %collective-permute-done.14.refs_2_, bf16[32,3584]{1,0:T(8,128)(2,1)} %collective-permute-done.15.refs_3_, ...), custom_call_target="tpu_custom_call" | custom-call | flops 1024 | bytes 1024 | tf_op jit(solution)/shard_map/add_parts/pallas_call | solution.py:87
  86.3 0.0 collective-permute-done.10.refs_1_
  86.3 0.0 collective-permute-done.11.refs_2_
  86.3 0.9 turn_wide.1
  87.2 0.6 collective-permute-start.17
  87.8 0.0 all-to-all-done.1.refs_4_
  87.8 6.4 %collective-permute-done.17.refs_2_ = bf16[32,4608]{1,0:T(8,128)(2,1)S(1)} collective-permute-done((bf16[32,4608]{1,0:T(8,128)(2,1)}, bf16[32,4608]{1,0:T(8,128)(2,1)S(1)}, u32[]{:S(2)}, u32[]{:S(2)}) %collective-permute-start.17) | collective-permute-done | bytes 294944 | tf_op jit(solution)/shard_map/ppermute | solution.py:36
  94.2 1.0 %copy-done.9 = f32[32,3584]{1,0:T(8,128)S(1)} copy-done((f32[32,3584]{1,0:T(8,128)S(1)}, f32[32,3584]{1,0:T(8,128)}, u32[]{:S(2)}) %copy-start.9) | copy-done | bytes 458776
  95.2 1.0 %finish.1 = (bf16[32,8192]{1,0:T(8,128)(2,1)}, f32[8,128]{1,0:T(8,128)}) custom-call(bf16[32,8192]{1,0:T(8,128)(2,1)S(1)} %copy-done.7, f32[32,4608]{1,0:T(8,128)S(1)} %get-tuple-element.86.refs_1_, bf16[32,4608]{1,0:T(8,128)(2,1)S(1)} %collective-permute-done.17.refs_2_, f32[32,3584]{1,0:T(8,128)S(1)} %copy-done.9, ...), custom_call_target="tpu_custom_call" | custom-call | flops 1024 | bytes 1024 | tf_op jit(solution)/shard_map/finish/pallas_call | solution.py:87
  (22 shorter events, 0.1 us)
Async XLA Ops:
  0.0 21.6 %all-to-all-start = ((bf16[16,256,128]{2,1,0:T(8,128)(2,1)}), bf16[16,256,128]{2,1,0:T(8,128)(2,1)S(1)}, u32[]{:S(2)}, u32[]{:S(2)}) async-start(bf16[16,256,128]{2,1,0:T(8,128)(2,1)} %bitcast.2), calls=%async_computation | async-start | bytes 2097152 | tf_op jit(solution)/shard_map/all_to_all | solution.py:400
  12.7 13.6 %collective-permute-start.3 = (bf16[256,1792]{1,0:T(8,128)(2,1)}, bf16[256,1792]{1,0:T(8,128)(2,1)}, u32[]{:S(2)}, u32[]{:S(2)}) collective-permute-start(bf16[256,1792]{1,0:T(8,128)(2,1)} %get-tuple-element.54), channel_id=1, source_target_pairs={{0,1},{1,0},{2,3},{3,2},{4,5},{5,4},{6,7},{7,6},{8,9},{9,8},{10,11... | collective-permute-start | bytes 2752520 | tf_op jit(solution)/shard_map/ppermute | solution.py:36
  13.0 13.4 %collective-permute-start.4 = (bf16[256,1792]{1,0:T(8,128)(2,1)}, bf16[256,1792]{1,0:T(8,128)(2,1)}, u32[]{:S(2)}, u32[]{:S(2)}) collective-permute-start(bf16[256,1792]{1,0:T(8,128)(2,1)} %get-tuple-element.55), channel_id=1, source_target_pairs={{0,1},{1,0},{2,3},{3,2},{4,5},{5,4},{6,7},{7,6},{8,9},{9,8},{10,11... | collective-permute-start | bytes 2752520 | tf_op jit(solution)/shard_map/ppermute | solution.py:36
  13.3 8.1 %copy-start.14 = (s32[512]{0:T(512)S(1)}, s32[512]{0:T(512)}, u32[]{:S(2)}) copy-start(s32[512]{0:T(512)} %param.15) | copy-start | bytes 6148
  13.3 8.3 %copy-start = (bf16[512,512]{1,0:T(8,128)(2,1)S(1)}, bf16[512,512]{1,0:T(8,128)(2,1)}, u32[]{:S(2)}) copy-start(bf16[512,512]{1,0:T(8,128)(2,1)} %refs_0_.7) | copy-start | bytes 1572868
  13.3 8.3 %copy-start.2 = (bf16[512,1024]{1,0:T(8,128)(2,1)S(1)}, bf16[512,1024]{1,0:T(8,128)(2,1)}, u32[]{:S(2)}) copy-start(bf16[512,1024]{1,0:T(8,128)(2,1)} %refs_1_.6) | copy-start | bytes 3145732
  13.3 8.3 %copy-start.13 = (s32[16]{0:T(128)S(1)}, s32[16]{0:T(128)}, u32[]{:S(2)}) copy-start(s32[16]{0:T(128)} %refs_1_.7) | copy-start | bytes 196
  20.7 10.6 %collective-permute-start = (bf16[256,1536]{1,0:T(8,128)(2,1)}, bf16[256,1536]{1,0:T(8,128)(2,1)}, u32[]{:S(2)}, u32[]{:S(2)}) collective-permute-start(bf16[256,1536]{1,0:T(8,128)(2,1)} %get-tuple-element.50), channel_id=1, source_target_pairs={{0,1},{1,0},{2,3},{3,2},{4,5},{5,4},{6,7},{7,6},{8,9},{9,8},{10,11... | collective-permute-start | bytes 2359304 | tf_op jit(solution)/shard_map/ppermute | solution.py:36
  21.0 10.4 %collective-permute-start.1 = (bf16[256,1536]{1,0:T(8,128)(2,1)}, bf16[256,1536]{1,0:T(8,128)(2,1)}, u32[]{:S(2)}, u32[]{:S(2)}) collective-permute-start(bf16[256,1536]{1,0:T(8,128)(2,1)} %get-tuple-element.51), channel_id=1, source_target_pairs={{0,1},{1,0},{2,3},{3,2},{4,5},{5,4},{6,7},{7,6},{8,9},{9,8},{10,11... | collective-permute-start | bytes 2359304 | tf_op jit(solution)/shard_map/ppermute | solution.py:36
  21.3 10.0 %collective-permute-start.2 = (bf16[256,1536]{1,0:T(8,128)(2,1)}, bf16[256,1536]{1,0:T(8,128)(2,1)}, u32[]{:S(2)}, u32[]{:S(2)}) collective-permute-start(bf16[256,1536]{1,0:T(8,128)(2,1)} %get-tuple-element.52), channel_id=1, source_target_pairs={{0,1},{1,0},{2,3},{3,2},{4,5},{5,4},{6,7},{7,6},{8,9},{9,8},{10,11... | collective-permute-start | bytes 2359304 | tf_op jit(solution)/shard_map/ppermute | solution.py:36
  21.7 0.7 copy-start.10
  25.8 0.6 copy-start.12
  29.8 29.2 %collective-permute-start.12 = (bf16[128,3584]{1,0:T(8,128)(2,1)}, bf16[128,3584]{1,0:T(8,128)(2,1)S(1)}, u32[]{:S(2)}, u32[]{:S(2)}) collective-permute-start(bf16[128,3584]{1,0:T(8,128)(2,1)} %get-tuple-element.74), channel_id=1, source_target_pairs={{0,8},{1,9},{2,10},{3,11},{4,12},{5,13},{6,14},{7,15},{8,0},{9,1},... | collective-permute-start | bytes 2752520 | tf_op jit(solution)/shard_map/ppermute | solution.py:36
  31.4 26.3 %copy-start.1 = (bf16[1024,512]{1,0:T(8,128)(2,1)S(1)}, bf16[1024,512]{1,0:T(8,128)(2,1)}, u32[]{:S(2)}) copy-start(bf16[1024,512]{1,0:T(8,128)(2,1)} %refs_0_.8) | copy-start | bytes 3145732
  35.4 23.7 %copy-start.3 = (bf16[128,3584]{1,0:T(8,128)(2,1)S(1)}, bf16[128,3584]{1,0:T(8,128)(2,1)}, u32[]{:S(2)}) copy-start(bf16[128,3584]{1,0:T(8,128)(2,1)} %get-tuple-element.73.refs_0_) | copy-start | bytes 2752516
  35.4 16.5 %collective-permute-start.5 = (bf16[64,2304]{1,0:T(8,128)(2,1)}, bf16[64,2304]{1,0:T(8,128)(2,1)S(1)}, u32[]{:S(2)}, u32[]{:S(2)}) collective-permute-start(bf16[64,2304]{1,0:T(8,128)(2,1)} %get-tuple-element.62), channel_id=1, source_target_pairs={{0,2},{1,3},{2,4},{3,5},{4,6},{5,7},{6,0},{7,1},{8,10},{9,11},{10,... | collective-permute-start | bytes 884744 | tf_op jit(solution)/shard_map/ppermute | solution.py:36
  36.2 15.7 %collective-permute-start.6 = (bf16[64,2304]{1,0:T(8,128)(2,1)}, bf16[64,2304]{1,0:T(8,128)(2,1)S(1)}, u32[]{:S(2)}, u32[]{:S(2)}) collective-permute-start(bf16[64,2304]{1,0:T(8,128)(2,1)} %get-tuple-element.63), channel_id=1, source_target_pairs={{0,6},{1,7},{2,0},{3,1},{4,2},{5,3},{6,4},{7,5},{8,14},{9,15},{10,... | collective-permute-start | bytes 884744 | tf_op jit(solution)/shard_map/ppermute | solution.py:36
  37.6 1.3 %collective-permute-start.7 = (bf16[256,128]{1,0:T(8,128)(2,1)S(1)}, bf16[256,128]{1,0:T(8,128)(2,1)S(1)}, u32[]{:S(2)}, u32[]{:S(2)}) collective-permute-start(bf16[256,128]{1,0:T(8,128)(2,1)S(1)} %get-tuple-element.64.refs_0_), channel_id=1, source_target_pairs={{0,1},{1,0},{2,3},{3,2},{4,5},{5,4},{6,7},{7,6},{8,9},{9,8},{10,11... | collective-permute-start | bytes 196616 | tf_op jit(solution)/shard_map/ppermute | solution.py:36
  38.9 0.7 copy-start.11
  39.6 6.6 %collective-permute-start.8 = (bf16[256,128]{1,0:T(8,128)(2,1)S(1)}, bf16[256,128]{1,0:T(8,128)(2,1)S(1)}, u32[]{:S(2)}, u32[]{:S(2)}) collective-permute-start(bf16[256,128]{1,0:T(8,128)(2,1)S(1)} %get-tuple-element.66.refs_0_), channel_id=1, source_target_pairs={{0,2},{1,3},{2,0},{3,1},{4,6},{5,7},{6,4},{7,5},{8,10},{9,11},{10,... | collective-permute-start | bytes 196616 | tf_op jit(solution)/shard_map/ppermute | solution.py:46
  46.2 5.6 %collective-permute-start.9 = (bf16[256,128]{1,0:T(8,128)(2,1)S(1)}, bf16[256,128]{1,0:T(8,128)(2,1)S(1)}, u32[]{:S(2)}, u32[]{:S(2)}) collective-permute-start(bf16[256,128]{1,0:T(8,128)(2,1)S(1)} %get-tuple-element.68.refs_0_), channel_id=1, source_target_pairs={{0,6},{1,7},{2,4},{3,5},{4,2},{5,3},{6,0},{7,1},{8,14},{9,15},{10,... | collective-permute-start | bytes 196616 | tf_op jit(solution)/shard_map/ppermute | solution.py:46
  51.8 1.1 %copy-start.5 = (bf16[64,4608]{1,0:T(8,128)(2,1)S(1)}, bf16[64,4608]{1,0:T(8,128)(2,1)}, u32[]{:S(2)}) copy-start(bf16[64,4608]{1,0:T(8,128)(2,1)} %get-tuple-element.60.refs_0_) | copy-start | bytes 1769476
  52.9 1.1 %copy-start.6 = (bf16[64,4608]{1,0:T(8,128)(2,1)S(1)}, bf16[64,4608]{1,0:T(8,128)(2,1)}, u32[]{:S(2)}) copy-start(bf16[64,4608]{1,0:T(8,128)(2,1)} %get-tuple-element.61.refs_1_) | copy-start | bytes 1769476
  55.1 31.2 %collective-permute-start.10 = (bf16[64,4608]{1,0:T(8,128)(2,1)}, bf16[64,4608]{1,0:T(8,128)(2,1)S(1)}, u32[]{:S(2)}, u32[]{:S(2)}) collective-permute-start(bf16[64,4608]{1,0:T(8,128)(2,1)} %get-tuple-element.71), channel_id=1, source_target_pairs={{0,2},{1,3},{2,4},{3,5},{4,6},{5,7},{6,0},{7,1},{8,10},{9,11},{10,... | collective-permute-start | bytes 1769480 | tf_op jit(solution)/shard_map/ppermute | solution.py:36
  56.8 29.5 %collective-permute-start.11 = (bf16[64,4608]{1,0:T(8,128)(2,1)}, bf16[64,4608]{1,0:T(8,128)(2,1)S(1)}, u32[]{:S(2)}, u32[]{:S(2)}) collective-permute-start(bf16[64,4608]{1,0:T(8,128)(2,1)} %get-tuple-element.72), channel_id=1, source_target_pairs={{0,6},{1,7},{2,0},{3,1},{4,2},{5,3},{6,4},{7,5},{8,14},{9,15},{10,... | collective-permute-start | bytes 1769480 | tf_op jit(solution)/shard_map/ppermute | solution.py:36
  57.1 5.9 %collective-permute-start.16 = (bf16[256,128]{1,0:T(8,128)(2,1)S(1)}, bf16[256,128]{1,0:T(8,128)(2,1)S(1)}, u32[]{:S(2)}, u32[]{:S(2)}) collective-permute-start(bf16[256,128]{1,0:T(8,128)(2,1)S(1)} %get-tuple-element.81.refs_0_), channel_id=1, source_target_pairs={{0,8},{1,9},{2,10},{3,11},{4,12},{5,13},{6,14},{7,15},{8,0},{9,1},... | collective-permute-start | bytes 196616 | tf_op jit(solution)/shard_map/ppermute | solution.py:36
  59.1 27.3 %copy-start.4 = (bf16[64,4608]{1,0:T(8,128)(2,1)S(1)}, bf16[64,4608]{1,0:T(8,128)(2,1)}, u32[]{:S(2)}) copy-start(bf16[64,4608]{1,0:T(8,128)(2,1)} %get-tuple-element.59.refs_0_) | copy-start | bytes 1769476
  60.0 16.5 %collective-permute-start.13 = (bf16[32,3584]{1,0:T(8,128)(2,1)}, bf16[32,3584]{1,0:T(8,128)(2,1)S(1)}, u32[]{:S(2)}, u32[]{:S(2)}) collective-permute-start(bf16[32,3584]{1,0:T(8,128)(2,1)} %get-tuple-element.78), channel_id=1, source_target_pairs={{0,2},{1,3},{2,4},{3,5},{4,6},{5,7},{6,0},{7,1},{8,10},{9,11},{10,... | collective-permute-start | bytes 688136 | tf_op jit(solution)/shard_map/ppermute | solution.py:36
  63.0 14.8 %collective-permute-start.14 = (bf16[32,3584]{1,0:T(8,128)(2,1)}, bf16[32,3584]{1,0:T(8,128)(2,1)}, u32[]{:S(2)}, u32[]{:S(2)}) collective-permute-start(bf16[32,3584]{1,0:T(8,128)(2,1)} %get-tuple-element.79), channel_id=1, source_target_pairs={{0,4},{1,5},{2,6},{3,7},{4,0},{5,1},{6,2},{7,3},{8,12},{9,13},{10,... | collective-permute-start | bytes 688136 | tf_op jit(solution)/shard_map/ppermute | solution.py:36
  63.0 22.1 %collective-permute-start.15 = (bf16[32,3584]{1,0:T(8,128)(2,1)}, bf16[32,3584]{1,0:T(8,128)(2,1)}, u32[]{:S(2)}, u32[]{:S(2)}) collective-permute-start(bf16[32,3584]{1,0:T(8,128)(2,1)} %get-tuple-element.80), channel_id=1, source_target_pairs={{0,6},{1,7},{2,0},{3,1},{4,2},{5,3},{6,4},{7,5},{8,14},{9,15},{10,... | collective-permute-start | bytes 688136 | tf_op jit(solution)/shard_map/ppermute | solution.py:36
  63.8 30.3 %copy-start.7 = (bf16[32,8192]{1,0:T(8,128)(2,1)S(1)}, bf16[32,8192]{1,0:T(8,128)(2,1)}, u32[]{:S(2)}) copy-start(bf16[32,8192]{1,0:T(8,128)(2,1)} %refs_0_.9) | copy-start | bytes 1572868
  65.4 22.4 %all-to-all-start.1 = ((bf16[16,32,512]{2,1,0:T(8,128)(2,1)}), bf16[16,32,512]{2,1,0:T(8,128)(2,1)S(1)}, u32[]{:S(2)}, u32[]{:S(2)}) async-start(bf16[16,32,512]{2,1,0:T(8,128)(2,1)} %get-tuple-element.89), calls=%async_computation.1 | async-start | bytes 1048576 | tf_op jit(solution)/shard_map/all_to_all | solution.py:431
  86.3 0.9 copy-start.8
  87.2 6.9 %collective-permute-start.17 = (bf16[32,4608]{1,0:T(8,128)(2,1)}, bf16[32,4608]{1,0:T(8,128)(2,1)S(1)}, u32[]{:S(2)}, u32[]{:S(2)}) collective-permute-start(bf16[32,4608]{1,0:T(8,128)(2,1)} %get-tuple-element.87), channel_id=1, source_target_pairs={{0,8},{1,9},{2,10},{3,11},{4,12},{5,13},{6,14},{7,15},{8,0},{9,1},... | collective-permute-start | bytes 884744 | tf_op jit(solution)/shard_map/ppermute | solution.py:36
  94.2 1.0 %copy-start.9 = (f32[32,3584]{1,0:T(8,128)S(1)}, f32[32,3584]{1,0:T(8,128)}, u32[]{:S(2)}) copy-start(f32[32,3584]{1,0:T(8,128)} %copy-done.8) | copy-start | bytes 1376260

commit v4 on v3

--- a/solution.py
+++ b/solution.py
@@ -14,7 +14,7 @@
 WIDE = 4608
 VMEM_LIMIT = 16 * 1024 * 1024
 PRODUCT_LIMIT = 56 * 1024 * 1024
-CHIP_LIMIT = 56 * 1024 * 1024
+CHIP_LIMIT = 48 * 1024 * 1024
 NARROW_CHUNK = 1792
 WIDE_CHUNK = 1536
 
@@ -105,39 +105,44 @@
 
 def product(x, w, order, first, width, chunk, after=()):
     chunks = width // chunk
+    sub = chunk // 2
+    subs = 2 * chunks
 
     def kernel(x_ref, w_ref, *refs):
         away_refs = refs[:chunks]
         own_ref, rows_ref, held_ref, done_ref, sems, away_sems, own_sems = refs[chunks:]
 
         def copy(i):
-            cols = pl.ds(pl.multiple_of(first + i * chunk, 128), chunk)
+            cols = pl.ds(pl.multiple_of(first + i * sub, 128), sub)
             return pltpu.make_async_copy(w_ref.at[:, cols], held_ref.at[i], sems.at[i])
 
         def leave(i):
-            return pltpu.make_async_copy(done_ref.at[i, :256], away_refs[i], away_sems.at[i])
+            return pltpu.make_async_copy(
+                done_ref.at[i, :256],
+                away_refs[i // 2].at[:, pl.ds(i % 2 * sub, sub)],
+                away_sems.at[i],
+            )
 
         def stay(i):
-            cols = pl.ds(i * chunk, chunk)
             return pltpu.make_async_copy(
-                done_ref.at[i, 256:], own_ref.at[:, cols], own_sems.at[i]
+                done_ref.at[i, 256:], own_ref.at[:, pl.ds(i * sub, sub)], own_sems.at[i]
             )
 
-        for i in range(chunks):
+        for i in range(subs):
             copy(i).start()
         for i, (yy, xx) in enumerate(order):
             for cc, top in ((1, 0), (0, 256)):
                 rows_ref[top + i * 32 : top + (i + 1) * 32, :] = x_ref[
                     rows_at(partner(yy, xx, cc), 32), :
                 ]
-        for i in range(chunks):
+        for i in range(subs):
             copy(i).wait()
             done_ref[i] = jnp.dot(
                 rows_ref[...], held_ref[i], preferred_element_type=F32
             ).astype(BF16)
             leave(i).start()
             stay(i).start()
-        for i in range(chunks):
+        for i in range(subs):
             leave(i).wait()
             stay(i).wait()
 
@@ -152,47 +157,49 @@
         out_specs=[HBM] * (chunks + 1),
         scratch_shapes=[
             pltpu.VMEM((512, 512), BF16),
-            pltpu.VMEM((chunks, 512, chunk), BF16),
-            pltpu.VMEM((chunks, 512, chunk), BF16),
-            pltpu.SemaphoreType.DMA((chunks,)),
-            pltpu.SemaphoreType.DMA((chunks,)),
-            pltpu.SemaphoreType.DMA((chunks,)),
+            pltpu.VMEM((subs, 512, sub), BF16),
+            pltpu.VMEM((subs, 512, sub), BF16),
+            pltpu.SemaphoreType.DMA((subs,)),
+            pltpu.SemaphoreType.DMA((subs,)),
+            pltpu.SemaphoreType.DMA((subs,)),
         ],
     )
 
 
 def chip_sum(name, own, away, blocks, split, after=()):
     chunk = away[0].shape[1]
-    chunks = len(away)
+    sub = chunk // 2
+    subs = 2 * len(away)
     width = own.shape[1]
     half = width // 2
-    step = 256
-    rows = [own.shape[0] // blocks] * blocks
-    size = rows[0]
+    step = 128
+    size = own.shape[0] // blocks
     shapes = []
     for d in range(blocks):
         shapes += [(size, half)] * 2 if d == split else [(size, width)]
 
     def kernel(own_ref, *refs):
-        away_refs, outs = refs[:chunks], refs[chunks : chunks + len(shapes)]
-        held_ref, came_ref, own_sems, away_sems = refs[chunks + len(shapes) :]
+        away_refs, outs = refs[: len(away)], refs[len(away) : len(away) + len(shapes)]
+        held_ref, came_ref, own_sems, away_sems = refs[len(away) + len(shapes) :]
 
         def load_own(i):
             return pltpu.make_async_copy(
-                own_ref.at[:, pl.ds(i * chunk, chunk)], held_ref.at[i], own_sems.at[i]
+                own_ref.at[:, pl.ds(i * sub, sub)], held_ref.at[i], own_sems.at[i]
             )
 
         def load_away(i):
-            return pltpu.make_async_copy(away_refs[i], came_ref.at[i], away_sems.at[i])
-
-        for i in range(chunks):
+            return pltpu.make_async_copy(
+                away_refs[i // 2].at[:, pl.ds(i % 2 * sub, sub)], came_ref.at[i], away_sems.at[i]
+            )
+
+        for i in range(subs):
             load_own(i).start()
             load_away(i).start()
-        for i in range(chunks):
+        for i in range(subs):
             load_own(i).wait()
             load_away(i).wait()
-            for part in range(0, chunk, step):
-                first = i * chunk + part
+            for part in range(0, sub, step):
+                first = i * sub + part
                 total = plus(
                     held_ref[i, :, part : part + step], came_ref[i, :, part : part + step]
                 ).astype(BF16)
@@ -212,14 +219,14 @@
         name,
         [whole(shape, BF16) for shape in shapes],
         (own, *away),
-        [HBM] * (1 + chunks),
+        [HBM] * (1 + len(away)),
         after,
         limit=CHIP_LIMIT,
         scratch_shapes=[
-            pltpu.VMEM((chunks, own.shape[0], chunk), BF16),
-            pltpu.VMEM((chunks, own.shape[0], chunk), BF16),
-            pltpu.SemaphoreType.DMA((chunks,)),
-            pltpu.SemaphoreType.DMA((chunks,)),
+            pltpu.VMEM((subs, own.shape[0], sub), BF16),
+            pltpu.VMEM((subs, own.shape[0], sub), BF16),
+            pltpu.SemaphoreType.DMA((subs,)),
+            pltpu.SemaphoreType.DMA((subs,)),
         ],
     )
 
@@ -401,29 +408,31 @@
         fresh_adapter_bundle.reshape(16, 256, 128), "tp", split_axis=0, concat_axis=0, tiled=True
     )
     narrow = x.shape[0] * 16 - WIDE
-    *narrow_away, narrow_own, mark = product(x, w, Y_MAJOR, WIDE, narrow, NARROW_CHUNK)
+    *narrow_away, narrow_own, mark = product(x, w, Y_MAJOR, WIDE, narrow, NARROW_CHUNK, [slot])
     narrow_in = [send(away, 0, 0, 1) for away in narrow_away]
     *wide_away, wide_own, mark = product(x, w, X_MAJOR, 0, WIDE, WIDE_CHUNK, [mark])
     wide_in = [send(away, 0, 0, 1) for away in wide_away]
 
+    keep, away, mark = chip_sum(
+        "chip_narrow", narrow_own, narrow_in, 2, None, [mark, maps]
+    )
+    narrow_y = send(away, 1, 0, 0)
+    here, right, far_right, far_left, left, mark = chip_sum(
+        "chip_wide", wide_own, wide_in, 4, 2, [away]
+    )
+    far_right, far_left = send(far_right, 0, 1, 0), send(far_left, 0, 3, 0)
+
     part, mark = shrink_part(x, resident_down_maps, slot, target, maps, [mark])
     part_in = send(part, 0, 0, 1)
-
-    keep, away, mark = chip_sum("chip_narrow", narrow_own, narrow_in, 2, None, [mark])
-    narrow_y = send(away, 1, 0, 0)
-    here, right, far_right, far_left, left, mark = chip_sum(
-        "chip_wide", wide_own, wide_in, 4, 2, [mark]
-    )
-    far_right, far_left = send(far_right, 0, 1, 0), send(far_left, 0, 3, 0)
     part, mark = add_parts([part, part_in], [mark])
     part_in = trade(part, lambda x: x ^ 1)
     part, mark = add_parts([part, part_in], [mark])
     part_in = trade(part, lambda x: 3 - x)
+
+    right, left, mark = near(right, left, far_right, far_left, [mark])
+    from_left, from_right = send(right, 0, 1, 0), send(left, 0, 3, 0)
     part, mark = add_parts([part, part_in], [mark])
     other = send(part, 1, 0, 0)
-
-    right, left, mark = near(right, left, far_right, far_left, [mark])
-    from_left, from_right = send(right, 0, 1, 0), send(left, 0, 3, 0)
     table, mark = up_table(resident_up_maps, target, maps, [mark])
     *low, mark = turn_narrow(keep, narrow_y, [mark])
     low_in = [send(low[d], 0, d, 0) for d in (1, 2, 3)]

time: 96.7 us -> 93.4 us (0.966)
  the two profiles are of different devices: /device:TPU:230 before, /device:TPU:1 now
where the time goes in v4:
time: 93.4 us; the launch traced here: 92.9 us
  Pallas kernels  31 us (33%)
  waiting for transfers between devices  29.5 us (32%)
  starting transfers between devices  29 us (31%)
  local copies, waits for them, and re-layouts  3.26 us (3%)
    pallas_call x15, Pallas kernels, call(): pl.pallas_call(body, in_specs=list(specs or [VM] * count) + [LATER] * len...  31 us
    ppermute x2, waiting for transfers between devices, trade(): return lax.ppermute(array, 'tp', pairs)  17.1 us
    ppermute x16, starting transfers between devices, send(): return lax.ppermute(array, 'tp', route(yy, xx, cc))  15.3 us
    all_to_all x1, starting transfers between devices, local(): lax.all_to_all(fresh_adapter_bundle.reshape(16, 256, 128), 'tp', split_ax...  6.83 us
    all_to_all x1, starting transfers between devices, local(): lax.all_to_all(raised, 'tp', split_axis=0, concat_axis=0, tiled=True)  6.75 us
    all_to_all x1, waiting for transfers between devices, local(): lax.all_to_all(raised, 'tp', split_axis=0, concat_axis=0, tiled=True)  6.51 us
    ppermute x16, waiting for transfers between devices, send(): return lax.ppermute(array, 'tp', route(yy, xx, cc))  5.83 us
  transfers between devices with their start and end apart: 20, of which 6 were waited for; matrix products, arithmetic and copies ran while one was open for 2% of the time, Pallas kernels for 32%

profile of v4, /device:TPU:1, one launch (start us, length us, event | category | flops | bytes accessed | tf_op | source)
XLA Modules:
  0.0 92.9 jit_solution(11425787618289651373)
XLA Ops:
  0.0 6.8 %all-to-all-start = ((bf16[16,256,128]{2,1,0:T(8,128)(2,1)}), bf16[16,256,128]{2,1,0:T(8,128)(2,1)S(1)}, u32[]{:S(2)}, u32[]{:S(2)}) async-start(bf16[16,256,128]{2,1,0:T(8,128)(2,1)} %bitcast.2), calls=%async_computation | async-start | bytes 2097152 | tf_op jit(solution)/shard_map/all_to_all | solution.py:407
  6.8 1.5 %copy.9.refs_2_.refs_3_ = s32[512,1]{1,0:T(8,128)} copy(s32[512,1]{0,1:T(1,128)} %bitcast.3) | data formatting | bytes 4096 | tf_op jit(solution)/shard_map/reshape | solution.py:404
  8.4 6.7 %product.2 = (bf16[256,1792]{1,0:T(8,128)(2,1)}, bf16[256,1792]{1,0:T(8,128)(2,1)}, bf16[256,3584]{1,0:T(8,128)(2,1)}, f32[8,128]{1,0:T(8,128)}) custom-call(bf16[512,512]{1,0:T(8,128)(2,1)} %refs_0_.7, bf16[512,8192]{1,0:T(8,128)(2,1)} %refs_1_.5, s32[512,1]{1,0:T(8,128)} %copy.9.refs_2_.refs_3_), custom_call_target="tpu_custom_call" | custom-call | flops 1024 | bytes 1024 | tf_op jit(solution)/shard_map/product/pallas_call | solution.py:87
  15.1 0.2 collective-permute-start.3
  15.3 0.4 collective-permute-start.4
  15.7 8.1 %product.3 = (bf16[256,1536]{1,0:T(8,128)(2,1)}, bf16[256,1536]{1,0:T(8,128)(2,1)}, bf16[256,1536]{1,0:T(8,128)(2,1)}, bf16[256,4608]{1,0:T(8,128)(2,1)}, f32[8,128]{1,0:T(8,128)}) custom-call(bf16[512,512]{1,0:T(8,128)(2,1)} %refs_0_.7, bf16[512,8192]{1,0:T(8,128)(2,1)} %refs_1_.5, f32[8,128]{1,0:T(8,128)} %get-tuple-element.47.refs_2_), custom_call_target="tpu_custom_call" | custom-call | flops 1024 | bytes 1024 | tf_op jit(solution)/shard_map/product/pallas_call | solution.py:87
  23.8 0.2 collective-permute-start
  24.0 0.4 collective-permute-start.1
  24.4 0.1 collective-permute-start.2
  24.5 0.0 collective-permute-done.3.refs_1_
  24.5 0.0 collective-permute-done.4.refs_2_
  24.5 0.0 all-to-all-done.refs_4_.refs_2_
  24.5 0.0 copy-start.7
  24.5 0.7 copy-done.7
  25.2 2.1 %chip_narrow.1 = (bf16[128,3584]{1,0:T(8,128)(2,1)S(1)}, bf16[128,3584]{1,0:T(8,128)(2,1)S(1)}, f32[8,128]{1,0:T(8,128)}) custom-call(bf16[256,3584]{1,0:T(8,128)(2,1)} %get-tuple-element.52.refs_0_, bf16[256,1792]{1,0:T(8,128)(2,1)S(1)} %collective-permute-done.3.refs_1_, bf16[256,1792]{1,0:T(8,128)(2,1)S(1)} %collective-permute-done.4.refs_2_, ...), custom_call_target="tpu_custom_call" | custom-call | flops 1024 | bytes 1024 | tf_op jit(solution)/shard_map/chip_narrow/pallas_call | solution.py:87
  27.3 1.7 %collective-permute-start.11 = (bf16[128,3584]{1,0:T(8,128)(2,1)S(1)}, bf16[128,3584]{1,0:T(8,128)(2,1)S(1)}, u32[]{:S(2)}, u32[]{:S(2)}) collective-permute-start(bf16[128,3584]{1,0:T(8,128)(2,1)S(1)} %get-tuple-element.56.refs_4_), channel_id=1, source_target_pairs={{0,8},{1,9},{2,10},{3,11},{4,12},{5,13},{6,14},{7,15},{8,0},{9,1},... | collective-permute-start | bytes 2752520 | tf_op jit(solution)/shard_map/ppermute | solution.py:36
  29.1 0.0 collective-permute-done.refs_1_
  29.1 0.0 collective-permute-done.1.refs_2_
  29.1 0.0 collective-permute-done.2.refs_3_
  29.1 0.0 copy-start
  29.1 0.0 copy-start.1
  29.1 0.0 copy-start.3
  29.1 0.0 copy-start.8
  29.1 2.6 %chip_wide.1 = (bf16[64,4608]{1,0:T(8,128)(2,1)S(1)}, bf16[64,4608]{1,0:T(8,128)(2,1)S(1)}, bf16[64,2304]{1,0:T(8,128)(2,1)S(1)}, bf16[64,2304]{1,0:T(8,128)(2,1...) custom-call(bf16[256,4608]{1,0:T(8,128)(2,1)} %get-tuple-element.48.refs_0_, ...), custom_call_target="tpu_custom_call" | custom-call | flops 1024 | bytes 1024 | tf_op jit(solution)/shard_map/chip_wide/pallas_call | solution.py:87
  31.8 1.3 %collective-permute-start.5 = (bf16[64,2304]{1,0:T(8,128)(2,1)S(1)}, bf16[64,2304]{1,0:T(8,128)(2,1)S(1)}, u32[]{:S(2)}, u32[]{:S(2)}) collective-permute-start(bf16[64,2304]{1,0:T(8,128)(2,1)S(1)} %get-tuple-element.60), channel_id=1, source_target_pairs={{0,2},{1,3},{2,4},{3,5},{4,6},{5,7},{6,0},{7,1},{8,10},{9,11},{10,... | collective-permute-start | bytes 884744 | tf_op jit(solution)/shard_map/ppermute | solution.py:36
  33.0 1.5 %collective-permute-start.6 = (bf16[64,2304]{1,0:T(8,128)(2,1)S(1)}, bf16[64,2304]{1,0:T(8,128)(2,1)S(1)}, u32[]{:S(2)}, u32[]{:S(2)}) collective-permute-start(bf16[64,2304]{1,0:T(8,128)(2,1)S(1)} %get-tuple-element.61), channel_id=1, source_target_pairs={{0,6},{1,7},{2,0},{3,1},{4,2},{5,3},{6,4},{7,5},{8,14},{9,15},{10,... | collective-permute-start | bytes 884744 | tf_op jit(solution)/shard_map/ppermute | solution.py:36
  34.5 0.0 copy-done.1
  34.5 0.0 copy-start.2
  34.6 3.4 %shrink_part.1 = (bf16[256,128]{1,0:T(8,128)(2,1)S(1)}, f32[8,128]{1,0:T(8,128)S(1)}) custom-call(bf16[512,512]{1,0:T(8,128)(2,1)S(1)} %copy-done, bf16[512,1024]{1,0:T(8,128)(2,1)S(1)} %copy-done.3, s32[512,1]{1,0:T(8,128)S(1)} %copy-done.1, s32[16]{0:T(128)S(1)} %copy-done.8, bf16[16,256,128]{2,1,0:T(8,128)(2,1)S(1)} %all-to-all-done.refs_4_.refs_2_, ...), custom_call_target="tpu_custom_call" | custom-call | flops 1024 | bytes 1024 | tf_op jit(solution)/shard_map/shrink_part/pallas_call | solution.py:87
  38.0 1.1 %collective-permute-start.7 = (bf16[256,128]{1,0:T(8,128)(2,1)S(1)}, bf16[256,128]{1,0:T(8,128)(2,1)S(1)}, u32[]{:S(2)}, u32[]{:S(2)}) collective-permute-start(bf16[256,128]{1,0:T(8,128)(2,1)S(1)} %get-tuple-element.63.refs_0_), channel_id=1, source_target_pairs={{0,1},{1,0},{2,3},{3,2},{4,5},{5,4},{6,7},{7,6},{8,9},{9,8},{10,11... | collective-permute-start | bytes 196616 | tf_op jit(solution)/shard_map/ppermute | solution.py:36
  39.0 0.9 collective-permute-done.7.refs_1_
  40.0 0.1 collective-permute-start.8
  40.1 3.4 %collective-permute-done.8.refs_1_ = bf16[256,128]{1,0:T(8,128)(2,1)S(1)} collective-permute-done((bf16[256,128]{1,0:T(8,128)(2,1)S(1)}, bf16[256,128]{1,0:T(8,128)(2,1)S(1)}, u32[]{:S(2)}, u32[]{:S(2)}) %collective-permute-start.8) | collective-permute-done | bytes 65568 | tf_op jit(solution)/shard_map/ppermute | solution.py:46
  43.5 0.0 collective-permute-done.5.refs_2_
  43.5 0.0 collective-permute-done.6.refs_3_
  43.5 1.1 %near.1 = (bf16[64,4608]{1,0:T(8,128)(2,1)}, bf16[64,4608]{1,0:T(8,128)(2,1)}, f32[8,128]{1,0:T(8,128)S(1)}) custom-call(bf16[64,4608]{1,0:T(8,128)(2,1)S(1)} %get-tuple-element.58.refs_0_, bf16[64,4608]{1,0:T(8,128)(2,1)S(1)} %get-tuple-element.59.refs_1_, bf16[64,2304]{1,0:T(8,128)(2,1)S(1)} %collective-permute-done.5.refs_2_, ...), custom_call_target="tpu_custom_call" | custom-call | flops 1024 | bytes 1024 | tf_op jit(solution)/shard_map/near/pallas_call | solution.py:87
  44.7 0.0 collective-permute-start.9
  44.7 2.7 %collective-permute-start.10 = (bf16[64,4608]{1,0:T(8,128)(2,1)}, bf16[64,4608]{1,0:T(8,128)(2,1)S(1)}, u32[]{:S(2)}, u32[]{:S(2)}) collective-permute-start(bf16[64,4608]{1,0:T(8,128)(2,1)} %get-tuple-element.69), channel_id=1, source_target_pairs={{0,6},{1,7},{2,0},{3,1},{4,2},{5,3},{6,4},{7,5},{8,14},{9,15},{10,... | collective-permute-start | bytes 1769480 | tf_op jit(solution)/shard_map/ppermute | solution.py:36
  47.3 0.0 collective-permute-start.12
  47.4 13.7 %collective-permute-done.12.refs_1_ = bf16[256,128]{1,0:T(8,128)(2,1)S(1)} collective-permute-done((bf16[256,128]{1,0:T(8,128)(2,1)S(1)}, bf16[256,128]{1,0:T(8,128)(2,1)S(1)}, u32[]{:S(2)}, u32[]{:S(2)}) %collective-permute-start.12) | collective-permute-done | bytes 65568 | tf_op jit(solution)/shard_map/ppermute | solution.py:46
  61.1 1.1 %collective-permute-start.16 = (bf16[256,128]{1,0:T(8,128)(2,1)S(1)}, bf16[256,128]{1,0:T(8,128)(2,1)S(1)}, u32[]{:S(2)}, u32[]{:S(2)}) collective-permute-start(bf16[256,128]{1,0:T(8,128)(2,1)S(1)} %get-tuple-element.79.refs_0_), channel_id=1, source_target_pairs={{0,8},{1,9},{2,10},{3,11},{4,12},{5,13},{6,14},{7,15},{8,0},{9,1},... | collective-permute-start | bytes 196616 | tf_op jit(solution)/shard_map/ppermute | solution.py:36
  62.2 0.0 copy-done.2
  62.2 1.3 %up_table.1 = (bf16[1024,512]{1,0:T(8,128)(2,1)S(1)}, f32[8,128]{1,0:T(8,128)S(1)}) custom-call(bf16[1024,512]{1,0:T(8,128)(2,1)S(1)} %copy-done.2, s32[16]{0:T(128)S(1)} %copy-done.8, bf16[16,256,128]{2,1,0:T(8,128)(2,1)S(1)} %all-to-all-done.refs_4_.refs_2_, f32[8,128]{1,0:T(8,128)S(1)} %get-tuple-element.73.refs_3_), custom_call_target="tpu_custom_call" | custom-call | flops 1024 | bytes 1024 | tf_op jit(solution)/shard_map/up_table/pallas_call | solution.py:87
  63.5 0.0 collective-permute-done.11.refs_1_
  63.6 0.9 %turn_narrow.1 = (bf16[32,3584]{1,0:T(8,128)(2,1)S(1)}, bf16[32,3584]{1,0:T(8,128)(2,1)}, bf16[32,3584]{1,0:T(8,128)(2,1)}, bf16[32,3584]{1,0:T(8,128)(2,1)}, f32[8,128]{1,0:T(8,128)S(1)}) custom-call(bf16[128,3584]{1,0:T(8,128)(2,1)S(1)} %get-tuple-element.70.refs_0_, bf16[128,3584]{1,0:T(8,128)(2,1)S(1)} %collective-permute-done.11.refs_1_, ...), custom_call_target="tpu_custom_call" | custom-call | flops 1024 | bytes 1024 | tf_op jit(solution)/shard_map/turn_narrow/pallas_call | solution.py:87
  64.5 0.5 collective-permute-start.13
  65.0 3.1 %collective-permute-start.14 = (bf16[32,3584]{1,0:T(8,128)(2,1)}, bf16[32,3584]{1,0:T(8,128)(2,1)S(1)}, u32[]{:S(2)}, u32[]{:S(2)}) collective-permute-start(bf16[32,3584]{1,0:T(8,128)(2,1)} %get-tuple-element.77), channel_id=1, source_target_pairs={{0,4},{1,5},{2,6},{3,7},{4,0},{5,1},{6,2},{7,3},{8,12},{9,13},{10,... | collective-permute-start | bytes 688136 | tf_op jit(solution)/shard_map/ppermute | solution.py:36
  68.1 0.0 collective-permute-done.16.refs_1_
  68.1 0.0 collective-permute-start.15
  68.1 1.6 %raise_features.1 = (bf16[16,32,512]{2,1,0:T(8,128)(2,1)}, f32[8,128]{1,0:T(8,128)S(1)}) custom-call(bf16[256,128]{1,0:T(8,128)(2,1)S(1)} %get-tuple-element.79.refs_0_, bf16[256,128]{1,0:T(8,128)(2,1)S(1)} %collective-permute-done.16.refs_1_, bf16[1024,512]{1,0:T(8,128)(2,1)S(1)} %get-tuple-element.80.refs_2_, s32[512,1]{1,0:T(8,128)S(1)} %copy-done.1, ...), custom_call_target="tpu_custom_call" | custom-call | flops 1024 | bytes 1024 | tf_op jit(solution)/shard_map/raise_features/pallas_call | solution.py:87
  69.7 6.8 %all-to-all-start.1 = ((bf16[16,32,512]{2,1,0:T(8,128)(2,1)}), bf16[16,32,512]{2,1,0:T(8,128)(2,1)S(1)}, u32[]{:S(2)}, u32[]{:S(2)}) async-start(bf16[16,32,512]{2,1,0:T(8,128)(2,1)} %get-tuple-element.87), calls=%async_computation.1 | async-start | bytes 1048576 | tf_op jit(solution)/shard_map/all_to_all | solution.py:440
  76.4 0.0 collective-permute-done.13.refs_1_
  76.4 0.0 collective-permute-done.14.refs_2_
  76.4 0.3 collective-permute-done.15.refs_3_
  76.7 1.0 %add_parts.7 = (f32[32,3584]{1,0:T(8,128)S(1)}, f32[8,128]{1,0:T(8,128)S(1)}) custom-call(bf16[32,3584]{1,0:T(8,128)(2,1)S(1)} %get-tuple-element.75.refs_0_, bf16[32,3584]{1,0:T(8,128)(2,1)S(1)} %collective-permute-done.13.refs_1_, bf16[32,3584]{1,0:T(8,128)(2,1)S(1)} %collective-permute-done.14.refs_2_, bf16[32,3584]{1,0:T(8,128)(2,1)} %collective-permute-done.15.refs_3_, ...), custom_call_target="tpu_custom_call" | custom-call | flops 1024 | bytes 1024 | tf_op jit(solution)/shard_map/add_parts/pallas_call | solution.py:87
  77.8 0.0 collective-permute-done.9.refs_1_
  77.8 0.0 collective-permute-done.10.refs_2_
  77.8 0.9 turn_wide.1
  78.7 0.0 copy-done.5
  78.7 1.1 %collective-permute-start.17 = (bf16[32,4608]{1,0:T(8,128)(2,1)}, bf16[32,4608]{1,0:T(8,128)(2,1)S(1)}, u32[]{:S(2)}, u32[]{:S(2)}) collective-permute-start(bf16[32,4608]{1,0:T(8,128)(2,1)} %get-tuple-element.85), channel_id=1, source_target_pairs={{0,8},{1,9},{2,10},{3,11},{4,12},{5,13},{6,14},{7,15},{8,0},{9,1},... | collective-permute-start | bytes 884744 | tf_op jit(solution)/shard_map/ppermute | solution.py:36
  79.8 6.5 %all-to-all-done.1.refs_4_ = bf16[16,32,512]{2,1,0:T(8,128)(2,1)S(1)} async-done(((bf16[16,32,512]{2,1,0:T(8,128)(2,1)}), bf16[16,32,512]{2,1,0:T(8,128)(2,1)S(1)}, u32[]{:S(2)}, u32[]{:S(2)}) %all-to-all-start.1) | async-done | bytes 524320 | tf_op jit(solution)/shard_map/all_to_all | solution.py:440
  86.3 4.6 %collective-permute-done.17.refs_2_ = bf16[32,4608]{1,0:T(8,128)(2,1)S(1)} collective-permute-done((bf16[32,4608]{1,0:T(8,128)(2,1)}, bf16[32,4608]{1,0:T(8,128)(2,1)S(1)}, u32[]{:S(2)}, u32[]{:S(2)}) %collective-permute-start.17) | collective-permute-done | bytes 294944 | tf_op jit(solution)/shard_map/ppermute | solution.py:36
  90.9 1.0 %copy-done.6 = f32[32,3584]{1,0:T(8,128)S(1)} copy-done((f32[32,3584]{1,0:T(8,128)S(1)}, f32[32,3584]{1,0:T(8,128)}, u32[]{:S(2)}) %copy-start.6) | copy-done | bytes 458776
  91.9 1.0 %finish.1 = (bf16[32,8192]{1,0:T(8,128)(2,1)}, f32[8,128]{1,0:T(8,128)}) custom-call(bf16[32,8192]{1,0:T(8,128)(2,1)S(1)} %copy-done.4, f32[32,4608]{1,0:T(8,128)S(1)} %get-tuple-element.84.refs_1_, bf16[32,4608]{1,0:T(8,128)(2,1)S(1)} %collective-permute-done.17.refs_2_, f32[32,3584]{1,0:T(8,128)S(1)} %copy-done.6, ...), custom_call_target="tpu_custom_call" | custom-call | flops 1024 | bytes 1024 | tf_op jit(solution)/shard_map/finish/pallas_call | solution.py:87
  (10 shorter events, 0.1 us)
Async XLA Ops:
  0.0 24.5 %all-to-all-start = ((bf16[16,256,128]{2,1,0:T(8,128)(2,1)}), bf16[16,256,128]{2,1,0:T(8,128)(2,1)S(1)}, u32[]{:S(2)}, u32[]{:S(2)}) async-start(bf16[16,256,128]{2,1,0:T(8,128)(2,1)} %bitcast.2), calls=%async_computation | async-start | bytes 2097152 | tf_op jit(solution)/shard_map/all_to_all | solution.py:407
  15.1 9.4 %collective-permute-start.3 = (bf16[256,1792]{1,0:T(8,128)(2,1)}, bf16[256,1792]{1,0:T(8,128)(2,1)S(1)}, u32[]{:S(2)}, u32[]{:S(2)}) collective-permute-start(bf16[256,1792]{1,0:T(8,128)(2,1)} %get-tuple-element.53), channel_id=1, source_target_pairs={{0,1},{1,0},{2,3},{3,2},{4,5},{5,4},{6,7},{7,6},{8,9},{9,8},{10,11... | collective-permute-start | bytes 2752520 | tf_op jit(solution)/shard_map/ppermute | solution.py:36
  15.3 9.2 %collective-permute-start.4 = (bf16[256,1792]{1,0:T(8,128)(2,1)}, bf16[256,1792]{1,0:T(8,128)(2,1)S(1)}, u32[]{:S(2)}, u32[]{:S(2)}) collective-permute-start(bf16[256,1792]{1,0:T(8,128)(2,1)} %get-tuple-element.54), channel_id=1, source_target_pairs={{0,1},{1,0},{2,3},{3,2},{4,5},{5,4},{6,7},{7,6},{8,9},{9,8},{10,11... | collective-permute-start | bytes 2752520 | tf_op jit(solution)/shard_map/ppermute | solution.py:36
  23.8 5.3 %collective-permute-start = (bf16[256,1536]{1,0:T(8,128)(2,1)}, bf16[256,1536]{1,0:T(8,128)(2,1)}, u32[]{:S(2)}, u32[]{:S(2)}) collective-permute-start(bf16[256,1536]{1,0:T(8,128)(2,1)} %get-tuple-element.49), channel_id=1, source_target_pairs={{0,1},{1,0},{2,3},{3,2},{4,5},{5,4},{6,7},{7,6},{8,9},{9,8},{10,11... | collective-permute-start | bytes 2359304 | tf_op jit(solution)/shard_map/ppermute | solution.py:36
  24.0 5.1 %collective-permute-start.1 = (bf16[256,1536]{1,0:T(8,128)(2,1)}, bf16[256,1536]{1,0:T(8,128)(2,1)}, u32[]{:S(2)}, u32[]{:S(2)}) collective-permute-start(bf16[256,1536]{1,0:T(8,128)(2,1)} %get-tuple-element.50), channel_id=1, source_target_pairs={{0,1},{1,0},{2,3},{3,2},{4,5},{5,4},{6,7},{7,6},{8,9},{9,8},{10,11... | collective-permute-start | bytes 2359304 | tf_op jit(solution)/shard_map/ppermute | solution.py:36
  24.4 4.7 %collective-permute-start.2 = (bf16[256,1536]{1,0:T(8,128)(2,1)}, bf16[256,1536]{1,0:T(8,128)(2,1)}, u32[]{:S(2)}, u32[]{:S(2)}) collective-permute-start(bf16[256,1536]{1,0:T(8,128)(2,1)} %get-tuple-element.51), channel_id=1, source_target_pairs={{0,1},{1,0},{2,3},{3,2},{4,5},{5,4},{6,7},{7,6},{8,9},{9,8},{10,11... | collective-permute-start | bytes 2359304 | tf_op jit(solution)/shard_map/ppermute | solution.py:36
  24.5 0.7 copy-start.7
  27.3 36.2 %collective-permute-start.11 = (bf16[128,3584]{1,0:T(8,128)(2,1)S(1)}, bf16[128,3584]{1,0:T(8,128)(2,1)S(1)}, u32[]{:S(2)}, u32[]{:S(2)}) collective-permute-start(bf16[128,3584]{1,0:T(8,128)(2,1)S(1)} %get-tuple-element.56.refs_4_), channel_id=1, source_target_pairs={{0,8},{1,9},{2,10},{3,11},{4,12},{5,13},{6,14},{7,15},{8,0},{9,1},... | collective-permute-start | bytes 2752520 | tf_op jit(solution)/shard_map/ppermute | solution.py:36
  29.1 5.5 %copy-start = (bf16[512,512]{1,0:T(8,128)(2,1)S(1)}, bf16[512,512]{1,0:T(8,128)(2,1)}, u32[]{:S(2)}) copy-start(bf16[512,512]{1,0:T(8,128)(2,1)} %refs_0_.7) | copy-start | bytes 1572868
  29.1 5.5 %copy-start.1 = (s32[512,1]{1,0:T(8,128)S(1)}, s32[512,1]{1,0:T(8,128)}, u32[]{:S(2)}) copy-start(s32[512,1]{1,0:T(8,128)} %copy.9.refs_2_.refs_3_) | copy-start | bytes 6148
  29.1 5.4 %copy-start.3 = (bf16[512,1024]{1,0:T(8,128)(2,1)S(1)}, bf16[512,1024]{1,0:T(8,128)(2,1)}, u32[]{:S(2)}) copy-start(bf16[512,1024]{1,0:T(8,128)(2,1)} %refs_1_.6) | copy-start | bytes 3145732
  29.1 5.4 %copy-start.8 = (s32[16]{0:T(128)S(1)}, s32[16]{0:T(128)}, u32[]{:S(2)}) copy-start(s32[16]{0:T(128)} %refs_1_.7) | copy-start | bytes 196
  31.8 11.7 %collective-permute-start.5 = (bf16[64,2304]{1,0:T(8,128)(2,1)S(1)}, bf16[64,2304]{1,0:T(8,128)(2,1)S(1)}, u32[]{:S(2)}, u32[]{:S(2)}) collective-permute-start(bf16[64,2304]{1,0:T(8,128)(2,1)S(1)} %get-tuple-element.60), channel_id=1, source_target_pairs={{0,2},{1,3},{2,4},{3,5},{4,6},{5,7},{6,0},{7,1},{8,10},{9,11},{10,... | collective-permute-start | bytes 884744 | tf_op jit(solution)/shard_map/ppermute | solution.py:36
  33.0 10.5 %collective-permute-start.6 = (bf16[64,2304]{1,0:T(8,128)(2,1)S(1)}, bf16[64,2304]{1,0:T(8,128)(2,1)S(1)}, u32[]{:S(2)}, u32[]{:S(2)}) collective-permute-start(bf16[64,2304]{1,0:T(8,128)(2,1)S(1)} %get-tuple-element.61), channel_id=1, source_target_pairs={{0,6},{1,7},{2,0},{3,1},{4,2},{5,3},{6,4},{7,5},{8,14},{9,15},{10,... | collective-permute-start | bytes 884744 | tf_op jit(solution)/shard_map/ppermute | solution.py:36
  34.5 27.6 %copy-start.2 = (bf16[1024,512]{1,0:T(8,128)(2,1)S(1)}, bf16[1024,512]{1,0:T(8,128)(2,1)}, u32[]{:S(2)}) copy-start(bf16[1024,512]{1,0:T(8,128)(2,1)} %refs_0_.8) | copy-start | bytes 3145732
  38.0 2.0 %collective-permute-start.7 = (bf16[256,128]{1,0:T(8,128)(2,1)S(1)}, bf16[256,128]{1,0:T(8,128)(2,1)S(1)}, u32[]{:S(2)}, u32[]{:S(2)}) collective-permute-start(bf16[256,128]{1,0:T(8,128)(2,1)S(1)} %get-tuple-element.63.refs_0_), channel_id=1, source_target_pairs={{0,1},{1,0},{2,3},{3,2},{4,5},{5,4},{6,7},{7,6},{8,9},{9,8},{10,11... | collective-permute-start | bytes 196616 | tf_op jit(solution)/shard_map/ppermute | solution.py:36
  40.0 3.5 %collective-permute-start.8 = (bf16[256,128]{1,0:T(8,128)(2,1)S(1)}, bf16[256,128]{1,0:T(8,128)(2,1)S(1)}, u32[]{:S(2)}, u32[]{:S(2)}) collective-permute-start(bf16[256,128]{1,0:T(8,128)(2,1)S(1)} %get-tuple-element.65.refs_0_), channel_id=1, source_target_pairs={{0,2},{1,3},{2,0},{3,1},{4,6},{5,7},{6,4},{7,5},{8,10},{9,11},{10,... | collective-permute-start | bytes 196616 | tf_op jit(solution)/shard_map/ppermute | solution.py:46
  44.7 33.1 %collective-permute-start.9 = (bf16[64,4608]{1,0:T(8,128)(2,1)}, bf16[64,4608]{1,0:T(8,128)(2,1)S(1)}, u32[]{:S(2)}, u32[]{:S(2)}) collective-permute-start(bf16[64,4608]{1,0:T(8,128)(2,1)} %get-tuple-element.68), channel_id=1, source_target_pairs={{0,2},{1,3},{2,4},{3,5},{4,6},{5,7},{6,0},{7,1},{8,10},{9,11},{10,... | collective-permute-start | bytes 1769480 | tf_op jit(solution)/shard_map/ppermute | solution.py:36
  44.7 33.2 %collective-permute-start.10 = (bf16[64,4608]{1,0:T(8,128)(2,1)}, bf16[64,4608]{1,0:T(8,128)(2,1)S(1)}, u32[]{:S(2)}, u32[]{:S(2)}) collective-permute-start(bf16[64,4608]{1,0:T(8,128)(2,1)} %get-tuple-element.69), channel_id=1, source_target_pairs={{0,6},{1,7},{2,0},{3,1},{4,2},{5,3},{6,4},{7,5},{8,14},{9,15},{10,... | collective-permute-start | bytes 1769480 | tf_op jit(solution)/shard_map/ppermute | solution.py:36
  47.3 13.8 %collective-permute-start.12 = (bf16[256,128]{1,0:T(8,128)(2,1)S(1)}, bf16[256,128]{1,0:T(8,128)(2,1)S(1)}, u32[]{:S(2)}, u32[]{:S(2)}) collective-permute-start(bf16[256,128]{1,0:T(8,128)(2,1)S(1)} %get-tuple-element.71.refs_0_), channel_id=1, source_target_pairs={{0,6},{1,7},{2,4},{3,5},{4,2},{5,3},{6,0},{7,1},{8,14},{9,15},{10,... | collective-permute-start | bytes 196616 | tf_op jit(solution)/shard_map/ppermute | solution.py:46
  61.1 7.0 %collective-permute-start.16 = (bf16[256,128]{1,0:T(8,128)(2,1)S(1)}, bf16[256,128]{1,0:T(8,128)(2,1)S(1)}, u32[]{:S(2)}, u32[]{:S(2)}) collective-permute-start(bf16[256,128]{1,0:T(8,128)(2,1)S(1)} %get-tuple-element.79.refs_0_), channel_id=1, source_target_pairs={{0,8},{1,9},{2,10},{3,11},{4,12},{5,13},{6,14},{7,15},{8,0},{9,1},... | collective-permute-start | bytes 196616 | tf_op jit(solution)/shard_map/ppermute | solution.py:36
  64.5 11.9 %collective-permute-start.13 = (bf16[32,3584]{1,0:T(8,128)(2,1)}, bf16[32,3584]{1,0:T(8,128)(2,1)S(1)}, u32[]{:S(2)}, u32[]{:S(2)}) collective-permute-start(bf16[32,3584]{1,0:T(8,128)(2,1)} %get-tuple-element.76), channel_id=1, source_target_pairs={{0,2},{1,3},{2,4},{3,5},{4,6},{5,7},{6,0},{7,1},{8,10},{9,11},{10,... | collective-permute-start | bytes 688136 | tf_op jit(solution)/shard_map/ppermute | solution.py:36
  65.0 11.5 %collective-permute-start.14 = (bf16[32,3584]{1,0:T(8,128)(2,1)}, bf16[32,3584]{1,0:T(8,128)(2,1)S(1)}, u32[]{:S(2)}, u32[]{:S(2)}) collective-permute-start(bf16[32,3584]{1,0:T(8,128)(2,1)} %get-tuple-element.77), channel_id=1, source_target_pairs={{0,4},{1,5},{2,6},{3,7},{4,0},{5,1},{6,2},{7,3},{8,12},{9,13},{10,... | collective-permute-start | bytes 688136 | tf_op jit(solution)/shard_map/ppermute | solution.py:36
  68.1 8.7 %collective-permute-start.15 = (bf16[32,3584]{1,0:T(8,128)(2,1)}, bf16[32,3584]{1,0:T(8,128)(2,1)}, u32[]{:S(2)}, u32[]{:S(2)}) collective-permute-start(bf16[32,3584]{1,0:T(8,128)(2,1)} %get-tuple-element.78), channel_id=1, source_target_pairs={{0,6},{1,7},{2,0},{3,1},{4,2},{5,3},{6,4},{7,5},{8,14},{9,15},{10,... | collective-permute-start | bytes 688136 | tf_op jit(solution)/shard_map/ppermute | solution.py:36
  68.1 22.8 %copy-start.4 = (bf16[32,8192]{1,0:T(8,128)(2,1)S(1)}, bf16[32,8192]{1,0:T(8,128)(2,1)}, u32[]{:S(2)}) copy-start(bf16[32,8192]{1,0:T(8,128)(2,1)} %refs_0_.9) | copy-start | bytes 1572868
  69.7 16.6 %all-to-all-start.1 = ((bf16[16,32,512]{2,1,0:T(8,128)(2,1)}), bf16[16,32,512]{2,1,0:T(8,128)(2,1)S(1)}, u32[]{:S(2)}, u32[]{:S(2)}) async-start(bf16[16,32,512]{2,1,0:T(8,128)(2,1)} %get-tuple-element.87), calls=%async_computation.1 | async-start | bytes 1048576 | tf_op jit(solution)/shard_map/all_to_all | solution.py:440
  77.8 0.9 copy-start.5
  78.7 12.2 %collective-permute-start.17 = (bf16[32,4608]{1,0:T(8,128)(2,1)}, bf16[32,4608]{1,0:T(8,128)(2,1)S(1)}, u32[]{:S(2)}, u32[]{:S(2)}) collective-permute-start(bf16[32,4608]{1,0:T(8,128)(2,1)} %get-tuple-element.85), channel_id=1, source_target_pairs={{0,8},{1,9},{2,10},{3,11},{4,12},{5,13},{6,14},{7,15},{8,0},{9,1},... | collective-permute-start | bytes 884744 | tf_op jit(solution)/shard_map/ppermute | solution.py:36
  90.9 1.0 %copy-start.6 = (f32[32,3584]{1,0:T(8,128)S(1)}, f32[32,3584]{1,0:T(8,128)}, u32[]{:S(2)}) copy-start(f32[32,3584]{1,0:T(8,128)} %copy-done.5) | copy-start | bytes 1376260

commit v5 on v4

--- a/solution.py
+++ b/solution.py
@@ -12,6 +12,7 @@
 F32 = jnp.float32
 BF16 = jnp.bfloat16
 WIDE = 4608
+CUT = 2560
 VMEM_LIMIT = 16 * 1024 * 1024
 PRODUCT_LIMIT = 56 * 1024 * 1024
 CHIP_LIMIT = 48 * 1024 * 1024
@@ -261,15 +262,16 @@
 def turn_wide(here, from_left, from_right, after=()):
     width = here.shape[1]
 
-    def kernel(here_ref, from_left_ref, from_right_ref, keep_ref, send_ref):
+    def kernel(here_ref, from_left_ref, from_right_ref, keep_ref, send_ref, rest_ref):
         total = plus(here_ref[...], from_left_ref[...], from_right_ref[...])
         keep_ref[...] = total[:32]
-        send_ref[...] = total[32:].astype(BF16)
+        send_ref[...] = total[32:, :CUT].astype(BF16)
+        rest_ref[...] = total[32:, CUT:].astype(BF16)
 
     return call(
         kernel,
         "turn_wide",
-        [whole((32, width), F32), whole((32, width), BF16)],
+        [whole((32, width), F32), whole((32, CUT), BF16), whole((32, width - CUT), BF16)],
         (here, from_left, from_right),
         after=after,
     )
@@ -284,6 +286,11 @@
 
 def lanes(rows):
     return lax.broadcasted_iota(jnp.int32, (rows, 128), 1)
+
+
+def slot_columns(slot_ref):
+    row = slot_ref[...].astype(F32)
+    return jnp.broadcast_to(row, (128, 512)).T.astype(jnp.int32)
 
 
 def resident_slot(slot, target_ref):
@@ -300,7 +307,7 @@
     chooser = jnp.where(row == source, 1.0, 0.0).astype(BF16)
     split = jnp.dot(x, chooser, preferred_element_type=F32).astype(BF16)
     even, odd = split[:, :256], split[:, 256:]
-    slot = jnp.broadcast_to(slot_ref[...], (512, 128))
+    slot = slot_columns(slot_ref)
     kept = resident_slot(slot, target_ref)
     high = (lanes(512) >= RANK).astype(jnp.int32)
     acc = jnp.zeros((512, 128), F32)
@@ -356,7 +363,7 @@
     both = jnp.concatenate(
         [jnp.where(left, packed, turned), jnp.where(left, turned, packed)], axis=0
     )
-    slot = jnp.broadcast_to(slot_ref[...], (512, 128))
+    slot = slot_columns(slot_ref)
     high = (lanes(512) >= RANK).astype(jnp.int32)
     raised = jnp.concatenate(
         [jnp.where(slot == 2 * j + high, both, 0.0).astype(BF16) for j in range(CHIPS)], axis=1
@@ -376,12 +383,16 @@
 
 
 def finish_kernel(
-    residual_ref, wide_ref, wide_y_ref, narrow_ref, delta_ref, out_ref
+    residual_ref, wide_ref, wide_y_ref, rest_y_ref, narrow_ref, delta_ref, out_ref
 ):
     for t in range(16):
         cols = slice(t * 512, (t + 1) * 512)
         if (t + 1) * 512 <= WIDE:
-            base = wide_ref[:, cols] + wide_y_ref[:, cols].astype(F32)
+            if (t + 1) * 512 <= CUT:
+                other = wide_y_ref[:, cols]
+            else:
+                other = rest_y_ref[:, t * 512 - CUT : (t + 1) * 512 - CUT]
+            base = wide_ref[:, cols] + other.astype(F32)
         else:
             part = slice(t * 512 - WIDE, (t + 1) * 512 - WIDE)
             base = narrow_ref[:, part]
@@ -401,14 +412,14 @@
     request_adapter_slot,
 ):
     x, w = attention_output, output_projection_weight
-    slot = request_adapter_slot.reshape(512, 1)
+    slot = request_adapter_slot.reshape(1, 512)
     target = fresh_slot_targets
 
     maps = lax.all_to_all(
         fresh_adapter_bundle.reshape(16, 256, 128), "tp", split_axis=0, concat_axis=0, tiled=True
     )
     narrow = x.shape[0] * 16 - WIDE
-    *narrow_away, narrow_own, mark = product(x, w, Y_MAJOR, WIDE, narrow, NARROW_CHUNK, [slot])
+    *narrow_away, narrow_own, mark = product(x, w, Y_MAJOR, WIDE, narrow, NARROW_CHUNK)
     narrow_in = [send(away, 0, 0, 1) for away in narrow_away]
     *wide_away, wide_own, mark = product(x, w, X_MAJOR, 0, WIDE, WIDE_CHUNK, [mark])
     wide_in = [send(away, 0, 0, 1) for away in wide_away]
@@ -428,25 +439,26 @@
     part_in = trade(part, lambda x: x ^ 1)
     part, mark = add_parts([part, part_in], [mark])
     part_in = trade(part, lambda x: 3 - x)
+    part, mark = add_parts([part, part_in], [mark])
+    other = send(part, 1, 0, 0)
 
     right, left, mark = near(right, left, far_right, far_left, [mark])
     from_left, from_right = send(right, 0, 1, 0), send(left, 0, 3, 0)
-    part, mark = add_parts([part, part_in], [mark])
-    other = send(part, 1, 0, 0)
     table, mark = up_table(resident_up_maps, target, maps, [mark])
     *low, mark = turn_narrow(keep, narrow_y, [mark])
     low_in = [send(low[d], 0, d, 0) for d in (1, 2, 3)]
     raised, mark = raise_features(part, other, table, slot, [mark])
     delta = lax.all_to_all(raised, "tp", split_axis=0, concat_axis=0, tiled=True)
 
+    wide_keep, wide_send, wide_rest, mark = turn_wide(here, from_left, from_right, [mark])
+    wide_y = send(wide_send, 1, 0, 0)
+    rest_y = send(wide_rest, 1, 0, 0)
     narrow_sum, mark = add_parts([low[0], *low_in], [mark], F32)
-    wide_keep, wide_send, mark = turn_wide(here, from_left, from_right, [mark])
-    wide_y = send(wide_send, 1, 0, 0)
     hidden, _ = call(
         finish_kernel,
         "finish",
         [whole((32, 8192), BF16)],
-        (residual, wide_keep, wide_y, narrow_sum, delta),
+        (residual, wide_keep, wide_y, rest_y, narrow_sum, delta),
     )
     return hidden
 

time: 93.4 us -> 85.1 us (0.911)
  waiting for transfers between devices: 29.5 us -> 20.1 us
  starting transfers between devices: 29 us -> 31.8 us
  Pallas kernels: 31 us -> 28.9 us
    ppermute x2, waiting for transfers between devices: 17.1 us -> 6.54 us  [trade(): return lax.ppermute(array, 'tp', pairs)]
    ppermute x16 -> x17, waiting for transfers between devices: 5.83 us -> 13.5 us  [send(): return lax.ppermute(array, 'tp', route(yy, xx, cc))]
    all_to_all x1, waiting for transfers between devices: 6.51 us -> 0.01 us  [local(): lax.all_to_all(raised, 'tp', split_axis=0, concat_axis=0, tiled=True)]
    pallas_call x15, Pallas kernels: 31 us -> 28.9 us  [call(): pl.pallas_call(body, in_specs=list(specs or [VM] * count) + [LATER] * len...]
    unnamed x18 -> x24, local copies, waits for them, and re-layouts: 1.73 us -> 3.73 us
    ppermute x16 -> x17, starting transfers between devices: 15.3 us -> 17 us  [send(): return lax.ppermute(array, 'tp', route(yy, xx, cc))]
    reshape x1 -> x0, local copies, waits for them, and re-layouts: 1.53 us -> none  [local(): slot = request_adapter_slot.reshape(512, 1)]
    ppermute x2, starting transfers between devices: 0.13 us -> 1.36 us  [trade(): return lax.ppermute(array, 'tp', pairs)]
  transfers between devices with their start and end apart: 20 -> 21, of which waited for: 6 -> 5; matrix products, arithmetic and copies ran while one was open for 2% -> 0% of each run, Pallas kernels for 32% -> 33%
where the time goes in v5:
time: 85.1 us; the launch traced here: 84.7 us
  starting transfers between devices  31.8 us (37%)
  Pallas kernels  28.9 us (34%)
  waiting for transfers between devices  20.1 us (24%)
  local copies, waits for them, and re-layouts  3.73 us (4%)
    pallas_call x15, Pallas kernels, call(): pl.pallas_call(body, in_specs=list(specs or [VM] * count) + [LATER] * len...  28.9 us
    ppermute x17, starting transfers between devices, send(): return lax.ppermute(array, 'tp', route(yy, xx, cc))  17 us
    ppermute x17, waiting for transfers between devices, send(): return lax.ppermute(array, 'tp', route(yy, xx, cc))  13.5 us
    all_to_all x1, starting transfers between devices, local(): lax.all_to_all(fresh_adapter_bundle.reshape(16, 256, 128), 'tp', split_ax...  6.83 us
    all_to_all x1, starting transfers between devices, local(): lax.all_to_all(raised, 'tp', split_axis=0, concat_axis=0, tiled=True)  6.57 us
    ppermute x2, waiting for transfers between devices, trade(): return lax.ppermute(array, 'tp', pairs)  6.54 us
    unnamed x24, local copies, waits for them, and re-layouts  3.73 us
  transfers between devices with their start and end apart: 21, of which 5 were waited for; matrix products, arithmetic and copies ran while one was open for 0% of the time, Pallas kernels for 33%

profile of v5, /device:TPU:1, one launch (start us, length us, event | category | flops | bytes accessed | tf_op | source)
XLA Modules:
  0.0 84.7 jit_solution(15644880856521432495)
XLA Ops:
  0.0 6.8 %all-to-all-start = ((bf16[16,256,128]{2,1,0:T(8,128)(2,1)}), bf16[16,256,128]{2,1,0:T(8,128)(2,1)S(1)}, u32[]{:S(2)}, u32[]{:S(2)}) async-start(bf16[16,256,128]{2,1,0:T(8,128)(2,1)} %bitcast.4), calls=%async_computation | async-start | bytes 2097152 | tf_op jit(solution)/shard_map/all_to_all | solution.py:418
  6.8 6.7 %product.2 = (bf16[256,1792]{1,0:T(8,128)(2,1)}, bf16[256,1792]{1,0:T(8,128)(2,1)}, bf16[256,3584]{1,0:T(8,128)(2,1)}, f32[8,128]{1,0:T(8,128)}) custom-call(bf16[512,512]{1,0:T(8,128)(2,1)} %refs_0_.7, bf16[512,8192]{1,0:T(8,128)(2,1)} %refs_1_.5), custom_call_target="tpu_custom_call" | custom-call | flops 1024 | bytes 1024 | tf_op jit(solution)/shard_map/product/pallas_call | solution.py:88
  13.6 0.2 collective-permute-start.3
  13.8 0.4 collective-permute-start.4
  14.2 8.1 %product.3 = (bf16[256,1536]{1,0:T(8,128)(2,1)}, bf16[256,1536]{1,0:T(8,128)(2,1)}, bf16[256,1536]{1,0:T(8,128)(2,1)}, bf16[256,4608]{1,0:T(8,128)(2,1)}, f32[8,128]{1,0:T(8,128)}) custom-call(bf16[512,512]{1,0:T(8,128)(2,1)} %refs_0_.7, bf16[512,8192]{1,0:T(8,128)(2,1)} %refs_1_.5, f32[8,128]{1,0:T(8,128)} %get-tuple-element.48.refs_2_), custom_call_target="tpu_custom_call" | custom-call | flops 1024 | bytes 1024 | tf_op jit(solution)/shard_map/product/pallas_call | solution.py:88
  22.2 0.2 collective-permute-start
  22.4 0.4 collective-permute-start.1
  22.8 0.1 collective-permute-start.2
  22.9 0.0 collective-permute-done.3.refs_1_
  22.9 0.0 collective-permute-done.4.refs_2_
  22.9 0.0 all-to-all-done.refs_4_.refs_2_
  23.0 0.7 copy-done.7
  23.6 2.1 %chip_narrow.1 = (bf16[128,3584]{1,0:T(8,128)(2,1)S(1)}, bf16[128,3584]{1,0:T(8,128)(2,1)S(1)}, f32[8,128]{1,0:T(8,128)}) custom-call(bf16[256,3584]{1,0:T(8,128)(2,1)} %get-tuple-element.53.refs_0_, bf16[256,1792]{1,0:T(8,128)(2,1)S(1)} %collective-permute-done.3.refs_1_, bf16[256,1792]{1,0:T(8,128)(2,1)S(1)} %collective-permute-done.4.refs_2_, ...), custom_call_target="tpu_custom_call" | custom-call | flops 1024 | bytes 1024 | tf_op jit(solution)/shard_map/chip_narrow/pallas_call | solution.py:88
  25.8 1.7 %collective-permute-start.13 = (bf16[128,3584]{1,0:T(8,128)(2,1)S(1)}, bf16[128,3584]{1,0:T(8,128)(2,1)S(1)}, u32[]{:S(2)}, u32[]{:S(2)}) collective-permute-start(bf16[128,3584]{1,0:T(8,128)(2,1)S(1)} %get-tuple-element.57.refs_4_), channel_id=1, source_target_pairs={{0,8},{1,9},{2,10},{3,11},{4,12},{5,13},{6,14},{7,15},{8,0},{9,1},... | collective-permute-start | bytes 2752520 | tf_op jit(solution)/shard_map/ppermute | solution.py:37
  27.5 0.0 collective-permute-done.refs_1_
  27.5 0.0 collective-permute-done.1.refs_2_
  27.5 0.0 collective-permute-done.2.refs_3_
  27.5 0.0 copy-start
  27.5 0.0 copy-start.1
  27.5 0.0 copy-start.6
  27.6 0.0 copy-start.8
  27.6 2.6 %chip_wide.1 = (bf16[64,4608]{1,0:T(8,128)(2,1)S(1)}, bf16[64,4608]{1,0:T(8,128)(2,1)S(1)}, bf16[64,2304]{1,0:T(8,128)(2,1)S(1)}, bf16[64,2304]{1,0:T(8,128)(2,1...) custom-call(bf16[256,4608]{1,0:T(8,128)(2,1)} %get-tuple-element.49.refs_0_, ...), custom_call_target="tpu_custom_call" | custom-call | flops 1024 | bytes 1024 | tf_op jit(solution)/shard_map/chip_wide/pallas_call | solution.py:88
  30.2 1.3 %collective-permute-start.5 = (bf16[64,2304]{1,0:T(8,128)(2,1)S(1)}, bf16[64,2304]{1,0:T(8,128)(2,1)S(1)}, u32[]{:S(2)}, u32[]{:S(2)}) collective-permute-start(bf16[64,2304]{1,0:T(8,128)(2,1)S(1)} %get-tuple-element.61), channel_id=1, source_target_pairs={{0,2},{1,3},{2,4},{3,5},{4,6},{5,7},{6,0},{7,1},{8,10},{9,11},{10,... | collective-permute-start | bytes 884744 | tf_op jit(solution)/shard_map/ppermute | solution.py:37
  31.5 1.5 %collective-permute-start.6 = (bf16[64,2304]{1,0:T(8,128)(2,1)S(1)}, bf16[64,2304]{1,0:T(8,128)(2,1)S(1)}, u32[]{:S(2)}, u32[]{:S(2)}) collective-permute-start(bf16[64,2304]{1,0:T(8,128)(2,1)S(1)} %get-tuple-element.62), channel_id=1, source_target_pairs={{0,6},{1,7},{2,0},{3,1},{4,2},{5,3},{6,4},{7,5},{8,14},{9,15},{10,... | collective-permute-start | bytes 884744 | tf_op jit(solution)/shard_map/ppermute | solution.py:37
  33.0 0.0 copy-start.2
  33.0 3.3 %shrink_part.1 = (bf16[256,128]{1,0:T(8,128)(2,1)S(1)}, f32[8,128]{1,0:T(8,128)S(1)}) custom-call(bf16[512,512]{1,0:T(8,128)(2,1)S(1)} %copy-done, bf16[512,1024]{1,0:T(8,128)(2,1)S(1)} %copy-done.1, s32[1,512]{1,0:T(1,128)S(1)} %bitcast.2, s32[16]{0:T(128)S(1)} %copy-done.8, bf16[16,256,128]{2,1,0:T(8,128)(2,1)S(1)} %all-to-all-done.refs_4_.refs_2_, ...), custom_call_target="tpu_custom_call" | custom-call | flops 1024 | bytes 1024 | tf_op jit(solution)/shard_map/shrink_part/pallas_call | solution.py:88
  36.3 1.1 %collective-permute-start.7 = (bf16[256,128]{1,0:T(8,128)(2,1)S(1)}, bf16[256,128]{1,0:T(8,128)(2,1)S(1)}, u32[]{:S(2)}, u32[]{:S(2)}) collective-permute-start(bf16[256,128]{1,0:T(8,128)(2,1)S(1)} %get-tuple-element.64.refs_0_), channel_id=1, source_target_pairs={{0,1},{1,0},{2,3},{3,2},{4,5},{5,4},{6,7},{7,6},{8,9},{9,8},{10,11... | collective-permute-start | bytes 196616 | tf_op jit(solution)/shard_map/ppermute | solution.py:37
  37.4 0.9 %collective-permute-done.7.refs_1_ = bf16[256,128]{1,0:T(8,128)(2,1)S(1)} collective-permute-done((bf16[256,128]{1,0:T(8,128)(2,1)S(1)}, bf16[256,128]{1,0:T(8,128)(2,1)S(1)}, u32[]{:S(2)}, u32[]{:S(2)}) %collective-permute-start.7) | collective-permute-done | bytes 65568 | tf_op jit(solution)/shard_map/ppermute | solution.py:37
  38.3 0.1 collective-permute-start.8
  38.4 3.4 %collective-permute-done.8.refs_1_ = bf16[256,128]{1,0:T(8,128)(2,1)S(1)} collective-permute-done((bf16[256,128]{1,0:T(8,128)(2,1)S(1)}, bf16[256,128]{1,0:T(8,128)(2,1)S(1)}, u32[]{:S(2)}, u32[]{:S(2)}) %collective-permute-start.8) | collective-permute-done | bytes 65568 | tf_op jit(solution)/shard_map/ppermute | solution.py:47
  41.8 1.3 %collective-permute-start.9 = (bf16[256,128]{1,0:T(8,128)(2,1)S(1)}, bf16[256,128]{1,0:T(8,128)(2,1)S(1)}, u32[]{:S(2)}, u32[]{:S(2)}) collective-permute-start(bf16[256,128]{1,0:T(8,128)(2,1)S(1)} %get-tuple-element.68.refs_0_), channel_id=1, source_target_pairs={{0,6},{1,7},{2,4},{3,5},{4,2},{5,3},{6,0},{7,1},{8,14},{9,15},{10,... | collective-permute-start | bytes 196616 | tf_op jit(solution)/shard_map/ppermute | solution.py:47
  43.1 3.1 %collective-permute-done.9.refs_1_ = bf16[256,128]{1,0:T(8,128)(2,1)S(1)} collective-permute-done((bf16[256,128]{1,0:T(8,128)(2,1)S(1)}, bf16[256,128]{1,0:T(8,128)(2,1)S(1)}, u32[]{:S(2)}, u32[]{:S(2)}) %collective-permute-start.9) | collective-permute-done | bytes 65568 | tf_op jit(solution)/shard_map/ppermute | solution.py:47
  46.2 0.0 collective-permute-done.5.refs_2_
  46.2 0.0 collective-permute-done.6.refs_3_
  46.3 0.9 %near.1 = (bf16[64,4608]{1,0:T(8,128)(2,1)}, bf16[64,4608]{1,0:T(8,128)(2,1)S(1)}, f32[8,128]{1,0:T(8,128)S(1)}) custom-call(bf16[64,4608]{1,0:T(8,128)(2,1)S(1)} %get-tuple-element.59.refs_0_, bf16[64,4608]{1,0:T(8,128)(2,1)S(1)} %get-tuple-element.60.refs_1_, bf16[64,2304]{1,0:T(8,128)(2,1)S(1)} %collective-permute-done.5.refs_2_, ...), custom_call_target="tpu_custom_call" | custom-call | flops 1024 | bytes 1024 | tf_op jit(solution)/shard_map/near/pallas_call | solution.py:88
  47.2 0.0 collective-permute-start.10
  47.2 2.7 %collective-permute-start.11 = (bf16[64,4608]{1,0:T(8,128)(2,1)S(1)}, bf16[64,4608]{1,0:T(8,128)(2,1)S(1)}, u32[]{:S(2)}, u32[]{:S(2)}) collective-permute-start(bf16[64,4608]{1,0:T(8,128)(2,1)S(1)} %get-tuple-element.72), channel_id=1, source_target_pairs={{0,6},{1,7},{2,0},{3,1},{4,2},{5,3},{6,4},{7,5},{8,14},{9,15},{10,... | collective-permute-start | bytes 1769480 | tf_op jit(solution)/shard_map/ppermute | solution.py:37
  49.8 1.0 %collective-permute-start.12 = (bf16[256,128]{1,0:T(8,128)(2,1)S(1)}, bf16[256,128]{1,0:T(8,128)(2,1)S(1)}, u32[]{:S(2)}, u32[]{:S(2)}) collective-permute-start(bf16[256,128]{1,0:T(8,128)(2,1)S(1)} %get-tuple-element.73.refs_0_), channel_id=1, source_target_pairs={{0,8},{1,9},{2,10},{3,11},{4,12},{5,13},{6,14},{7,15},{8,0},{9,1},... | collective-permute-start | bytes 196616 | tf_op jit(solution)/shard_map/ppermute | solution.py:37
  50.8 1.3 %up_table.1 = (bf16[1024,512]{1,0:T(8,128)(2,1)S(1)}, f32[8,128]{1,0:T(8,128)S(1)}) custom-call(bf16[1024,512]{1,0:T(8,128)(2,1)S(1)} %copy-done.2, s32[16]{0:T(128)S(1)} %copy-done.8, bf16[16,256,128]{2,1,0:T(8,128)(2,1)S(1)} %all-to-all-done.refs_4_.refs_2_, f32[8,128]{1,0:T(8,128)S(1)} %get-tuple-element.74.refs_3_), custom_call_target="tpu_custom_call" | custom-call | flops 1024 | bytes 1024 | tf_op jit(solution)/shard_map/up_table/pallas_call | solution.py:88
  52.2 0.0 collective-permute-done.13.refs_1_
  52.2 0.2 turn_narrow.1
  52.4 0.7 copy-done.4
  53.1 0.7 copy-done.10
  53.8 0.7 copy-done.11
  54.5 0.0 collective-permute-done.12.refs_1_
  54.5 1.7 %raise_features.1 = (bf16[16,32,512]{2,1,0:T(8,128)(2,1)}, f32[8,128]{1,0:T(8,128)S(1)}) custom-call(bf16[256,128]{1,0:T(8,128)(2,1)S(1)} %get-tuple-element.73.refs_0_, bf16[256,128]{1,0:T(8,128)(2,1)S(1)} %collective-permute-done.12.refs_1_, bf16[1024,512]{1,0:T(8,128)(2,1)S(1)} %get-tuple-element.75.refs_2_, s32[1,512]{1,0:T(1,128)S(1)} %bitcast.3, ...), custom_call_target="tpu_custom_call" | custom-call | flops 1024 | bytes 1024 | tf_op jit(solution)/shard_map/raise_features/pallas_call | solution.py:88
  56.2 6.6 %all-to-all-start.1 = ((bf16[16,32,512]{2,1,0:T(8,128)(2,1)}), bf16[16,32,512]{2,1,0:T(8,128)(2,1)S(1)}, u32[]{:S(2)}, u32[]{:S(2)}) async-start(bf16[16,32,512]{2,1,0:T(8,128)(2,1)} %get-tuple-element.89), calls=%async_computation.1 | async-start | bytes 1048576 | tf_op jit(solution)/shard_map/all_to_all | solution.py:451
  62.8 1.4 %collective-permute-start.16 = (bf16[32,3584]{1,0:T(8,128)(2,1)}, bf16[32,3584]{1,0:T(8,128)(2,1)S(1)}, u32[]{:S(2)}, u32[]{:S(2)}) collective-permute-start(bf16[32,3584]{1,0:T(8,128)(2,1)} %copy-done.11), channel_id=1, source_target_pairs={{0,2},{1,3},{2,4},{3,5},{4,6},{5,7},{6,0},{7,1},{8,10},{9,11},{10,... | collective-permute-start | bytes 688136 | tf_op jit(solution)/shard_map/ppermute | solution.py:37
  64.2 2.4 %collective-permute-start.17 = (bf16[32,3584]{1,0:T(8,128)(2,1)}, bf16[32,3584]{1,0:T(8,128)(2,1)S(1)}, u32[]{:S(2)}, u32[]{:S(2)}) collective-permute-start(bf16[32,3584]{1,0:T(8,128)(2,1)} %copy-done.10), channel_id=1, source_target_pairs={{0,4},{1,5},{2,6},{3,7},{4,0},{5,1},{6,2},{7,3},{8,12},{9,13},{10,... | collective-permute-start | bytes 688136 | tf_op jit(solution)/shard_map/ppermute | solution.py:37
  66.6 1.2 %collective-permute-start.18 = (bf16[32,3584]{1,0:T(8,128)(2,1)}, bf16[32,3584]{1,0:T(8,128)(2,1)S(1)}, u32[]{:S(2)}, u32[]{:S(2)}) collective-permute-start(bf16[32,3584]{1,0:T(8,128)(2,1)} %copy-done.9), channel_id=1, source_target_pairs={{0,6},{1,7},{2,0},{3,1},{4,2},{5,3},{6,4},{7,5},{8,14},{9,15},{10,... | collective-permute-start | bytes 688136 | tf_op jit(solution)/shard_map/ppermute | solution.py:37
  67.8 0.0 collective-permute-done.10.refs_1_
  67.8 0.0 collective-permute-done.11.refs_2_
  67.8 0.2 turn_wide.1
  68.0 1.3 %collective-permute-start.14 = (bf16[32,2560]{1,0:T(8,128)(2,1)S(1)}, bf16[32,2560]{1,0:T(8,128)(2,1)S(1)}, u32[]{:S(2)}, u32[]{:S(2)}) collective-permute-start(bf16[32,2560]{1,0:T(8,128)(2,1)S(1)} %get-tuple-element.81), channel_id=1, source_target_pairs={{0,8},{1,9},{2,10},{3,11},{4,12},{5,13},{6,14},{7,15},{8,0},{9,1},... | collective-permute-start | bytes 491528 | tf_op jit(solution)/shard_map/ppermute | solution.py:37
  69.3 0.2 collective-permute-start.15
  69.5 7.5 %collective-permute-done.16.refs_1_ = bf16[32,3584]{1,0:T(8,128)(2,1)S(1)} collective-permute-done((bf16[32,3584]{1,0:T(8,128)(2,1)}, bf16[32,3584]{1,0:T(8,128)(2,1)S(1)}, u32[]{:S(2)}, u32[]{:S(2)}) %collective-permute-start.16) | collective-permute-done | bytes 229408 | tf_op jit(solution)/shard_map/ppermute | solution.py:37
  77.1 5.0 %collective-permute-done.17.refs_2_ = bf16[32,3584]{1,0:T(8,128)(2,1)S(1)} collective-permute-done((bf16[32,3584]{1,0:T(8,128)(2,1)}, bf16[32,3584]{1,0:T(8,128)(2,1)S(1)}, u32[]{:S(2)}, u32[]{:S(2)}) %collective-permute-start.17) | collective-permute-done | bytes 229408 | tf_op jit(solution)/shard_map/ppermute | solution.py:37
  82.1 0.0 collective-permute-done.18.refs_3_
  82.1 0.9 %copy-done.5 = bf16[32,3584]{1,0:T(8,128)(2,1)S(1)} copy-done((bf16[32,3584]{1,0:T(8,128)(2,1)S(1)}, bf16[32,3584]{1,0:T(8,128)(2,1)}, u32[]{:S(2)}) %copy-start.5) | copy-done | bytes 229400
  83.0 0.6 add_parts.7
  83.7 0.0 collective-permute-done.15.refs_3_
  83.7 0.0 collective-permute-done.14.refs_2_
  83.7 0.0 all-to-all-done.1.refs_5_
  83.7 1.0 %finish.1 = (bf16[32,8192]{1,0:T(8,128)(2,1)}, f32[8,128]{1,0:T(8,128)}) custom-call(bf16[32,8192]{1,0:T(8,128)(2,1)S(1)} %copy-done.3, f32[32,4608]{1,0:T(8,128)S(1)} %get-tuple-element.80.refs_1_, bf16[32,2560]{1,0:T(8,128)(2,1)S(1)} %collective-permute-done.14.refs_2_, bf16[32,2048]{1,0:T(8,128)(2,1)S(1)} %collective-permute-done.15.refs_3_, ...), custom_call_target="tpu_custom_call" | custom-call | flops 1024 | bytes 1024 | tf_op jit(solution)/shard_map/finish/pallas_call | solution.py:88
  (17 shorter events, 0.1 us)
Async XLA Ops:
  0.0 23.0 %all-to-all-start = ((bf16[16,256,128]{2,1,0:T(8,128)(2,1)}), bf16[16,256,128]{2,1,0:T(8,128)(2,1)S(1)}, u32[]{:S(2)}, u32[]{:S(2)}) async-start(bf16[16,256,128]{2,1,0:T(8,128)(2,1)} %bitcast.4), calls=%async_computation | async-start | bytes 2097152 | tf_op jit(solution)/shard_map/all_to_all | solution.py:418
  13.6 9.4 %collective-permute-start.3 = (bf16[256,1792]{1,0:T(8,128)(2,1)}, bf16[256,1792]{1,0:T(8,128)(2,1)S(1)}, u32[]{:S(2)}, u32[]{:S(2)}) collective-permute-start(bf16[256,1792]{1,0:T(8,128)(2,1)} %get-tuple-element.54), channel_id=1, source_target_pairs={{0,1},{1,0},{2,3},{3,2},{4,5},{5,4},{6,7},{7,6},{8,9},{9,8},{10,11... | collective-permute-start | bytes 2752520 | tf_op jit(solution)/shard_map/ppermute | solution.py:37
  13.8 9.2 %collective-permute-start.4 = (bf16[256,1792]{1,0:T(8,128)(2,1)}, bf16[256,1792]{1,0:T(8,128)(2,1)S(1)}, u32[]{:S(2)}, u32[]{:S(2)}) collective-permute-start(bf16[256,1792]{1,0:T(8,128)(2,1)} %get-tuple-element.55), channel_id=1, source_target_pairs={{0,1},{1,0},{2,3},{3,2},{4,5},{5,4},{6,7},{7,6},{8,9},{9,8},{10,11... | collective-permute-start | bytes 2752520 | tf_op jit(solution)/shard_map/ppermute | solution.py:37
  22.2 5.3 %collective-permute-start = (bf16[256,1536]{1,0:T(8,128)(2,1)}, bf16[256,1536]{1,0:T(8,128)(2,1)}, u32[]{:S(2)}, u32[]{:S(2)}) collective-permute-start(bf16[256,1536]{1,0:T(8,128)(2,1)} %get-tuple-element.50), channel_id=1, source_target_pairs={{0,1},{1,0},{2,3},{3,2},{4,5},{5,4},{6,7},{7,6},{8,9},{9,8},{10,11... | collective-permute-start | bytes 2359304 | tf_op jit(solution)/shard_map/ppermute | solution.py:37
  22.4 5.1 %collective-permute-start.1 = (bf16[256,1536]{1,0:T(8,128)(2,1)}, bf16[256,1536]{1,0:T(8,128)(2,1)}, u32[]{:S(2)}, u32[]{:S(2)}) collective-permute-start(bf16[256,1536]{1,0:T(8,128)(2,1)} %get-tuple-element.51), channel_id=1, source_target_pairs={{0,1},{1,0},{2,3},{3,2},{4,5},{5,4},{6,7},{7,6},{8,9},{9,8},{10,11... | collective-permute-start | bytes 2359304 | tf_op jit(solution)/shard_map/ppermute | solution.py:37
  22.8 4.7 %collective-permute-start.2 = (bf16[256,1536]{1,0:T(8,128)(2,1)}, bf16[256,1536]{1,0:T(8,128)(2,1)}, u32[]{:S(2)}, u32[]{:S(2)}) collective-permute-start(bf16[256,1536]{1,0:T(8,128)(2,1)} %get-tuple-element.52), channel_id=1, source_target_pairs={{0,1},{1,0},{2,3},{3,2},{4,5},{5,4},{6,7},{7,6},{8,9},{9,8},{10,11... | collective-permute-start | bytes 2359304 | tf_op jit(solution)/shard_map/ppermute | solution.py:37
  23.0 0.7 copy-start.7
  25.8 26.4 %collective-permute-start.13 = (bf16[128,3584]{1,0:T(8,128)(2,1)S(1)}, bf16[128,3584]{1,0:T(8,128)(2,1)S(1)}, u32[]{:S(2)}, u32[]{:S(2)}) collective-permute-start(bf16[128,3584]{1,0:T(8,128)(2,1)S(1)} %get-tuple-element.57.refs_4_), channel_id=1, source_target_pairs={{0,8},{1,9},{2,10},{3,11},{4,12},{5,13},{6,14},{7,15},{8,0},{9,1},... | collective-permute-start | bytes 2752520 | tf_op jit(solution)/shard_map/ppermute | solution.py:37
  27.5 5.4 %copy-start = (bf16[512,512]{1,0:T(8,128)(2,1)S(1)}, bf16[512,512]{1,0:T(8,128)(2,1)}, u32[]{:S(2)}) copy-start(bf16[512,512]{1,0:T(8,128)(2,1)} %refs_0_.7) | copy-start | bytes 1572868
  27.5 5.4 %copy-start.1 = (bf16[512,1024]{1,0:T(8,128)(2,1)S(1)}, bf16[512,1024]{1,0:T(8,128)(2,1)}, u32[]{:S(2)}) copy-start(bf16[512,1024]{1,0:T(8,128)(2,1)} %refs_1_.6) | copy-start | bytes 3145732
  27.5 5.4 %copy-start.6 = (s32[512]{0:T(512)S(1)}, s32[512]{0:T(512)}, u32[]{:S(2)}) copy-start(s32[512]{0:T(512)} %param.15) | copy-start | bytes 6148
  27.6 5.4 %copy-start.8 = (s32[16]{0:T(128)S(1)}, s32[16]{0:T(128)}, u32[]{:S(2)}) copy-start(s32[16]{0:T(128)} %refs_1_.7) | copy-start | bytes 196
  30.2 16.0 %collective-permute-start.5 = (bf16[64,2304]{1,0:T(8,128)(2,1)S(1)}, bf16[64,2304]{1,0:T(8,128)(2,1)S(1)}, u32[]{:S(2)}, u32[]{:S(2)}) collective-permute-start(bf16[64,2304]{1,0:T(8,128)(2,1)S(1)} %get-tuple-element.61), channel_id=1, source_target_pairs={{0,2},{1,3},{2,4},{3,5},{4,6},{5,7},{6,0},{7,1},{8,10},{9,11},{10,... | collective-permute-start | bytes 884744 | tf_op jit(solution)/shard_map/ppermute | solution.py:37
  31.5 14.8 %collective-permute-start.6 = (bf16[64,2304]{1,0:T(8,128)(2,1)S(1)}, bf16[64,2304]{1,0:T(8,128)(2,1)S(1)}, u32[]{:S(2)}, u32[]{:S(2)}) collective-permute-start(bf16[64,2304]{1,0:T(8,128)(2,1)S(1)} %get-tuple-element.62), channel_id=1, source_target_pairs={{0,6},{1,7},{2,0},{3,1},{4,2},{5,3},{6,4},{7,5},{8,14},{9,15},{10,... | collective-permute-start | bytes 884744 | tf_op jit(solution)/shard_map/ppermute | solution.py:37
  33.0 17.8 %copy-start.2 = (bf16[1024,512]{1,0:T(8,128)(2,1)S(1)}, bf16[1024,512]{1,0:T(8,128)(2,1)}, u32[]{:S(2)}) copy-start(bf16[1024,512]{1,0:T(8,128)(2,1)} %refs_0_.8) | copy-start | bytes 3145732
  36.3 2.0 %collective-permute-start.7 = (bf16[256,128]{1,0:T(8,128)(2,1)S(1)}, bf16[256,128]{1,0:T(8,128)(2,1)S(1)}, u32[]{:S(2)}, u32[]{:S(2)}) collective-permute-start(bf16[256,128]{1,0:T(8,128)(2,1)S(1)} %get-tuple-element.64.refs_0_), channel_id=1, source_target_pairs={{0,1},{1,0},{2,3},{3,2},{4,5},{5,4},{6,7},{7,6},{8,9},{9,8},{10,11... | collective-permute-start | bytes 196616 | tf_op jit(solution)/shard_map/ppermute | solution.py:37
  38.3 3.5 %collective-permute-start.8 = (bf16[256,128]{1,0:T(8,128)(2,1)S(1)}, bf16[256,128]{1,0:T(8,128)(2,1)S(1)}, u32[]{:S(2)}, u32[]{:S(2)}) collective-permute-start(bf16[256,128]{1,0:T(8,128)(2,1)S(1)} %get-tuple-element.66.refs_0_), channel_id=1, source_target_pairs={{0,2},{1,3},{2,0},{3,1},{4,6},{5,7},{6,4},{7,5},{8,10},{9,11},{10,... | collective-permute-start | bytes 196616 | tf_op jit(solution)/shard_map/ppermute | solution.py:47
  41.8 4.4 %collective-permute-start.9 = (bf16[256,128]{1,0:T(8,128)(2,1)S(1)}, bf16[256,128]{1,0:T(8,128)(2,1)S(1)}, u32[]{:S(2)}, u32[]{:S(2)}) collective-permute-start(bf16[256,128]{1,0:T(8,128)(2,1)S(1)} %get-tuple-element.68.refs_0_), channel_id=1, source_target_pairs={{0,6},{1,7},{2,4},{3,5},{4,2},{5,3},{6,0},{7,1},{8,14},{9,15},{10,... | collective-permute-start | bytes 196616 | tf_op jit(solution)/shard_map/ppermute | solution.py:47
  47.2 20.6 %collective-permute-start.10 = (bf16[64,4608]{1,0:T(8,128)(2,1)}, bf16[64,4608]{1,0:T(8,128)(2,1)S(1)}, u32[]{:S(2)}, u32[]{:S(2)}) collective-permute-start(bf16[64,4608]{1,0:T(8,128)(2,1)} %get-tuple-element.71), channel_id=1, source_target_pairs={{0,2},{1,3},{2,4},{3,5},{4,6},{5,7},{6,0},{7,1},{8,10},{9,11},{10,... | collective-permute-start | bytes 1769480 | tf_op jit(solution)/shard_map/ppermute | solution.py:37
  47.2 20.6 %collective-permute-start.11 = (bf16[64,4608]{1,0:T(8,128)(2,1)S(1)}, bf16[64,4608]{1,0:T(8,128)(2,1)S(1)}, u32[]{:S(2)}, u32[]{:S(2)}) collective-permute-start(bf16[64,4608]{1,0:T(8,128)(2,1)S(1)} %get-tuple-element.72), channel_id=1, source_target_pairs={{0,6},{1,7},{2,0},{3,1},{4,2},{5,3},{6,4},{7,5},{8,14},{9,15},{10,... | collective-permute-start | bytes 1769480 | tf_op jit(solution)/shard_map/ppermute | solution.py:37
  49.8 4.6 %collective-permute-start.12 = (bf16[256,128]{1,0:T(8,128)(2,1)S(1)}, bf16[256,128]{1,0:T(8,128)(2,1)S(1)}, u32[]{:S(2)}, u32[]{:S(2)}) collective-permute-start(bf16[256,128]{1,0:T(8,128)(2,1)S(1)} %get-tuple-element.73.refs_0_), channel_id=1, source_target_pairs={{0,8},{1,9},{2,10},{3,11},{4,12},{5,13},{6,14},{7,15},{8,0},{9,1},... | collective-permute-start | bytes 196616 | tf_op jit(solution)/shard_map/ppermute | solution.py:37
  52.4 0.7 copy-start.4
  53.1 0.7 copy-start.10
  53.8 0.7 copy-start.11
  54.5 1.7 %copy-start.9 = (bf16[32,3584]{1,0:T(8,128)(2,1)}, bf16[32,3584]{1,0:T(8,128)(2,1)S(1)}, u32[]{:S(2)}) copy-start(bf16[32,3584]{1,0:T(8,128)(2,1)S(1)} %get-tuple-element.86) | copy-start | bytes 688132
  54.5 29.2 %copy-start.3 = (bf16[32,8192]{1,0:T(8,128)(2,1)S(1)}, bf16[32,8192]{1,0:T(8,128)(2,1)}, u32[]{:S(2)}) copy-start(bf16[32,8192]{1,0:T(8,128)(2,1)} %refs_0_.9) | copy-start | bytes 1572868
  56.2 27.5 %all-to-all-start.1 = ((bf16[16,32,512]{2,1,0:T(8,128)(2,1)}), bf16[16,32,512]{2,1,0:T(8,128)(2,1)S(1)}, u32[]{:S(2)}, u32[]{:S(2)}) async-start(bf16[16,32,512]{2,1,0:T(8,128)(2,1)} %get-tuple-element.89), calls=%async_computation.1 | async-start | bytes 1048576 | tf_op jit(solution)/shard_map/all_to_all | solution.py:451
  62.8 14.3 %collective-permute-start.16 = (bf16[32,3584]{1,0:T(8,128)(2,1)}, bf16[32,3584]{1,0:T(8,128)(2,1)S(1)}, u32[]{:S(2)}, u32[]{:S(2)}) collective-permute-start(bf16[32,3584]{1,0:T(8,128)(2,1)} %copy-done.11), channel_id=1, source_target_pairs={{0,2},{1,3},{2,4},{3,5},{4,6},{5,7},{6,0},{7,1},{8,10},{9,11},{10,... | collective-permute-start | bytes 688136 | tf_op jit(solution)/shard_map/ppermute | solution.py:37
  64.2 17.9 %collective-permute-start.17 = (bf16[32,3584]{1,0:T(8,128)(2,1)}, bf16[32,3584]{1,0:T(8,128)(2,1)S(1)}, u32[]{:S(2)}, u32[]{:S(2)}) collective-permute-start(bf16[32,3584]{1,0:T(8,128)(2,1)} %copy-done.10), channel_id=1, source_target_pairs={{0,4},{1,5},{2,6},{3,7},{4,0},{5,1},{6,2},{7,3},{8,12},{9,13},{10,... | collective-permute-start | bytes 688136 | tf_op jit(solution)/shard_map/ppermute | solution.py:37
  66.6 15.5 %collective-permute-start.18 = (bf16[32,3584]{1,0:T(8,128)(2,1)}, bf16[32,3584]{1,0:T(8,128)(2,1)S(1)}, u32[]{:S(2)}, u32[]{:S(2)}) collective-permute-start(bf16[32,3584]{1,0:T(8,128)(2,1)} %copy-done.9), channel_id=1, source_target_pairs={{0,6},{1,7},{2,0},{3,1},{4,2},{5,3},{6,4},{7,5},{8,14},{9,15},{10,... | collective-permute-start | bytes 688136 | tf_op jit(solution)/shard_map/ppermute | solution.py:37
  68.0 15.7 %collective-permute-start.14 = (bf16[32,2560]{1,0:T(8,128)(2,1)S(1)}, bf16[32,2560]{1,0:T(8,128)(2,1)S(1)}, u32[]{:S(2)}, u32[]{:S(2)}) collective-permute-start(bf16[32,2560]{1,0:T(8,128)(2,1)S(1)} %get-tuple-element.81), channel_id=1, source_target_pairs={{0,8},{1,9},{2,10},{3,11},{4,12},{5,13},{6,14},{7,15},{8,0},{9,1},... | collective-permute-start | bytes 491528 | tf_op jit(solution)/shard_map/ppermute | solution.py:37
  69.3 14.4 %collective-permute-start.15 = (bf16[32,2048]{1,0:T(8,128)(2,1)S(1)}, bf16[32,2048]{1,0:T(8,128)(2,1)S(1)}, u32[]{:S(2)}, u32[]{:S(2)}) collective-permute-start(bf16[32,2048]{1,0:T(8,128)(2,1)S(1)} %get-tuple-element.82), channel_id=1, source_target_pairs={{0,8},{1,9},{2,10},{3,11},{4,12},{5,13},{6,14},{7,15},{8,0},{9,1},... | collective-permute-start | bytes 393224 | tf_op jit(solution)/shard_map/ppermute | solution.py:37
  82.1 0.9 %copy-start.5 = (bf16[32,3584]{1,0:T(8,128)(2,1)S(1)}, bf16[32,3584]{1,0:T(8,128)(2,1)}, u32[]{:S(2)}) copy-start(bf16[32,3584]{1,0:T(8,128)(2,1)} %copy-done.4) | copy-start | bytes 688132

commit v6 on v5

--- a/solution.py
+++ b/solution.py
@@ -311,16 +311,18 @@
     kept = resident_slot(slot, target_ref)
     high = (lanes(512) >= RANK).astype(jnp.int32)
     acc = jnp.zeros((512, 128), F32)
-    for k in range(CHIPS):
-        part = jnp.dot(x, down_ref[:, k * 128 : (k + 1) * 128], preferred_element_type=F32)
-        acc += jnp.where(kept == 2 * k + high, part, 0.0)
-        maps = maps_ref[2 * k]
-        part = jnp.where(
-            high == 0,
-            jnp.dot(even, maps, preferred_element_type=F32),
-            jnp.dot(odd, maps, preferred_element_type=F32),
+    for k in range(0, CHIPS, 2):
+        resident = jnp.dot(
+            x, down_ref[:, k * 128 : (k + 2) * 128], preferred_element_type=F32
         )
-        acc += jnp.where(slot == target_ref[k], part, 0.0)
+        maps = jnp.concatenate([maps_ref[2 * k], maps_ref[2 * k + 2]], axis=1)
+        of_even = jnp.dot(even, maps, preferred_element_type=F32)
+        of_odd = jnp.dot(odd, maps, preferred_element_type=F32)
+        for i in range(2):
+            cols = slice(i * 128, (i + 1) * 128)
+            acc += jnp.where(kept == 2 * (k + i) + high, resident[:, cols], 0.0)
+            part = jnp.where(high == 0, of_even[:, cols], of_odd[:, cols])
+            acc += jnp.where(slot == target_ref[k + i], part, 0.0)
     acc = acc + pltpu.roll(acc, RANK, 1)
     out_ref[...] = jnp.where(lanes(256) < RANK, acc[:256], acc[256:]).astype(BF16)
 
@@ -425,7 +427,7 @@
     wide_in = [send(away, 0, 0, 1) for away in wide_away]
 
     keep, away, mark = chip_sum(
-        "chip_narrow", narrow_own, narrow_in, 2, None, [mark, maps]
+        "chip_narrow", narrow_own, narrow_in, 2, None, [maps]
     )
     narrow_y = send(away, 1, 0, 0)
     here, right, far_right, far_left, left, mark = chip_sum(

time: 85.1 us -> 84.6 us (level)
  Pallas kernels: 28.9 us -> 28 us
    pallas_call x15, Pallas kernels: 28.9 us -> 28 us  [call(): pl.pallas_call(body, in_specs=list(specs or [VM] * count) + [LATER] * len...]
    unnamed x24 -> x22, local copies, waits for them, and re-layouts: 3.73 us -> 3.08 us
  transfers between devices with their start and end apart: 21 -> 21, of which waited for: 5 -> 6; matrix products, arithmetic and copies ran while one was open for 0% -> 0% of each run, Pallas kernels for 33% -> 32%
where the time goes in v6:
time: 84.6 us; the launch traced here: 84.2 us
  starting transfers between devices  32.3 us (38%)
  Pallas kernels  28 us (33%)
  waiting for transfers between devices  20.6 us (24%)
  local copies, waits for them, and re-layouts  3.08 us (4%)
    pallas_call x15, Pallas kernels, call(): pl.pallas_call(body, in_specs=list(specs or [VM] * count) + [LATER] * len...  28 us
    ppermute x17, starting transfers between devices, send(): return lax.ppermute(array, 'tp', route(yy, xx, cc))  17.4 us
    ppermute x17, waiting for transfers between devices, send(): return lax.ppermute(array, 'tp', route(yy, xx, cc))  13.9 us
    all_to_all x1, starting transfers between devices, local(): lax.all_to_all(fresh_adapter_bundle.reshape(16, 256, 128), 'tp', split_ax...  6.83 us
    ppermute x2, waiting for transfers between devices, trade(): return lax.ppermute(array, 'tp', pairs)  6.75 us
    all_to_all x1, starting transfers between devices, local(): lax.all_to_all(raised, 'tp', split_axis=0, concat_axis=0, tiled=True)  6.19 us
    unnamed x22, local copies, waits for them, and re-layouts  3.08 us
    ppermute x2, starting transfers between devices, trade(): return lax.ppermute(array, 'tp', pairs)  1.92 us
  transfers between devices with their start and end apart: 21, of which 6 were waited for; matrix products, arithmetic and copies ran while one was open for 0% of the time, Pallas kernels for 32%

profile of v6, /device:TPU:1, one launch (start us, length us, event | category | flops | bytes accessed | tf_op | source)
XLA Modules:
  0.0 84.2 jit_solution(17609476782065022977)
XLA Ops:
  0.0 6.8 %all-to-all-start = ((bf16[16,256,128]{2,1,0:T(8,128)(2,1)}), bf16[16,256,128]{2,1,0:T(8,128)(2,1)S(1)}, u32[]{:S(2)}, u32[]{:S(2)}) async-start(bf16[16,256,128]{2,1,0:T(8,128)(2,1)} %bitcast.4), calls=%async_computation | async-start | bytes 2097152 | tf_op jit(solution)/shard_map/all_to_all | solution.py:420
  6.8 6.7 %product.2 = (bf16[256,1792]{1,0:T(8,128)(2,1)}, bf16[256,1792]{1,0:T(8,128)(2,1)}, bf16[256,3584]{1,0:T(8,128)(2,1)}, f32[8,128]{1,0:T(8,128)}) custom-call(bf16[512,512]{1,0:T(8,128)(2,1)} %refs_0_.7, bf16[512,8192]{1,0:T(8,128)(2,1)} %refs_1_.5), custom_call_target="tpu_custom_call" | custom-call | flops 1024 | bytes 1024 | tf_op jit(solution)/shard_map/product/pallas_call | solution.py:88
  13.6 0.2 collective-permute-start.3
  13.8 0.4 collective-permute-start.4
  14.2 8.1 %product.3 = (bf16[256,1536]{1,0:T(8,128)(2,1)}, bf16[256,1536]{1,0:T(8,128)(2,1)}, bf16[256,1536]{1,0:T(8,128)(2,1)}, bf16[256,4608]{1,0:T(8,128)(2,1)}, f32[8,128]{1,0:T(8,128)}) custom-call(bf16[512,512]{1,0:T(8,128)(2,1)} %refs_0_.7, bf16[512,8192]{1,0:T(8,128)(2,1)} %refs_1_.5, f32[8,128]{1,0:T(8,128)} %get-tuple-element.47.refs_2_), custom_call_target="tpu_custom_call" | custom-call | flops 1024 | bytes 1024 | tf_op jit(solution)/shard_map/product/pallas_call | solution.py:88
  22.3 0.2 collective-permute-start
  22.5 0.4 collective-permute-start.1
  22.9 0.1 collective-permute-start.2
  23.0 0.0 collective-permute-done.3.refs_1_
  23.0 0.0 collective-permute-done.4.refs_2_
  23.0 0.0 all-to-all-done.refs_3_.refs_4_.refs_2_
  23.0 2.1 %chip_narrow.1 = (bf16[128,3584]{1,0:T(8,128)(2,1)S(1)}, bf16[128,3584]{1,0:T(8,128)(2,1)S(1)}, f32[8,128]{1,0:T(8,128)}) custom-call(bf16[256,3584]{1,0:T(8,128)(2,1)} %get-tuple-element.52.refs_0_, bf16[256,1792]{1,0:T(8,128)(2,1)S(1)} %collective-permute-done.3.refs_1_, bf16[256,1792]{1,0:T(8,128)(2,1)S(1)} %collective-permute-done.4.refs_2_, ...), custom_call_target="tpu_custom_call" | custom-call | flops 1024 | bytes 1024 | tf_op jit(solution)/shard_map/chip_narrow/pallas_call | solution.py:88
  25.2 1.7 %collective-permute-start.13 = (bf16[128,3584]{1,0:T(8,128)(2,1)S(1)}, bf16[128,3584]{1,0:T(8,128)(2,1)S(1)}, u32[]{:S(2)}, u32[]{:S(2)}) collective-permute-start(bf16[128,3584]{1,0:T(8,128)(2,1)S(1)} %get-tuple-element.55.refs_4_), channel_id=1, source_target_pairs={{0,8},{1,9},{2,10},{3,11},{4,12},{5,13},{6,14},{7,15},{8,0},{9,1},... | collective-permute-start | bytes 2752520 | tf_op jit(solution)/shard_map/ppermute | solution.py:37
  26.9 0.0 collective-permute-done.refs_1_
  26.9 0.0 collective-permute-done.1.refs_2_
  26.9 0.4 collective-permute-done.2.refs_3_
  27.3 2.6 %chip_wide.1 = (bf16[64,4608]{1,0:T(8,128)(2,1)S(1)}, bf16[64,4608]{1,0:T(8,128)(2,1)S(1)}, bf16[64,2304]{1,0:T(8,128)(2,1)S(1)}, bf16[64,2304]{1,0:T(8,128)(2,1...) custom-call(bf16[256,4608]{1,0:T(8,128)(2,1)} %get-tuple-element.48.refs_0_, ...), custom_call_target="tpu_custom_call" | custom-call | flops 1024 | bytes 1024 | tf_op jit(solution)/shard_map/chip_wide/pallas_call | solution.py:88
  29.9 1.5 %collective-permute-start.5 = (bf16[64,2304]{1,0:T(8,128)(2,1)S(1)}, bf16[64,2304]{1,0:T(8,128)(2,1)S(1)}, u32[]{:S(2)}, u32[]{:S(2)}) collective-permute-start(bf16[64,2304]{1,0:T(8,128)(2,1)S(1)} %get-tuple-element.59), channel_id=1, source_target_pairs={{0,2},{1,3},{2,4},{3,5},{4,6},{5,7},{6,0},{7,1},{8,10},{9,11},{10,... | collective-permute-start | bytes 884744 | tf_op jit(solution)/shard_map/ppermute | solution.py:37
  31.4 1.5 %collective-permute-start.6 = (bf16[64,2304]{1,0:T(8,128)(2,1)S(1)}, bf16[64,2304]{1,0:T(8,128)(2,1)S(1)}, u32[]{:S(2)}, u32[]{:S(2)}) collective-permute-start(bf16[64,2304]{1,0:T(8,128)(2,1)S(1)} %get-tuple-element.60), channel_id=1, source_target_pairs={{0,6},{1,7},{2,0},{3,1},{4,2},{5,3},{6,4},{7,5},{8,14},{9,15},{10,... | collective-permute-start | bytes 884744 | tf_op jit(solution)/shard_map/ppermute | solution.py:37
  32.9 0.0 copy-done
  32.9 0.0 copy-done.1
  32.9 0.0 copy-done.6
  32.9 0.0 copy-done.7
  32.9 0.0 copy-start.2
  32.9 2.3 %shrink_part.1 = (bf16[256,128]{1,0:T(8,128)(2,1)S(1)}, f32[8,128]{1,0:T(8,128)S(1)}) custom-call(bf16[512,512]{1,0:T(8,128)(2,1)S(1)} %copy-done, bf16[512,1024]{1,0:T(8,128)(2,1)S(1)} %copy-done.1, s32[1,512]{1,0:T(1,128)S(1)} %bitcast.2, s32[16]{0:T(128)S(1)} %copy-done.7, bf16[16,256,128]{2,1,0:T(8,128)(2,1)S(1)} %all-to-all-done.refs_3_.refs_4_.refs_2_, ...), custom_call_target="tpu_custom_call" | custom-call | flops 1024 | bytes 1024 | tf_op jit(solution)/shard_map/shrink_part/pallas_call | solution.py:88
  35.2 0.7 collective-permute-start.7
  35.9 0.9 %collective-permute-done.7.refs_1_ = bf16[256,128]{1,0:T(8,128)(2,1)S(1)} collective-permute-done((bf16[256,128]{1,0:T(8,128)(2,1)S(1)}, bf16[256,128]{1,0:T(8,128)(2,1)S(1)}, u32[]{:S(2)}, u32[]{:S(2)}) %collective-permute-start.7) | collective-permute-done | bytes 65568 | tf_op jit(solution)/shard_map/ppermute | solution.py:37
  36.8 0.4 collective-permute-start.8
  37.2 3.9 %collective-permute-done.8.refs_1_ = bf16[256,128]{1,0:T(8,128)(2,1)S(1)} collective-permute-done((bf16[256,128]{1,0:T(8,128)(2,1)S(1)}, bf16[256,128]{1,0:T(8,128)(2,1)S(1)}, u32[]{:S(2)}, u32[]{:S(2)}) %collective-permute-start.8) | collective-permute-done | bytes 65568 | tf_op jit(solution)/shard_map/ppermute | solution.py:47
  41.1 1.6 %collective-permute-start.9 = (bf16[256,128]{1,0:T(8,128)(2,1)S(1)}, bf16[256,128]{1,0:T(8,128)(2,1)S(1)}, u32[]{:S(2)}, u32[]{:S(2)}) collective-permute-start(bf16[256,128]{1,0:T(8,128)(2,1)S(1)} %get-tuple-element.66.refs_0_), channel_id=1, source_target_pairs={{0,6},{1,7},{2,4},{3,5},{4,2},{5,3},{6,0},{7,1},{8,14},{9,15},{10,... | collective-permute-start | bytes 196616 | tf_op jit(solution)/shard_map/ppermute | solution.py:47
  42.7 2.8 %collective-permute-done.9.refs_1_ = bf16[256,128]{1,0:T(8,128)(2,1)S(1)} collective-permute-done((bf16[256,128]{1,0:T(8,128)(2,1)S(1)}, bf16[256,128]{1,0:T(8,128)(2,1)S(1)}, u32[]{:S(2)}, u32[]{:S(2)}) %collective-permute-start.9) | collective-permute-done | bytes 65568 | tf_op jit(solution)/shard_map/ppermute | solution.py:47
  45.5 0.0 collective-permute-done.5.refs_2_
  45.5 0.0 collective-permute-done.6.refs_3_
  45.6 0.9 %near.1 = (bf16[64,4608]{1,0:T(8,128)(2,1)}, bf16[64,4608]{1,0:T(8,128)(2,1)S(1)}, f32[8,128]{1,0:T(8,128)S(1)}) custom-call(bf16[64,4608]{1,0:T(8,128)(2,1)S(1)} %get-tuple-element.57.refs_0_, bf16[64,4608]{1,0:T(8,128)(2,1)S(1)} %get-tuple-element.58.refs_1_, bf16[64,2304]{1,0:T(8,128)(2,1)S(1)} %collective-permute-done.5.refs_2_, ...), custom_call_target="tpu_custom_call" | custom-call | flops 1024 | bytes 1024 | tf_op jit(solution)/shard_map/near/pallas_call | solution.py:88
  46.5 0.0 collective-permute-start.10
  46.5 2.7 %collective-permute-start.11 = (bf16[64,4608]{1,0:T(8,128)(2,1)S(1)}, bf16[64,4608]{1,0:T(8,128)(2,1)S(1)}, u32[]{:S(2)}, u32[]{:S(2)}) collective-permute-start(bf16[64,4608]{1,0:T(8,128)(2,1)S(1)} %get-tuple-element.70), channel_id=1, source_target_pairs={{0,6},{1,7},{2,0},{3,1},{4,2},{5,3},{6,4},{7,5},{8,14},{9,15},{10,... | collective-permute-start | bytes 1769480 | tf_op jit(solution)/shard_map/ppermute | solution.py:37
  49.1 1.5 %collective-permute-start.12 = (bf16[256,128]{1,0:T(8,128)(2,1)S(1)}, bf16[256,128]{1,0:T(8,128)(2,1)S(1)}, u32[]{:S(2)}, u32[]{:S(2)}) collective-permute-start(bf16[256,128]{1,0:T(8,128)(2,1)S(1)} %get-tuple-element.71.refs_0_), channel_id=1, source_target_pairs={{0,8},{1,9},{2,10},{3,11},{4,12},{5,13},{6,14},{7,15},{8,0},{9,1},... | collective-permute-start | bytes 196616 | tf_op jit(solution)/shard_map/ppermute | solution.py:37
  50.6 0.0 copy-done.2
  50.6 1.3 %up_table.1 = (bf16[1024,512]{1,0:T(8,128)(2,1)S(1)}, f32[8,128]{1,0:T(8,128)S(1)}) custom-call(bf16[1024,512]{1,0:T(8,128)(2,1)S(1)} %copy-done.2, s32[16]{0:T(128)S(1)} %copy-done.7, bf16[16,256,128]{2,1,0:T(8,128)(2,1)S(1)} %all-to-all-done.refs_3_.refs_4_.refs_2_, f32[8,128]{1,0:T(8,128)S(1)} %get-tuple-element.72.refs_3_), custom_call_target="tpu_custom_call" | custom-call | flops 1024 | bytes 1024 | tf_op jit(solution)/shard_map/up_table/pallas_call | solution.py:88
  52.0 0.0 collective-permute-done.13.refs_1_
  52.0 0.2 turn_narrow.1
  52.2 0.7 copy-done.4
  52.9 0.7 copy-done.9
  53.6 0.7 copy-done.10
  54.3 0.0 collective-permute-done.12.refs_1_
  54.3 1.7 %raise_features.1 = (bf16[16,32,512]{2,1,0:T(8,128)(2,1)}, f32[8,128]{1,0:T(8,128)S(1)}) custom-call(bf16[256,128]{1,0:T(8,128)(2,1)S(1)} %get-tuple-element.71.refs_0_, bf16[256,128]{1,0:T(8,128)(2,1)S(1)} %collective-permute-done.12.refs_1_, bf16[1024,512]{1,0:T(8,128)(2,1)S(1)} %get-tuple-element.73.refs_2_, s32[1,512]{1,0:T(1,128)S(1)} %bitcast.3, ...), custom_call_target="tpu_custom_call" | custom-call | flops 1024 | bytes 1024 | tf_op jit(solution)/shard_map/raise_features/pallas_call | solution.py:88
  56.1 6.2 %all-to-all-start.1 = ((bf16[16,32,512]{2,1,0:T(8,128)(2,1)}), bf16[16,32,512]{2,1,0:T(8,128)(2,1)S(1)}, u32[]{:S(2)}, u32[]{:S(2)}) async-start(bf16[16,32,512]{2,1,0:T(8,128)(2,1)} %get-tuple-element.87), calls=%async_computation.1 | async-start | bytes 1048576 | tf_op jit(solution)/shard_map/all_to_all | solution.py:453
  62.3 1.4 %collective-permute-start.16 = (bf16[32,3584]{1,0:T(8,128)(2,1)}, bf16[32,3584]{1,0:T(8,128)(2,1)S(1)}, u32[]{:S(2)}, u32[]{:S(2)}) collective-permute-start(bf16[32,3584]{1,0:T(8,128)(2,1)} %copy-done.10), channel_id=1, source_target_pairs={{0,2},{1,3},{2,4},{3,5},{4,6},{5,7},{6,0},{7,1},{8,10},{9,11},{10,... | collective-permute-start | bytes 688136 | tf_op jit(solution)/shard_map/ppermute | solution.py:37
  63.6 2.4 %collective-permute-start.17 = (bf16[32,3584]{1,0:T(8,128)(2,1)}, bf16[32,3584]{1,0:T(8,128)(2,1)S(1)}, u32[]{:S(2)}, u32[]{:S(2)}) collective-permute-start(bf16[32,3584]{1,0:T(8,128)(2,1)} %copy-done.9), channel_id=1, source_target_pairs={{0,4},{1,5},{2,6},{3,7},{4,0},{5,1},{6,2},{7,3},{8,12},{9,13},{10,... | collective-permute-start | bytes 688136 | tf_op jit(solution)/shard_map/ppermute | solution.py:37
  66.1 1.2 %collective-permute-start.18 = (bf16[32,3584]{1,0:T(8,128)(2,1)}, bf16[32,3584]{1,0:T(8,128)(2,1)S(1)}, u32[]{:S(2)}, u32[]{:S(2)}) collective-permute-start(bf16[32,3584]{1,0:T(8,128)(2,1)} %copy-done.8), channel_id=1, source_target_pairs={{0,6},{1,7},{2,0},{3,1},{4,2},{5,3},{6,4},{7,5},{8,14},{9,15},{10,... | collective-permute-start | bytes 688136 | tf_op jit(solution)/shard_map/ppermute | solution.py:37
  67.2 0.0 collective-permute-done.10.refs_1_
  67.2 0.0 collective-permute-done.11.refs_2_
  67.2 0.2 turn_wide.1
  67.4 1.3 %collective-permute-start.14 = (bf16[32,2560]{1,0:T(8,128)(2,1)S(1)}, bf16[32,2560]{1,0:T(8,128)(2,1)S(1)}, u32[]{:S(2)}, u32[]{:S(2)}) collective-permute-start(bf16[32,2560]{1,0:T(8,128)(2,1)S(1)} %get-tuple-element.79), channel_id=1, source_target_pairs={{0,8},{1,9},{2,10},{3,11},{4,12},{5,13},{6,14},{7,15},{8,0},{9,1},... | collective-permute-start | bytes 491528 | tf_op jit(solution)/shard_map/ppermute | solution.py:37
  68.8 0.2 collective-permute-start.15
  69.0 7.5 %collective-permute-done.16.refs_1_ = bf16[32,3584]{1,0:T(8,128)(2,1)S(1)} collective-permute-done((bf16[32,3584]{1,0:T(8,128)(2,1)}, bf16[32,3584]{1,0:T(8,128)(2,1)S(1)}, u32[]{:S(2)}, u32[]{:S(2)}) %collective-permute-start.16) | collective-permute-done | bytes 229408 | tf_op jit(solution)/shard_map/ppermute | solution.py:37
  76.5 5.0 %collective-permute-done.17.refs_2_ = bf16[32,3584]{1,0:T(8,128)(2,1)S(1)} collective-permute-done((bf16[32,3584]{1,0:T(8,128)(2,1)}, bf16[32,3584]{1,0:T(8,128)(2,1)S(1)}, u32[]{:S(2)}, u32[]{:S(2)}) %collective-permute-start.17) | collective-permute-done | bytes 229408 | tf_op jit(solution)/shard_map/ppermute | solution.py:37
  81.6 0.0 collective-permute-done.18.refs_3_
  81.6 0.9 %copy-done.5 = bf16[32,3584]{1,0:T(8,128)(2,1)S(1)} copy-done((bf16[32,3584]{1,0:T(8,128)(2,1)S(1)}, bf16[32,3584]{1,0:T(8,128)(2,1)}, u32[]{:S(2)}) %copy-start.5) | copy-done | bytes 229400
  82.5 0.6 add_parts.7
  83.2 0.0 collective-permute-done.15.refs_3_
  83.2 0.0 collective-permute-done.14.refs_2_
  83.2 0.0 all-to-all-done.1.refs_5_
  83.2 1.0 %finish.1 = (bf16[32,8192]{1,0:T(8,128)(2,1)}, f32[8,128]{1,0:T(8,128)}) custom-call(bf16[32,8192]{1,0:T(8,128)(2,1)S(1)} %copy-done.3, f32[32,4608]{1,0:T(8,128)S(1)} %get-tuple-element.78.refs_1_, bf16[32,2560]{1,0:T(8,128)(2,1)S(1)} %collective-permute-done.14.refs_2_, bf16[32,2048]{1,0:T(8,128)(2,1)S(1)} %collective-permute-done.15.refs_3_, ...), custom_call_target="tpu_custom_call" | custom-call | flops 1024 | bytes 1024 | tf_op jit(solution)/shard_map/finish/pallas_call | solution.py:88
  (15 shorter events, 0.1 us)
Async XLA Ops:
  0.0 23.0 %all-to-all-start = ((bf16[16,256,128]{2,1,0:T(8,128)(2,1)}), bf16[16,256,128]{2,1,0:T(8,128)(2,1)S(1)}, u32[]{:S(2)}, u32[]{:S(2)}) async-start(bf16[16,256,128]{2,1,0:T(8,128)(2,1)} %bitcast.4), calls=%async_computation | async-start | bytes 2097152 | tf_op jit(solution)/shard_map/all_to_all | solution.py:420
  13.6 9.4 %collective-permute-start.3 = (bf16[256,1792]{1,0:T(8,128)(2,1)}, bf16[256,1792]{1,0:T(8,128)(2,1)S(1)}, u32[]{:S(2)}, u32[]{:S(2)}) collective-permute-start(bf16[256,1792]{1,0:T(8,128)(2,1)} %get-tuple-element.53), channel_id=1, source_target_pairs={{0,1},{1,0},{2,3},{3,2},{4,5},{5,4},{6,7},{7,6},{8,9},{9,8},{10,11... | collective-permute-start | bytes 2752520 | tf_op jit(solution)/shard_map/ppermute | solution.py:37
  13.8 9.2 %collective-permute-start.4 = (bf16[256,1792]{1,0:T(8,128)(2,1)}, bf16[256,1792]{1,0:T(8,128)(2,1)S(1)}, u32[]{:S(2)}, u32[]{:S(2)}) collective-permute-start(bf16[256,1792]{1,0:T(8,128)(2,1)} %get-tuple-element.54), channel_id=1, source_target_pairs={{0,1},{1,0},{2,3},{3,2},{4,5},{5,4},{6,7},{7,6},{8,9},{9,8},{10,11... | collective-permute-start | bytes 2752520 | tf_op jit(solution)/shard_map/ppermute | solution.py:37
  22.3 4.6 %collective-permute-start = (bf16[256,1536]{1,0:T(8,128)(2,1)}, bf16[256,1536]{1,0:T(8,128)(2,1)}, u32[]{:S(2)}, u32[]{:S(2)}) collective-permute-start(bf16[256,1536]{1,0:T(8,128)(2,1)} %get-tuple-element.49), channel_id=1, source_target_pairs={{0,1},{1,0},{2,3},{3,2},{4,5},{5,4},{6,7},{7,6},{8,9},{9,8},{10,11... | collective-permute-start | bytes 2359304 | tf_op jit(solution)/shard_map/ppermute | solution.py:37
  22.5 4.4 %collective-permute-start.1 = (bf16[256,1536]{1,0:T(8,128)(2,1)}, bf16[256,1536]{1,0:T(8,128)(2,1)}, u32[]{:S(2)}, u32[]{:S(2)}) collective-permute-start(bf16[256,1536]{1,0:T(8,128)(2,1)} %get-tuple-element.50), channel_id=1, source_target_pairs={{0,1},{1,0},{2,3},{3,2},{4,5},{5,4},{6,7},{7,6},{8,9},{9,8},{10,11... | collective-permute-start | bytes 2359304 | tf_op jit(solution)/shard_map/ppermute | solution.py:37
  22.9 4.4 %collective-permute-start.2 = (bf16[256,1536]{1,0:T(8,128)(2,1)}, bf16[256,1536]{1,0:T(8,128)(2,1)}, u32[]{:S(2)}, u32[]{:S(2)}) collective-permute-start(bf16[256,1536]{1,0:T(8,128)(2,1)} %get-tuple-element.51), channel_id=1, source_target_pairs={{0,1},{1,0},{2,3},{3,2},{4,5},{5,4},{6,7},{7,6},{8,9},{9,8},{10,11... | collective-permute-start | bytes 2359304 | tf_op jit(solution)/shard_map/ppermute | solution.py:37
  25.2 26.8 %collective-permute-start.13 = (bf16[128,3584]{1,0:T(8,128)(2,1)S(1)}, bf16[128,3584]{1,0:T(8,128)(2,1)S(1)}, u32[]{:S(2)}, u32[]{:S(2)}) collective-permute-start(bf16[128,3584]{1,0:T(8,128)(2,1)S(1)} %get-tuple-element.55.refs_4_), channel_id=1, source_target_pairs={{0,8},{1,9},{2,10},{3,11},{4,12},{5,13},{6,14},{7,15},{8,0},{9,1},... | collective-permute-start | bytes 2752520 | tf_op jit(solution)/shard_map/ppermute | solution.py:37
  27.3 5.6 %copy-start = (bf16[512,512]{1,0:T(8,128)(2,1)S(1)}, bf16[512,512]{1,0:T(8,128)(2,1)}, u32[]{:S(2)}) copy-start(bf16[512,512]{1,0:T(8,128)(2,1)} %refs_0_.7) | copy-start | bytes 1572868
  27.3 5.6 %copy-start.1 = (bf16[512,1024]{1,0:T(8,128)(2,1)S(1)}, bf16[512,1024]{1,0:T(8,128)(2,1)}, u32[]{:S(2)}) copy-start(bf16[512,1024]{1,0:T(8,128)(2,1)} %refs_1_.6) | copy-start | bytes 3145732
  27.3 5.6 %copy-start.6 = (s32[512]{0:T(512)S(1)}, s32[512]{0:T(512)}, u32[]{:S(2)}) copy-start(s32[512]{0:T(512)} %param.15) | copy-start | bytes 6148
  27.3 5.6 %copy-start.7 = (s32[16]{0:T(128)S(1)}, s32[16]{0:T(128)}, u32[]{:S(2)}) copy-start(s32[16]{0:T(128)} %refs_1_.7) | copy-start | bytes 196
  29.9 15.6 %collective-permute-start.5 = (bf16[64,2304]{1,0:T(8,128)(2,1)S(1)}, bf16[64,2304]{1,0:T(8,128)(2,1)S(1)}, u32[]{:S(2)}, u32[]{:S(2)}) collective-permute-start(bf16[64,2304]{1,0:T(8,128)(2,1)S(1)} %get-tuple-element.59), channel_id=1, source_target_pairs={{0,2},{1,3},{2,4},{3,5},{4,6},{5,7},{6,0},{7,1},{8,10},{9,11},{10,... | collective-permute-start | bytes 884744 | tf_op jit(solution)/shard_map/ppermute | solution.py:37
  31.4 14.2 %collective-permute-start.6 = (bf16[64,2304]{1,0:T(8,128)(2,1)S(1)}, bf16[64,2304]{1,0:T(8,128)(2,1)S(1)}, u32[]{:S(2)}, u32[]{:S(2)}) collective-permute-start(bf16[64,2304]{1,0:T(8,128)(2,1)S(1)} %get-tuple-element.60), channel_id=1, source_target_pairs={{0,6},{1,7},{2,0},{3,1},{4,2},{5,3},{6,4},{7,5},{8,14},{9,15},{10,... | collective-permute-start | bytes 884744 | tf_op jit(solution)/shard_map/ppermute | solution.py:37
  32.9 17.7 %copy-start.2 = (bf16[1024,512]{1,0:T(8,128)(2,1)S(1)}, bf16[1024,512]{1,0:T(8,128)(2,1)}, u32[]{:S(2)}) copy-start(bf16[1024,512]{1,0:T(8,128)(2,1)} %refs_0_.8) | copy-start | bytes 3145732
  35.2 1.6 %collective-permute-start.7 = (bf16[256,128]{1,0:T(8,128)(2,1)S(1)}, bf16[256,128]{1,0:T(8,128)(2,1)S(1)}, u32[]{:S(2)}, u32[]{:S(2)}) collective-permute-start(bf16[256,128]{1,0:T(8,128)(2,1)S(1)} %get-tuple-element.62.refs_0_), channel_id=1, source_target_pairs={{0,1},{1,0},{2,3},{3,2},{4,5},{5,4},{6,7},{7,6},{8,9},{9,8},{10,11... | collective-permute-start | bytes 196616 | tf_op jit(solution)/shard_map/ppermute | solution.py:37
  36.8 4.3 %collective-permute-start.8 = (bf16[256,128]{1,0:T(8,128)(2,1)S(1)}, bf16[256,128]{1,0:T(8,128)(2,1)S(1)}, u32[]{:S(2)}, u32[]{:S(2)}) collective-permute-start(bf16[256,128]{1,0:T(8,128)(2,1)S(1)} %get-tuple-element.64.refs_0_), channel_id=1, source_target_pairs={{0,2},{1,3},{2,0},{3,1},{4,6},{5,7},{6,4},{7,5},{8,10},{9,11},{10,... | collective-permute-start | bytes 196616 | tf_op jit(solution)/shard_map/ppermute | solution.py:47
  41.1 4.4 %collective-permute-start.9 = (bf16[256,128]{1,0:T(8,128)(2,1)S(1)}, bf16[256,128]{1,0:T(8,128)(2,1)S(1)}, u32[]{:S(2)}, u32[]{:S(2)}) collective-permute-start(bf16[256,128]{1,0:T(8,128)(2,1)S(1)} %get-tuple-element.66.refs_0_), channel_id=1, source_target_pairs={{0,6},{1,7},{2,4},{3,5},{4,2},{5,3},{6,0},{7,1},{8,14},{9,15},{10,... | collective-permute-start | bytes 196616 | tf_op jit(solution)/shard_map/ppermute | solution.py:47
  46.5 20.8 %collective-permute-start.10 = (bf16[64,4608]{1,0:T(8,128)(2,1)}, bf16[64,4608]{1,0:T(8,128)(2,1)S(1)}, u32[]{:S(2)}, u32[]{:S(2)}) collective-permute-start(bf16[64,4608]{1,0:T(8,128)(2,1)} %get-tuple-element.69), channel_id=1, source_target_pairs={{0,2},{1,3},{2,4},{3,5},{4,6},{5,7},{6,0},{7,1},{8,10},{9,11},{10,... | collective-permute-start | bytes 1769480 | tf_op jit(solution)/shard_map/ppermute | solution.py:37
  46.5 20.8 %collective-permute-start.11 = (bf16[64,4608]{1,0:T(8,128)(2,1)S(1)}, bf16[64,4608]{1,0:T(8,128)(2,1)S(1)}, u32[]{:S(2)}, u32[]{:S(2)}) collective-permute-start(bf16[64,4608]{1,0:T(8,128)(2,1)S(1)} %get-tuple-element.70), channel_id=1, source_target_pairs={{0,6},{1,7},{2,0},{3,1},{4,2},{5,3},{6,4},{7,5},{8,14},{9,15},{10,... | collective-permute-start | bytes 1769480 | tf_op jit(solution)/shard_map/ppermute | solution.py:37
  49.1 5.2 %collective-permute-start.12 = (bf16[256,128]{1,0:T(8,128)(2,1)S(1)}, bf16[256,128]{1,0:T(8,128)(2,1)S(1)}, u32[]{:S(2)}, u32[]{:S(2)}) collective-permute-start(bf16[256,128]{1,0:T(8,128)(2,1)S(1)} %get-tuple-element.71.refs_0_), channel_id=1, source_target_pairs={{0,8},{1,9},{2,10},{3,11},{4,12},{5,13},{6,14},{7,15},{8,0},{9,1},... | collective-permute-start | bytes 196616 | tf_op jit(solution)/shard_map/ppermute | solution.py:37
  52.2 0.7 copy-start.4
  52.9 0.7 copy-start.9
  53.6 0.7 copy-start.10
  54.3 1.7 %copy-start.8 = (bf16[32,3584]{1,0:T(8,128)(2,1)}, bf16[32,3584]{1,0:T(8,128)(2,1)S(1)}, u32[]{:S(2)}) copy-start(bf16[32,3584]{1,0:T(8,128)(2,1)S(1)} %get-tuple-element.84) | copy-start | bytes 688132
  54.3 28.8 %copy-start.3 = (bf16[32,8192]{1,0:T(8,128)(2,1)S(1)}, bf16[32,8192]{1,0:T(8,128)(2,1)}, u32[]{:S(2)}) copy-start(bf16[32,8192]{1,0:T(8,128)(2,1)} %refs_0_.9) | copy-start | bytes 1572868
  56.1 27.1 %all-to-all-start.1 = ((bf16[16,32,512]{2,1,0:T(8,128)(2,1)}), bf16[16,32,512]{2,1,0:T(8,128)(2,1)S(1)}, u32[]{:S(2)}, u32[]{:S(2)}) async-start(bf16[16,32,512]{2,1,0:T(8,128)(2,1)} %get-tuple-element.87), calls=%async_computation.1 | async-start | bytes 1048576 | tf_op jit(solution)/shard_map/all_to_all | solution.py:453
  62.3 14.3 %collective-permute-start.16 = (bf16[32,3584]{1,0:T(8,128)(2,1)}, bf16[32,3584]{1,0:T(8,128)(2,1)S(1)}, u32[]{:S(2)}, u32[]{:S(2)}) collective-permute-start(bf16[32,3584]{1,0:T(8,128)(2,1)} %copy-done.10), channel_id=1, source_target_pairs={{0,2},{1,3},{2,4},{3,5},{4,6},{5,7},{6,0},{7,1},{8,10},{9,11},{10,... | collective-permute-start | bytes 688136 | tf_op jit(solution)/shard_map/ppermute | solution.py:37
  63.6 17.9 %collective-permute-start.17 = (bf16[32,3584]{1,0:T(8,128)(2,1)}, bf16[32,3584]{1,0:T(8,128)(2,1)S(1)}, u32[]{:S(2)}, u32[]{:S(2)}) collective-permute-start(bf16[32,3584]{1,0:T(8,128)(2,1)} %copy-done.9), channel_id=1, source_target_pairs={{0,4},{1,5},{2,6},{3,7},{4,0},{5,1},{6,2},{7,3},{8,12},{9,13},{10,... | collective-permute-start | bytes 688136 | tf_op jit(solution)/shard_map/ppermute | solution.py:37
  66.1 15.5 %collective-permute-start.18 = (bf16[32,3584]{1,0:T(8,128)(2,1)}, bf16[32,3584]{1,0:T(8,128)(2,1)S(1)}, u32[]{:S(2)}, u32[]{:S(2)}) collective-permute-start(bf16[32,3584]{1,0:T(8,128)(2,1)} %copy-done.8), channel_id=1, source_target_pairs={{0,6},{1,7},{2,0},{3,1},{4,2},{5,3},{6,4},{7,5},{8,14},{9,15},{10,... | collective-permute-start | bytes 688136 | tf_op jit(solution)/shard_map/ppermute | solution.py:37
  67.4 15.7 %collective-permute-start.14 = (bf16[32,2560]{1,0:T(8,128)(2,1)S(1)}, bf16[32,2560]{1,0:T(8,128)(2,1)S(1)}, u32[]{:S(2)}, u32[]{:S(2)}) collective-permute-start(bf16[32,2560]{1,0:T(8,128)(2,1)S(1)} %get-tuple-element.79), channel_id=1, source_target_pairs={{0,8},{1,9},{2,10},{3,11},{4,12},{5,13},{6,14},{7,15},{8,0},{9,1},... | collective-permute-start | bytes 491528 | tf_op jit(solution)/shard_map/ppermute | solution.py:37
  68.8 14.4 %collective-permute-start.15 = (bf16[32,2048]{1,0:T(8,128)(2,1)S(1)}, bf16[32,2048]{1,0:T(8,128)(2,1)S(1)}, u32[]{:S(2)}, u32[]{:S(2)}) collective-permute-start(bf16[32,2048]{1,0:T(8,128)(2,1)S(1)} %get-tuple-element.80), channel_id=1, source_target_pairs={{0,8},{1,9},{2,10},{3,11},{4,12},{5,13},{6,14},{7,15},{8,0},{9,1},... | collective-permute-start | bytes 393224 | tf_op jit(solution)/shard_map/ppermute | solution.py:37
  81.6 0.9 %copy-start.5 = (bf16[32,3584]{1,0:T(8,128)(2,1)S(1)}, bf16[32,3584]{1,0:T(8,128)(2,1)}, u32[]{:S(2)}) copy-start(bf16[32,3584]{1,0:T(8,128)(2,1)} %copy-done.4) | copy-start | bytes 688132

commit v7 on v6

--- a/solution.py
+++ b/solution.py
@@ -245,34 +245,53 @@
     )
 
 
+def near_rest(right, left, after=()):
+    half = right.shape[1] // 2
+
+    def kernel(right_ref, left_ref, to_right_ref, to_left_ref):
+        to_right_ref[...] = right_ref[:, half:]
+        to_left_ref[...] = left_ref[:, :half]
+
+    return call(
+        kernel, "near_rest", [whole((64, half), BF16)] * 2, (right, left), after=after
+    )
+
+
 def near(right, left, far_right, far_left, after=()):
     half = right.shape[1] // 2
 
     def kernel(right_ref, left_ref, far_right_ref, far_left_ref, to_right_ref, to_left_ref):
-        to_right_ref[:, :half] = plus(right_ref[:, :half], far_right_ref[...]).astype(BF16)
-        to_right_ref[:, half:] = right_ref[:, half:]
-        to_left_ref[:, :half] = left_ref[:, :half]
-        to_left_ref[:, half:] = plus(left_ref[:, half:], far_left_ref[...]).astype(BF16)
-
-    return call(
-        kernel, "near", [whole(right.shape, BF16)] * 2, (right, left, far_right, far_left), after=after
+        to_right_ref[...] = plus(right_ref[:, :half], far_right_ref[...]).astype(BF16)
+        to_left_ref[...] = plus(left_ref[:, half:], far_left_ref[...]).astype(BF16)
+
+    return call(
+        kernel,
+        "near",
+        [whole((64, half), BF16)] * 2,
+        (right, left, far_right, far_left),
+        after=after,
     )
 
 
 def turn_wide(here, from_left, from_right, after=()):
     width = here.shape[1]
-
-    def kernel(here_ref, from_left_ref, from_right_ref, keep_ref, send_ref, rest_ref):
-        total = plus(here_ref[...], from_left_ref[...], from_right_ref[...])
-        keep_ref[...] = total[:32]
-        send_ref[...] = total[32:, :CUT].astype(BF16)
-        rest_ref[...] = total[32:, CUT:].astype(BF16)
+    half = width // 2
+
+    def kernel(here_ref, *refs):
+        left_near, left_rest, right_near, right_rest, keep_ref, send_ref, rest_ref = refs
+        low = plus(here_ref[:, :half], left_near[...], right_rest[...])
+        high = plus(here_ref[:, half:], left_rest[...], right_near[...])
+        keep_ref[:, :half] = low[:32]
+        keep_ref[:, half:] = high[:32]
+        send_ref[:, :half] = low[32:].astype(BF16)
+        send_ref[:, half:] = high[32:, : CUT - half].astype(BF16)
+        rest_ref[...] = high[32:, CUT - half :].astype(BF16)
 
     return call(
         kernel,
         "turn_wide",
         [whole((32, width), F32), whole((32, CUT), BF16), whole((32, width - CUT), BF16)],
-        (here, from_left, from_right),
+        (here, *from_left, *from_right),
         after=after,
     )
 
@@ -439,20 +458,23 @@
     part_in = send(part, 0, 0, 1)
     part, mark = add_parts([part, part_in], [mark])
     part_in = trade(part, lambda x: x ^ 1)
+    near_right, near_left, mark = near(right, left, far_right, far_left, [mark])
     part, mark = add_parts([part, part_in], [mark])
     part_in = trade(part, lambda x: 3 - x)
+    rest_right, rest_left, mark = near_rest(right, left, [mark])
+    rest_right, rest_left = send(rest_right, 0, 1, 0), send(rest_left, 0, 3, 0)
     part, mark = add_parts([part, part_in], [mark])
     other = send(part, 1, 0, 0)
 
-    right, left, mark = near(right, left, far_right, far_left, [mark])
-    from_left, from_right = send(right, 0, 1, 0), send(left, 0, 3, 0)
+    near_right, near_left = send(near_right, 0, 1, 0), send(near_left, 0, 3, 0)
     table, mark = up_table(resident_up_maps, target, maps, [mark])
     *low, mark = turn_narrow(keep, narrow_y, [mark])
     low_in = [send(low[d], 0, d, 0) for d in (1, 2, 3)]
+    wide_keep, wide_send, wide_rest, mark = turn_wide(
+        here, (near_right, rest_right), (near_left, rest_left), [mark]
+    )
     raised, mark = raise_features(part, other, table, slot, [mark])
     delta = lax.all_to_all(raised, "tp", split_axis=0, concat_axis=0, tiled=True)
-
-    wide_keep, wide_send, wide_rest, mark = turn_wide(here, from_left, from_right, [mark])
     wide_y = send(wide_send, 1, 0, 0)
     rest_y = send(wide_rest, 1, 0, 0)
     narrow_sum, mark = add_parts([low[0], *low_in], [mark], F32)

time: 84.6 us -> 88.6 us (1.047)
  waiting for transfers between devices: 20.6 us -> 26.6 us
  local copies, waits for them, and re-layouts: 3.08 us -> 0.02 us
  starting transfers between devices: 32.3 us -> 33.7 us
    ppermute x17 -> x19, waiting for transfers between devices: 13.9 us -> 25.4 us  [send(): return lax.ppermute(array, 'tp', route(yy, xx, cc))]
    ppermute x2, waiting for transfers between devices: 6.75 us -> 1.26 us  [trade(): return lax.ppermute(array, 'tp', pairs)]
    unnamed x22 -> x12, local copies, waits for them, and re-layouts: 3.08 us -> 0.02 us
    ppermute x17 -> x19, starting transfers between devices: 17.4 us -> 18.9 us  [send(): return lax.ppermute(array, 'tp', route(yy, xx, cc))]
    pallas_call x15 -> x16, Pallas kernels: 28 us -> 27.7 us  [call(): pl.pallas_call(body, in_specs=list(specs or [VM] * count) + [LATER] * len...]
  transfers between devices with their start and end apart: 21 -> 23, of which waited for: 6 -> 10; matrix products, arithmetic and copies ran while one was open for 0% -> 0% of each run, Pallas kernels for 32% -> 28%
where the time goes in v7:
time: 88.6 us; the launch traced here: 88.2 us
  starting transfers between devices  33.7 us (38%)
  Pallas kernels  27.7 us (31%)
  waiting for transfers between devices  26.6 us (30%)
    pallas_call x16, Pallas kernels, call(): pl.pallas_call(body, in_specs=list(specs or [VM] * count) + [LATER] * len...  27.7 us
    ppermute x19, waiting for transfers between devices, send(): return lax.ppermute(array, 'tp', route(yy, xx, cc))  25.4 us
    ppermute x19, starting transfers between devices, send(): return lax.ppermute(array, 'tp', route(yy, xx, cc))  18.9 us
    all_to_all x1, starting transfers between devices, local(): lax.all_to_all(fresh_adapter_bundle.reshape(16, 256, 128), 'tp', split_ax...  6.83 us
    all_to_all x1, starting transfers between devices, local(): lax.all_to_all(raised, 'tp', split_axis=0, concat_axis=0, tiled=True)  6.06 us
    ppermute x2, starting transfers between devices, trade(): return lax.ppermute(array, 'tp', pairs)  1.92 us
  transfers between devices with their start and end apart: 23, of which 10 were waited for; matrix products, arithmetic and copies ran while one was open for 0% of the time, Pallas kernels for 28%

profile of v7, /device:TPU:1, one launch (start us, length us, event | category | flops | bytes accessed | tf_op | source)
XLA Modules:
  0.0 88.2 jit_solution(10315252022799760093)
XLA Ops:
  0.0 6.8 %all-to-all-start = ((bf16[16,256,128]{2,1,0:T(8,128)(2,1)}), bf16[16,256,128]{2,1,0:T(8,128)(2,1)S(1)}, u32[]{:S(2)}, u32[]{:S(2)}) async-start(bf16[16,256,128]{2,1,0:T(8,128)(2,1)} %bitcast.4), calls=%async_computation | async-start | bytes 2097152 | tf_op jit(solution)/shard_map/all_to_all | solution.py:439
  6.8 6.7 %product.2 = (bf16[256,1792]{1,0:T(8,128)(2,1)}, bf16[256,1792]{1,0:T(8,128)(2,1)}, bf16[256,3584]{1,0:T(8,128)(2,1)}, f32[8,128]{1,0:T(8,128)}) custom-call(bf16[512,512]{1,0:T(8,128)(2,1)} %refs_0_.7, bf16[512,8192]{1,0:T(8,128)(2,1)} %refs_1_.5), custom_call_target="tpu_custom_call" | custom-call | flops 1024 | bytes 1024 | tf_op jit(solution)/shard_map/product/pallas_call | solution.py:88
  13.6 0.2 collective-permute-start.3
  13.8 0.4 collective-permute-start.4
  14.2 8.0 %product.3 = (bf16[256,1536]{1,0:T(8,128)(2,1)}, bf16[256,1536]{1,0:T(8,128)(2,1)}, bf16[256,1536]{1,0:T(8,128)(2,1)}, bf16[256,4608]{1,0:T(8,128)(2,1)}, f32[8,128]{1,0:T(8,128)}) custom-call(bf16[512,512]{1,0:T(8,128)(2,1)} %refs_0_.7, bf16[512,8192]{1,0:T(8,128)(2,1)} %refs_1_.5, f32[8,128]{1,0:T(8,128)} %get-tuple-element.50.refs_2_), custom_call_target="tpu_custom_call" | custom-call | flops 1024 | bytes 1024 | tf_op jit(solution)/shard_map/product/pallas_call | solution.py:88
  22.2 0.2 collective-permute-start
  22.4 0.4 collective-permute-start.1
  22.8 0.1 collective-permute-start.2
  22.9 0.0 collective-permute-done.3.refs_1_
  22.9 0.0 collective-permute-done.4.refs_2_
  22.9 0.0 all-to-all-done.refs_3_.refs_4_.refs_2_
  22.9 2.1 %chip_narrow.1 = (bf16[128,3584]{1,0:T(8,128)(2,1)S(1)}, bf16[128,3584]{1,0:T(8,128)(2,1)S(1)}, f32[8,128]{1,0:T(8,128)}) custom-call(bf16[256,3584]{1,0:T(8,128)(2,1)} %get-tuple-element.55.refs_0_, bf16[256,1792]{1,0:T(8,128)(2,1)S(1)} %collective-permute-done.3.refs_1_, bf16[256,1792]{1,0:T(8,128)(2,1)S(1)} %collective-permute-done.4.refs_2_, ...), custom_call_target="tpu_custom_call" | custom-call | flops 1024 | bytes 1024 | tf_op jit(solution)/shard_map/chip_narrow/pallas_call | solution.py:88
  25.1 1.7 %collective-permute-start.13 = (bf16[128,3584]{1,0:T(8,128)(2,1)S(1)}, bf16[128,3584]{1,0:T(8,128)(2,1)S(1)}, u32[]{:S(2)}, u32[]{:S(2)}) collective-permute-start(bf16[128,3584]{1,0:T(8,128)(2,1)S(1)} %get-tuple-element.58.refs_4_), channel_id=1, source_target_pairs={{0,8},{1,9},{2,10},{3,11},{4,12},{5,13},{6,14},{7,15},{8,0},{9,1},... | collective-permute-start | bytes 2752520 | tf_op jit(solution)/shard_map/ppermute | solution.py:37
  26.8 0.0 collective-permute-done.refs_1_
  26.8 0.0 collective-permute-done.1.refs_2_
  26.8 0.4 collective-permute-done.2.refs_3_
  27.2 2.6 %chip_wide.1 = (bf16[64,4608]{1,0:T(8,128)(2,1)S(1)}, bf16[64,4608]{1,0:T(8,128)(2,1)S(1)}, bf16[64,2304]{1,0:T(8,128)(2,1)S(1)}, bf16[64,2304]{1,0:T(8,128)(2,1...) custom-call(bf16[256,4608]{1,0:T(8,128)(2,1)} %get-tuple-element.51.refs_0_, ...), custom_call_target="tpu_custom_call" | custom-call | flops 1024 | bytes 1024 | tf_op jit(solution)/shard_map/chip_wide/pallas_call | solution.py:88
  29.8 1.5 %collective-permute-start.5 = (bf16[64,2304]{1,0:T(8,128)(2,1)S(1)}, bf16[64,2304]{1,0:T(8,128)(2,1)S(1)}, u32[]{:S(2)}, u32[]{:S(2)}) collective-permute-start(bf16[64,2304]{1,0:T(8,128)(2,1)S(1)} %get-tuple-element.62), channel_id=1, source_target_pairs={{0,2},{1,3},{2,4},{3,5},{4,6},{5,7},{6,0},{7,1},{8,10},{9,11},{10,... | collective-permute-start | bytes 884744 | tf_op jit(solution)/shard_map/ppermute | solution.py:37
  31.3 1.5 %collective-permute-start.6 = (bf16[64,2304]{1,0:T(8,128)(2,1)S(1)}, bf16[64,2304]{1,0:T(8,128)(2,1)S(1)}, u32[]{:S(2)}, u32[]{:S(2)}) collective-permute-start(bf16[64,2304]{1,0:T(8,128)(2,1)S(1)} %get-tuple-element.63), channel_id=1, source_target_pairs={{0,6},{1,7},{2,0},{3,1},{4,2},{5,3},{6,4},{7,5},{8,14},{9,15},{10,... | collective-permute-start | bytes 884744 | tf_op jit(solution)/shard_map/ppermute | solution.py:37
  32.8 0.0 copy-done
  32.8 0.0 copy-done.1
  32.8 0.0 copy-done.4
  32.8 0.0 copy-done.5
  32.8 0.0 copy-start.2
  32.8 2.3 %shrink_part.1 = (bf16[256,128]{1,0:T(8,128)(2,1)S(1)}, f32[8,128]{1,0:T(8,128)S(1)}) custom-call(bf16[512,512]{1,0:T(8,128)(2,1)S(1)} %copy-done, bf16[512,1024]{1,0:T(8,128)(2,1)S(1)} %copy-done.1, s32[1,512]{1,0:T(1,128)S(1)} %bitcast.2, s32[16]{0:T(128)S(1)} %copy-done.5, bf16[16,256,128]{2,1,0:T(8,128)(2,1)S(1)} %all-to-all-done.refs_3_.refs_4_.refs_2_, ...), custom_call_target="tpu_custom_call" | custom-call | flops 1024 | bytes 1024 | tf_op jit(solution)/shard_map/shrink_part/pallas_call | solution.py:88
  35.1 0.7 collective-permute-start.7
  35.8 0.9 %collective-permute-done.7.refs_1_ = bf16[256,128]{1,0:T(8,128)(2,1)S(1)} collective-permute-done((bf16[256,128]{1,0:T(8,128)(2,1)S(1)}, bf16[256,128]{1,0:T(8,128)(2,1)S(1)}, u32[]{:S(2)}, u32[]{:S(2)}) %collective-permute-start.7) | collective-permute-done | bytes 65568 | tf_op jit(solution)/shard_map/ppermute | solution.py:37
  36.7 0.4 collective-permute-start.9
  37.1 2.5 %collective-permute-done.5.refs_2_ = bf16[64,2304]{1,0:T(8,128)(2,1)S(1)} collective-permute-done((bf16[64,2304]{1,0:T(8,128)(2,1)S(1)}, bf16[64,2304]{1,0:T(8,128)(2,1)S(1)}, u32[]{:S(2)}, u32[]{:S(2)}) %collective-permute-start.5) | collective-permute-done | bytes 294944 | tf_op jit(solution)/shard_map/ppermute | solution.py:37
  39.6 0.0 collective-permute-done.6.refs_3_
  39.6 0.1 near.1
  39.7 1.2 %collective-permute-done.9.refs_1_ = bf16[256,128]{1,0:T(8,128)(2,1)S(1)} collective-permute-done((bf16[256,128]{1,0:T(8,128)(2,1)S(1)}, bf16[256,128]{1,0:T(8,128)(2,1)S(1)}, u32[]{:S(2)}, u32[]{:S(2)}) %collective-permute-start.9) | collective-permute-done | bytes 65568 | tf_op jit(solution)/shard_map/ppermute | solution.py:47
  41.0 1.6 %collective-permute-start.14 = (bf16[256,128]{1,0:T(8,128)(2,1)S(1)}, bf16[256,128]{1,0:T(8,128)(2,1)S(1)}, u32[]{:S(2)}, u32[]{:S(2)}) collective-permute-start(bf16[256,128]{1,0:T(8,128)(2,1)S(1)} %get-tuple-element.76.refs_0_), channel_id=1, source_target_pairs={{0,6},{1,7},{2,4},{3,5},{4,2},{5,3},{6,0},{7,1},{8,14},{9,15},{10,... | collective-permute-start | bytes 196616 | tf_op jit(solution)/shard_map/ppermute | solution.py:47
  42.6 0.3 collective-permute-start.10
  42.9 2.5 %collective-permute-start.12 = (bf16[64,2304]{1,0:T(8,128)(2,1)S(1)}, bf16[64,2304]{1,0:T(8,128)(2,1)S(1)}, u32[]{:S(2)}, u32[]{:S(2)}) collective-permute-start(bf16[64,2304]{1,0:T(8,128)(2,1)S(1)} %get-tuple-element.74), channel_id=1, source_target_pairs={{0,6},{1,7},{2,0},{3,1},{4,2},{5,3},{6,4},{7,5},{8,14},{9,15},{10,... | collective-permute-start | bytes 884744 | tf_op jit(solution)/shard_map/ppermute | solution.py:37
  45.4 0.0 collective-permute-start.11
  45.4 0.0 collective-permute-done.14.refs_1_
  45.4 1.4 %collective-permute-start.8 = (bf16[64,2304]{1,0:T(8,128)(2,1)S(1)}, bf16[64,2304]{1,0:T(8,128)(2,1)S(1)}, u32[]{:S(2)}, u32[]{:S(2)}) collective-permute-start(bf16[64,2304]{1,0:T(8,128)(2,1)S(1)} %get-tuple-element.68), channel_id=1, source_target_pairs={{0,2},{1,3},{2,4},{3,5},{4,6},{5,7},{6,0},{7,1},{8,10},{9,11},{10,... | collective-permute-start | bytes 884744 | tf_op jit(solution)/shard_map/ppermute | solution.py:37
  46.8 0.1 collective-permute-done.13.refs_1_
  47.0 1.6 %collective-permute-start.20 = (bf16[256,128]{1,0:T(8,128)(2,1)S(1)}, bf16[256,128]{1,0:T(8,128)(2,1)S(1)}, u32[]{:S(2)}, u32[]{:S(2)}) collective-permute-start(bf16[256,128]{1,0:T(8,128)(2,1)S(1)} %get-tuple-element.88.refs_0_), channel_id=1, source_target_pairs={{0,8},{1,9},{2,10},{3,11},{4,12},{5,13},{6,14},{7,15},{8,0},{9,1},... | collective-permute-start | bytes 196616 | tf_op jit(solution)/shard_map/ppermute | solution.py:37
  48.6 0.0 copy-done.2
  48.6 1.4 %up_table.1 = (bf16[1024,512]{1,0:T(8,128)(2,1)S(1)}, f32[8,128]{1,0:T(8,128)S(1)}) custom-call(bf16[1024,512]{1,0:T(8,128)(2,1)S(1)} %copy-done.2, s32[16]{0:T(128)S(1)} %copy-done.5, bf16[16,256,128]{2,1,0:T(8,128)(2,1)S(1)} %all-to-all-done.refs_3_.refs_4_.refs_2_, f32[8,128]{1,0:T(8,128)S(1)} %get-tuple-element.78.refs_3_), custom_call_target="tpu_custom_call" | custom-call | flops 1024 | bytes 1024 | tf_op jit(solution)/shard_map/up_table/pallas_call | solution.py:88
  49.9 0.2 turn_narrow.1
  50.2 2.2 %collective-permute-done.10.refs_2_ = bf16[64,2304]{1,0:T(8,128)(2,1)S(1)} collective-permute-done((bf16[64,2304]{1,0:T(8,128)(2,1)S(1)}, bf16[64,2304]{1,0:T(8,128)(2,1)S(1)}, u32[]{:S(2)}, u32[]{:S(2)}) %collective-permute-start.10) | collective-permute-done | bytes 294944 | tf_op jit(solution)/shard_map/ppermute | solution.py:37
  52.4 0.0 collective-permute-done.12.refs_4_
  52.4 3.9 %collective-permute-done.11.refs_3_ = bf16[64,2304]{1,0:T(8,128)(2,1)S(1)} collective-permute-done((bf16[64,2304]{1,0:T(8,128)(2,1)S(1)}, bf16[64,2304]{1,0:T(8,128)(2,1)S(1)}, u32[]{:S(2)}, u32[]{:S(2)}) %collective-permute-start.11) | collective-permute-done | bytes 294944 | tf_op jit(solution)/shard_map/ppermute | solution.py:37
  56.3 2.4 %collective-permute-done.8.refs_1_ = bf16[64,2304]{1,0:T(8,128)(2,1)S(1)} collective-permute-done((bf16[64,2304]{1,0:T(8,128)(2,1)S(1)}, bf16[64,2304]{1,0:T(8,128)(2,1)S(1)}, u32[]{:S(2)}, u32[]{:S(2)}) %collective-permute-start.8) | collective-permute-done | bytes 294944 | tf_op jit(solution)/shard_map/ppermute | solution.py:37
  58.7 0.7 turn_wide.1
  59.4 0.0 collective-permute-done.20.refs_1_
  59.4 1.7 %raise_features.1 = (bf16[16,32,512]{2,1,0:T(8,128)(2,1)}, f32[8,128]{1,0:T(8,128)S(1)}) custom-call(bf16[256,128]{1,0:T(8,128)(2,1)S(1)} %get-tuple-element.88.refs_0_, bf16[256,128]{1,0:T(8,128)(2,1)S(1)} %collective-permute-done.20.refs_1_, bf16[1024,512]{1,0:T(8,128)(2,1)S(1)} %get-tuple-element.89.refs_2_, s32[1,512]{1,0:T(1,128)S(1)} %bitcast.3, ...), custom_call_target="tpu_custom_call" | custom-call | flops 1024 | bytes 1024 | tf_op jit(solution)/shard_map/raise_features/pallas_call | solution.py:88
  61.2 6.1 %all-to-all-start.1 = ((bf16[16,32,512]{2,1,0:T(8,128)(2,1)}), bf16[16,32,512]{2,1,0:T(8,128)(2,1)S(1)}, u32[]{:S(2)}, u32[]{:S(2)}) async-start(bf16[16,32,512]{2,1,0:T(8,128)(2,1)} %get-tuple-element.93), calls=%async_computation.1 | async-start | bytes 1048576 | tf_op jit(solution)/shard_map/all_to_all | solution.py:477
  67.2 1.4 %collective-permute-start.17 = (bf16[32,3584]{1,0:T(8,128)(2,1)S(1)}, bf16[32,3584]{1,0:T(8,128)(2,1)S(1)}, u32[]{:S(2)}, u32[]{:S(2)}) collective-permute-start(bf16[32,3584]{1,0:T(8,128)(2,1)S(1)} %get-tuple-element.85), channel_id=1, source_target_pairs={{0,2},{1,3},{2,4},{3,5},{4,6},{5,7},{6,0},{7,1},{8,10},{9,11},{10,... | collective-permute-start | bytes 688136 | tf_op jit(solution)/shard_map/ppermute | solution.py:37
  68.6 2.4 %collective-permute-start.18 = (bf16[32,3584]{1,0:T(8,128)(2,1)S(1)}, bf16[32,3584]{1,0:T(8,128)(2,1)S(1)}, u32[]{:S(2)}, u32[]{:S(2)}) collective-permute-start(bf16[32,3584]{1,0:T(8,128)(2,1)S(1)} %get-tuple-element.86), channel_id=1, source_target_pairs={{0,4},{1,5},{2,6},{3,7},{4,0},{5,1},{6,2},{7,3},{8,12},{9,13},{10,... | collective-permute-start | bytes 688136 | tf_op jit(solution)/shard_map/ppermute | solution.py:37
  71.0 1.2 %collective-permute-start.19 = (bf16[32,3584]{1,0:T(8,128)(2,1)S(1)}, bf16[32,3584]{1,0:T(8,128)(2,1)S(1)}, u32[]{:S(2)}, u32[]{:S(2)}) collective-permute-start(bf16[32,3584]{1,0:T(8,128)(2,1)S(1)} %get-tuple-element.87), channel_id=1, source_target_pairs={{0,6},{1,7},{2,0},{3,1},{4,2},{5,3},{6,4},{7,5},{8,14},{9,15},{10,... | collective-permute-start | bytes 688136 | tf_op jit(solution)/shard_map/ppermute | solution.py:37
  72.2 1.2 %collective-permute-start.15 = (bf16[32,2560]{1,0:T(8,128)(2,1)S(1)}, bf16[32,2560]{1,0:T(8,128)(2,1)S(1)}, u32[]{:S(2)}, u32[]{:S(2)}) collective-permute-start(bf16[32,2560]{1,0:T(8,128)(2,1)S(1)} %get-tuple-element.82), channel_id=1, source_target_pairs={{0,8},{1,9},{2,10},{3,11},{4,12},{5,13},{6,14},{7,15},{8,0},{9,1},... | collective-permute-start | bytes 491528 | tf_op jit(solution)/shard_map/ppermute | solution.py:37
  73.4 0.3 collective-permute-start.16
  73.6 7.8 %collective-permute-done.17.refs_1_ = bf16[32,3584]{1,0:T(8,128)(2,1)S(1)} collective-permute-done((bf16[32,3584]{1,0:T(8,128)(2,1)S(1)}, bf16[32,3584]{1,0:T(8,128)(2,1)S(1)}, u32[]{:S(2)}, u32[]{:S(2)}) %collective-permute-start.17) | collective-permute-done | bytes 229408 | tf_op jit(solution)/shard_map/ppermute | solution.py:37
  81.5 5.1 %collective-permute-done.18.refs_2_ = bf16[32,3584]{1,0:T(8,128)(2,1)S(1)} collective-permute-done((bf16[32,3584]{1,0:T(8,128)(2,1)S(1)}, bf16[32,3584]{1,0:T(8,128)(2,1)S(1)}, u32[]{:S(2)}, u32[]{:S(2)}) %collective-permute-start.18) | collective-permute-done | bytes 229408 | tf_op jit(solution)/shard_map/ppermute | solution.py:37
  86.5 0.0 collective-permute-done.19.refs_3_
  86.5 0.6 add_parts.7
  87.2 0.0 collective-permute-done.16.refs_3_
  87.2 0.0 collective-permute-done.15.refs_2_
  87.2 0.0 all-to-all-done.1.refs_5_
  87.2 1.0 %finish.1 = (bf16[32,8192]{1,0:T(8,128)(2,1)}, f32[8,128]{1,0:T(8,128)}) custom-call(bf16[32,8192]{1,0:T(8,128)(2,1)S(1)} %copy-done.3, f32[32,4608]{1,0:T(8,128)S(1)} %get-tuple-element.81.refs_1_, bf16[32,2560]{1,0:T(8,128)(2,1)S(1)} %collective-permute-done.15.refs_2_, bf16[32,2048]{1,0:T(8,128)(2,1)S(1)} %collective-permute-done.16.refs_3_, ...), custom_call_target="tpu_custom_call" | custom-call | flops 1024 | bytes 1024 | tf_op jit(solution)/shard_map/finish/pallas_call | solution.py:88
  (10 shorter events, 0.1 us)
Async XLA Ops:
  0.0 22.9 %all-to-all-start = ((bf16[16,256,128]{2,1,0:T(8,128)(2,1)}), bf16[16,256,128]{2,1,0:T(8,128)(2,1)S(1)}, u32[]{:S(2)}, u32[]{:S(2)}) async-start(bf16[16,256,128]{2,1,0:T(8,128)(2,1)} %bitcast.4), calls=%async_computation | async-start | bytes 2097152 | tf_op jit(solution)/shard_map/all_to_all | solution.py:439
  13.6 9.3 %collective-permute-start.3 = (bf16[256,1792]{1,0:T(8,128)(2,1)}, bf16[256,1792]{1,0:T(8,128)(2,1)S(1)}, u32[]{:S(2)}, u32[]{:S(2)}) collective-permute-start(bf16[256,1792]{1,0:T(8,128)(2,1)} %get-tuple-element.56), channel_id=1, source_target_pairs={{0,1},{1,0},{2,3},{3,2},{4,5},{5,4},{6,7},{7,6},{8,9},{9,8},{10,11... | collective-permute-start | bytes 2752520 | tf_op jit(solution)/shard_map/ppermute | solution.py:37
  13.8 9.2 %collective-permute-start.4 = (bf16[256,1792]{1,0:T(8,128)(2,1)}, bf16[256,1792]{1,0:T(8,128)(2,1)S(1)}, u32[]{:S(2)}, u32[]{:S(2)}) collective-permute-start(bf16[256,1792]{1,0:T(8,128)(2,1)} %get-tuple-element.57), channel_id=1, source_target_pairs={{0,1},{1,0},{2,3},{3,2},{4,5},{5,4},{6,7},{7,6},{8,9},{9,8},{10,11... | collective-permute-start | bytes 2752520 | tf_op jit(solution)/shard_map/ppermute | solution.py:37
  22.2 4.6 %collective-permute-start = (bf16[256,1536]{1,0:T(8,128)(2,1)}, bf16[256,1536]{1,0:T(8,128)(2,1)}, u32[]{:S(2)}, u32[]{:S(2)}) collective-permute-start(bf16[256,1536]{1,0:T(8,128)(2,1)} %get-tuple-element.52), channel_id=1, source_target_pairs={{0,1},{1,0},{2,3},{3,2},{4,5},{5,4},{6,7},{7,6},{8,9},{9,8},{10,11... | collective-permute-start | bytes 2359304 | tf_op jit(solution)/shard_map/ppermute | solution.py:37
  22.4 4.4 %collective-permute-start.1 = (bf16[256,1536]{1,0:T(8,128)(2,1)}, bf16[256,1536]{1,0:T(8,128)(2,1)}, u32[]{:S(2)}, u32[]{:S(2)}) collective-permute-start(bf16[256,1536]{1,0:T(8,128)(2,1)} %get-tuple-element.53), channel_id=1, source_target_pairs={{0,1},{1,0},{2,3},{3,2},{4,5},{5,4},{6,7},{7,6},{8,9},{9,8},{10,11... | collective-permute-start | bytes 2359304 | tf_op jit(solution)/shard_map/ppermute | solution.py:37
  22.8 4.4 %collective-permute-start.2 = (bf16[256,1536]{1,0:T(8,128)(2,1)}, bf16[256,1536]{1,0:T(8,128)(2,1)}, u32[]{:S(2)}, u32[]{:S(2)}) collective-permute-start(bf16[256,1536]{1,0:T(8,128)(2,1)} %get-tuple-element.54), channel_id=1, source_target_pairs={{0,1},{1,0},{2,3},{3,2},{4,5},{5,4},{6,7},{7,6},{8,9},{9,8},{10,11... | collective-permute-start | bytes 2359304 | tf_op jit(solution)/shard_map/ppermute | solution.py:37
  25.1 21.9 %collective-permute-start.13 = (bf16[128,3584]{1,0:T(8,128)(2,1)S(1)}, bf16[128,3584]{1,0:T(8,128)(2,1)S(1)}, u32[]{:S(2)}, u32[]{:S(2)}) collective-permute-start(bf16[128,3584]{1,0:T(8,128)(2,1)S(1)} %get-tuple-element.58.refs_4_), channel_id=1, source_target_pairs={{0,8},{1,9},{2,10},{3,11},{4,12},{5,13},{6,14},{7,15},{8,0},{9,1},... | collective-permute-start | bytes 2752520 | tf_op jit(solution)/shard_map/ppermute | solution.py:37
  27.2 5.6 %copy-start = (bf16[512,512]{1,0:T(8,128)(2,1)S(1)}, bf16[512,512]{1,0:T(8,128)(2,1)}, u32[]{:S(2)}) copy-start(bf16[512,512]{1,0:T(8,128)(2,1)} %refs_0_.7) | copy-start | bytes 1572868
  27.2 5.6 %copy-start.1 = (bf16[512,1024]{1,0:T(8,128)(2,1)S(1)}, bf16[512,1024]{1,0:T(8,128)(2,1)}, u32[]{:S(2)}) copy-start(bf16[512,1024]{1,0:T(8,128)(2,1)} %refs_1_.6) | copy-start | bytes 3145732
  27.2 5.6 %copy-start.4 = (s32[512]{0:T(512)S(1)}, s32[512]{0:T(512)}, u32[]{:S(2)}) copy-start(s32[512]{0:T(512)} %param.15) | copy-start | bytes 6148
  27.2 5.6 %copy-start.5 = (s32[16]{0:T(128)S(1)}, s32[16]{0:T(128)}, u32[]{:S(2)}) copy-start(s32[16]{0:T(128)} %refs_1_.7) | copy-start | bytes 196
  29.8 9.8 %collective-permute-start.5 = (bf16[64,2304]{1,0:T(8,128)(2,1)S(1)}, bf16[64,2304]{1,0:T(8,128)(2,1)S(1)}, u32[]{:S(2)}, u32[]{:S(2)}) collective-permute-start(bf16[64,2304]{1,0:T(8,128)(2,1)S(1)} %get-tuple-element.62), channel_id=1, source_target_pairs={{0,2},{1,3},{2,4},{3,5},{4,6},{5,7},{6,0},{7,1},{8,10},{9,11},{10,... | collective-permute-start | bytes 884744 | tf_op jit(solution)/shard_map/ppermute | solution.py:37
  31.3 8.3 %collective-permute-start.6 = (bf16[64,2304]{1,0:T(8,128)(2,1)S(1)}, bf16[64,2304]{1,0:T(8,128)(2,1)S(1)}, u32[]{:S(2)}, u32[]{:S(2)}) collective-permute-start(bf16[64,2304]{1,0:T(8,128)(2,1)S(1)} %get-tuple-element.63), channel_id=1, source_target_pairs={{0,6},{1,7},{2,0},{3,1},{4,2},{5,3},{6,4},{7,5},{8,14},{9,15},{10,... | collective-permute-start | bytes 884744 | tf_op jit(solution)/shard_map/ppermute | solution.py:37
  32.8 15.8 %copy-start.2 = (bf16[1024,512]{1,0:T(8,128)(2,1)S(1)}, bf16[1024,512]{1,0:T(8,128)(2,1)}, u32[]{:S(2)}) copy-start(bf16[1024,512]{1,0:T(8,128)(2,1)} %refs_0_.8) | copy-start | bytes 3145732
  35.1 1.6 %collective-permute-start.7 = (bf16[256,128]{1,0:T(8,128)(2,1)S(1)}, bf16[256,128]{1,0:T(8,128)(2,1)S(1)}, u32[]{:S(2)}, u32[]{:S(2)}) collective-permute-start(bf16[256,128]{1,0:T(8,128)(2,1)S(1)} %get-tuple-element.65.refs_0_), channel_id=1, source_target_pairs={{0,1},{1,0},{2,3},{3,2},{4,5},{5,4},{6,7},{7,6},{8,9},{9,8},{10,11... | collective-permute-start | bytes 196616 | tf_op jit(solution)/shard_map/ppermute | solution.py:37
  36.7 4.3 %collective-permute-start.9 = (bf16[256,128]{1,0:T(8,128)(2,1)S(1)}, bf16[256,128]{1,0:T(8,128)(2,1)S(1)}, u32[]{:S(2)}, u32[]{:S(2)}) collective-permute-start(bf16[256,128]{1,0:T(8,128)(2,1)S(1)} %get-tuple-element.69.refs_0_), channel_id=1, source_target_pairs={{0,2},{1,3},{2,0},{3,1},{4,6},{5,7},{6,4},{7,5},{8,10},{9,11},{10,... | collective-permute-start | bytes 196616 | tf_op jit(solution)/shard_map/ppermute | solution.py:47
  41.0 4.4 %collective-permute-start.14 = (bf16[256,128]{1,0:T(8,128)(2,1)S(1)}, bf16[256,128]{1,0:T(8,128)(2,1)S(1)}, u32[]{:S(2)}, u32[]{:S(2)}) collective-permute-start(bf16[256,128]{1,0:T(8,128)(2,1)S(1)} %get-tuple-element.76.refs_0_), channel_id=1, source_target_pairs={{0,6},{1,7},{2,4},{3,5},{4,2},{5,3},{6,0},{7,1},{8,14},{9,15},{10,... | collective-permute-start | bytes 196616 | tf_op jit(solution)/shard_map/ppermute | solution.py:47
  42.6 9.8 %collective-permute-start.10 = (bf16[64,2304]{1,0:T(8,128)(2,1)S(1)}, bf16[64,2304]{1,0:T(8,128)(2,1)S(1)}, u32[]{:S(2)}, u32[]{:S(2)}) collective-permute-start(bf16[64,2304]{1,0:T(8,128)(2,1)S(1)} %get-tuple-element.72), channel_id=1, source_target_pairs={{0,2},{1,3},{2,4},{3,5},{4,6},{5,7},{6,0},{7,1},{8,10},{9,11},{10,... | collective-permute-start | bytes 884744 | tf_op jit(solution)/shard_map/ppermute | solution.py:37
  42.9 9.5 %collective-permute-start.12 = (bf16[64,2304]{1,0:T(8,128)(2,1)S(1)}, bf16[64,2304]{1,0:T(8,128)(2,1)S(1)}, u32[]{:S(2)}, u32[]{:S(2)}) collective-permute-start(bf16[64,2304]{1,0:T(8,128)(2,1)S(1)} %get-tuple-element.74), channel_id=1, source_target_pairs={{0,6},{1,7},{2,0},{3,1},{4,2},{5,3},{6,4},{7,5},{8,14},{9,15},{10,... | collective-permute-start | bytes 884744 | tf_op jit(solution)/shard_map/ppermute | solution.py:37
  45.4 11.0 %collective-permute-start.11 = (bf16[64,2304]{1,0:T(8,128)(2,1)S(1)}, bf16[64,2304]{1,0:T(8,128)(2,1)S(1)}, u32[]{:S(2)}, u32[]{:S(2)}) collective-permute-start(bf16[64,2304]{1,0:T(8,128)(2,1)S(1)} %get-tuple-element.73), channel_id=1, source_target_pairs={{0,6},{1,7},{2,0},{3,1},{4,2},{5,3},{6,4},{7,5},{8,14},{9,15},{10,... | collective-permute-start | bytes 884744 | tf_op jit(solution)/shard_map/ppermute | solution.py:37
  45.4 13.3 %collective-permute-start.8 = (bf16[64,2304]{1,0:T(8,128)(2,1)S(1)}, bf16[64,2304]{1,0:T(8,128)(2,1)S(1)}, u32[]{:S(2)}, u32[]{:S(2)}) collective-permute-start(bf16[64,2304]{1,0:T(8,128)(2,1)S(1)} %get-tuple-element.68), channel_id=1, source_target_pairs={{0,2},{1,3},{2,4},{3,5},{4,6},{5,7},{6,0},{7,1},{8,10},{9,11},{10,... | collective-permute-start | bytes 884744 | tf_op jit(solution)/shard_map/ppermute | solution.py:37
  47.0 12.5 %collective-permute-start.20 = (bf16[256,128]{1,0:T(8,128)(2,1)S(1)}, bf16[256,128]{1,0:T(8,128)(2,1)S(1)}, u32[]{:S(2)}, u32[]{:S(2)}) collective-permute-start(bf16[256,128]{1,0:T(8,128)(2,1)S(1)} %get-tuple-element.88.refs_0_), channel_id=1, source_target_pairs={{0,8},{1,9},{2,10},{3,11},{4,12},{5,13},{6,14},{7,15},{8,0},{9,1},... | collective-permute-start | bytes 196616 | tf_op jit(solution)/shard_map/ppermute | solution.py:37
  58.7 28.4 %copy-start.3 = (bf16[32,8192]{1,0:T(8,128)(2,1)S(1)}, bf16[32,8192]{1,0:T(8,128)(2,1)}, u32[]{:S(2)}) copy-start(bf16[32,8192]{1,0:T(8,128)(2,1)} %refs_0_.9) | copy-start | bytes 1572868
  61.2 26.0 %all-to-all-start.1 = ((bf16[16,32,512]{2,1,0:T(8,128)(2,1)}), bf16[16,32,512]{2,1,0:T(8,128)(2,1)S(1)}, u32[]{:S(2)}, u32[]{:S(2)}) async-start(bf16[16,32,512]{2,1,0:T(8,128)(2,1)} %get-tuple-element.93), calls=%async_computation.1 | async-start | bytes 1048576 | tf_op jit(solution)/shard_map/all_to_all | solution.py:477
  67.2 14.2 %collective-permute-start.17 = (bf16[32,3584]{1,0:T(8,128)(2,1)S(1)}, bf16[32,3584]{1,0:T(8,128)(2,1)S(1)}, u32[]{:S(2)}, u32[]{:S(2)}) collective-permute-start(bf16[32,3584]{1,0:T(8,128)(2,1)S(1)} %get-tuple-element.85), channel_id=1, source_target_pairs={{0,2},{1,3},{2,4},{3,5},{4,6},{5,7},{6,0},{7,1},{8,10},{9,11},{10,... | collective-permute-start | bytes 688136 | tf_op jit(solution)/shard_map/ppermute | solution.py:37
  68.6 17.9 %collective-permute-start.18 = (bf16[32,3584]{1,0:T(8,128)(2,1)S(1)}, bf16[32,3584]{1,0:T(8,128)(2,1)S(1)}, u32[]{:S(2)}, u32[]{:S(2)}) collective-permute-start(bf16[32,3584]{1,0:T(8,128)(2,1)S(1)} %get-tuple-element.86), channel_id=1, source_target_pairs={{0,4},{1,5},{2,6},{3,7},{4,0},{5,1},{6,2},{7,3},{8,12},{9,13},{10,... | collective-permute-start | bytes 688136 | tf_op jit(solution)/shard_map/ppermute | solution.py:37
  71.0 15.5 %collective-permute-start.19 = (bf16[32,3584]{1,0:T(8,128)(2,1)S(1)}, bf16[32,3584]{1,0:T(8,128)(2,1)S(1)}, u32[]{:S(2)}, u32[]{:S(2)}) collective-permute-start(bf16[32,3584]{1,0:T(8,128)(2,1)S(1)} %get-tuple-element.87), channel_id=1, source_target_pairs={{0,6},{1,7},{2,0},{3,1},{4,2},{5,3},{6,4},{7,5},{8,14},{9,15},{10,... | collective-permute-start | bytes 688136 | tf_op jit(solution)/shard_map/ppermute | solution.py:37
  72.2 15.0 %collective-permute-start.15 = (bf16[32,2560]{1,0:T(8,128)(2,1)S(1)}, bf16[32,2560]{1,0:T(8,128)(2,1)S(1)}, u32[]{:S(2)}, u32[]{:S(2)}) collective-permute-start(bf16[32,2560]{1,0:T(8,128)(2,1)S(1)} %get-tuple-element.82), channel_id=1, source_target_pairs={{0,8},{1,9},{2,10},{3,11},{4,12},{5,13},{6,14},{7,15},{8,0},{9,1},... | collective-permute-start | bytes 491528 | tf_op jit(solution)/shard_map/ppermute | solution.py:37
  73.4 13.8 %collective-permute-start.16 = (bf16[32,2048]{1,0:T(8,128)(2,1)}, bf16[32,2048]{1,0:T(8,128)(2,1)S(1)}, u32[]{:S(2)}, u32[]{:S(2)}) collective-permute-start(bf16[32,2048]{1,0:T(8,128)(2,1)} %get-tuple-element.83), channel_id=1, source_target_pairs={{0,8},{1,9},{2,10},{3,11},{4,12},{5,13},{6,14},{7,15},{8,0},{9,1},... | collective-permute-start | bytes 393224 | tf_op jit(solution)/shard_map/ppermute | solution.py:37

commit v8 on v7

--- a/solution.py
+++ b/solution.py
@@ -468,12 +468,12 @@
 
     near_right, near_left = send(near_right, 0, 1, 0), send(near_left, 0, 3, 0)
     table, mark = up_table(resident_up_maps, target, maps, [mark])
+    raised, mark = raise_features(part, other, table, slot, [mark])
     *low, mark = turn_narrow(keep, narrow_y, [mark])
     low_in = [send(low[d], 0, d, 0) for d in (1, 2, 3)]
     wide_keep, wide_send, wide_rest, mark = turn_wide(
         here, (near_right, rest_right), (near_left, rest_left), [mark]
     )
-    raised, mark = raise_features(part, other, table, slot, [mark])
     delta = lax.all_to_all(raised, "tp", split_axis=0, concat_axis=0, tiled=True)
     wide_y = send(wide_send, 1, 0, 0)
     rest_y = send(wide_rest, 1, 0, 0)

time: 88.6 us -> 87.7 us (0.990)
  waiting for transfers between devices: 26.6 us -> 23.3 us
  local copies, waits for them, and re-layouts: 0.02 us -> 2 us
  Pallas kernels: 27.7 us -> 29.4 us
  starting transfers between devices: 33.7 us -> 32.4 us
    ppermute x19, waiting for transfers between devices: 25.4 us -> 19.2 us  [send(): return lax.ppermute(array, 'tp', route(yy, xx, cc))]
    ppermute x2, waiting for transfers between devices: 1.26 us -> 4.02 us  [trade(): return lax.ppermute(array, 'tp', pairs)]
    unnamed x12 -> x20, local copies, waits for them, and re-layouts: 0.02 us -> 2 us
    pallas_call x16, Pallas kernels: 27.7 us -> 29.4 us  [call(): pl.pallas_call(body, in_specs=list(specs or [VM] * count) + [LATER] * len...]
    ppermute x19, starting transfers between devices: 18.9 us -> 18 us  [send(): return lax.ppermute(array, 'tp', route(yy, xx, cc))]
  transfers between devices with their start and end apart: 23 -> 23, of which waited for: 10 -> 8; matrix products, arithmetic and copies ran while one was open for 0% -> 0% of each run, Pallas kernels for 28% -> 33%
where the time goes in v8:
time: 87.7 us; the launch traced here: 87.3 us
  starting transfers between devices  32.4 us (37%)
  Pallas kernels  29.4 us (34%)
  waiting for transfers between devices  23.3 us (27%)
  local copies, waits for them, and re-layouts  2 us (2%)
    pallas_call x16, Pallas kernels, call(): pl.pallas_call(body, in_specs=list(specs or [VM] * count) + [LATER] * len...  29.4 us
    ppermute x19, waiting for transfers between devices, send(): return lax.ppermute(array, 'tp', route(yy, xx, cc))  19.2 us
    ppermute x19, starting transfers between devices, send(): return lax.ppermute(array, 'tp', route(yy, xx, cc))  18 us
    all_to_all x1, starting transfers between devices, local(): lax.all_to_all(fresh_adapter_bundle.reshape(16, 256, 128), 'tp', split_ax...  6.83 us
    all_to_all x1, starting transfers between devices, local(): lax.all_to_all(raised, 'tp', split_axis=0, concat_axis=0, tiled=True)  6.21 us
    ppermute x2, waiting for transfers between devices, trade(): return lax.ppermute(array, 'tp', pairs)  4.02 us
    unnamed x20, local copies, waits for them, and re-layouts  2 us
  transfers between devices with their start and end apart: 23, of which 8 were waited for; matrix products, arithmetic and copies ran while one was open for 0% of the time, Pallas kernels for 33%

profile of v8, /device:TPU:1, one launch (start us, length us, event | category | flops | bytes accessed | tf_op | source)
XLA Modules:
  0.0 87.3 jit_solution(13627745836533283952)
XLA Ops:
  0.0 6.8 %all-to-all-start = ((bf16[16,256,128]{2,1,0:T(8,128)(2,1)}), bf16[16,256,128]{2,1,0:T(8,128)(2,1)S(1)}, u32[]{:S(2)}, u32[]{:S(2)}) async-start(bf16[16,256,128]{2,1,0:T(8,128)(2,1)} %bitcast.4), calls=%async_computation | async-start | bytes 2097152 | tf_op jit(solution)/shard_map/all_to_all | solution.py:439
  6.8 6.7 %product.2 = (bf16[256,1792]{1,0:T(8,128)(2,1)}, bf16[256,1792]{1,0:T(8,128)(2,1)}, bf16[256,3584]{1,0:T(8,128)(2,1)}, f32[8,128]{1,0:T(8,128)}) custom-call(bf16[512,512]{1,0:T(8,128)(2,1)} %refs_0_.7, bf16[512,8192]{1,0:T(8,128)(2,1)} %refs_1_.5), custom_call_target="tpu_custom_call" | custom-call | flops 1024 | bytes 1024 | tf_op jit(solution)/shard_map/product/pallas_call | solution.py:88
  13.6 0.2 collective-permute-start.3
  13.8 0.4 collective-permute-start.4
  14.2 8.0 %product.3 = (bf16[256,1536]{1,0:T(8,128)(2,1)}, bf16[256,1536]{1,0:T(8,128)(2,1)}, bf16[256,1536]{1,0:T(8,128)(2,1)}, bf16[256,4608]{1,0:T(8,128)(2,1)}, f32[8,128]{1,0:T(8,128)}) custom-call(bf16[512,512]{1,0:T(8,128)(2,1)} %refs_0_.7, bf16[512,8192]{1,0:T(8,128)(2,1)} %refs_1_.5, f32[8,128]{1,0:T(8,128)} %get-tuple-element.50.refs_2_), custom_call_target="tpu_custom_call" | custom-call | flops 1024 | bytes 1024 | tf_op jit(solution)/shard_map/product/pallas_call | solution.py:88
  22.2 0.2 collective-permute-start
  22.4 0.4 collective-permute-start.1
  22.8 0.1 collective-permute-start.2
  22.9 0.0 collective-permute-done.3.refs_1_
  22.9 0.0 collective-permute-done.4.refs_2_
  22.9 0.0 all-to-all-done.refs_3_.refs_4_.refs_2_
  22.9 2.6 %chip_narrow.1 = (bf16[128,3584]{1,0:T(8,128)(2,1)S(1)}, bf16[128,3584]{1,0:T(8,128)(2,1)}, f32[8,128]{1,0:T(8,128)}) custom-call(bf16[256,3584]{1,0:T(8,128)(2,1)} %get-tuple-element.55.refs_0_, bf16[256,1792]{1,0:T(8,128)(2,1)S(1)} %collective-permute-done.3.refs_1_, bf16[256,1792]{1,0:T(8,128)(2,1)S(1)} %collective-permute-done.4.refs_2_, ...), custom_call_target="tpu_custom_call" | custom-call | flops 1024 | bytes 1024 | tf_op jit(solution)/shard_map/chip_narrow/pallas_call | solution.py:88
  25.5 0.9 %copy-done.3 = bf16[128,3584]{1,0:T(8,128)(2,1)} copy-done((bf16[128,3584]{1,0:T(8,128)(2,1)}, bf16[128,3584]{1,0:T(8,128)(2,1)S(1)}, u32[]{:S(2)}) %copy-start.3) | copy-done | bytes 917528
  26.4 1.6 %collective-permute-start.13 = (bf16[128,3584]{1,0:T(8,128)(2,1)}, bf16[128,3584]{1,0:T(8,128)(2,1)S(1)}, u32[]{:S(2)}, u32[]{:S(2)}) collective-permute-start(bf16[128,3584]{1,0:T(8,128)(2,1)} %get-tuple-element.58.refs_4_), channel_id=1, source_target_pairs={{0,8},{1,9},{2,10},{3,11},{4,12},{5,13},{6,14},{7,15},{8,0},{9,1},... | collective-permute-start | bytes 2752520 | tf_op jit(solution)/shard_map/ppermute | solution.py:37
  28.1 0.0 collective-permute-done.refs_1_
  28.1 0.0 collective-permute-done.1.refs_2_
  28.1 0.0 collective-permute-done.2.refs_3_
  28.1 0.0 copy-start
  28.1 0.0 copy-start.1
  28.1 0.0 copy-start.6
  28.1 0.0 copy-start.7
  28.1 2.6 %chip_wide.1 = (bf16[64,4608]{1,0:T(8,128)(2,1)S(1)}, bf16[64,4608]{1,0:T(8,128)(2,1)S(1)}, bf16[64,2304]{1,0:T(8,128)(2,1)S(1)}, bf16[64,2304]{1,0:T(8,128)(2,1...) custom-call(bf16[256,4608]{1,0:T(8,128)(2,1)} %get-tuple-element.51.refs_0_, ...), custom_call_target="tpu_custom_call" | custom-call | flops 1024 | bytes 1024 | tf_op jit(solution)/shard_map/chip_wide/pallas_call | solution.py:88
  30.8 1.3 %collective-permute-start.5 = (bf16[64,2304]{1,0:T(8,128)(2,1)S(1)}, bf16[64,2304]{1,0:T(8,128)(2,1)S(1)}, u32[]{:S(2)}, u32[]{:S(2)}) collective-permute-start(bf16[64,2304]{1,0:T(8,128)(2,1)S(1)} %get-tuple-element.62), channel_id=1, source_target_pairs={{0,2},{1,3},{2,4},{3,5},{4,6},{5,7},{6,0},{7,1},{8,10},{9,11},{10,... | collective-permute-start | bytes 884744 | tf_op jit(solution)/shard_map/ppermute | solution.py:37
  32.0 1.5 %collective-permute-start.6 = (bf16[64,2304]{1,0:T(8,128)(2,1)S(1)}, bf16[64,2304]{1,0:T(8,128)(2,1)S(1)}, u32[]{:S(2)}, u32[]{:S(2)}) collective-permute-start(bf16[64,2304]{1,0:T(8,128)(2,1)S(1)} %get-tuple-element.63), channel_id=1, source_target_pairs={{0,6},{1,7},{2,0},{3,1},{4,2},{5,3},{6,4},{7,5},{8,14},{9,15},{10,... | collective-permute-start | bytes 884744 | tf_op jit(solution)/shard_map/ppermute | solution.py:37
  33.5 0.0 copy-start.2
  33.5 2.3 %shrink_part.1 = (bf16[256,128]{1,0:T(8,128)(2,1)S(1)}, f32[8,128]{1,0:T(8,128)S(1)}) custom-call(bf16[512,512]{1,0:T(8,128)(2,1)S(1)} %copy-done, bf16[512,1024]{1,0:T(8,128)(2,1)S(1)} %copy-done.1, s32[1,512]{1,0:T(1,128)S(1)} %bitcast.2, s32[16]{0:T(128)S(1)} %copy-done.7, bf16[16,256,128]{2,1,0:T(8,128)(2,1)S(1)} %all-to-all-done.refs_3_.refs_4_.refs_2_, ...), custom_call_target="tpu_custom_call" | custom-call | flops 1024 | bytes 1024 | tf_op jit(solution)/shard_map/shrink_part/pallas_call | solution.py:88
  35.8 1.1 %collective-permute-start.7 = (bf16[256,128]{1,0:T(8,128)(2,1)S(1)}, bf16[256,128]{1,0:T(8,128)(2,1)S(1)}, u32[]{:S(2)}, u32[]{:S(2)}) collective-permute-start(bf16[256,128]{1,0:T(8,128)(2,1)S(1)} %get-tuple-element.65.refs_0_), channel_id=1, source_target_pairs={{0,1},{1,0},{2,3},{3,2},{4,5},{5,4},{6,7},{7,6},{8,9},{9,8},{10,11... | collective-permute-start | bytes 196616 | tf_op jit(solution)/shard_map/ppermute | solution.py:37
  36.9 0.9 %collective-permute-done.7.refs_1_ = bf16[256,128]{1,0:T(8,128)(2,1)S(1)} collective-permute-done((bf16[256,128]{1,0:T(8,128)(2,1)S(1)}, bf16[256,128]{1,0:T(8,128)(2,1)S(1)}, u32[]{:S(2)}, u32[]{:S(2)}) %collective-permute-start.7) | collective-permute-done | bytes 65568 | tf_op jit(solution)/shard_map/ppermute | solution.py:37
  37.8 0.1 collective-permute-start.9
  37.9 2.3 %collective-permute-done.5.refs_2_ = bf16[64,2304]{1,0:T(8,128)(2,1)S(1)} collective-permute-done((bf16[64,2304]{1,0:T(8,128)(2,1)S(1)}, bf16[64,2304]{1,0:T(8,128)(2,1)S(1)}, u32[]{:S(2)}, u32[]{:S(2)}) %collective-permute-start.5) | collective-permute-done | bytes 294944 | tf_op jit(solution)/shard_map/ppermute | solution.py:37
  40.2 0.0 collective-permute-done.6.refs_3_
  40.2 0.1 near.1
  40.4 1.7 %collective-permute-done.9.refs_1_ = bf16[256,128]{1,0:T(8,128)(2,1)S(1)} collective-permute-done((bf16[256,128]{1,0:T(8,128)(2,1)S(1)}, bf16[256,128]{1,0:T(8,128)(2,1)S(1)}, u32[]{:S(2)}, u32[]{:S(2)}) %collective-permute-start.9) | collective-permute-done | bytes 65568 | tf_op jit(solution)/shard_map/ppermute | solution.py:47
  42.1 1.3 %collective-permute-start.14 = (bf16[256,128]{1,0:T(8,128)(2,1)S(1)}, bf16[256,128]{1,0:T(8,128)(2,1)S(1)}, u32[]{:S(2)}, u32[]{:S(2)}) collective-permute-start(bf16[256,128]{1,0:T(8,128)(2,1)S(1)} %get-tuple-element.76.refs_0_), channel_id=1, source_target_pairs={{0,6},{1,7},{2,4},{3,5},{4,2},{5,3},{6,0},{7,1},{8,14},{9,15},{10,... | collective-permute-start | bytes 196616 | tf_op jit(solution)/shard_map/ppermute | solution.py:47
  43.4 0.9 near_rest.1
  44.3 2.3 %collective-permute-done.14.refs_1_ = bf16[256,128]{1,0:T(8,128)(2,1)S(1)} collective-permute-done((bf16[256,128]{1,0:T(8,128)(2,1)S(1)}, bf16[256,128]{1,0:T(8,128)(2,1)S(1)}, u32[]{:S(2)}, u32[]{:S(2)}) %collective-permute-start.14) | collective-permute-done | bytes 65568 | tf_op jit(solution)/shard_map/ppermute | solution.py:47
  46.5 0.4 collective-permute-start.15
  47.0 0.0 collective-permute-start.10
  47.0 2.7 %collective-permute-start.12 = (bf16[64,2304]{1,0:T(8,128)(2,1)}, bf16[64,2304]{1,0:T(8,128)(2,1)}, u32[]{:S(2)}, u32[]{:S(2)}) collective-permute-start(bf16[64,2304]{1,0:T(8,128)(2,1)} %get-tuple-element.74), channel_id=1, source_target_pairs={{0,6},{1,7},{2,0},{3,1},{4,2},{5,3},{6,4},{7,5},{8,14},{9,15},{10,... | collective-permute-start | bytes 884744 | tf_op jit(solution)/shard_map/ppermute | solution.py:37
  49.7 1.3 %up_table.1 = (bf16[1024,512]{1,0:T(8,128)(2,1)S(1)}, f32[8,128]{1,0:T(8,128)S(1)}) custom-call(bf16[1024,512]{1,0:T(8,128)(2,1)S(1)} %copy-done.2, s32[16]{0:T(128)S(1)} %copy-done.7, bf16[16,256,128]{2,1,0:T(8,128)(2,1)S(1)} %all-to-all-done.refs_3_.refs_4_.refs_2_, f32[8,128]{1,0:T(8,128)S(1)} %get-tuple-element.79.refs_3_), custom_call_target="tpu_custom_call" | custom-call | flops 1024 | bytes 1024 | tf_op jit(solution)/shard_map/up_table/pallas_call | solution.py:88
  51.0 0.0 collective-permute-done.15.refs_1_
  51.0 1.7 %raise_features.1 = (bf16[16,32,512]{2,1,0:T(8,128)(2,1)}, f32[8,128]{1,0:T(8,128)S(1)}) custom-call(bf16[256,128]{1,0:T(8,128)(2,1)S(1)} %get-tuple-element.78.refs_0_, bf16[256,128]{1,0:T(8,128)(2,1)S(1)} %collective-permute-done.15.refs_1_, bf16[1024,512]{1,0:T(8,128)(2,1)S(1)} %get-tuple-element.80.refs_2_, s32[1,512]{1,0:T(1,128)S(1)} %bitcast.3, ...), custom_call_target="tpu_custom_call" | custom-call | flops 1024 | bytes 1024 | tf_op jit(solution)/shard_map/raise_features/pallas_call | solution.py:88
  52.8 6.2 %all-to-all-start.1 = ((bf16[16,32,512]{2,1,0:T(8,128)(2,1)}), bf16[16,32,512]{2,1,0:T(8,128)(2,1)S(1)}, u32[]{:S(2)}, u32[]{:S(2)}) async-start(bf16[16,32,512]{2,1,0:T(8,128)(2,1)} %get-tuple-element.93), calls=%async_computation.1 | async-start | bytes 1048576 | tf_op jit(solution)/shard_map/all_to_all | solution.py:477
  59.0 2.6 %collective-permute-start.11 = (bf16[64,2304]{1,0:T(8,128)(2,1)}, bf16[64,2304]{1,0:T(8,128)(2,1)S(1)}, u32[]{:S(2)}, u32[]{:S(2)}) collective-permute-start(bf16[64,2304]{1,0:T(8,128)(2,1)} %copy-done.9), channel_id=1, source_target_pairs={{0,6},{1,7},{2,0},{3,1},{4,2},{5,3},{6,4},{7,5},{8,14},{9,15},{10,... | collective-permute-start | bytes 884744 | tf_op jit(solution)/shard_map/ppermute | solution.py:37
  61.6 0.0 collective-permute-start.8
  61.6 0.2 turn_narrow.1
  61.8 0.3 collective-permute-start.18
  62.1 3.6 %collective-permute-start.19 = (bf16[32,3584]{1,0:T(8,128)(2,1)S(1)}, bf16[32,3584]{1,0:T(8,128)(2,1)S(1)}, u32[]{:S(2)}, u32[]{:S(2)}) collective-permute-start(bf16[32,3584]{1,0:T(8,128)(2,1)S(1)} %get-tuple-element.89), channel_id=1, source_target_pairs={{0,4},{1,5},{2,6},{3,7},{4,0},{5,1},{6,2},{7,3},{8,12},{9,13},{10,... | collective-permute-start | bytes 688136 | tf_op jit(solution)/shard_map/ppermute | solution.py:37
  65.8 0.0 collective-permute-done.12.refs_4_
  65.8 7.5 %collective-permute-done.11.refs_3_ = bf16[64,2304]{1,0:T(8,128)(2,1)S(1)} collective-permute-done((bf16[64,2304]{1,0:T(8,128)(2,1)}, bf16[64,2304]{1,0:T(8,128)(2,1)S(1)}, u32[]{:S(2)}, u32[]{:S(2)}) %collective-permute-start.11) | collective-permute-done | bytes 294944 | tf_op jit(solution)/shard_map/ppermute | solution.py:37
  73.3 1.4 %collective-permute-done.8.refs_1_ = bf16[64,2304]{1,0:T(8,128)(2,1)S(1)} collective-permute-done((bf16[64,2304]{1,0:T(8,128)(2,1)}, bf16[64,2304]{1,0:T(8,128)(2,1)S(1)}, u32[]{:S(2)}, u32[]{:S(2)}) %collective-permute-start.8) | collective-permute-done | bytes 294944 | tf_op jit(solution)/shard_map/ppermute | solution.py:37
  74.7 1.3 %turn_wide.1 = (f32[32,4608]{1,0:T(8,128)S(1)}, bf16[32,2560]{1,0:T(8,128)(2,1)S(1)}, bf16[32,2048]{1,0:T(8,128)(2,1)S(1)}, f32[8,128]{1,0:T(8,128)S(1)}) custom-call(bf16[64,4608]{1,0:T(8,128)(2,1)S(1)} %get-tuple-element.59.refs_0_, bf16[64,2304]{1,0:T(8,128)(2,1)S(1)} %collective-permute-done.8.refs_1_, bf16[64,2304]{1,0:T(8,128)(2,1)} %collective-permute-done.10.refs_2_, ...), custom_call_target="tpu_custom_call" | custom-call | flops 1024 | bytes 1024 | tf_op jit(solution)/shard_map/turn_wide/pallas_call | solution.py:88
  75.9 1.3 %collective-permute-start.16 = (bf16[32,2560]{1,0:T(8,128)(2,1)S(1)}, bf16[32,2560]{1,0:T(8,128)(2,1)S(1)}, u32[]{:S(2)}, u32[]{:S(2)}) collective-permute-start(bf16[32,2560]{1,0:T(8,128)(2,1)S(1)} %get-tuple-element.85), channel_id=1, source_target_pairs={{0,8},{1,9},{2,10},{3,11},{4,12},{5,13},{6,14},{7,15},{8,0},{9,1},... | collective-permute-start | bytes 491528 | tf_op jit(solution)/shard_map/ppermute | solution.py:37
  77.3 0.2 collective-permute-start.17
  77.5 2.1 %collective-permute-done.18.refs_1_ = bf16[32,3584]{1,0:T(8,128)(2,1)S(1)} collective-permute-done((bf16[32,3584]{1,0:T(8,128)(2,1)S(1)}, bf16[32,3584]{1,0:T(8,128)(2,1)S(1)}, u32[]{:S(2)}, u32[]{:S(2)}) %collective-permute-start.18) | collective-permute-done | bytes 229408 | tf_op jit(solution)/shard_map/ppermute | solution.py:37
  79.6 5.0 %collective-permute-done.19.refs_2_ = bf16[32,3584]{1,0:T(8,128)(2,1)S(1)} collective-permute-done((bf16[32,3584]{1,0:T(8,128)(2,1)S(1)}, bf16[32,3584]{1,0:T(8,128)(2,1)S(1)}, u32[]{:S(2)}, u32[]{:S(2)}) %collective-permute-start.19) | collective-permute-done | bytes 229408 | tf_op jit(solution)/shard_map/ppermute | solution.py:37
  84.6 0.0 collective-permute-done.20.refs_3_
  84.6 0.6 add_parts.7
  85.2 0.0 all-to-all-done.1.refs_5_
  85.3 0.0 collective-permute-done.17.refs_3_
  85.3 0.0 collective-permute-done.16.refs_2_
  85.3 0.0 copy-start.5
  85.3 1.0 %copy-done.5 = bf16[32,8192]{1,0:T(8,128)(2,1)S(1)} copy-done((bf16[32,8192]{1,0:T(8,128)(2,1)S(1)}, bf16[32,8192]{1,0:T(8,128)(2,1)}, u32[]{:S(2)}) %copy-start.5) | copy-done | bytes 524312
  86.3 1.0 %finish.1 = (bf16[32,8192]{1,0:T(8,128)(2,1)}, f32[8,128]{1,0:T(8,128)}) custom-call(bf16[32,8192]{1,0:T(8,128)(2,1)S(1)} %copy-done.5, f32[32,4608]{1,0:T(8,128)S(1)} %get-tuple-element.84.refs_1_, bf16[32,2560]{1,0:T(8,128)(2,1)S(1)} %collective-permute-done.16.refs_2_, bf16[32,2048]{1,0:T(8,128)(2,1)S(1)} %collective-permute-done.17.refs_3_, ...), custom_call_target="tpu_custom_call" | custom-call | flops 1024 | bytes 1024 | tf_op jit(solution)/shard_map/finish/pallas_call | solution.py:88
  (18 shorter events, 0.1 us)
Async XLA Ops:
  0.0 22.9 %all-to-all-start = ((bf16[16,256,128]{2,1,0:T(8,128)(2,1)}), bf16[16,256,128]{2,1,0:T(8,128)(2,1)S(1)}, u32[]{:S(2)}, u32[]{:S(2)}) async-start(bf16[16,256,128]{2,1,0:T(8,128)(2,1)} %bitcast.4), calls=%async_computation | async-start | bytes 2097152 | tf_op jit(solution)/shard_map/all_to_all | solution.py:439
  13.6 9.3 %collective-permute-start.3 = (bf16[256,1792]{1,0:T(8,128)(2,1)}, bf16[256,1792]{1,0:T(8,128)(2,1)S(1)}, u32[]{:S(2)}, u32[]{:S(2)}) collective-permute-start(bf16[256,1792]{1,0:T(8,128)(2,1)} %get-tuple-element.56), channel_id=1, source_target_pairs={{0,1},{1,0},{2,3},{3,2},{4,5},{5,4},{6,7},{7,6},{8,9},{9,8},{10,11... | collective-permute-start | bytes 2752520 | tf_op jit(solution)/shard_map/ppermute | solution.py:37
  13.8 9.2 %collective-permute-start.4 = (bf16[256,1792]{1,0:T(8,128)(2,1)}, bf16[256,1792]{1,0:T(8,128)(2,1)S(1)}, u32[]{:S(2)}, u32[]{:S(2)}) collective-permute-start(bf16[256,1792]{1,0:T(8,128)(2,1)} %get-tuple-element.57), channel_id=1, source_target_pairs={{0,1},{1,0},{2,3},{3,2},{4,5},{5,4},{6,7},{7,6},{8,9},{9,8},{10,11... | collective-permute-start | bytes 2752520 | tf_op jit(solution)/shard_map/ppermute | solution.py:37
  22.2 5.9 %collective-permute-start = (bf16[256,1536]{1,0:T(8,128)(2,1)}, bf16[256,1536]{1,0:T(8,128)(2,1)}, u32[]{:S(2)}, u32[]{:S(2)}) collective-permute-start(bf16[256,1536]{1,0:T(8,128)(2,1)} %get-tuple-element.52), channel_id=1, source_target_pairs={{0,1},{1,0},{2,3},{3,2},{4,5},{5,4},{6,7},{7,6},{8,9},{9,8},{10,11... | collective-permute-start | bytes 2359304 | tf_op jit(solution)/shard_map/ppermute | solution.py:37
  22.4 5.7 %collective-permute-start.1 = (bf16[256,1536]{1,0:T(8,128)(2,1)}, bf16[256,1536]{1,0:T(8,128)(2,1)}, u32[]{:S(2)}, u32[]{:S(2)}) collective-permute-start(bf16[256,1536]{1,0:T(8,128)(2,1)} %get-tuple-element.53), channel_id=1, source_target_pairs={{0,1},{1,0},{2,3},{3,2},{4,5},{5,4},{6,7},{7,6},{8,9},{9,8},{10,11... | collective-permute-start | bytes 2359304 | tf_op jit(solution)/shard_map/ppermute | solution.py:37
  22.8 5.3 %collective-permute-start.2 = (bf16[256,1536]{1,0:T(8,128)(2,1)}, bf16[256,1536]{1,0:T(8,128)(2,1)}, u32[]{:S(2)}, u32[]{:S(2)}) collective-permute-start(bf16[256,1536]{1,0:T(8,128)(2,1)} %get-tuple-element.54), channel_id=1, source_target_pairs={{0,1},{1,0},{2,3},{3,2},{4,5},{5,4},{6,7},{7,6},{8,9},{9,8},{10,11... | collective-permute-start | bytes 2359304 | tf_op jit(solution)/shard_map/ppermute | solution.py:37
  25.5 0.9 %copy-start.3 = (bf16[128,3584]{1,0:T(8,128)(2,1)}, bf16[128,3584]{1,0:T(8,128)(2,1)S(1)}, u32[]{:S(2)}) copy-start(bf16[128,3584]{1,0:T(8,128)(2,1)S(1)} %get-tuple-element.75.refs_0_) | copy-start | bytes 2752516
  26.4 35.2 %collective-permute-start.13 = (bf16[128,3584]{1,0:T(8,128)(2,1)}, bf16[128,3584]{1,0:T(8,128)(2,1)S(1)}, u32[]{:S(2)}, u32[]{:S(2)}) collective-permute-start(bf16[128,3584]{1,0:T(8,128)(2,1)} %get-tuple-element.58.refs_4_), channel_id=1, source_target_pairs={{0,8},{1,9},{2,10},{3,11},{4,12},{5,13},{6,14},{7,15},{8,0},{9,1},... | collective-permute-start | bytes 2752520 | tf_op jit(solution)/shard_map/ppermute | solution.py:37
  28.1 5.4 %copy-start = (bf16[512,512]{1,0:T(8,128)(2,1)S(1)}, bf16[512,512]{1,0:T(8,128)(2,1)}, u32[]{:S(2)}) copy-start(bf16[512,512]{1,0:T(8,128)(2,1)} %refs_0_.7) | copy-start | bytes 1572868
  28.1 5.4 %copy-start.1 = (bf16[512,1024]{1,0:T(8,128)(2,1)S(1)}, bf16[512,1024]{1,0:T(8,128)(2,1)}, u32[]{:S(2)}) copy-start(bf16[512,1024]{1,0:T(8,128)(2,1)} %refs_1_.6) | copy-start | bytes 3145732
  28.1 5.4 %copy-start.6 = (s32[512]{0:T(512)S(1)}, s32[512]{0:T(512)}, u32[]{:S(2)}) copy-start(s32[512]{0:T(512)} %param.15) | copy-start | bytes 6148
  28.1 5.4 %copy-start.7 = (s32[16]{0:T(128)S(1)}, s32[16]{0:T(128)}, u32[]{:S(2)}) copy-start(s32[16]{0:T(128)} %refs_1_.7) | copy-start | bytes 196
  30.8 9.4 %collective-permute-start.5 = (bf16[64,2304]{1,0:T(8,128)(2,1)S(1)}, bf16[64,2304]{1,0:T(8,128)(2,1)S(1)}, u32[]{:S(2)}, u32[]{:S(2)}) collective-permute-start(bf16[64,2304]{1,0:T(8,128)(2,1)S(1)} %get-tuple-element.62), channel_id=1, source_target_pairs={{0,2},{1,3},{2,4},{3,5},{4,6},{5,7},{6,0},{7,1},{8,10},{9,11},{10,... | collective-permute-start | bytes 884744 | tf_op jit(solution)/shard_map/ppermute | solution.py:37
  32.0 8.2 %collective-permute-start.6 = (bf16[64,2304]{1,0:T(8,128)(2,1)S(1)}, bf16[64,2304]{1,0:T(8,128)(2,1)S(1)}, u32[]{:S(2)}, u32[]{:S(2)}) collective-permute-start(bf16[64,2304]{1,0:T(8,128)(2,1)S(1)} %get-tuple-element.63), channel_id=1, source_target_pairs={{0,6},{1,7},{2,0},{3,1},{4,2},{5,3},{6,4},{7,5},{8,14},{9,15},{10,... | collective-permute-start | bytes 884744 | tf_op jit(solution)/shard_map/ppermute | solution.py:37
  33.5 16.2 %copy-start.2 = (bf16[1024,512]{1,0:T(8,128)(2,1)S(1)}, bf16[1024,512]{1,0:T(8,128)(2,1)}, u32[]{:S(2)}) copy-start(bf16[1024,512]{1,0:T(8,128)(2,1)} %refs_0_.8) | copy-start | bytes 3145732
  35.8 2.0 %collective-permute-start.7 = (bf16[256,128]{1,0:T(8,128)(2,1)S(1)}, bf16[256,128]{1,0:T(8,128)(2,1)S(1)}, u32[]{:S(2)}, u32[]{:S(2)}) collective-permute-start(bf16[256,128]{1,0:T(8,128)(2,1)S(1)} %get-tuple-element.65.refs_0_), channel_id=1, source_target_pairs={{0,1},{1,0},{2,3},{3,2},{4,5},{5,4},{6,7},{7,6},{8,9},{9,8},{10,11... | collective-permute-start | bytes 196616 | tf_op jit(solution)/shard_map/ppermute | solution.py:37
  37.8 4.3 %collective-permute-start.9 = (bf16[256,128]{1,0:T(8,128)(2,1)S(1)}, bf16[256,128]{1,0:T(8,128)(2,1)S(1)}, u32[]{:S(2)}, u32[]{:S(2)}) collective-permute-start(bf16[256,128]{1,0:T(8,128)(2,1)S(1)} %get-tuple-element.69.refs_0_), channel_id=1, source_target_pairs={{0,2},{1,3},{2,0},{3,1},{4,6},{5,7},{6,4},{7,5},{8,10},{9,11},{10,... | collective-permute-start | bytes 196616 | tf_op jit(solution)/shard_map/ppermute | solution.py:47
  40.3 12.4 %copy-start.8 = (bf16[64,2304]{1,0:T(8,128)(2,1)}, bf16[64,2304]{1,0:T(8,128)(2,1)S(1)}, u32[]{:S(2)}) copy-start(bf16[64,2304]{1,0:T(8,128)(2,1)S(1)} %get-tuple-element.68) | copy-start | bytes 884740
  40.3 12.4 %copy-start.9 = (bf16[64,2304]{1,0:T(8,128)(2,1)}, bf16[64,2304]{1,0:T(8,128)(2,1)S(1)}, u32[]{:S(2)}) copy-start(bf16[64,2304]{1,0:T(8,128)(2,1)S(1)} %get-tuple-element.73) | copy-start | bytes 884740
  42.1 4.4 %collective-permute-start.14 = (bf16[256,128]{1,0:T(8,128)(2,1)S(1)}, bf16[256,128]{1,0:T(8,128)(2,1)S(1)}, u32[]{:S(2)}, u32[]{:S(2)}) collective-permute-start(bf16[256,128]{1,0:T(8,128)(2,1)S(1)} %get-tuple-element.76.refs_0_), channel_id=1, source_target_pairs={{0,6},{1,7},{2,4},{3,5},{4,2},{5,3},{6,0},{7,1},{8,14},{9,15},{10,... | collective-permute-start | bytes 196616 | tf_op jit(solution)/shard_map/ppermute | solution.py:47
  44.3 17.4 %copy-start.4 = (bf16[128,3584]{1,0:T(8,128)(2,1)S(1)}, bf16[128,3584]{1,0:T(8,128)(2,1)}, u32[]{:S(2)}) copy-start(bf16[128,3584]{1,0:T(8,128)(2,1)} %copy-done.3) | copy-start | bytes 2752516
  46.5 4.5 %collective-permute-start.15 = (bf16[256,128]{1,0:T(8,128)(2,1)S(1)}, bf16[256,128]{1,0:T(8,128)(2,1)S(1)}, u32[]{:S(2)}, u32[]{:S(2)}) collective-permute-start(bf16[256,128]{1,0:T(8,128)(2,1)S(1)} %get-tuple-element.78.refs_0_), channel_id=1, source_target_pairs={{0,8},{1,9},{2,10},{3,11},{4,12},{5,13},{6,14},{7,15},{8,0},{9,1},... | collective-permute-start | bytes 196616 | tf_op jit(solution)/shard_map/ppermute | solution.py:37
  47.0 15.1 %collective-permute-start.10 = (bf16[64,2304]{1,0:T(8,128)(2,1)}, bf16[64,2304]{1,0:T(8,128)(2,1)}, u32[]{:S(2)}, u32[]{:S(2)}) collective-permute-start(bf16[64,2304]{1,0:T(8,128)(2,1)} %get-tuple-element.72), channel_id=1, source_target_pairs={{0,2},{1,3},{2,4},{3,5},{4,6},{5,7},{6,0},{7,1},{8,10},{9,11},{10,... | collective-permute-start | bytes 884744 | tf_op jit(solution)/shard_map/ppermute | solution.py:37
  47.0 18.8 %collective-permute-start.12 = (bf16[64,2304]{1,0:T(8,128)(2,1)}, bf16[64,2304]{1,0:T(8,128)(2,1)}, u32[]{:S(2)}, u32[]{:S(2)}) collective-permute-start(bf16[64,2304]{1,0:T(8,128)(2,1)} %get-tuple-element.74), channel_id=1, source_target_pairs={{0,6},{1,7},{2,0},{3,1},{4,2},{5,3},{6,4},{7,5},{8,14},{9,15},{10,... | collective-permute-start | bytes 884744 | tf_op jit(solution)/shard_map/ppermute | solution.py:37
  52.8 32.5 %all-to-all-start.1 = ((bf16[16,32,512]{2,1,0:T(8,128)(2,1)}), bf16[16,32,512]{2,1,0:T(8,128)(2,1)S(1)}, u32[]{:S(2)}, u32[]{:S(2)}) async-start(bf16[16,32,512]{2,1,0:T(8,128)(2,1)} %get-tuple-element.93), calls=%async_computation.1 | async-start | bytes 1048576 | tf_op jit(solution)/shard_map/all_to_all | solution.py:477
  59.0 14.3 %collective-permute-start.11 = (bf16[64,2304]{1,0:T(8,128)(2,1)}, bf16[64,2304]{1,0:T(8,128)(2,1)S(1)}, u32[]{:S(2)}, u32[]{:S(2)}) collective-permute-start(bf16[64,2304]{1,0:T(8,128)(2,1)} %copy-done.9), channel_id=1, source_target_pairs={{0,6},{1,7},{2,0},{3,1},{4,2},{5,3},{6,4},{7,5},{8,14},{9,15},{10,... | collective-permute-start | bytes 884744 | tf_op jit(solution)/shard_map/ppermute | solution.py:37
  61.6 13.1 %collective-permute-start.8 = (bf16[64,2304]{1,0:T(8,128)(2,1)}, bf16[64,2304]{1,0:T(8,128)(2,1)S(1)}, u32[]{:S(2)}, u32[]{:S(2)}) collective-permute-start(bf16[64,2304]{1,0:T(8,128)(2,1)} %copy-done.8), channel_id=1, source_target_pairs={{0,2},{1,3},{2,4},{3,5},{4,6},{5,7},{6,0},{7,1},{8,10},{9,11},{10,... | collective-permute-start | bytes 884744 | tf_op jit(solution)/shard_map/ppermute | solution.py:37
  61.8 17.8 %collective-permute-start.18 = (bf16[32,3584]{1,0:T(8,128)(2,1)S(1)}, bf16[32,3584]{1,0:T(8,128)(2,1)S(1)}, u32[]{:S(2)}, u32[]{:S(2)}) collective-permute-start(bf16[32,3584]{1,0:T(8,128)(2,1)S(1)} %get-tuple-element.88), channel_id=1, source_target_pairs={{0,2},{1,3},{2,4},{3,5},{4,6},{5,7},{6,0},{7,1},{8,10},{9,11},{10,... | collective-permute-start | bytes 688136 | tf_op jit(solution)/shard_map/ppermute | solution.py:37
  62.1 22.5 %collective-permute-start.19 = (bf16[32,3584]{1,0:T(8,128)(2,1)S(1)}, bf16[32,3584]{1,0:T(8,128)(2,1)S(1)}, u32[]{:S(2)}, u32[]{:S(2)}) collective-permute-start(bf16[32,3584]{1,0:T(8,128)(2,1)S(1)} %get-tuple-element.89), channel_id=1, source_target_pairs={{0,4},{1,5},{2,6},{3,7},{4,0},{5,1},{6,2},{7,3},{8,12},{9,13},{10,... | collective-permute-start | bytes 688136 | tf_op jit(solution)/shard_map/ppermute | solution.py:37
  65.8 18.9 %collective-permute-start.20 = (bf16[32,3584]{1,0:T(8,128)(2,1)S(1)}, bf16[32,3584]{1,0:T(8,128)(2,1)S(1)}, u32[]{:S(2)}, u32[]{:S(2)}) collective-permute-start(bf16[32,3584]{1,0:T(8,128)(2,1)S(1)} %get-tuple-element.90), channel_id=1, source_target_pairs={{0,6},{1,7},{2,0},{3,1},{4,2},{5,3},{6,4},{7,5},{8,14},{9,15},{10,... | collective-permute-start | bytes 688136 | tf_op jit(solution)/shard_map/ppermute | solution.py:37
  75.9 9.3 %collective-permute-start.16 = (bf16[32,2560]{1,0:T(8,128)(2,1)S(1)}, bf16[32,2560]{1,0:T(8,128)(2,1)S(1)}, u32[]{:S(2)}, u32[]{:S(2)}) collective-permute-start(bf16[32,2560]{1,0:T(8,128)(2,1)S(1)} %get-tuple-element.85), channel_id=1, source_target_pairs={{0,8},{1,9},{2,10},{3,11},{4,12},{5,13},{6,14},{7,15},{8,0},{9,1},... | collective-permute-start | bytes 491528 | tf_op jit(solution)/shard_map/ppermute | solution.py:37
  77.3 8.0 %collective-permute-start.17 = (bf16[32,2048]{1,0:T(8,128)(2,1)S(1)}, bf16[32,2048]{1,0:T(8,128)(2,1)S(1)}, u32[]{:S(2)}, u32[]{:S(2)}) collective-permute-start(bf16[32,2048]{1,0:T(8,128)(2,1)S(1)} %get-tuple-element.86), channel_id=1, source_target_pairs={{0,8},{1,9},{2,10},{3,11},{4,12},{5,13},{6,14},{7,15},{8,0},{9,1},... | collective-permute-start | bytes 393224 | tf_op jit(solution)/shard_map/ppermute | solution.py:37
  85.3 1.0 %copy-start.5 = (bf16[32,8192]{1,0:T(8,128)(2,1)S(1)}, bf16[32,8192]{1,0:T(8,128)(2,1)}, u32[]{:S(2)}) copy-start(bf16[32,8192]{1,0:T(8,128)(2,1)} %refs_0_.9) | copy-start | bytes 1572868

commit v9 on v6

--- a/solution.py
+++ b/solution.py
@@ -385,7 +385,7 @@
 
 
 def finish_kernel(
-    residual_ref, wide_ref, wide_y_ref, rest_y_ref, narrow_ref, delta_ref, out_ref
+    residual_ref, wide_ref, wide_y_ref, rest_y_ref, low_ref, narrow_ref, delta_ref, out_ref
 ):
     for t in range(16):
         cols = slice(t * 512, (t + 1) * 512)
@@ -397,7 +397,7 @@
             base = wide_ref[:, cols] + other.astype(F32)
         else:
             part = slice(t * 512 - WIDE, (t + 1) * 512 - WIDE)
-            base = narrow_ref[:, part]
+            base = plus(low_ref[:, part], narrow_ref[:, part])
         out_ref[:, cols] = (
             residual_ref[:, cols].astype(F32) + base + delta_ref[t].astype(F32)
         ).astype(BF16)
@@ -448,19 +448,19 @@
     from_left, from_right = send(right, 0, 1, 0), send(left, 0, 3, 0)
     table, mark = up_table(resident_up_maps, target, maps, [mark])
     *low, mark = turn_narrow(keep, narrow_y, [mark])
-    low_in = [send(low[d], 0, d, 0) for d in (1, 2, 3)]
+    low_in = [send(low[d], 0, d, 0) for d in (2, 1, 3)]
     raised, mark = raise_features(part, other, table, slot, [mark])
     delta = lax.all_to_all(raised, "tp", split_axis=0, concat_axis=0, tiled=True)
 
     wide_keep, wide_send, wide_rest, mark = turn_wide(here, from_left, from_right, [mark])
     wide_y = send(wide_send, 1, 0, 0)
     rest_y = send(wide_rest, 1, 0, 0)
-    narrow_sum, mark = add_parts([low[0], *low_in], [mark], F32)
+    narrow_sum, mark = add_parts(low_in, [mark], F32)
     hidden, _ = call(
         finish_kernel,
         "finish",
         [whole((32, 8192), BF16)],
-        (residual, wide_keep, wide_y, rest_y, narrow_sum, delta),
+        (residual, wide_keep, wide_y, rest_y, low[0], narrow_sum, delta),
     )
     return hidden
 

time: 84.6 us -> 84.5 us (level)
  no operation moved by 1% of the time
where the time goes in v9:
time: 84.5 us; the launch traced here: 84.1 us
  starting transfers between devices  32.9 us (39%)
  Pallas kernels  28 us (33%)
  waiting for transfers between devices  19.9 us (24%)
  local copies, waits for them, and re-layouts  3.07 us (4%)
    pallas_call x15, Pallas kernels, call(): pl.pallas_call(body, in_specs=list(specs or [VM] * count) + [LATER] * len...  28 us
    ppermute x17, starting transfers between devices, send(): return lax.ppermute(array, 'tp', route(yy, xx, cc))  18 us
    ppermute x17, waiting for transfers between devices, send(): return lax.ppermute(array, 'tp', route(yy, xx, cc))  13.2 us
    all_to_all x1, starting transfers between devices, local(): lax.all_to_all(fresh_adapter_bundle.reshape(16, 256, 128), 'tp', split_ax...  6.83 us
    ppermute x2, waiting for transfers between devices, trade(): return lax.ppermute(array, 'tp', pairs)  6.75 us
    all_to_all x1, starting transfers between devices, local(): lax.all_to_all(raised, 'tp', split_axis=0, concat_axis=0, tiled=True)  6.19 us
    unnamed x22, local copies, waits for them, and re-layouts  3.07 us
    ppermute x2, starting transfers between devices, trade(): return lax.ppermute(array, 'tp', pairs)  1.92 us
  transfers between devices with their start and end apart: 21, of which 6 were waited for; matrix products, arithmetic and copies ran while one was open for 0% of the time, Pallas kernels for 32%

profile of v9, /device:TPU:1, one launch (start us, length us, event | category | flops | bytes accessed | tf_op | source)
XLA Modules:
  0.0 84.1 jit_solution(14525119155226761510)
XLA Ops:
  0.0 6.8 %all-to-all-start = ((bf16[16,256,128]{2,1,0:T(8,128)(2,1)}), bf16[16,256,128]{2,1,0:T(8,128)(2,1)S(1)}, u32[]{:S(2)}, u32[]{:S(2)}) async-start(bf16[16,256,128]{2,1,0:T(8,128)(2,1)} %bitcast.4), calls=%async_computation | async-start | bytes 2097152 | tf_op jit(solution)/shard_map/all_to_all | solution.py:420
  6.8 6.7 %product.2 = (bf16[256,1792]{1,0:T(8,128)(2,1)}, bf16[256,1792]{1,0:T(8,128)(2,1)}, bf16[256,3584]{1,0:T(8,128)(2,1)}, f32[8,128]{1,0:T(8,128)}) custom-call(bf16[512,512]{1,0:T(8,128)(2,1)} %refs_0_.7, bf16[512,8192]{1,0:T(8,128)(2,1)} %refs_1_.5), custom_call_target="tpu_custom_call" | custom-call | flops 1024 | bytes 1024 | tf_op jit(solution)/shard_map/product/pallas_call | solution.py:88
  13.6 0.2 collective-permute-start.3
  13.8 0.4 collective-permute-start.4
  14.2 8.1 %product.3 = (bf16[256,1536]{1,0:T(8,128)(2,1)}, bf16[256,1536]{1,0:T(8,128)(2,1)}, bf16[256,1536]{1,0:T(8,128)(2,1)}, bf16[256,4608]{1,0:T(8,128)(2,1)}, f32[8,128]{1,0:T(8,128)}) custom-call(bf16[512,512]{1,0:T(8,128)(2,1)} %refs_0_.7, bf16[512,8192]{1,0:T(8,128)(2,1)} %refs_1_.5, f32[8,128]{1,0:T(8,128)} %get-tuple-element.47.refs_2_), custom_call_target="tpu_custom_call" | custom-call | flops 1024 | bytes 1024 | tf_op jit(solution)/shard_map/product/pallas_call | solution.py:88
  22.3 0.2 collective-permute-start
  22.5 0.4 collective-permute-start.1
  22.9 0.1 collective-permute-start.2
  23.0 0.0 collective-permute-done.3.refs_1_
  23.0 0.0 collective-permute-done.4.refs_2_
  23.0 0.0 all-to-all-done.refs_3_.refs_4_.refs_2_
  23.0 2.1 %chip_narrow.1 = (bf16[128,3584]{1,0:T(8,128)(2,1)S(1)}, bf16[128,3584]{1,0:T(8,128)(2,1)S(1)}, f32[8,128]{1,0:T(8,128)}) custom-call(bf16[256,3584]{1,0:T(8,128)(2,1)} %get-tuple-element.52.refs_0_, bf16[256,1792]{1,0:T(8,128)(2,1)S(1)} %collective-permute-done.3.refs_1_, bf16[256,1792]{1,0:T(8,128)(2,1)S(1)} %collective-permute-done.4.refs_2_, ...), custom_call_target="tpu_custom_call" | custom-call | flops 1024 | bytes 1024 | tf_op jit(solution)/shard_map/chip_narrow/pallas_call | solution.py:88
  25.2 1.7 %collective-permute-start.13 = (bf16[128,3584]{1,0:T(8,128)(2,1)S(1)}, bf16[128,3584]{1,0:T(8,128)(2,1)S(1)}, u32[]{:S(2)}, u32[]{:S(2)}) collective-permute-start(bf16[128,3584]{1,0:T(8,128)(2,1)S(1)} %get-tuple-element.55.refs_4_), channel_id=1, source_target_pairs={{0,8},{1,9},{2,10},{3,11},{4,12},{5,13},{6,14},{7,15},{8,0},{9,1},... | collective-permute-start | bytes 2752520 | tf_op jit(solution)/shard_map/ppermute | solution.py:37
  26.9 0.0 collective-permute-done.refs_1_
  26.9 0.0 collective-permute-done.1.refs_2_
  26.9 0.4 collective-permute-done.2.refs_3_
  27.3 2.6 %chip_wide.1 = (bf16[64,4608]{1,0:T(8,128)(2,1)S(1)}, bf16[64,4608]{1,0:T(8,128)(2,1)S(1)}, bf16[64,2304]{1,0:T(8,128)(2,1)S(1)}, bf16[64,2304]{1,0:T(8,128)(2,1...) custom-call(bf16[256,4608]{1,0:T(8,128)(2,1)} %get-tuple-element.48.refs_0_, ...), custom_call_target="tpu_custom_call" | custom-call | flops 1024 | bytes 1024 | tf_op jit(solution)/shard_map/chip_wide/pallas_call | solution.py:88
  29.9 1.5 %collective-permute-start.5 = (bf16[64,2304]{1,0:T(8,128)(2,1)S(1)}, bf16[64,2304]{1,0:T(8,128)(2,1)S(1)}, u32[]{:S(2)}, u32[]{:S(2)}) collective-permute-start(bf16[64,2304]{1,0:T(8,128)(2,1)S(1)} %get-tuple-element.59), channel_id=1, source_target_pairs={{0,2},{1,3},{2,4},{3,5},{4,6},{5,7},{6,0},{7,1},{8,10},{9,11},{10,... | collective-permute-start | bytes 884744 | tf_op jit(solution)/shard_map/ppermute | solution.py:37
  31.4 1.5 %collective-permute-start.6 = (bf16[64,2304]{1,0:T(8,128)(2,1)S(1)}, bf16[64,2304]{1,0:T(8,128)(2,1)S(1)}, u32[]{:S(2)}, u32[]{:S(2)}) collective-permute-start(bf16[64,2304]{1,0:T(8,128)(2,1)S(1)} %get-tuple-element.60), channel_id=1, source_target_pairs={{0,6},{1,7},{2,0},{3,1},{4,2},{5,3},{6,4},{7,5},{8,14},{9,15},{10,... | collective-permute-start | bytes 884744 | tf_op jit(solution)/shard_map/ppermute | solution.py:37
  32.9 0.0 copy-done
  32.9 0.0 copy-done.1
  32.9 0.0 copy-done.6
  32.9 0.0 copy-done.7
  32.9 0.0 copy-start.2
  32.9 2.3 %shrink_part.1 = (bf16[256,128]{1,0:T(8,128)(2,1)S(1)}, f32[8,128]{1,0:T(8,128)S(1)}) custom-call(bf16[512,512]{1,0:T(8,128)(2,1)S(1)} %copy-done, bf16[512,1024]{1,0:T(8,128)(2,1)S(1)} %copy-done.1, s32[1,512]{1,0:T(1,128)S(1)} %bitcast.2, s32[16]{0:T(128)S(1)} %copy-done.7, bf16[16,256,128]{2,1,0:T(8,128)(2,1)S(1)} %all-to-all-done.refs_3_.refs_4_.refs_2_, ...), custom_call_target="tpu_custom_call" | custom-call | flops 1024 | bytes 1024 | tf_op jit(solution)/shard_map/shrink_part/pallas_call | solution.py:88
  35.2 0.7 collective-permute-start.7
  35.9 0.9 %collective-permute-done.7.refs_1_ = bf16[256,128]{1,0:T(8,128)(2,1)S(1)} collective-permute-done((bf16[256,128]{1,0:T(8,128)(2,1)S(1)}, bf16[256,128]{1,0:T(8,128)(2,1)S(1)}, u32[]{:S(2)}, u32[]{:S(2)}) %collective-permute-start.7) | collective-permute-done | bytes 65568 | tf_op jit(solution)/shard_map/ppermute | solution.py:37
  36.8 0.4 collective-permute-start.8
  37.2 3.9 %collective-permute-done.8.refs_1_ = bf16[256,128]{1,0:T(8,128)(2,1)S(1)} collective-permute-done((bf16[256,128]{1,0:T(8,128)(2,1)S(1)}, bf16[256,128]{1,0:T(8,128)(2,1)S(1)}, u32[]{:S(2)}, u32[]{:S(2)}) %collective-permute-start.8) | collective-permute-done | bytes 65568 | tf_op jit(solution)/shard_map/ppermute | solution.py:47
  41.1 1.6 %collective-permute-start.9 = (bf16[256,128]{1,0:T(8,128)(2,1)S(1)}, bf16[256,128]{1,0:T(8,128)(2,1)S(1)}, u32[]{:S(2)}, u32[]{:S(2)}) collective-permute-start(bf16[256,128]{1,0:T(8,128)(2,1)S(1)} %get-tuple-element.66.refs_0_), channel_id=1, source_target_pairs={{0,6},{1,7},{2,4},{3,5},{4,2},{5,3},{6,0},{7,1},{8,14},{9,15},{10,... | collective-permute-start | bytes 196616 | tf_op jit(solution)/shard_map/ppermute | solution.py:47
  42.7 2.8 %collective-permute-done.9.refs_1_ = bf16[256,128]{1,0:T(8,128)(2,1)S(1)} collective-permute-done((bf16[256,128]{1,0:T(8,128)(2,1)S(1)}, bf16[256,128]{1,0:T(8,128)(2,1)S(1)}, u32[]{:S(2)}, u32[]{:S(2)}) %collective-permute-start.9) | collective-permute-done | bytes 65568 | tf_op jit(solution)/shard_map/ppermute | solution.py:47
  45.5 0.0 collective-permute-done.5.refs_2_
  45.5 0.0 collective-permute-done.6.refs_3_
  45.6 0.9 %near.1 = (bf16[64,4608]{1,0:T(8,128)(2,1)}, bf16[64,4608]{1,0:T(8,128)(2,1)S(1)}, f32[8,128]{1,0:T(8,128)S(1)}) custom-call(bf16[64,4608]{1,0:T(8,128)(2,1)S(1)} %get-tuple-element.57.refs_0_, bf16[64,4608]{1,0:T(8,128)(2,1)S(1)} %get-tuple-element.58.refs_1_, bf16[64,2304]{1,0:T(8,128)(2,1)S(1)} %collective-permute-done.5.refs_2_, ...), custom_call_target="tpu_custom_call" | custom-call | flops 1024 | bytes 1024 | tf_op jit(solution)/shard_map/near/pallas_call | solution.py:88
  46.5 0.0 collective-permute-start.10
  46.5 2.7 %collective-permute-start.11 = (bf16[64,4608]{1,0:T(8,128)(2,1)S(1)}, bf16[64,4608]{1,0:T(8,128)(2,1)S(1)}, u32[]{:S(2)}, u32[]{:S(2)}) collective-permute-start(bf16[64,4608]{1,0:T(8,128)(2,1)S(1)} %get-tuple-element.70), channel_id=1, source_target_pairs={{0,6},{1,7},{2,0},{3,1},{4,2},{5,3},{6,4},{7,5},{8,14},{9,15},{10,... | collective-permute-start | bytes 1769480 | tf_op jit(solution)/shard_map/ppermute | solution.py:37
  49.1 1.5 %collective-permute-start.12 = (bf16[256,128]{1,0:T(8,128)(2,1)S(1)}, bf16[256,128]{1,0:T(8,128)(2,1)S(1)}, u32[]{:S(2)}, u32[]{:S(2)}) collective-permute-start(bf16[256,128]{1,0:T(8,128)(2,1)S(1)} %get-tuple-element.71.refs_0_), channel_id=1, source_target_pairs={{0,8},{1,9},{2,10},{3,11},{4,12},{5,13},{6,14},{7,15},{8,0},{9,1},... | collective-permute-start | bytes 196616 | tf_op jit(solution)/shard_map/ppermute | solution.py:37
  50.6 1.3 %up_table.1 = (bf16[1024,512]{1,0:T(8,128)(2,1)S(1)}, f32[8,128]{1,0:T(8,128)S(1)}) custom-call(bf16[1024,512]{1,0:T(8,128)(2,1)S(1)} %copy-done.2, s32[16]{0:T(128)S(1)} %copy-done.7, bf16[16,256,128]{2,1,0:T(8,128)(2,1)S(1)} %all-to-all-done.refs_3_.refs_4_.refs_2_, f32[8,128]{1,0:T(8,128)S(1)} %get-tuple-element.72.refs_3_), custom_call_target="tpu_custom_call" | custom-call | flops 1024 | bytes 1024 | tf_op jit(solution)/shard_map/up_table/pallas_call | solution.py:88
  52.0 0.0 collective-permute-done.13.refs_1_
  52.0 0.2 turn_narrow.1
  52.2 0.7 copy-done.4
  52.9 0.7 copy-done.9
  53.6 0.7 copy-done.10
  54.3 0.0 collective-permute-done.12.refs_1_
  54.3 1.7 %raise_features.1 = (bf16[16,32,512]{2,1,0:T(8,128)(2,1)}, f32[8,128]{1,0:T(8,128)S(1)}) custom-call(bf16[256,128]{1,0:T(8,128)(2,1)S(1)} %get-tuple-element.71.refs_0_, bf16[256,128]{1,0:T(8,128)(2,1)S(1)} %collective-permute-done.12.refs_1_, bf16[1024,512]{1,0:T(8,128)(2,1)S(1)} %get-tuple-element.73.refs_2_, s32[1,512]{1,0:T(1,128)S(1)} %bitcast.3, ...), custom_call_target="tpu_custom_call" | custom-call | flops 1024 | bytes 1024 | tf_op jit(solution)/shard_map/raise_features/pallas_call | solution.py:88
  56.1 0.0 copy-done.8
  56.1 6.2 %all-to-all-start.1 = ((bf16[16,32,512]{2,1,0:T(8,128)(2,1)}), bf16[16,32,512]{2,1,0:T(8,128)(2,1)S(1)}, u32[]{:S(2)}, u32[]{:S(2)}) async-start(bf16[16,32,512]{2,1,0:T(8,128)(2,1)} %get-tuple-element.87), calls=%async_computation.1 | async-start | bytes 1048576 | tf_op jit(solution)/shard_map/all_to_all | solution.py:453
  62.3 2.9 %collective-permute-start.16 = (bf16[32,3584]{1,0:T(8,128)(2,1)}, bf16[32,3584]{1,0:T(8,128)(2,1)S(1)}, u32[]{:S(2)}, u32[]{:S(2)}) collective-permute-start(bf16[32,3584]{1,0:T(8,128)(2,1)} %copy-done.10), channel_id=1, source_target_pairs={{0,4},{1,5},{2,6},{3,7},{4,0},{5,1},{6,2},{7,3},{8,12},{9,13},{10,... | collective-permute-start | bytes 688136 | tf_op jit(solution)/shard_map/ppermute | solution.py:37
  65.2 0.3 collective-permute-start.17
  65.5 2.4 %collective-permute-start.18 = (bf16[32,3584]{1,0:T(8,128)(2,1)}, bf16[32,3584]{1,0:T(8,128)(2,1)S(1)}, u32[]{:S(2)}, u32[]{:S(2)}) collective-permute-start(bf16[32,3584]{1,0:T(8,128)(2,1)} %copy-done.8), channel_id=1, source_target_pairs={{0,6},{1,7},{2,0},{3,1},{4,2},{5,3},{6,4},{7,5},{8,14},{9,15},{10,... | collective-permute-start | bytes 688136 | tf_op jit(solution)/shard_map/ppermute | solution.py:37
  67.8 0.0 collective-permute-done.10.refs_1_
  67.8 0.0 collective-permute-done.11.refs_2_
  67.8 0.2 turn_wide.1
  68.1 1.3 %collective-permute-start.14 = (bf16[32,2560]{1,0:T(8,128)(2,1)S(1)}, bf16[32,2560]{1,0:T(8,128)(2,1)S(1)}, u32[]{:S(2)}, u32[]{:S(2)}) collective-permute-start(bf16[32,2560]{1,0:T(8,128)(2,1)S(1)} %get-tuple-element.79), channel_id=1, source_target_pairs={{0,8},{1,9},{2,10},{3,11},{4,12},{5,13},{6,14},{7,15},{8,0},{9,1},... | collective-permute-start | bytes 491528 | tf_op jit(solution)/shard_map/ppermute | solution.py:37
  69.4 0.2 collective-permute-start.15
  69.6 7.1 %collective-permute-done.16.refs_0_ = bf16[32,3584]{1,0:T(8,128)(2,1)S(1)} collective-permute-done((bf16[32,3584]{1,0:T(8,128)(2,1)}, bf16[32,3584]{1,0:T(8,128)(2,1)S(1)}, u32[]{:S(2)}, u32[]{:S(2)}) %collective-permute-start.16) | collective-permute-done | bytes 229408 | tf_op jit(solution)/shard_map/ppermute | solution.py:37
  76.7 4.8 %collective-permute-done.17.refs_1_ = bf16[32,3584]{1,0:T(8,128)(2,1)S(1)} collective-permute-done((bf16[32,3584]{1,0:T(8,128)(2,1)}, bf16[32,3584]{1,0:T(8,128)(2,1)S(1)}, u32[]{:S(2)}, u32[]{:S(2)}) %collective-permute-start.17) | collective-permute-done | bytes 229408 | tf_op jit(solution)/shard_map/ppermute | solution.py:37
  81.5 0.0 collective-permute-done.18.refs_2_
  81.5 0.6 add_parts.7
  82.1 0.0 collective-permute-done.15.refs_3_
  82.1 0.0 collective-permute-done.14.refs_2_
  82.1 0.0 all-to-all-done.1.refs_6_
  82.1 0.9 %copy-done.5 = bf16[32,3584]{1,0:T(8,128)(2,1)S(1)} copy-done((bf16[32,3584]{1,0:T(8,128)(2,1)S(1)}, bf16[32,3584]{1,0:T(8,128)(2,1)}, u32[]{:S(2)}) %copy-start.5) | copy-done | bytes 229400
  83.1 1.0 %finish.1 = (bf16[32,8192]{1,0:T(8,128)(2,1)}, f32[8,128]{1,0:T(8,128)}) custom-call(bf16[32,8192]{1,0:T(8,128)(2,1)S(1)} %copy-done.3, f32[32,4608]{1,0:T(8,128)S(1)} %get-tuple-element.78.refs_1_, bf16[32,2560]{1,0:T(8,128)(2,1)S(1)} %collective-permute-done.14.refs_2_, bf16[32,2048]{1,0:T(8,128)(2,1)S(1)} %collective-permute-done.15.refs_3_, ...), custom_call_target="tpu_custom_call" | custom-call | flops 1024 | bytes 1024 | tf_op jit(solution)/shard_map/finish/pallas_call | solution.py:88
  (15 shorter events, 0.1 us)
Async XLA Ops:
  0.0 23.0 %all-to-all-start = ((bf16[16,256,128]{2,1,0:T(8,128)(2,1)}), bf16[16,256,128]{2,1,0:T(8,128)(2,1)S(1)}, u32[]{:S(2)}, u32[]{:S(2)}) async-start(bf16[16,256,128]{2,1,0:T(8,128)(2,1)} %bitcast.4), calls=%async_computation | async-start | bytes 2097152 | tf_op jit(solution)/shard_map/all_to_all | solution.py:420
  13.6 9.4 %collective-permute-start.3 = (bf16[256,1792]{1,0:T(8,128)(2,1)}, bf16[256,1792]{1,0:T(8,128)(2,1)S(1)}, u32[]{:S(2)}, u32[]{:S(2)}) collective-permute-start(bf16[256,1792]{1,0:T(8,128)(2,1)} %get-tuple-element.53), channel_id=1, source_target_pairs={{0,1},{1,0},{2,3},{3,2},{4,5},{5,4},{6,7},{7,6},{8,9},{9,8},{10,11... | collective-permute-start | bytes 2752520 | tf_op jit(solution)/shard_map/ppermute | solution.py:37
  13.8 9.2 %collective-permute-start.4 = (bf16[256,1792]{1,0:T(8,128)(2,1)}, bf16[256,1792]{1,0:T(8,128)(2,1)S(1)}, u32[]{:S(2)}, u32[]{:S(2)}) collective-permute-start(bf16[256,1792]{1,0:T(8,128)(2,1)} %get-tuple-element.54), channel_id=1, source_target_pairs={{0,1},{1,0},{2,3},{3,2},{4,5},{5,4},{6,7},{7,6},{8,9},{9,8},{10,11... | collective-permute-start | bytes 2752520 | tf_op jit(solution)/shard_map/ppermute | solution.py:37
  22.3 4.6 %collective-permute-start = (bf16[256,1536]{1,0:T(8,128)(2,1)}, bf16[256,1536]{1,0:T(8,128)(2,1)}, u32[]{:S(2)}, u32[]{:S(2)}) collective-permute-start(bf16[256,1536]{1,0:T(8,128)(2,1)} %get-tuple-element.49), channel_id=1, source_target_pairs={{0,1},{1,0},{2,3},{3,2},{4,5},{5,4},{6,7},{7,6},{8,9},{9,8},{10,11... | collective-permute-start | bytes 2359304 | tf_op jit(solution)/shard_map/ppermute | solution.py:37
  22.5 4.4 %collective-permute-start.1 = (bf16[256,1536]{1,0:T(8,128)(2,1)}, bf16[256,1536]{1,0:T(8,128)(2,1)}, u32[]{:S(2)}, u32[]{:S(2)}) collective-permute-start(bf16[256,1536]{1,0:T(8,128)(2,1)} %get-tuple-element.50), channel_id=1, source_target_pairs={{0,1},{1,0},{2,3},{3,2},{4,5},{5,4},{6,7},{7,6},{8,9},{9,8},{10,11... | collective-permute-start | bytes 2359304 | tf_op jit(solution)/shard_map/ppermute | solution.py:37
  22.9 4.4 %collective-permute-start.2 = (bf16[256,1536]{1,0:T(8,128)(2,1)}, bf16[256,1536]{1,0:T(8,128)(2,1)}, u32[]{:S(2)}, u32[]{:S(2)}) collective-permute-start(bf16[256,1536]{1,0:T(8,128)(2,1)} %get-tuple-element.51), channel_id=1, source_target_pairs={{0,1},{1,0},{2,3},{3,2},{4,5},{5,4},{6,7},{7,6},{8,9},{9,8},{10,11... | collective-permute-start | bytes 2359304 | tf_op jit(solution)/shard_map/ppermute | solution.py:37
  25.2 26.8 %collective-permute-start.13 = (bf16[128,3584]{1,0:T(8,128)(2,1)S(1)}, bf16[128,3584]{1,0:T(8,128)(2,1)S(1)}, u32[]{:S(2)}, u32[]{:S(2)}) collective-permute-start(bf16[128,3584]{1,0:T(8,128)(2,1)S(1)} %get-tuple-element.55.refs_4_), channel_id=1, source_target_pairs={{0,8},{1,9},{2,10},{3,11},{4,12},{5,13},{6,14},{7,15},{8,0},{9,1},... | collective-permute-start | bytes 2752520 | tf_op jit(solution)/shard_map/ppermute | solution.py:37
  27.3 5.6 %copy-start = (bf16[512,512]{1,0:T(8,128)(2,1)S(1)}, bf16[512,512]{1,0:T(8,128)(2,1)}, u32[]{:S(2)}) copy-start(bf16[512,512]{1,0:T(8,128)(2,1)} %refs_0_.7) | copy-start | bytes 1572868
  27.3 5.6 %copy-start.1 = (bf16[512,1024]{1,0:T(8,128)(2,1)S(1)}, bf16[512,1024]{1,0:T(8,128)(2,1)}, u32[]{:S(2)}) copy-start(bf16[512,1024]{1,0:T(8,128)(2,1)} %refs_1_.6) | copy-start | bytes 3145732
  27.3 5.6 %copy-start.6 = (s32[512]{0:T(512)S(1)}, s32[512]{0:T(512)}, u32[]{:S(2)}) copy-start(s32[512]{0:T(512)} %param.15) | copy-start | bytes 6148
  27.3 5.6 %copy-start.7 = (s32[16]{0:T(128)S(1)}, s32[16]{0:T(128)}, u32[]{:S(2)}) copy-start(s32[16]{0:T(128)} %refs_1_.7) | copy-start | bytes 196
  29.9 15.6 %collective-permute-start.5 = (bf16[64,2304]{1,0:T(8,128)(2,1)S(1)}, bf16[64,2304]{1,0:T(8,128)(2,1)S(1)}, u32[]{:S(2)}, u32[]{:S(2)}) collective-permute-start(bf16[64,2304]{1,0:T(8,128)(2,1)S(1)} %get-tuple-element.59), channel_id=1, source_target_pairs={{0,2},{1,3},{2,4},{3,5},{4,6},{5,7},{6,0},{7,1},{8,10},{9,11},{10,... | collective-permute-start | bytes 884744 | tf_op jit(solution)/shard_map/ppermute | solution.py:37
  31.4 14.2 %collective-permute-start.6 = (bf16[64,2304]{1,0:T(8,128)(2,1)S(1)}, bf16[64,2304]{1,0:T(8,128)(2,1)S(1)}, u32[]{:S(2)}, u32[]{:S(2)}) collective-permute-start(bf16[64,2304]{1,0:T(8,128)(2,1)S(1)} %get-tuple-element.60), channel_id=1, source_target_pairs={{0,6},{1,7},{2,0},{3,1},{4,2},{5,3},{6,4},{7,5},{8,14},{9,15},{10,... | collective-permute-start | bytes 884744 | tf_op jit(solution)/shard_map/ppermute | solution.py:37
  32.9 17.7 %copy-start.2 = (bf16[1024,512]{1,0:T(8,128)(2,1)S(1)}, bf16[1024,512]{1,0:T(8,128)(2,1)}, u32[]{:S(2)}) copy-start(bf16[1024,512]{1,0:T(8,128)(2,1)} %refs_0_.8) | copy-start | bytes 3145732
  35.2 1.6 %collective-permute-start.7 = (bf16[256,128]{1,0:T(8,128)(2,1)S(1)}, bf16[256,128]{1,0:T(8,128)(2,1)S(1)}, u32[]{:S(2)}, u32[]{:S(2)}) collective-permute-start(bf16[256,128]{1,0:T(8,128)(2,1)S(1)} %get-tuple-element.62.refs_0_), channel_id=1, source_target_pairs={{0,1},{1,0},{2,3},{3,2},{4,5},{5,4},{6,7},{7,6},{8,9},{9,8},{10,11... | collective-permute-start | bytes 196616 | tf_op jit(solution)/shard_map/ppermute | solution.py:37
  36.8 4.3 %collective-permute-start.8 = (bf16[256,128]{1,0:T(8,128)(2,1)S(1)}, bf16[256,128]{1,0:T(8,128)(2,1)S(1)}, u32[]{:S(2)}, u32[]{:S(2)}) collective-permute-start(bf16[256,128]{1,0:T(8,128)(2,1)S(1)} %get-tuple-element.64.refs_0_), channel_id=1, source_target_pairs={{0,2},{1,3},{2,0},{3,1},{4,6},{5,7},{6,4},{7,5},{8,10},{9,11},{10,... | collective-permute-start | bytes 196616 | tf_op jit(solution)/shard_map/ppermute | solution.py:47
  41.1 4.4 %collective-permute-start.9 = (bf16[256,128]{1,0:T(8,128)(2,1)S(1)}, bf16[256,128]{1,0:T(8,128)(2,1)S(1)}, u32[]{:S(2)}, u32[]{:S(2)}) collective-permute-start(bf16[256,128]{1,0:T(8,128)(2,1)S(1)} %get-tuple-element.66.refs_0_), channel_id=1, source_target_pairs={{0,6},{1,7},{2,4},{3,5},{4,2},{5,3},{6,0},{7,1},{8,14},{9,15},{10,... | collective-permute-start | bytes 196616 | tf_op jit(solution)/shard_map/ppermute | solution.py:47
  46.5 21.4 %collective-permute-start.10 = (bf16[64,4608]{1,0:T(8,128)(2,1)}, bf16[64,4608]{1,0:T(8,128)(2,1)S(1)}, u32[]{:S(2)}, u32[]{:S(2)}) collective-permute-start(bf16[64,4608]{1,0:T(8,128)(2,1)} %get-tuple-element.69), channel_id=1, source_target_pairs={{0,2},{1,3},{2,4},{3,5},{4,6},{5,7},{6,0},{7,1},{8,10},{9,11},{10,... | collective-permute-start | bytes 1769480 | tf_op jit(solution)/shard_map/ppermute | solution.py:37
  46.5 21.4 %collective-permute-start.11 = (bf16[64,4608]{1,0:T(8,128)(2,1)S(1)}, bf16[64,4608]{1,0:T(8,128)(2,1)S(1)}, u32[]{:S(2)}, u32[]{:S(2)}) collective-permute-start(bf16[64,4608]{1,0:T(8,128)(2,1)S(1)} %get-tuple-element.70), channel_id=1, source_target_pairs={{0,6},{1,7},{2,0},{3,1},{4,2},{5,3},{6,4},{7,5},{8,14},{9,15},{10,... | collective-permute-start | bytes 1769480 | tf_op jit(solution)/shard_map/ppermute | solution.py:37
  49.1 5.2 %collective-permute-start.12 = (bf16[256,128]{1,0:T(8,128)(2,1)S(1)}, bf16[256,128]{1,0:T(8,128)(2,1)S(1)}, u32[]{:S(2)}, u32[]{:S(2)}) collective-permute-start(bf16[256,128]{1,0:T(8,128)(2,1)S(1)} %get-tuple-element.71.refs_0_), channel_id=1, source_target_pairs={{0,8},{1,9},{2,10},{3,11},{4,12},{5,13},{6,14},{7,15},{8,0},{9,1},... | collective-permute-start | bytes 196616 | tf_op jit(solution)/shard_map/ppermute | solution.py:37
  52.2 0.7 copy-start.4
  52.9 0.7 copy-start.9
  53.6 0.7 copy-start.10
  54.3 1.7 %copy-start.8 = (bf16[32,3584]{1,0:T(8,128)(2,1)}, bf16[32,3584]{1,0:T(8,128)(2,1)S(1)}, u32[]{:S(2)}) copy-start(bf16[32,3584]{1,0:T(8,128)(2,1)S(1)} %get-tuple-element.84) | copy-start | bytes 688132
  54.3 27.8 %copy-start.3 = (bf16[32,8192]{1,0:T(8,128)(2,1)S(1)}, bf16[32,8192]{1,0:T(8,128)(2,1)}, u32[]{:S(2)}) copy-start(bf16[32,8192]{1,0:T(8,128)(2,1)} %refs_0_.9) | copy-start | bytes 1572868
  56.1 26.0 %all-to-all-start.1 = ((bf16[16,32,512]{2,1,0:T(8,128)(2,1)}), bf16[16,32,512]{2,1,0:T(8,128)(2,1)S(1)}, u32[]{:S(2)}, u32[]{:S(2)}) async-start(bf16[16,32,512]{2,1,0:T(8,128)(2,1)} %get-tuple-element.87), calls=%async_computation.1 | async-start | bytes 1048576 | tf_op jit(solution)/shard_map/all_to_all | solution.py:453
  62.3 14.4 %collective-permute-start.16 = (bf16[32,3584]{1,0:T(8,128)(2,1)}, bf16[32,3584]{1,0:T(8,128)(2,1)S(1)}, u32[]{:S(2)}, u32[]{:S(2)}) collective-permute-start(bf16[32,3584]{1,0:T(8,128)(2,1)} %copy-done.10), channel_id=1, source_target_pairs={{0,4},{1,5},{2,6},{3,7},{4,0},{5,1},{6,2},{7,3},{8,12},{9,13},{10,... | collective-permute-start | bytes 688136 | tf_op jit(solution)/shard_map/ppermute | solution.py:37
  65.2 16.3 %collective-permute-start.17 = (bf16[32,3584]{1,0:T(8,128)(2,1)}, bf16[32,3584]{1,0:T(8,128)(2,1)S(1)}, u32[]{:S(2)}, u32[]{:S(2)}) collective-permute-start(bf16[32,3584]{1,0:T(8,128)(2,1)} %copy-done.9), channel_id=1, source_target_pairs={{0,2},{1,3},{2,4},{3,5},{4,6},{5,7},{6,0},{7,1},{8,10},{9,11},{10,... | collective-permute-start | bytes 688136 | tf_op jit(solution)/shard_map/ppermute | solution.py:37
  65.5 16.0 %collective-permute-start.18 = (bf16[32,3584]{1,0:T(8,128)(2,1)}, bf16[32,3584]{1,0:T(8,128)(2,1)S(1)}, u32[]{:S(2)}, u32[]{:S(2)}) collective-permute-start(bf16[32,3584]{1,0:T(8,128)(2,1)} %copy-done.8), channel_id=1, source_target_pairs={{0,6},{1,7},{2,0},{3,1},{4,2},{5,3},{6,4},{7,5},{8,14},{9,15},{10,... | collective-permute-start | bytes 688136 | tf_op jit(solution)/shard_map/ppermute | solution.py:37
  68.1 14.0 %collective-permute-start.14 = (bf16[32,2560]{1,0:T(8,128)(2,1)S(1)}, bf16[32,2560]{1,0:T(8,128)(2,1)S(1)}, u32[]{:S(2)}, u32[]{:S(2)}) collective-permute-start(bf16[32,2560]{1,0:T(8,128)(2,1)S(1)} %get-tuple-element.79), channel_id=1, source_target_pairs={{0,8},{1,9},{2,10},{3,11},{4,12},{5,13},{6,14},{7,15},{8,0},{9,1},... | collective-permute-start | bytes 491528 | tf_op jit(solution)/shard_map/ppermute | solution.py:37
  69.4 12.7 %collective-permute-start.15 = (bf16[32,2048]{1,0:T(8,128)(2,1)S(1)}, bf16[32,2048]{1,0:T(8,128)(2,1)S(1)}, u32[]{:S(2)}, u32[]{:S(2)}) collective-permute-start(bf16[32,2048]{1,0:T(8,128)(2,1)S(1)} %get-tuple-element.80), channel_id=1, source_target_pairs={{0,8},{1,9},{2,10},{3,11},{4,12},{5,13},{6,14},{7,15},{8,0},{9,1},... | collective-permute-start | bytes 393224 | tf_op jit(solution)/shard_map/ppermute | solution.py:37
  82.1 0.9 %copy-start.5 = (bf16[32,3584]{1,0:T(8,128)(2,1)S(1)}, bf16[32,3584]{1,0:T(8,128)(2,1)}, u32[]{:S(2)}) copy-start(bf16[32,3584]{1,0:T(8,128)(2,1)} %copy-done.4) | copy-start | bytes 688132

commit v10 on v9

--- a/solution.py
+++ b/solution.py
@@ -447,9 +447,9 @@
     right, left, mark = near(right, left, far_right, far_left, [mark])
     from_left, from_right = send(right, 0, 1, 0), send(left, 0, 3, 0)
     table, mark = up_table(resident_up_maps, target, maps, [mark])
+    raised, mark = raise_features(part, other, table, slot, [mark])
     *low, mark = turn_narrow(keep, narrow_y, [mark])
     low_in = [send(low[d], 0, d, 0) for d in (2, 1, 3)]
-    raised, mark = raise_features(part, other, table, slot, [mark])
     delta = lax.all_to_all(raised, "tp", split_axis=0, concat_axis=0, tiled=True)
 
     wide_keep, wide_send, wide_rest, mark = turn_wide(here, from_left, from_right, [mark])

time: 84.5 us -> 84.5 us (level)
  Pallas kernels: 28 us -> 29.7 us
  starting transfers between devices: 32.9 us -> 31.8 us
    pallas_call x15, Pallas kernels: 28 us -> 29.7 us  [call(): pl.pallas_call(body, in_specs=list(specs or [VM] * count) + [LATER] * len...]
    ppermute x17, starting transfers between devices: 18 us -> 17 us  [send(): return lax.ppermute(array, 'tp', route(yy, xx, cc))]
    unnamed x22 -> x20, local copies, waits for them, and re-layouts: 3.07 us -> 2.65 us
  transfers between devices with their start and end apart: 21 -> 21, of which waited for: 6 -> 6; matrix products, arithmetic and copies ran while one was open for 0% -> 0% of each run, Pallas kernels for 32% -> 34%
where the time goes in v10:
time: 84.5 us; the launch traced here: 84.1 us
  starting transfers between devices  31.8 us (38%)
  Pallas kernels  29.7 us (35%)
  waiting for transfers between devices  19.7 us (23%)
  local copies, waits for them, and re-layouts  2.65 us (3%)
    pallas_call x15, Pallas kernels, call(): pl.pallas_call(body, in_specs=list(specs or [VM] * count) + [LATER] * len...  29.7 us
    ppermute x17, starting transfers between devices, send(): return lax.ppermute(array, 'tp', route(yy, xx, cc))  17 us
    ppermute x17, waiting for transfers between devices, send(): return lax.ppermute(array, 'tp', route(yy, xx, cc))  12.4 us
    ppermute x2, waiting for transfers between devices, trade(): return lax.ppermute(array, 'tp', pairs)  7.31 us
    all_to_all x1, starting transfers between devices, local(): lax.all_to_all(fresh_adapter_bundle.reshape(16, 256, 128), 'tp', split_ax...  6.83 us
    all_to_all x1, starting transfers between devices, local(): lax.all_to_all(raised, 'tp', split_axis=0, concat_axis=0, tiled=True)  6.58 us
    unnamed x20, local copies, waits for them, and re-layouts  2.65 us
  transfers between devices with their start and end apart: 21, of which 6 were waited for; matrix products, arithmetic and copies ran while one was open for 0% of the time, Pallas kernels for 34%

profile of v10, /device:TPU:1, one launch (start us, length us, event | category | flops | bytes accessed | tf_op | source)
XLA Modules:
  0.0 84.1 jit_solution(9547058414569632915)
XLA Ops:
  0.0 6.8 %all-to-all-start = ((bf16[16,256,128]{2,1,0:T(8,128)(2,1)}), bf16[16,256,128]{2,1,0:T(8,128)(2,1)S(1)}, u32[]{:S(2)}, u32[]{:S(2)}) async-start(bf16[16,256,128]{2,1,0:T(8,128)(2,1)} %bitcast.4), calls=%async_computation | async-start | bytes 2097152 | tf_op jit(solution)/shard_map/all_to_all | solution.py:420
  6.8 6.7 %product.2 = (bf16[256,1792]{1,0:T(8,128)(2,1)}, bf16[256,1792]{1,0:T(8,128)(2,1)}, bf16[256,3584]{1,0:T(8,128)(2,1)}, f32[8,128]{1,0:T(8,128)}) custom-call(bf16[512,512]{1,0:T(8,128)(2,1)} %refs_0_.7, bf16[512,8192]{1,0:T(8,128)(2,1)} %refs_1_.5), custom_call_target="tpu_custom_call" | custom-call | flops 1024 | bytes 1024 | tf_op jit(solution)/shard_map/product/pallas_call | solution.py:88
  13.6 0.2 collective-permute-start.3
  13.7 0.4 collective-permute-start.4
  14.2 8.0 %product.3 = (bf16[256,1536]{1,0:T(8,128)(2,1)}, bf16[256,1536]{1,0:T(8,128)(2,1)}, bf16[256,1536]{1,0:T(8,128)(2,1)}, bf16[256,4608]{1,0:T(8,128)(2,1)}, f32[8,128]{1,0:T(8,128)}) custom-call(bf16[512,512]{1,0:T(8,128)(2,1)} %refs_0_.7, bf16[512,8192]{1,0:T(8,128)(2,1)} %refs_1_.5, f32[8,128]{1,0:T(8,128)} %get-tuple-element.47.refs_2_), custom_call_target="tpu_custom_call" | custom-call | flops 1024 | bytes 1024 | tf_op jit(solution)/shard_map/product/pallas_call | solution.py:88
  22.2 0.2 collective-permute-start
  22.4 0.4 collective-permute-start.1
  22.8 0.1 collective-permute-start.2
  22.9 0.0 collective-permute-done.3.refs_1_
  22.9 0.0 collective-permute-done.4.refs_2_
  22.9 0.0 all-to-all-done.refs_3_.refs_4_.refs_2_
  22.9 2.5 %chip_narrow.1 = (bf16[128,3584]{1,0:T(8,128)(2,1)S(1)}, bf16[128,3584]{1,0:T(8,128)(2,1)}, f32[8,128]{1,0:T(8,128)}) custom-call(bf16[256,3584]{1,0:T(8,128)(2,1)} %get-tuple-element.52.refs_0_, bf16[256,1792]{1,0:T(8,128)(2,1)S(1)} %collective-permute-done.3.refs_1_, bf16[256,1792]{1,0:T(8,128)(2,1)S(1)} %collective-permute-done.4.refs_2_, ...), custom_call_target="tpu_custom_call" | custom-call | flops 1024 | bytes 1024 | tf_op jit(solution)/shard_map/chip_narrow/pallas_call | solution.py:88
  25.5 0.0 copy-start.3
  25.5 0.9 %copy-done.3 = bf16[128,3584]{1,0:T(8,128)(2,1)} copy-done((bf16[128,3584]{1,0:T(8,128)(2,1)}, bf16[128,3584]{1,0:T(8,128)(2,1)S(1)}, u32[]{:S(2)}) %copy-start.3) | copy-done | bytes 917528
  26.4 1.6 %collective-permute-start.12 = (bf16[128,3584]{1,0:T(8,128)(2,1)}, bf16[128,3584]{1,0:T(8,128)(2,1)S(1)}, u32[]{:S(2)}, u32[]{:S(2)}) collective-permute-start(bf16[128,3584]{1,0:T(8,128)(2,1)} %get-tuple-element.55.refs_4_), channel_id=1, source_target_pairs={{0,8},{1,9},{2,10},{3,11},{4,12},{5,13},{6,14},{7,15},{8,0},{9,1},... | collective-permute-start | bytes 2752520 | tf_op jit(solution)/shard_map/ppermute | solution.py:37
  28.0 0.0 collective-permute-done.refs_1_
  28.0 0.0 collective-permute-done.1.refs_2_
  28.0 0.0 collective-permute-done.2.refs_3_
  28.0 0.0 copy-start
  28.1 0.0 copy-start.1
  28.1 0.0 copy-start.8
  28.1 0.0 copy-start.9
  28.1 2.6 %chip_wide.1 = (bf16[64,4608]{1,0:T(8,128)(2,1)S(1)}, bf16[64,4608]{1,0:T(8,128)(2,1)S(1)}, bf16[64,2304]{1,0:T(8,128)(2,1)S(1)}, bf16[64,2304]{1,0:T(8,128)(2,1...) custom-call(bf16[256,4608]{1,0:T(8,128)(2,1)} %get-tuple-element.48.refs_0_, ...), custom_call_target="tpu_custom_call" | custom-call | flops 1024 | bytes 1024 | tf_op jit(solution)/shard_map/chip_wide/pallas_call | solution.py:88
  30.7 1.3 %collective-permute-start.5 = (bf16[64,2304]{1,0:T(8,128)(2,1)S(1)}, bf16[64,2304]{1,0:T(8,128)(2,1)S(1)}, u32[]{:S(2)}, u32[]{:S(2)}) collective-permute-start(bf16[64,2304]{1,0:T(8,128)(2,1)S(1)} %get-tuple-element.59), channel_id=1, source_target_pairs={{0,2},{1,3},{2,4},{3,5},{4,6},{5,7},{6,0},{7,1},{8,10},{9,11},{10,... | collective-permute-start | bytes 884744 | tf_op jit(solution)/shard_map/ppermute | solution.py:37
  32.0 1.5 %collective-permute-start.6 = (bf16[64,2304]{1,0:T(8,128)(2,1)S(1)}, bf16[64,2304]{1,0:T(8,128)(2,1)S(1)}, u32[]{:S(2)}, u32[]{:S(2)}) collective-permute-start(bf16[64,2304]{1,0:T(8,128)(2,1)S(1)} %get-tuple-element.60), channel_id=1, source_target_pairs={{0,6},{1,7},{2,0},{3,1},{4,2},{5,3},{6,4},{7,5},{8,14},{9,15},{10,... | collective-permute-start | bytes 884744 | tf_op jit(solution)/shard_map/ppermute | solution.py:37
  33.5 0.0 copy-start.2
  33.5 2.3 %shrink_part.1 = (bf16[256,128]{1,0:T(8,128)(2,1)S(1)}, f32[8,128]{1,0:T(8,128)S(1)}) custom-call(bf16[512,512]{1,0:T(8,128)(2,1)S(1)} %copy-done, bf16[512,1024]{1,0:T(8,128)(2,1)S(1)} %copy-done.1, s32[1,512]{1,0:T(1,128)S(1)} %bitcast.2, s32[16]{0:T(128)S(1)} %copy-done.9, bf16[16,256,128]{2,1,0:T(8,128)(2,1)S(1)} %all-to-all-done.refs_3_.refs_4_.refs_2_, ...), custom_call_target="tpu_custom_call" | custom-call | flops 1024 | bytes 1024 | tf_op jit(solution)/shard_map/shrink_part/pallas_call | solution.py:88
  35.8 1.1 %collective-permute-start.7 = (bf16[256,128]{1,0:T(8,128)(2,1)S(1)}, bf16[256,128]{1,0:T(8,128)(2,1)S(1)}, u32[]{:S(2)}, u32[]{:S(2)}) collective-permute-start(bf16[256,128]{1,0:T(8,128)(2,1)S(1)} %get-tuple-element.62.refs_0_), channel_id=1, source_target_pairs={{0,1},{1,0},{2,3},{3,2},{4,5},{5,4},{6,7},{7,6},{8,9},{9,8},{10,11... | collective-permute-start | bytes 196616 | tf_op jit(solution)/shard_map/ppermute | solution.py:37
  36.9 0.9 %collective-permute-done.7.refs_1_ = bf16[256,128]{1,0:T(8,128)(2,1)S(1)} collective-permute-done((bf16[256,128]{1,0:T(8,128)(2,1)S(1)}, bf16[256,128]{1,0:T(8,128)(2,1)S(1)}, u32[]{:S(2)}, u32[]{:S(2)}) %collective-permute-start.7) | collective-permute-done | bytes 65568 | tf_op jit(solution)/shard_map/ppermute | solution.py:37
  37.8 0.1 collective-permute-start.8
  37.9 4.2 %collective-permute-done.8.refs_1_ = bf16[256,128]{1,0:T(8,128)(2,1)S(1)} collective-permute-done((bf16[256,128]{1,0:T(8,128)(2,1)S(1)}, bf16[256,128]{1,0:T(8,128)(2,1)S(1)}, u32[]{:S(2)}, u32[]{:S(2)}) %collective-permute-start.8) | collective-permute-done | bytes 65568 | tf_op jit(solution)/shard_map/ppermute | solution.py:47
  42.1 1.3 %collective-permute-start.9 = (bf16[256,128]{1,0:T(8,128)(2,1)S(1)}, bf16[256,128]{1,0:T(8,128)(2,1)S(1)}, u32[]{:S(2)}, u32[]{:S(2)}) collective-permute-start(bf16[256,128]{1,0:T(8,128)(2,1)S(1)} %get-tuple-element.66.refs_0_), channel_id=1, source_target_pairs={{0,6},{1,7},{2,4},{3,5},{4,2},{5,3},{6,0},{7,1},{8,14},{9,15},{10,... | collective-permute-start | bytes 196616 | tf_op jit(solution)/shard_map/ppermute | solution.py:47
  43.4 3.1 %collective-permute-done.9.refs_1_ = bf16[256,128]{1,0:T(8,128)(2,1)S(1)} collective-permute-done((bf16[256,128]{1,0:T(8,128)(2,1)S(1)}, bf16[256,128]{1,0:T(8,128)(2,1)S(1)}, u32[]{:S(2)}, u32[]{:S(2)}) %collective-permute-start.9) | collective-permute-done | bytes 65568 | tf_op jit(solution)/shard_map/ppermute | solution.py:47
  46.5 0.0 collective-permute-done.5.refs_2_
  46.5 0.0 collective-permute-done.6.refs_3_
  46.5 1.1 %near.1 = (bf16[64,4608]{1,0:T(8,128)(2,1)}, bf16[64,4608]{1,0:T(8,128)(2,1)}, f32[8,128]{1,0:T(8,128)S(1)}) custom-call(bf16[64,4608]{1,0:T(8,128)(2,1)S(1)} %get-tuple-element.57.refs_0_, bf16[64,4608]{1,0:T(8,128)(2,1)S(1)} %get-tuple-element.58.refs_1_, bf16[64,2304]{1,0:T(8,128)(2,1)S(1)} %collective-permute-done.5.refs_2_, ...), custom_call_target="tpu_custom_call" | custom-call | flops 1024 | bytes 1024 | tf_op jit(solution)/shard_map/near/pallas_call | solution.py:88
  47.7 0.0 collective-permute-start.10
  47.7 2.7 %collective-permute-start.11 = (bf16[64,4608]{1,0:T(8,128)(2,1)}, bf16[64,4608]{1,0:T(8,128)(2,1)}, u32[]{:S(2)}, u32[]{:S(2)}) collective-permute-start(bf16[64,4608]{1,0:T(8,128)(2,1)} %get-tuple-element.70), channel_id=1, source_target_pairs={{0,6},{1,7},{2,0},{3,1},{4,2},{5,3},{6,4},{7,5},{8,14},{9,15},{10,... | collective-permute-start | bytes 1769480 | tf_op jit(solution)/shard_map/ppermute | solution.py:37
  50.3 0.4 collective-permute-start.13
  50.7 1.4 %up_table.1 = (bf16[1024,512]{1,0:T(8,128)(2,1)S(1)}, f32[8,128]{1,0:T(8,128)S(1)}) custom-call(bf16[1024,512]{1,0:T(8,128)(2,1)S(1)} %copy-done.2, s32[16]{0:T(128)S(1)} %copy-done.9, bf16[16,256,128]{2,1,0:T(8,128)(2,1)S(1)} %all-to-all-done.refs_3_.refs_4_.refs_2_, f32[8,128]{1,0:T(8,128)S(1)} %get-tuple-element.73.refs_3_), custom_call_target="tpu_custom_call" | custom-call | flops 1024 | bytes 1024 | tf_op jit(solution)/shard_map/up_table/pallas_call | solution.py:88
  52.1 1.8 %collective-permute-done.13.refs_1_ = bf16[256,128]{1,0:T(8,128)(2,1)S(1)} collective-permute-done((bf16[256,128]{1,0:T(8,128)(2,1)S(1)}, bf16[256,128]{1,0:T(8,128)(2,1)S(1)}, u32[]{:S(2)}, u32[]{:S(2)}) %collective-permute-start.13) | collective-permute-done | bytes 65568 | tf_op jit(solution)/shard_map/ppermute | solution.py:37
  53.9 1.7 %raise_features.1 = (bf16[16,32,512]{2,1,0:T(8,128)(2,1)}, f32[8,128]{1,0:T(8,128)S(1)}) custom-call(bf16[256,128]{1,0:T(8,128)(2,1)S(1)} %get-tuple-element.72.refs_0_, bf16[256,128]{1,0:T(8,128)(2,1)S(1)} %collective-permute-done.13.refs_1_, bf16[1024,512]{1,0:T(8,128)(2,1)S(1)} %get-tuple-element.74.refs_2_, s32[1,512]{1,0:T(1,128)S(1)} %bitcast.3, ...), custom_call_target="tpu_custom_call" | custom-call | flops 1024 | bytes 1024 | tf_op jit(solution)/shard_map/raise_features/pallas_call | solution.py:88
  55.6 6.6 %all-to-all-start.1 = ((bf16[16,32,512]{2,1,0:T(8,128)(2,1)}), bf16[16,32,512]{2,1,0:T(8,128)(2,1)S(1)}, u32[]{:S(2)}, u32[]{:S(2)}) async-start(bf16[16,32,512]{2,1,0:T(8,128)(2,1)} %get-tuple-element.87), calls=%async_computation.1 | async-start | bytes 1048576 | tf_op jit(solution)/shard_map/all_to_all | solution.py:453
  62.1 0.0 collective-permute-done.12.refs_1_
  62.2 0.2 turn_narrow.1
  62.4 0.7 copy-done.6
  63.1 2.9 %collective-permute-start.16 = (bf16[32,3584]{1,0:T(8,128)(2,1)S(1)}, bf16[32,3584]{1,0:T(8,128)(2,1)S(1)}, u32[]{:S(2)}, u32[]{:S(2)}) collective-permute-start(bf16[32,3584]{1,0:T(8,128)(2,1)S(1)} %get-tuple-element.82), channel_id=1, source_target_pairs={{0,4},{1,5},{2,6},{3,7},{4,0},{5,1},{6,2},{7,3},{8,12},{9,13},{10,... | collective-permute-start | bytes 688136 | tf_op jit(solution)/shard_map/ppermute | solution.py:37
  66.0 0.3 collective-permute-start.17
  66.3 2.4 %collective-permute-start.18 = (bf16[32,3584]{1,0:T(8,128)(2,1)S(1)}, bf16[32,3584]{1,0:T(8,128)(2,1)S(1)}, u32[]{:S(2)}, u32[]{:S(2)}) collective-permute-start(bf16[32,3584]{1,0:T(8,128)(2,1)S(1)} %get-tuple-element.84), channel_id=1, source_target_pairs={{0,6},{1,7},{2,0},{3,1},{4,2},{5,3},{6,4},{7,5},{8,14},{9,15},{10,... | collective-permute-start | bytes 688136 | tf_op jit(solution)/shard_map/ppermute | solution.py:37
  68.6 0.0 collective-permute-done.10.refs_1_
  68.7 0.0 collective-permute-done.11.refs_2_
  68.7 1.4 %turn_wide.1 = (f32[32,4608]{1,0:T(8,128)S(1)}, bf16[32,2560]{1,0:T(8,128)(2,1)S(1)}, bf16[32,2048]{1,0:T(8,128)(2,1)S(1)}, f32[8,128]{1,0:T(8,128)S(1)}) custom-call(bf16[64,4608]{1,0:T(8,128)(2,1)S(1)} %get-tuple-element.56.refs_0_, bf16[64,4608]{1,0:T(8,128)(2,1)} %collective-permute-done.10.refs_1_, bf16[64,4608]{1,0:T(8,128)(2,1)} %collective-permute-done.11.refs_2_, ...), custom_call_target="tpu_custom_call" | custom-call | flops 1024 | bytes 1024 | tf_op jit(solution)/shard_map/turn_wide/pallas_call | solution.py:88
  70.1 1.3 %collective-permute-start.14 = (bf16[32,2560]{1,0:T(8,128)(2,1)S(1)}, bf16[32,2560]{1,0:T(8,128)(2,1)S(1)}, u32[]{:S(2)}, u32[]{:S(2)}) collective-permute-start(bf16[32,2560]{1,0:T(8,128)(2,1)S(1)} %get-tuple-element.79), channel_id=1, source_target_pairs={{0,8},{1,9},{2,10},{3,11},{4,12},{5,13},{6,14},{7,15},{8,0},{9,1},... | collective-permute-start | bytes 491528 | tf_op jit(solution)/shard_map/ppermute | solution.py:37
  71.4 0.2 collective-permute-start.15
  71.7 4.9 %collective-permute-done.16.refs_0_ = bf16[32,3584]{1,0:T(8,128)(2,1)S(1)} collective-permute-done((bf16[32,3584]{1,0:T(8,128)(2,1)S(1)}, bf16[32,3584]{1,0:T(8,128)(2,1)S(1)}, u32[]{:S(2)}, u32[]{:S(2)}) %collective-permute-start.16) | collective-permute-done | bytes 229408 | tf_op jit(solution)/shard_map/ppermute | solution.py:37
  76.6 4.8 %collective-permute-done.17.refs_1_ = bf16[32,3584]{1,0:T(8,128)(2,1)S(1)} collective-permute-done((bf16[32,3584]{1,0:T(8,128)(2,1)S(1)}, bf16[32,3584]{1,0:T(8,128)(2,1)S(1)}, u32[]{:S(2)}, u32[]{:S(2)}) %collective-permute-start.17) | collective-permute-done | bytes 229408 | tf_op jit(solution)/shard_map/ppermute | solution.py:37
  81.4 0.0 collective-permute-done.18.refs_2_
  81.4 0.6 add_parts.7
  82.0 0.0 all-to-all-done.1.refs_6_
  82.0 0.0 collective-permute-done.15.refs_3_
  82.0 0.0 collective-permute-done.14.refs_2_
  82.0 0.0 copy-start.5
  82.0 1.0 %copy-done.5 = bf16[32,8192]{1,0:T(8,128)(2,1)S(1)} copy-done((bf16[32,8192]{1,0:T(8,128)(2,1)S(1)}, bf16[32,8192]{1,0:T(8,128)(2,1)}, u32[]{:S(2)}) %copy-start.5) | copy-done | bytes 524312
  83.1 1.0 %finish.1 = (bf16[32,8192]{1,0:T(8,128)(2,1)}, f32[8,128]{1,0:T(8,128)}) custom-call(bf16[32,8192]{1,0:T(8,128)(2,1)S(1)} %copy-done.5, f32[32,4608]{1,0:T(8,128)S(1)} %get-tuple-element.78.refs_1_, bf16[32,2560]{1,0:T(8,128)(2,1)S(1)} %collective-permute-done.14.refs_2_, bf16[32,2048]{1,0:T(8,128)(2,1)S(1)} %collective-permute-done.15.refs_3_, ...), custom_call_target="tpu_custom_call" | custom-call | flops 1024 | bytes 1024 | tf_op jit(solution)/shard_map/finish/pallas_call | solution.py:88
  (13 shorter events, 0.1 us)
Async XLA Ops:
  0.0 22.9 %all-to-all-start = ((bf16[16,256,128]{2,1,0:T(8,128)(2,1)}), bf16[16,256,128]{2,1,0:T(8,128)(2,1)S(1)}, u32[]{:S(2)}, u32[]{:S(2)}) async-start(bf16[16,256,128]{2,1,0:T(8,128)(2,1)} %bitcast.4), calls=%async_computation | async-start | bytes 2097152 | tf_op jit(solution)/shard_map/all_to_all | solution.py:420
  13.6 9.3 %collective-permute-start.3 = (bf16[256,1792]{1,0:T(8,128)(2,1)}, bf16[256,1792]{1,0:T(8,128)(2,1)S(1)}, u32[]{:S(2)}, u32[]{:S(2)}) collective-permute-start(bf16[256,1792]{1,0:T(8,128)(2,1)} %get-tuple-element.53), channel_id=1, source_target_pairs={{0,1},{1,0},{2,3},{3,2},{4,5},{5,4},{6,7},{7,6},{8,9},{9,8},{10,11... | collective-permute-start | bytes 2752520 | tf_op jit(solution)/shard_map/ppermute | solution.py:37
  13.7 9.2 %collective-permute-start.4 = (bf16[256,1792]{1,0:T(8,128)(2,1)}, bf16[256,1792]{1,0:T(8,128)(2,1)S(1)}, u32[]{:S(2)}, u32[]{:S(2)}) collective-permute-start(bf16[256,1792]{1,0:T(8,128)(2,1)} %get-tuple-element.54), channel_id=1, source_target_pairs={{0,1},{1,0},{2,3},{3,2},{4,5},{5,4},{6,7},{7,6},{8,9},{9,8},{10,11... | collective-permute-start | bytes 2752520 | tf_op jit(solution)/shard_map/ppermute | solution.py:37
  22.2 5.8 %collective-permute-start = (bf16[256,1536]{1,0:T(8,128)(2,1)}, bf16[256,1536]{1,0:T(8,128)(2,1)}, u32[]{:S(2)}, u32[]{:S(2)}) collective-permute-start(bf16[256,1536]{1,0:T(8,128)(2,1)} %get-tuple-element.49), channel_id=1, source_target_pairs={{0,1},{1,0},{2,3},{3,2},{4,5},{5,4},{6,7},{7,6},{8,9},{9,8},{10,11... | collective-permute-start | bytes 2359304 | tf_op jit(solution)/shard_map/ppermute | solution.py:37
  22.4 5.7 %collective-permute-start.1 = (bf16[256,1536]{1,0:T(8,128)(2,1)}, bf16[256,1536]{1,0:T(8,128)(2,1)}, u32[]{:S(2)}, u32[]{:S(2)}) collective-permute-start(bf16[256,1536]{1,0:T(8,128)(2,1)} %get-tuple-element.50), channel_id=1, source_target_pairs={{0,1},{1,0},{2,3},{3,2},{4,5},{5,4},{6,7},{7,6},{8,9},{9,8},{10,11... | collective-permute-start | bytes 2359304 | tf_op jit(solution)/shard_map/ppermute | solution.py:37
  22.8 5.2 %collective-permute-start.2 = (bf16[256,1536]{1,0:T(8,128)(2,1)}, bf16[256,1536]{1,0:T(8,128)(2,1)}, u32[]{:S(2)}, u32[]{:S(2)}) collective-permute-start(bf16[256,1536]{1,0:T(8,128)(2,1)} %get-tuple-element.51), channel_id=1, source_target_pairs={{0,1},{1,0},{2,3},{3,2},{4,5},{5,4},{6,7},{7,6},{8,9},{9,8},{10,11... | collective-permute-start | bytes 2359304 | tf_op jit(solution)/shard_map/ppermute | solution.py:37
  25.5 0.9 %copy-start.3 = (bf16[128,3584]{1,0:T(8,128)(2,1)}, bf16[128,3584]{1,0:T(8,128)(2,1)S(1)}, u32[]{:S(2)}) copy-start(bf16[128,3584]{1,0:T(8,128)(2,1)S(1)} %get-tuple-element.71.refs_0_) | copy-start | bytes 2752516
  26.4 35.8 %collective-permute-start.12 = (bf16[128,3584]{1,0:T(8,128)(2,1)}, bf16[128,3584]{1,0:T(8,128)(2,1)S(1)}, u32[]{:S(2)}, u32[]{:S(2)}) collective-permute-start(bf16[128,3584]{1,0:T(8,128)(2,1)} %get-tuple-element.55.refs_4_), channel_id=1, source_target_pairs={{0,8},{1,9},{2,10},{3,11},{4,12},{5,13},{6,14},{7,15},{8,0},{9,1},... | collective-permute-start | bytes 2752520 | tf_op jit(solution)/shard_map/ppermute | solution.py:37
  28.0 5.4 %copy-start = (bf16[512,512]{1,0:T(8,128)(2,1)S(1)}, bf16[512,512]{1,0:T(8,128)(2,1)}, u32[]{:S(2)}) copy-start(bf16[512,512]{1,0:T(8,128)(2,1)} %refs_0_.7) | copy-start | bytes 1572868
  28.1 5.4 %copy-start.1 = (bf16[512,1024]{1,0:T(8,128)(2,1)S(1)}, bf16[512,1024]{1,0:T(8,128)(2,1)}, u32[]{:S(2)}) copy-start(bf16[512,1024]{1,0:T(8,128)(2,1)} %refs_1_.6) | copy-start | bytes 3145732
  28.1 5.4 %copy-start.8 = (s32[512]{0:T(512)S(1)}, s32[512]{0:T(512)}, u32[]{:S(2)}) copy-start(s32[512]{0:T(512)} %param.15) | copy-start | bytes 6148
  28.1 5.4 %copy-start.9 = (s32[16]{0:T(128)S(1)}, s32[16]{0:T(128)}, u32[]{:S(2)}) copy-start(s32[16]{0:T(128)} %refs_1_.7) | copy-start | bytes 196
  30.7 15.8 %collective-permute-start.5 = (bf16[64,2304]{1,0:T(8,128)(2,1)S(1)}, bf16[64,2304]{1,0:T(8,128)(2,1)S(1)}, u32[]{:S(2)}, u32[]{:S(2)}) collective-permute-start(bf16[64,2304]{1,0:T(8,128)(2,1)S(1)} %get-tuple-element.59), channel_id=1, source_target_pairs={{0,2},{1,3},{2,4},{3,5},{4,6},{5,7},{6,0},{7,1},{8,10},{9,11},{10,... | collective-permute-start | bytes 884744 | tf_op jit(solution)/shard_map/ppermute | solution.py:37
  32.0 14.5 %collective-permute-start.6 = (bf16[64,2304]{1,0:T(8,128)(2,1)S(1)}, bf16[64,2304]{1,0:T(8,128)(2,1)S(1)}, u32[]{:S(2)}, u32[]{:S(2)}) collective-permute-start(bf16[64,2304]{1,0:T(8,128)(2,1)S(1)} %get-tuple-element.60), channel_id=1, source_target_pairs={{0,6},{1,7},{2,0},{3,1},{4,2},{5,3},{6,4},{7,5},{8,14},{9,15},{10,... | collective-permute-start | bytes 884744 | tf_op jit(solution)/shard_map/ppermute | solution.py:37
  33.5 17.2 %copy-start.2 = (bf16[1024,512]{1,0:T(8,128)(2,1)S(1)}, bf16[1024,512]{1,0:T(8,128)(2,1)}, u32[]{:S(2)}) copy-start(bf16[1024,512]{1,0:T(8,128)(2,1)} %refs_0_.8) | copy-start | bytes 3145732
  35.8 2.0 %collective-permute-start.7 = (bf16[256,128]{1,0:T(8,128)(2,1)S(1)}, bf16[256,128]{1,0:T(8,128)(2,1)S(1)}, u32[]{:S(2)}, u32[]{:S(2)}) collective-permute-start(bf16[256,128]{1,0:T(8,128)(2,1)S(1)} %get-tuple-element.62.refs_0_), channel_id=1, source_target_pairs={{0,1},{1,0},{2,3},{3,2},{4,5},{5,4},{6,7},{7,6},{8,9},{9,8},{10,11... | collective-permute-start | bytes 196616 | tf_op jit(solution)/shard_map/ppermute | solution.py:37
  37.8 4.3 %collective-permute-start.8 = (bf16[256,128]{1,0:T(8,128)(2,1)S(1)}, bf16[256,128]{1,0:T(8,128)(2,1)S(1)}, u32[]{:S(2)}, u32[]{:S(2)}) collective-permute-start(bf16[256,128]{1,0:T(8,128)(2,1)S(1)} %get-tuple-element.64.refs_0_), channel_id=1, source_target_pairs={{0,2},{1,3},{2,0},{3,1},{4,6},{5,7},{6,4},{7,5},{8,10},{9,11},{10,... | collective-permute-start | bytes 196616 | tf_op jit(solution)/shard_map/ppermute | solution.py:47
  42.1 4.4 %collective-permute-start.9 = (bf16[256,128]{1,0:T(8,128)(2,1)S(1)}, bf16[256,128]{1,0:T(8,128)(2,1)S(1)}, u32[]{:S(2)}, u32[]{:S(2)}) collective-permute-start(bf16[256,128]{1,0:T(8,128)(2,1)S(1)} %get-tuple-element.66.refs_0_), channel_id=1, source_target_pairs={{0,6},{1,7},{2,4},{3,5},{4,2},{5,3},{6,0},{7,1},{8,14},{9,15},{10,... | collective-permute-start | bytes 196616 | tf_op jit(solution)/shard_map/ppermute | solution.py:47
  47.7 14.5 %copy-start.4 = (bf16[128,3584]{1,0:T(8,128)(2,1)S(1)}, bf16[128,3584]{1,0:T(8,128)(2,1)}, u32[]{:S(2)}) copy-start(bf16[128,3584]{1,0:T(8,128)(2,1)} %copy-done.3) | copy-start | bytes 2752516
  47.7 21.0 %collective-permute-start.10 = (bf16[64,4608]{1,0:T(8,128)(2,1)}, bf16[64,4608]{1,0:T(8,128)(2,1)}, u32[]{:S(2)}, u32[]{:S(2)}) collective-permute-start(bf16[64,4608]{1,0:T(8,128)(2,1)} %get-tuple-element.69), channel_id=1, source_target_pairs={{0,2},{1,3},{2,4},{3,5},{4,6},{5,7},{6,0},{7,1},{8,10},{9,11},{10,... | collective-permute-start | bytes 1769480 | tf_op jit(solution)/shard_map/ppermute | solution.py:37
  47.7 21.0 %collective-permute-start.11 = (bf16[64,4608]{1,0:T(8,128)(2,1)}, bf16[64,4608]{1,0:T(8,128)(2,1)}, u32[]{:S(2)}, u32[]{:S(2)}) collective-permute-start(bf16[64,4608]{1,0:T(8,128)(2,1)} %get-tuple-element.70), channel_id=1, source_target_pairs={{0,6},{1,7},{2,0},{3,1},{4,2},{5,3},{6,4},{7,5},{8,14},{9,15},{10,... | collective-permute-start | bytes 1769480 | tf_op jit(solution)/shard_map/ppermute | solution.py:37
  50.3 3.5 %collective-permute-start.13 = (bf16[256,128]{1,0:T(8,128)(2,1)S(1)}, bf16[256,128]{1,0:T(8,128)(2,1)S(1)}, u32[]{:S(2)}, u32[]{:S(2)}) collective-permute-start(bf16[256,128]{1,0:T(8,128)(2,1)S(1)} %get-tuple-element.72.refs_0_), channel_id=1, source_target_pairs={{0,8},{1,9},{2,10},{3,11},{4,12},{5,13},{6,14},{7,15},{8,0},{9,1},... | collective-permute-start | bytes 196616 | tf_op jit(solution)/shard_map/ppermute | solution.py:37
  55.6 26.4 %all-to-all-start.1 = ((bf16[16,32,512]{2,1,0:T(8,128)(2,1)}), bf16[16,32,512]{2,1,0:T(8,128)(2,1)S(1)}, u32[]{:S(2)}, u32[]{:S(2)}) async-start(bf16[16,32,512]{2,1,0:T(8,128)(2,1)} %get-tuple-element.87), calls=%async_computation.1 | async-start | bytes 1048576 | tf_op jit(solution)/shard_map/all_to_all | solution.py:453
  62.4 0.7 copy-start.6
  63.1 18.9 %copy-start.7 = (bf16[32,3584]{1,0:T(8,128)(2,1)S(1)}, bf16[32,3584]{1,0:T(8,128)(2,1)}, u32[]{:S(2)}) copy-start(bf16[32,3584]{1,0:T(8,128)(2,1)} %copy-done.6) | copy-start | bytes 688132
  63.1 13.5 %collective-permute-start.16 = (bf16[32,3584]{1,0:T(8,128)(2,1)S(1)}, bf16[32,3584]{1,0:T(8,128)(2,1)S(1)}, u32[]{:S(2)}, u32[]{:S(2)}) collective-permute-start(bf16[32,3584]{1,0:T(8,128)(2,1)S(1)} %get-tuple-element.82), channel_id=1, source_target_pairs={{0,4},{1,5},{2,6},{3,7},{4,0},{5,1},{6,2},{7,3},{8,12},{9,13},{10,... | collective-permute-start | bytes 688136 | tf_op jit(solution)/shard_map/ppermute | solution.py:37
  66.0 15.4 %collective-permute-start.17 = (bf16[32,3584]{1,0:T(8,128)(2,1)S(1)}, bf16[32,3584]{1,0:T(8,128)(2,1)S(1)}, u32[]{:S(2)}, u32[]{:S(2)}) collective-permute-start(bf16[32,3584]{1,0:T(8,128)(2,1)S(1)} %get-tuple-element.83), channel_id=1, source_target_pairs={{0,2},{1,3},{2,4},{3,5},{4,6},{5,7},{6,0},{7,1},{8,10},{9,11},{10,... | collective-permute-start | bytes 688136 | tf_op jit(solution)/shard_map/ppermute | solution.py:37
  66.3 15.1 %collective-permute-start.18 = (bf16[32,3584]{1,0:T(8,128)(2,1)S(1)}, bf16[32,3584]{1,0:T(8,128)(2,1)S(1)}, u32[]{:S(2)}, u32[]{:S(2)}) collective-permute-start(bf16[32,3584]{1,0:T(8,128)(2,1)S(1)} %get-tuple-element.84), channel_id=1, source_target_pairs={{0,6},{1,7},{2,0},{3,1},{4,2},{5,3},{6,4},{7,5},{8,14},{9,15},{10,... | collective-permute-start | bytes 688136 | tf_op jit(solution)/shard_map/ppermute | solution.py:37
  70.1 11.9 %collective-permute-start.14 = (bf16[32,2560]{1,0:T(8,128)(2,1)S(1)}, bf16[32,2560]{1,0:T(8,128)(2,1)S(1)}, u32[]{:S(2)}, u32[]{:S(2)}) collective-permute-start(bf16[32,2560]{1,0:T(8,128)(2,1)S(1)} %get-tuple-element.79), channel_id=1, source_target_pairs={{0,8},{1,9},{2,10},{3,11},{4,12},{5,13},{6,14},{7,15},{8,0},{9,1},... | collective-permute-start | bytes 491528 | tf_op jit(solution)/shard_map/ppermute | solution.py:37
  71.4 10.6 %collective-permute-start.15 = (bf16[32,2048]{1,0:T(8,128)(2,1)S(1)}, bf16[32,2048]{1,0:T(8,128)(2,1)S(1)}, u32[]{:S(2)}, u32[]{:S(2)}) collective-permute-start(bf16[32,2048]{1,0:T(8,128)(2,1)S(1)} %get-tuple-element.80), channel_id=1, source_target_pairs={{0,8},{1,9},{2,10},{3,11},{4,12},{5,13},{6,14},{7,15},{8,0},{9,1},... | collective-permute-start | bytes 393224 | tf_op jit(solution)/shard_map/ppermute | solution.py:37
  82.0 1.0 %copy-start.5 = (bf16[32,8192]{1,0:T(8,128)(2,1)S(1)}, bf16[32,8192]{1,0:T(8,128)(2,1)}, u32[]{:S(2)}) copy-start(bf16[32,8192]{1,0:T(8,128)(2,1)} %refs_0_.9) | copy-start | bytes 1572868
